TPU v7x, 512 devices: a whole 4x8x8 slice. The times are simulated.
512 devices in a mesh: macro: 16 (over z, core), krow: 32 (over x, y).
Axes of the slice: x: 4, y: 8, z: 8, core: 2. Of those that a mesh axis runs over, the one named last changes fastest.
Arguments:
- density: float32 [16, 16, 256, 256], P('macro', None, 'krow'), may hold values from -4 to 4
- energies: float32 [4, 256, 256], P(None, 'krow'), may hold values from -2 to 2
- momentum: float32 [2, 16, 256, 256], P(None, None, 'krow'), may hold values from -6 to 6
- emitted: float32 [16, 2], P('macro'), may hold values from -4 to 4
- drive: float32 [3, 2], replicated, may hold values from -3 to 3
Outputs:
- density_next: float32 [16, 16, 256, 256], P('macro', None, 'krow')
- emitted_next: float32 [16, 2], P('macro')
All inputs are finite; a program needn't handle non-finite values.
Results may differ from a plain program's by a relative error of at most 0.00011.
Values sent between devices are 32-bit elements; how exact they have to be, the bound alone decides.
No kernel may reach another device: no remote copies, remote signals or barrier semaphores. Data moves between devices by JAX's collectives and lax.ppermute only.
A program may use at most 64 MiB of HBM per device.

v0:
```python
import math

import jax
import jax.numpy as jnp
from jax import lax
from jax.sharding import PartitionSpec as P

BANDS = 4


dephasing = 0.2
coulomb_strength = 0.25
coupling = 2.0
time_step = 0.1
screening_width = 1.0


def entering(part, axis, combine, identity):
    place = lax.axis_index(axis)
    gathered = lax.all_gather(part, axis)
    state = jnp.zeros_like(part) + jnp.asarray(identity, part.dtype)

    def one(lap, state):
        return combine(state, lax.dynamic_index_in_dim(gathered, lap, 0, False))

    return lax.fori_loop(0, place, one, state)


def upper_pairs():
    return [
        (row_band, col_band) for row_band in range(BANDS) for col_band in range(row_band + 1, BANDS)
    ]


def unpack(channels):
    pairs = upper_pairs()
    pair_count = len(pairs)
    nothing = jnp.zeros_like(channels[0])
    real_part = [[None] * BANDS for counter in range(BANDS)]
    imag_part = [[None] * BANDS for counter in range(BANDS)]
    for band_index in range(BANDS):
        real_part[band_index][band_index] = channels[band_index]
        imag_part[band_index][band_index] = nothing
    for position, (row_band, col_band) in enumerate(pairs):
        real_value = channels[BANDS + position]
        imag_value = channels[BANDS + pair_count + position]
        real_part[row_band][col_band] = real_value
        real_part[col_band][row_band] = real_value
        imag_part[row_band][col_band] = imag_value
        imag_part[col_band][row_band] = -imag_value
    return (real_part, imag_part)


def commute(hamilton, channels):
    left_real, left_imag = unpack(hamilton)
    right_real, right_imag = unpack(channels)

    def bracket_entry(row_band, col_band):
        bracket_real = 0.0
        bracket_imag = 0.0
        for middle in range(BANDS):
            bracket_real = (
                bracket_real
                + left_real[row_band][middle] * right_real[middle][col_band]
                - left_imag[row_band][middle] * right_imag[middle][col_band]
                - right_real[row_band][middle] * left_real[middle][col_band]
                + right_imag[row_band][middle] * left_imag[middle][col_band]
            )
            bracket_imag = (
                bracket_imag
                + left_real[row_band][middle] * right_imag[middle][col_band]
                + left_imag[row_band][middle] * right_real[middle][col_band]
                - right_real[row_band][middle] * left_imag[middle][col_band]
                - right_imag[row_band][middle] * left_real[middle][col_band]
            )
        return (bracket_real, bracket_imag)

    diagonal_rates = [bracket_entry(band_index, band_index)[1] for band_index in range(BANDS)]
    upper_real = []
    upper_imag = []
    for row_band, col_band in upper_pairs():
        bracket_real, bracket_imag = bracket_entry(row_band, col_band)
        upper_real.append(bracket_imag)
        upper_imag.append(-bracket_real)
    return diagonal_rates + upper_real + upper_imag


def coulomb_kernel(grid_size):
    offsets = jnp.arange(grid_size, dtype=jnp.int32)
    periodic = jnp.minimum(offsets, grid_size - offsets).astype(jnp.float32)
    squared = (
        periodic[:, None] * periodic[:, None]
        + periodic[None, :] * periodic[None, :]
        + screening_width * screening_width
    )
    kernel = coulomb_strength / jnp.sqrt(squared)
    return kernel - jnp.mean(kernel)


def dft_tables(grid_size):
    positions = jnp.arange(grid_size, dtype=jnp.int32)
    product = positions[:, None] * positions[None, :] % grid_size
    angles = product.astype(jnp.float32) * (2.0 * math.pi / grid_size)
    return (jnp.cos(angles), jnp.sin(angles))


def add_pair(earlier, later):
    return earlier + later


def split_channels(stacked):
    return [stacked[:, channel] for channel in range(stacked.shape[1])]


def per_device(density, energies, momentum, emitted, drive):
    points, channel_count, local_rows, grid_size = density.shape
    half_channels = channel_count // 2
    devices_row = lax.axis_size("krow")
    local_columns = grid_size // devices_row
    highest = lax.Precision.HIGHEST
    cosine_table, sine_table = dft_tables(grid_size)
    both_tables = jnp.concatenate([cosine_table, sine_table], axis=1)
    stacked_tables = jnp.concatenate([cosine_table, sine_table], axis=0)
    column_start = lax.axis_index("krow") * local_columns
    cosine_columns = lax.dynamic_slice_in_dim(cosine_table, column_start, local_columns, 1)
    sine_columns = lax.dynamic_slice_in_dim(sine_table, column_start, local_columns, 1)
    kernel = coulomb_kernel(grid_size)
    kernel_hat = jnp.dot(
        cosine_table, jnp.dot(kernel, cosine_columns, precision=highest), precision=highest
    ) - jnp.dot(sine_table, jnp.dot(kernel, sine_columns, precision=highest), precision=highest)
    weights = jnp.concatenate(
        [jnp.ones((BANDS,), jnp.float32), 2.0 * jnp.ones((channel_count - BANDS,), jnp.float32)]
    )
    off_diagonal = jnp.concatenate(
        [jnp.zeros((BANDS,), jnp.float32), jnp.ones((channel_count - BANDS,), jnp.float32)]
    )
    energy_full = jnp.concatenate(
        [energies, jnp.zeros((channel_count - BANDS, local_rows, grid_size), jnp.float32)], axis=0
    )
    weighted = momentum * weights[None, :, None, None]
    fractions = (0.0, 0.5, 0.5, 1.0)
    drive_rows = (0, 1, 1, 2)
    factors = (1.0, 2.0, 2.0, 1.0)
    rho_sum = jnp.zeros_like(density)
    emitted_sum = jnp.zeros_like(emitted)
    rho_rate = None
    emitted_rate = None
    for section in range(4):
        if section == 0:
            section_density = density
            section_emitted = emitted
        else:
            section_density = density + time_step * fractions[section] * rho_rate
            section_emitted = emitted + time_step * fractions[section] * emitted_rate
        partial_current = (
            jnp.einsum("icrk,pcrk->pi", weighted, section_density, precision=highest) / grid_size
        )
        totals = lax.psum(partial_current, "krow")
        group_total = jnp.sum(totals, axis=0)
        before = entering(group_total, "macro", add_pair, jnp.zeros_like(group_total))
        rates_emitted_rate = -coupling * (
            before[None, :] + jnp.cumsum(totals, axis=0) - 0.5 * totals
        )
        potential = drive[drive_rows[section]][None, :] + section_emitted
        hamilton = (
            energy_full[None]
            + potential[:, 0, None, None, None] * momentum[0][None]
            + potential[:, 1, None, None, None] * momentum[1][None]
        )
        real_in = section_density[0, :half_channels]
        block_count = real_in.shape[0]
        products = jnp.einsum(
            "nrk,kf->nrf",
            jnp.concatenate([real_in, section_density[0, half_channels:]], axis=0),
            both_tables,
            precision=highest,
        )
        convolve_spectrum_real = (
            products[:block_count, :, :grid_size] + products[block_count:, :, grid_size:]
        )
        convolve_spectrum_imag = (
            products[block_count:, :, :grid_size] - products[:block_count, :, grid_size:]
        )
        spectrum_real = lax.all_to_all(
            convolve_spectrum_real, "krow", split_axis=2, concat_axis=1, tiled=True
        )
        spectrum_imag = lax.all_to_all(
            convolve_spectrum_imag, "krow", split_axis=2, concat_axis=1, tiled=True
        )
        real_products = jnp.einsum("sr,crf->csf", stacked_tables, spectrum_real, precision=highest)
        imag_products = jnp.einsum("sr,crf->csf", stacked_tables, spectrum_imag, precision=highest)
        forward_real = (real_products[:, :grid_size] + imag_products[:, grid_size:]) * kernel_hat[
            None
        ]
        forward_imag = (imag_products[:, :grid_size] - real_products[:, grid_size:]) * kernel_hat[
            None
        ]
        real_products = jnp.einsum("sr,crf->csf", stacked_tables, forward_real, precision=highest)
        imag_products = jnp.einsum("sr,crf->csf", stacked_tables, forward_imag, precision=highest)
        inverse_real = real_products[:, :grid_size] - imag_products[:, grid_size:]
        inverse_imag = imag_products[:, :grid_size] + real_products[:, grid_size:]
        mixed_real = lax.all_to_all(inverse_real, "krow", split_axis=1, concat_axis=2, tiled=True)
        mixed_imag = lax.all_to_all(inverse_imag, "krow", split_axis=1, concat_axis=2, tiled=True)
        products = jnp.einsum(
            "nrk,kf->nrf",
            jnp.concatenate([mixed_real, mixed_imag], axis=0),
            both_tables,
            precision=highest,
        )
        normalize = 1.0 / (grid_size * grid_size)
        out_real = (
            products[:block_count, :, :grid_size] - products[block_count:, :, grid_size:]
        ) * normalize
        out_imag = (
            products[block_count:, :, :grid_size] + products[:block_count, :, grid_size:]
        ) * normalize
        point_results = [jnp.concatenate([out_real, out_imag], axis=0)]
        sigma = -jnp.stack(point_results, axis=0)
        channels = split_channels(section_density)
        local_rates = jnp.stack(commute(split_channels(hamilton), channels), axis=1)
        coulomb_rates = jnp.stack(commute(split_channels(sigma), channels), axis=1)
        rates_rho_rate = (
            local_rates
            + coulomb_rates
            - dephasing * off_diagonal[None, :, None, None] * section_density
        )
        rho_rate = rates_rho_rate
        emitted_rate = rates_emitted_rate
        rho_sum = rho_sum + factors[section] * rho_rate
        emitted_sum = emitted_sum + factors[section] * emitted_rate
    return (density + time_step / 6.0 * rho_sum, emitted + time_step / 6.0 * emitted_sum)


def solution(mesh):
    in_specs = (
        P("macro", None, "krow", None),
        P(None, "krow", None),
        P(None, None, "krow", None),
        P("macro", None),
        P(),
    )
    out_specs = (P("macro", None, "krow", None), P("macro", None))
    return jax.shard_map(
        per_device, mesh=mesh, in_specs=in_specs, out_specs=out_specs, check_vma=False
    )
```

profile of v0, /device:TPU:8, one launch (start us, length us, event | category | flops | bytes accessed | tf_op | source)
XLA Modules:
  0.0 526.8 jit_solution(6710661110099280466)
XLA Ops:
  3.7 10.2 %all-to-all-start = ((f32[32,1,512]{2,1,0:T(1,128)}), f32[32,1,512]{2,1,0:T(1,128)S(1)}, u32[]{:S(2)}, u32[]{:S(2)}) async-start(f32[32,1,512]{2,1,0:T(1,128)} %reshape.11277), calls=%async_computation | async-start | bytes 131072 | tf_op jit(solution)/shard_map/all_to_all | solution.py:184
  25.7 10.2 %all-to-all-start.1 = ((f32[32,1,512]{2,1,0:T(1,128)}), f32[32,1,512]{2,1,0:T(1,128)S(1)}, u32[]{:S(2)}, u32[]{:S(2)}) async-start(f32[32,1,512]{2,1,0:T(1,128)} %reshape.11275), calls=%async_computation.1 | async-start | bytes 131072 | tf_op jit(solution)/shard_map/all_to_all | solution.py:187
  57.2 7.6 %all-to-all-done.2 = f32[32,1,512]{2,1,0:T(1,128)S(1)} async-done(((f32[32,1,512]{2,1,0:T(1,128)}), f32[32,1,512]{2,1,0:T(1,128)S(1)}, u32[]{:S(2)}, u32[]{:S(2)}) %all-to-all-start.2) | async-done | bytes 65568 | tf_op jit(solution)/shard_map/all_to_all | solution.py:202
  64.8 6.0 %all-to-all-start.3 = ((f32[32,1,512]{2,1,0:T(1,128)}), f32[32,1,512]{2,1,0:T(1,128)}, u32[]{:S(2)}, u32[]{:S(2)}) async-start(f32[32,1,512]{2,1,0:T(1,128)} %reshape.11279), calls=%async_computation.3 | async-start | bytes 131072 | tf_op jit(solution)/shard_map/all_to_all | solution.py:203
  88.1 70.7 %all-reduce.2 = (f32[1,2]{1,0:T(1,128)S(1)}, f32[1,2]{1,0:T(1,128)S(1)}) all-reduce(f32[1,2]{1,0:T(1,128)S(1)} %fusion.7, f32[1,2]{1,0:T(1,128)S(1)} %fusion.5), channel_id=1, replica_groups=mesh['macro'=16,'krow'=32] {'krow'}, use_global_device_ids=true, to_apply=%region_1.2 | all-reduce | flops 4 | bytes 32 | tf_op jit(solution)/shard_map/psum | solution.py:158
  158.8 23.1 %all-gather.1 = f32[16,1,2]{2,1,0:T(1,128)S(1)} all-gather(f32[1,1,2]{2,1,0:T(1,128)S(1)} %bitcast.414), channel_id=1, replica_groups=mesh['macro'=16,'krow'=32] {'macro'}, dimensions={0}, use_global_device_ids=true | all-gather | bytes 136 | tf_op jit(solution)/shard_map/all_gather | solution.py:20
  181.9 14.3 %all-gather = f32[16,1,2]{2,1,0:T(1,128)S(1)} all-gather(f32[1,1,2]{2,1,0:T(1,128)S(1)} %bitcast.413), channel_id=1, replica_groups=mesh['macro'=16,'krow'=32] {'macro'}, dimensions={0}, use_global_device_ids=true | all-gather | bytes 136 | tf_op jit(solution)/shard_map/all_gather | solution.py:20
  209.9 7.7 %all-to-all-done.4 = f32[32,1,512]{2,1,0:T(1,128)S(1)} async-done(((f32[32,1,512]{2,1,0:T(1,128)}), f32[32,1,512]{2,1,0:T(1,128)S(1)}, u32[]{:S(2)}, u32[]{:S(2)}) %all-to-all-start.4) | async-done | bytes 65568 | tf_op jit(solution)/shard_map/all_to_all | solution.py:184
  217.7 5.5 %all-to-all-start.5 = ((f32[32,1,512]{2,1,0:T(1,128)}), f32[32,1,512]{2,1,0:T(1,128)}, u32[]{:S(2)}, u32[]{:S(2)}) async-start(f32[32,1,512]{2,1,0:T(1,128)} %reshape.11283), calls=%async_computation.5 | async-start | bytes 131072 | tf_op jit(solution)/shard_map/all_to_all | solution.py:187
  246.3 7.0 %all-to-all-done.6 = f32[32,1,512]{2,1,0:T(1,128)S(1)} async-done(((f32[32,1,512]{2,1,0:T(1,128)}), f32[32,1,512]{2,1,0:T(1,128)S(1)}, u32[]{:S(2)}, u32[]{:S(2)}) %all-to-all-start.6) | async-done | bytes 65568 | tf_op jit(solution)/shard_map/all_to_all | solution.py:202
  253.3 5.7 %all-to-all-start.7 = ((f32[32,1,512]{2,1,0:T(1,128)}), f32[32,1,512]{2,1,0:T(1,128)}, u32[]{:S(2)}, u32[]{:S(2)}) async-start(f32[32,1,512]{2,1,0:T(1,128)} %reshape.11287), calls=%async_computation.7 | async-start | bytes 131072 | tf_op jit(solution)/shard_map/all_to_all | solution.py:203
  262.2 5.9 %all-to-all-done.7 = f32[32,1,512]{2,1,0:T(1,128)} async-done(((f32[32,1,512]{2,1,0:T(1,128)}), f32[32,1,512]{2,1,0:T(1,128)}, u32[]{:S(2)}, u32[]{:S(2)}) %all-to-all-start.7) | async-done | bytes 65568 | tf_op jit(solution)/shard_map/all_to_all | solution.py:203
  282.6 7.6 %all-to-all-done.8 = f32[32,1,512]{2,1,0:T(1,128)S(1)} async-done(((f32[32,1,512]{2,1,0:T(1,128)}), f32[32,1,512]{2,1,0:T(1,128)S(1)}, u32[]{:S(2)}, u32[]{:S(2)}) %all-to-all-start.8) | async-done | bytes 65568 | tf_op jit(solution)/shard_map/all_to_all | solution.py:184
  290.2 5.7 %all-to-all-start.9 = ((f32[32,1,512]{2,1,0:T(1,128)}), f32[32,1,512]{2,1,0:T(1,128)}, u32[]{:S(2)}, u32[]{:S(2)}) async-start(f32[32,1,512]{2,1,0:T(1,128)} %reshape.11291), calls=%async_computation.9 | async-start | bytes 131072 | tf_op jit(solution)/shard_map/all_to_all | solution.py:187
  318.6 7.5 %all-to-all-done.10 = f32[32,1,512]{2,1,0:T(1,128)S(1)} async-done(((f32[32,1,512]{2,1,0:T(1,128)}), f32[32,1,512]{2,1,0:T(1,128)S(1)}, u32[]{:S(2)}, u32[]{:S(2)}) %all-to-all-start.10) | async-done | bytes 65568 | tf_op jit(solution)/shard_map/all_to_all | solution.py:202
  326.1 5.9 %all-to-all-start.11 = ((f32[32,1,512]{2,1,0:T(1,128)}), f32[32,1,512]{2,1,0:T(1,128)}, u32[]{:S(2)}, u32[]{:S(2)}) async-start(f32[32,1,512]{2,1,0:T(1,128)} %reshape.11295), calls=%async_computation.11 | async-start | bytes 131072 | tf_op jit(solution)/shard_map/all_to_all | solution.py:203
  350.6 70.7 %all-reduce.1 = (f32[1,2]{1,0:T(1,128)S(1)}, f32[1,2]{1,0:T(1,128)S(1)}) all-reduce(f32[1,2]{1,0:T(1,128)S(1)} %copy-done.41, f32[1,2]{1,0:T(1,128)S(1)} %fusion.1), channel_id=1, replica_groups=mesh['macro'=16,'krow'=32] {'krow'}, use_global_device_ids=true, to_apply=%region_7.8 | all-reduce | flops 4 | bytes 32 | tf_op jit(solution)/shard_map/psum | solution.py:158
  421.3 16.2 %all-gather.3 = f32[16,1,2]{2,1,0:T(1,128)S(1)} all-gather(f32[1,1,2]{2,1,0:T(1,128)S(1)} %bitcast.416), channel_id=1, replica_groups=mesh['macro'=16,'krow'=32] {'macro'}, dimensions={0}, use_global_device_ids=true | all-gather | bytes 136 | tf_op jit(solution)/shard_map/all_gather | solution.py:20
  437.5 14.3 %all-gather.2 = f32[16,1,2]{2,1,0:T(1,128)S(1)} all-gather(f32[1,1,2]{2,1,0:T(1,128)S(1)} %bitcast.415), channel_id=1, replica_groups=mesh['macro'=16,'krow'=32] {'macro'}, dimensions={0}, use_global_device_ids=true | all-gather | bytes 136 | tf_op jit(solution)/shard_map/all_gather | solution.py:20
  464.0 7.7 %all-to-all-done.12 = f32[32,1,512]{2,1,0:T(1,128)S(1)} async-done(((f32[32,1,512]{2,1,0:T(1,128)}), f32[32,1,512]{2,1,0:T(1,128)S(1)}, u32[]{:S(2)}, u32[]{:S(2)}) %all-to-all-start.12) | async-done | bytes 65568 | tf_op jit(solution)/shard_map/all_to_all | solution.py:184
  471.8 5.6 %all-to-all-start.13 = ((f32[32,1,512]{2,1,0:T(1,128)}), f32[32,1,512]{2,1,0:T(1,128)}, u32[]{:S(2)}, u32[]{:S(2)}) async-start(f32[32,1,512]{2,1,0:T(1,128)} %reshape.11299), calls=%async_computation.13 | async-start | bytes 131072 | tf_op jit(solution)/shard_map/all_to_all | solution.py:187
  480.5 5.9 %all-to-all-done.13 = f32[32,1,512]{2,1,0:T(1,128)} async-done(((f32[32,1,512]{2,1,0:T(1,128)}), f32[32,1,512]{2,1,0:T(1,128)}, u32[]{:S(2)}, u32[]{:S(2)}) %all-to-all-start.13) | async-done | bytes 65568 | tf_op jit(solution)/shard_map/all_to_all | solution.py:187
  500.1 7.0 %all-to-all-done.14 = f32[32,1,512]{2,1,0:T(1,128)S(1)} async-done(((f32[32,1,512]{2,1,0:T(1,128)}), f32[32,1,512]{2,1,0:T(1,128)S(1)}, u32[]{:S(2)}, u32[]{:S(2)}) %all-to-all-start.14) | async-done | bytes 65568 | tf_op jit(solution)/shard_map/all_to_all | solution.py:202
  515.4 5.9 %all-to-all-done.15 = f32[32,1,512]{2,1,0:T(1,128)S(1)} async-done(((f32[32,1,512]{2,1,0:T(1,128)}), f32[32,1,512]{2,1,0:T(1,128)S(1)}, u32[]{:S(2)}, u32[]{:S(2)}) %all-to-all-start.15) | async-done | bytes 65568 | tf_op jit(solution)/shard_map/all_to_all | solution.py:203
  (404 shorter events, 189.7 us)
Async XLA Ops:
  3.7 22.0 %all-to-all-start = ((f32[32,1,512]{2,1,0:T(1,128)}), f32[32,1,512]{2,1,0:T(1,128)S(1)}, u32[]{:S(2)}, u32[]{:S(2)}) async-start(f32[32,1,512]{2,1,0:T(1,128)} %reshape.11277), calls=%async_computation | async-start | bytes 131072 | tf_op jit(solution)/shard_map/all_to_all | solution.py:184
  25.7 19.2 %all-to-all-start.1 = ((f32[32,1,512]{2,1,0:T(1,128)}), f32[32,1,512]{2,1,0:T(1,128)S(1)}, u32[]{:S(2)}, u32[]{:S(2)}) async-start(f32[32,1,512]{2,1,0:T(1,128)} %reshape.11275), calls=%async_computation.1 | async-start | bytes 131072 | tf_op jit(solution)/shard_map/all_to_all | solution.py:187
  50.9 13.9 %all-to-all-start.2 = ((f32[32,1,512]{2,1,0:T(1,128)}), f32[32,1,512]{2,1,0:T(1,128)S(1)}, u32[]{:S(2)}, u32[]{:S(2)}) async-start(f32[32,1,512]{2,1,0:T(1,128)} %reshape.11281), calls=%async_computation.2 | async-start | bytes 131072 | tf_op jit(solution)/shard_map/all_to_all | solution.py:202
  56.0 14.8 %copy-start.21 = (f32[2,16,8,256]{3,2,1,0:T(8,128)S(1)}, f32[2,16,8,256]{3,2,1,0:T(8,128)}, u32[]{:S(2)}) copy-start(f32[2,16,8,256]{3,2,1,0:T(8,128)} %broadcast_multiply_fusion) | copy-start | bytes 786436
  64.8 15.1 %all-to-all-start.3 = ((f32[32,1,512]{2,1,0:T(1,128)}), f32[32,1,512]{2,1,0:T(1,128)}, u32[]{:S(2)}, u32[]{:S(2)}) async-start(f32[32,1,512]{2,1,0:T(1,128)} %reshape.11279), calls=%async_computation.3 | async-start | bytes 131072 | tf_op jit(solution)/shard_map/all_to_all | solution.py:203
  158.8 37.4 %copy-start.31 = (f32[1,2]{1,0:T(1,128)}, f32[1,2]{1,0:T(1,128)S(1)}, u32[]{:S(2)}) copy-start(f32[1,2]{1,0:T(1,128)S(1)} %get-tuple-element.196) | copy-start | bytes 28
  158.8 37.4 %copy-start.33 = (f32[1,2]{1,0:T(1,128)}, f32[1,2]{1,0:T(1,128)S(1)}, u32[]{:S(2)}) copy-start(f32[1,2]{1,0:T(1,128)S(1)} %get-tuple-element.197) | copy-start | bytes 28
  203.7 13.9 %all-to-all-start.4 = ((f32[32,1,512]{2,1,0:T(1,128)}), f32[32,1,512]{2,1,0:T(1,128)S(1)}, u32[]{:S(2)}, u32[]{:S(2)}) async-start(f32[32,1,512]{2,1,0:T(1,128)} %reshape.11285), calls=%async_computation.4 | async-start | bytes 131072 | tf_op jit(solution)/shard_map/all_to_all | solution.py:184
  209.9 14.1 %copy-start.4 = (f32[1,16,8,256]{3,2,1,0:T(8,128)}, f32[1,16,8,256]{3,2,1,0:T(8,128)S(1)}, u32[]{:S(2)}) copy-start(f32[1,16,8,256]{3,2,1,0:T(8,128)S(1)} %constant_dynamic-update-slice_fusion.34) | copy-start | bytes 393220
  217.7 14.7 %all-to-all-start.5 = ((f32[32,1,512]{2,1,0:T(1,128)}), f32[32,1,512]{2,1,0:T(1,128)}, u32[]{:S(2)}, u32[]{:S(2)}) async-start(f32[32,1,512]{2,1,0:T(1,128)} %reshape.11283), calls=%async_computation.5 | async-start | bytes 131072 | tf_op jit(solution)/shard_map/all_to_all | solution.py:187
  239.5 13.8 %all-to-all-start.6 = ((f32[32,1,512]{2,1,0:T(1,128)}), f32[32,1,512]{2,1,0:T(1,128)S(1)}, u32[]{:S(2)}, u32[]{:S(2)}) async-start(f32[32,1,512]{2,1,0:T(1,128)} %reshape.11289), calls=%async_computation.6 | async-start | bytes 131072 | tf_op jit(solution)/shard_map/all_to_all | solution.py:202
  253.3 14.8 %all-to-all-start.7 = ((f32[32,1,512]{2,1,0:T(1,128)}), f32[32,1,512]{2,1,0:T(1,128)}, u32[]{:S(2)}, u32[]{:S(2)}) async-start(f32[32,1,512]{2,1,0:T(1,128)} %reshape.11287), calls=%async_computation.7 | async-start | bytes 131072 | tf_op jit(solution)/shard_map/all_to_all | solution.py:203
  276.4 13.8 %all-to-all-start.8 = ((f32[32,1,512]{2,1,0:T(1,128)}), f32[32,1,512]{2,1,0:T(1,128)S(1)}, u32[]{:S(2)}, u32[]{:S(2)}) async-start(f32[32,1,512]{2,1,0:T(1,128)} %reshape.11293), calls=%async_computation.8 | async-start | bytes 131072 | tf_op jit(solution)/shard_map/all_to_all | solution.py:184
  282.6 14.2 %copy-start.9 = (f32[1,16,8,256]{3,2,1,0:T(8,128)}, f32[1,16,8,256]{3,2,1,0:T(8,128)S(1)}, u32[]{:S(2)}) copy-start(f32[1,16,8,256]{3,2,1,0:T(8,128)S(1)} %constant_dynamic-update-slice_fusion.65) | copy-start | bytes 393220
  290.2 14.8 %all-to-all-start.9 = ((f32[32,1,512]{2,1,0:T(1,128)}), f32[32,1,512]{2,1,0:T(1,128)}, u32[]{:S(2)}, u32[]{:S(2)}) async-start(f32[32,1,512]{2,1,0:T(1,128)} %reshape.11291), calls=%async_computation.9 | async-start | bytes 131072 | tf_op jit(solution)/shard_map/all_to_all | solution.py:187
  312.2 13.9 %all-to-all-start.10 = ((f32[32,1,512]{2,1,0:T(1,128)}), f32[32,1,512]{2,1,0:T(1,128)S(1)}, u32[]{:S(2)}, u32[]{:S(2)}) async-start(f32[32,1,512]{2,1,0:T(1,128)} %reshape.11297), calls=%async_computation.10 | async-start | bytes 131072 | tf_op jit(solution)/shard_map/all_to_all | solution.py:202
  317.0 28.8 %copy-start.11 = (f32[1,16,8,256]{3,2,1,0:T(8,128)}, f32[1,16,8,256]{3,2,1,0:T(8,128)S(1)}, u32[]{:S(2)}) copy-start(f32[1,16,8,256]{3,2,1,0:T(8,128)S(1)} %constant_dynamic-update-slice_fusion.64) | copy-start | bytes 393220
  317.4 14.6 %copy-start.22 = (f32[2,16,8,256]{3,2,1,0:T(8,128)S(1)}, f32[2,16,8,256]{3,2,1,0:T(8,128)}, u32[]{:S(2)}) copy-start(f32[2,16,8,256]{3,2,1,0:T(8,128)} %broadcast_multiply_fusion) | copy-start | bytes 786436
  326.1 15.0 %all-to-all-start.11 = ((f32[32,1,512]{2,1,0:T(1,128)}), f32[32,1,512]{2,1,0:T(1,128)}, u32[]{:S(2)}, u32[]{:S(2)}) async-start(f32[32,1,512]{2,1,0:T(1,128)} %reshape.11295), calls=%async_computation.11 | async-start | bytes 131072 | tf_op jit(solution)/shard_map/all_to_all | solution.py:203
  347.4 104.5 %copy-start.39 = (f32[1,2]{1,0:T(1,128)S(1)}, f32[1,2]{1,0:T(1,128)}, u32[]{:S(2)}) copy-start(f32[1,2]{1,0:T(1,128)} %copy.225) | copy-start | bytes 28
  457.4 14.4 %all-to-all-start.12 = ((f32[32,1,512]{2,1,0:T(1,128)}), f32[32,1,512]{2,1,0:T(1,128)S(1)}, u32[]{:S(2)}, u32[]{:S(2)}) async-start(f32[32,1,512]{2,1,0:T(1,128)} %reshape.11301), calls=%async_computation.12 | async-start | bytes 131072 | tf_op jit(solution)/shard_map/all_to_all | solution.py:184
  471.8 14.6 %all-to-all-start.13 = ((f32[32,1,512]{2,1,0:T(1,128)}), f32[32,1,512]{2,1,0:T(1,128)}, u32[]{:S(2)}, u32[]{:S(2)}) async-start(f32[32,1,512]{2,1,0:T(1,128)} %reshape.11299), calls=%async_computation.13 | async-start | bytes 131072 | tf_op jit(solution)/shard_map/all_to_all | solution.py:187
  493.2 13.9 %all-to-all-start.14 = ((f32[32,1,512]{2,1,0:T(1,128)}), f32[32,1,512]{2,1,0:T(1,128)S(1)}, u32[]{:S(2)}, u32[]{:S(2)}) async-start(f32[32,1,512]{2,1,0:T(1,128)} %reshape.11305), calls=%async_computation.14 | async-start | bytes 131072 | tf_op jit(solution)/shard_map/all_to_all | solution.py:202
  507.1 14.1 %all-to-all-start.15 = ((f32[32,1,512]{2,1,0:T(1,128)}), f32[32,1,512]{2,1,0:T(1,128)S(1)}, u32[]{:S(2)}, u32[]{:S(2)}) async-start(f32[32,1,512]{2,1,0:T(1,128)} %reshape.11303), calls=%async_computation.15 | async-start | bytes 131072 | tf_op jit(solution)/shard_map/all_to_all | solution.py:203
  (34 other events, 49.4 us)
where the time goes:
time: 535 us; the launch traced here: 527 us
  blocking collectives  209 us (39%)
  starting transfers between devices  92.9 us (17%)
  waiting for transfers between devices  92.6 us (17%)
  local copies, waits for them, and re-layouts  67.2 us (13%)
  other arithmetic  33.4 us (6%)
  matrix products  28.3 us (5%)
    psum x2, blocking collectives, per_device(): totals = lax.psum(partial_current, 'krow')  141 us
    all_gather x4, blocking collectives, entering(): gathered = lax.all_gather(part, axis)  68 us
    unnamed x119, local copies, waits for them, and re-layouts  38.8 us
    all_to_all x4, waiting for transfers between devices, per_device(): lax.all_to_all(inverse_real, 'krow', split_axis=1, concat_axis=2, tiled=T...  29.1 us
    all_to_all x4, starting transfers between devices, per_device(): lax.all_to_all(convolve_spectrum_imag, 'krow', split_axis=2, concat_axis=...  27 us
    all_to_all x4, starting transfers between devices, per_device(): lax.all_to_all(convolve_spectrum_real, 'krow', split_axis=2, concat_axis=...  24.4 us
    all_to_all x4, waiting for transfers between devices, per_device(): lax.all_to_all(convolve_spectrum_real, 'krow', split_axis=2, concat_axis=...  23.1 us
    all_to_all x4, starting transfers between devices, per_device(): lax.all_to_all(inverse_imag, 'krow', split_axis=1, concat_axis=2, tiled=T...  22.7 us
  transfers between devices with their start and end apart: 16, of which 16 were waited for; matrix products, arithmetic and copies ran while one was open for 9% of the time, Pallas kernels for 0%

commit v1 on v0

v1 whole, which is shorter than its diff:
```python
import functools

import jax
import jax.numpy as jnp
import numpy as np
from jax import lax
from jax.experimental import pallas as pl
from jax.experimental.pallas import tpu as pltpu
from jax.sharding import PartitionSpec as P

BANDS = 4
CHANNELS = 16
GRID = 256
ROWS = 8
LANES = 128
PEERS = 32
POINTS = 16

dephasing = 0.2
coulomb_strength = 0.25
coupling = 2.0
time_step = 0.1
screening_width = 1.0

PAIRS = [(a, b) for a in range(BANDS) for b in range(a + 1, BANDS)]


def coulomb_kernel():
    offsets = np.arange(GRID)
    periodic = np.minimum(offsets, GRID - offsets).astype(np.float64)
    squared = periodic[:, None] ** 2 + periodic[None, :] ** 2 + screening_width**2
    kernel = coulomb_strength / np.sqrt(squared)
    return kernel - np.mean(kernel)


def tables():
    positions = np.arange(GRID)
    angles = (positions[:, None] * positions[None, :] % GRID) * (2.0 * np.pi / GRID)
    basis = ((np.cos(angles) + np.sin(angles)) / np.sqrt(GRID)).astype(np.float32)
    high = basis.astype(jnp.bfloat16)
    low = (basis - high.astype(np.float32)).astype(jnp.bfloat16)
    spectrum = -np.real(np.fft.fft2(coulomb_kernel())).astype(np.float32)
    halves = np.stack([spectrum[:, :LANES], spectrum[:, LANES:]])
    return high, low, halves


def split(x):
    high = x.astype(jnp.bfloat16)
    low = (x - high.astype(jnp.float32)).astype(jnp.bfloat16)
    return high, low


def dot(a, b):
    return jnp.dot(a, b, preferred_element_type=jnp.float32)


def times_table(x, high_ref, low_ref):
    x_high, x_low = split(x)
    return dot(x_high, high_ref[...]) + (dot(x_low, high_ref[...]) + dot(x_high, low_ref[...]))


def table_times(y, high_ref, low_ref):
    y_high, y_low = split(y)
    return dot(high_ref[...], y_high) + (dot(high_ref[...], y_low) + dot(low_ref[...], y_high))


def send_rows(x, high_ref, low_ref, out_ref):
    spectra = times_table(x, high_ref, low_ref)
    for half in range(2):
        out_ref[:, half, :ROWS, :] = spectra[:, half * LANES : (half + 1) * LANES].reshape(
            CHANNELS, ROWS, LANES
        )


def first_kernel(density_ref, high_ref, low_ref, out_ref):
    send_rows(density_ref[...].reshape(CHANNELS * ROWS, GRID), high_ref, low_ref, out_ref)


def column_body(y, high_ref, low_ref, spectrum_ref):
    z = table_times(y, high_ref, low_ref) * spectrum_ref[...]
    return table_times(z, high_ref, low_ref)


def column_kernel(y_ref, high_ref, low_ref, spectrum_ref, out_ref):
    y = y_ref[...].reshape(GRID, LANES)
    w = column_body(y, high_ref, low_ref, spectrum_ref)
    out_ref[...] = w.reshape(PEERS, ROWS, LANES)


def column_carry_kernel(y_ref, carry_ref, high_ref, low_ref, spectrum_ref, out_ref):
    y = y_ref[:, :ROWS, :].reshape(GRID, LANES)
    w = column_body(y, high_ref, low_ref, spectrum_ref)
    out_ref[:, :ROWS, :] = w.reshape(PEERS, ROWS, LANES)
    out_ref[:, ROWS:, :] = jnp.broadcast_to(carry_ref[...][None], (PEERS, ROWS, LANES))


def unpack(channels):
    real = [[None] * BANDS for _ in range(BANDS)]
    imag = [[None] * BANDS for _ in range(BANDS)]
    for band in range(BANDS):
        real[band][band] = channels[band]
    for position, (a, b) in enumerate(PAIRS):
        real[a][b] = real[b][a] = channels[BANDS + position]
        value = channels[BANDS + len(PAIRS) + position]
        imag[a][b] = (value, 1)
        imag[b][a] = (value, -1)
    return real, imag


def signed_product(total, x, y, sign):
    term = x * y
    if total is None:
        return term if sign > 0 else -term
    return total + term if sign > 0 else total - term


def commute(hamilton, channels):
    hr, hi = unpack(hamilton)
    rr, ri = unpack(channels)

    def product(a, b):
        real = imag = None
        for m in range(BANDS):
            real = signed_product(real, hr[a][m], rr[m][b], 1)
            if hi[a][m] is not None and ri[m][b] is not None:
                real = signed_product(
                    real, hi[a][m][0], ri[m][b][0], -hi[a][m][1] * ri[m][b][1]
                )
            if ri[m][b] is not None:
                imag = signed_product(imag, hr[a][m], ri[m][b][0], ri[m][b][1])
            if hi[a][m] is not None:
                imag = signed_product(imag, hi[a][m][0], rr[m][b], hi[a][m][1])
        return real, imag

    diagonal = [2.0 * product(a, a)[1] for a in range(BANDS)]
    upper_real = []
    upper_imag = []
    for a, b in PAIRS:
        real_ab, imag_ab = product(a, b)
        real_ba, imag_ba = product(b, a)
        upper_real.append(imag_ab + imag_ba)
        upper_imag.append(real_ba - real_ab)
    return diagonal + upper_real + upper_imag


def state_kernel(section, *refs):
    refs = list(refs)
    back_ref, density_ref = refs.pop(0), refs.pop(0)
    state_refs = [density_ref] + [refs.pop(0) for _ in range(section)]
    energies_ref, momentum_ref, emitted_ref, drive_ref = (refs.pop(0) for _ in range(4))
    sums_ref = refs.pop(0) if section >= 2 else None
    high_ref, low_ref = refs.pop(0), refs.pop(0)
    out_ref = refs.pop(0)
    drive_row = (0, 1, 1, 2)[section]
    next_fraction = (0.5, 0.5, 1.0, None)[section]

    if section in (1, 3):
        arrived = jnp.sum(back_ref[:, :, ROWS:, :].reshape(PEERS, ROWS, LANES), axis=0)
        upstream = jnp.sum(arrived, axis=1, keepdims=True)
    if section >= 2:
        earlier = jnp.sum(sums_ref[...], axis=1, keepdims=True)
    rate_scale = -coupling / GRID
    if section == 0:
        shift = None
    elif section == 1:
        shift = [time_step * 0.5 * rate_scale * upstream[i : i + 1] for i in range(2)]
    elif section == 2:
        shift = [time_step * 0.5 * rate_scale * earlier[2 + i : 3 + i] for i in range(2)]
    else:
        shift = [time_step * rate_scale * upstream[i : i + 1] for i in range(2)]
    potential = []
    for i in range(2):
        value = drive_ref[drive_row : drive_row + 1, i : i + 1] + emitted_ref[:, i : i + 1]
        potential.append(value if shift is None else value + shift[i])

    spectra = jnp.concatenate(
        [back_ref[:, half, :ROWS, :].reshape(CHANNELS * ROWS, LANES) for half in range(2)], axis=1
    )
    sigma = times_table(spectra, high_ref, low_ref)

    state_ref = state_refs[-1]
    currents = {}
    new_rows = []
    for part in range(2):
        lanes = slice(part * LANES, (part + 1) * LANES)
        rho = [state_ref[c, :, lanes] for c in range(CHANNELS)]
        hamilton = []
        for c in range(CHANNELS):
            value = sigma[c * ROWS : (c + 1) * ROWS, lanes]
            value = value + potential[0] * momentum_ref[0, c, :, lanes]
            value = value + potential[1] * momentum_ref[1, c, :, lanes]
            if c < BANDS:
                value = value + energies_ref[c, :, lanes]
            hamilton.append(value)
        rates = commute(hamilton, rho)
        for c in range(CHANNELS):
            rate = rates[c] if c < BANDS else rates[c] - dephasing * rho[c]
            if section < 3:
                new = density_ref[c, :, lanes] + (time_step * next_fraction) * rate
                refs[0][c, :, lanes] = new
                if section in (0, 2):
                    weight = 1.0 if c < BANDS else 2.0
                    for i in range(2):
                        p = momentum_ref[i, c, :, lanes]
                        p = p if c < BANDS else weight * p
                        for which, value in ((0, rho[c]), (1, new)):
                            term = p * value
                            key = 2 * which + i
                            currents[key] = currents[key] + term if key in currents else term
            else:
                first, second, third, fourth = (r[c, :, lanes] for r in state_refs)
                base = (second + 2.0 * third + fourth - first) * (1.0 / 3.0)
                out_ref[c, :, lanes] = base + (time_step / 6.0) * rate

    if section < 3:
        state = refs[0][...].reshape(CHANNELS * ROWS, GRID)
        send_rows(state, high_ref, low_ref, out_ref)
    if section in (0, 2):
        tile = jnp.concatenate(
            [jnp.sum(currents[key], axis=0, keepdims=True) for key in range(4)]
            + [jnp.zeros((ROWS - 4, LANES), jnp.float32)],
            axis=0,
        )
        out_ref[:, :, ROWS:, :] = jnp.broadcast_to(tile, (CHANNELS, 2, ROWS, LANES))
    if section == 1:
        refs[1][...] = arrived
    if section == 3:
        for i in range(2):
            total = (
                earlier[i : i + 1]
                + 2.0 * earlier[2 + i : 3 + i]
                + 2.0 * upstream[i : i + 1]
                + upstream[2 + i : 3 + i]
            )
            refs[0][:, i : i + 1] = emitted_ref[:, i : i + 1] + (
                time_step / 6.0 * rate_scale
            ) * total


def call(body, outs, *args, flops=2 * 3 * 128 * 256 * 256):
    shapes = [jax.ShapeDtypeStruct(s, jnp.float32) for s in outs]
    vmem = pl.BlockSpec(memory_space=pltpu.VMEM)
    return pl.pallas_call(
        body,
        out_shape=shapes,
        in_specs=[vmem] * len(args),
        out_specs=[vmem] * len(outs),
        compiler_params=pltpu.CompilerParams(vmem_limit_bytes=24 * 1024 * 1024),
        cost_estimate=pl.CostEstimate(flops=flops, bytes_accessed=1 << 20, transcendentals=0),
    )(*args)


def swap(x):
    return lax.all_to_all(x, "krow", 0, 0, tiled=True)


def per_device(density, energies, momentum, emitted, drive):
    high_table, low_table, halves = tables()
    high, low = jnp.asarray(high_table), jnp.asarray(low_table)
    place = lax.axis_index("krow")
    spectrum = lax.dynamic_index_in_dim(jnp.asarray(halves), place % 2, 0, False)
    density = density.reshape(CHANNELS, ROWS, GRID)
    plain = (CHANNELS, 2, ROWS, LANES)
    carrying = (CHANNELS, 2, 2 * ROWS, LANES)
    state_shape = (CHANNELS, ROWS, GRID)
    downstream = [
        (m * PEERS + j, (m + j) * PEERS + j) for j in range(POINTS) for m in range(POINTS - j)
    ]
    own = jnp.where(place == 0, 0.5, 1.0)

    states = [density]
    sums = []
    (out,) = call(first_kernel, [plain], density, high, low)
    for section in range(4):
        carries = section in (1, 3)
        arrived = swap(out.reshape(PEERS, -1, LANES))
        if carries:
            totals = jnp.sum(arrived[:, ROWS:, :], axis=0) * own
            carry = lax.ppermute(totals, ("macro", "krow"), downstream)
            (mixed,) = call(
                column_carry_kernel, [arrived.shape], arrived, carry, high, low, spectrum
            )
        else:
            (mixed,) = call(column_kernel, [arrived.shape], arrived, high, low, spectrum)
        back = swap(mixed).reshape(CHANNELS, 2, -1, LANES)
        body = functools.partial(state_kernel, section)
        args = [back, *states, energies, momentum, emitted, drive, *sums, high, low]
        if section == 0 or section == 2:
            out, state = call(body, [carrying, state_shape], *args)
        elif section == 1:
            out, state, tile = call(body, [plain, state_shape, (ROWS, LANES)], *args)
            sums = [tile]
        else:
            density_next, emitted_next = call(body, [state_shape, (1, 2)], *args)
        if section < 3:
            states.append(state)
    return density_next.reshape(1, CHANNELS, ROWS, GRID), emitted_next


def solution(mesh):
    in_specs = (
        P("macro", None, "krow", None),
        P(None, "krow", None),
        P(None, None, "krow", None),
        P("macro", None),
        P(),
    )
    out_specs = (P("macro", None, "krow", None), P("macro", None))
    return jax.shard_map(
        per_device, mesh=mesh, in_specs=in_specs, out_specs=out_specs, check_vma=False
    )
```

time: 535 us -> 155 us (0.29); the launches traced: 527 us -> 154 us
  blocking collectives: 209 us -> 89.4 us
  starting transfers between devices: 92.9 us -> 21.7 us
  local copies, waits for them, and re-layouts: 67.2 us -> 2.85 us
  waiting for transfers between devices: 92.6 us -> 32.1 us
  other arithmetic: 33.4 us -> 0.08 us
  matrix products: 28.3 us -> 0 us
  Pallas kernels: 0 us -> 7.12 us
    psum x2 -> x0, blocking collectives: 141 us -> none  [per_device(): totals = lax.psum(partial_current, 'krow')]
    all_to_all x0 -> x5, blocking collectives: none -> 89.4 us  [swap(): return lax.all_to_all(x, 'krow', 0, 0, tiled=True)]
    all_to_all x16 -> x3, starting transfers between devices: 92.9 us -> 19.1 us  [swap(): return lax.all_to_all(x, 'krow', 0, 0, tiled=True)]
    all_gather x4 -> x0, blocking collectives: 68 us -> none  [entering(): gathered = lax.all_gather(part, axis)]
    all_to_all x16 -> x3, waiting for transfers between devices: 92.6 us -> 30.5 us  [swap(): return lax.all_to_all(x, 'krow', 0, 0, tiled=True)]
    unnamed x119 -> x23, local copies, waits for them, and re-layouts: 38.8 us -> 2.84 us
    dot_general x32 -> x0, matrix products: 28.3 us -> none  [the longest x4 10.4 us: per_device(): jnp.einsum('icrk,pcrk->pi', weighted, section_density, precision=highest)]
    all_to_all x33 -> x0, local copies, waits for them, and re-layouts: 19.4 us -> none  [the longest x8 5.18 us: per_device(): lax.all_to_all(inverse_real, 'krow', split_axis=1, concat_axis=2, tiled=T...]
  transfers between devices with their start and end apart: 16 -> 5, of which waited for: 16 -> 5; matrix products, arithmetic and copies ran while one was open for 9% -> 0% of each run, Pallas kernels for 0% -> 0%
where the time goes in v1:
time: 155 us; the launch traced here: 154 us
  blocking collectives  89.4 us (58%)
  waiting for transfers between devices  32.1 us (21%)
  starting transfers between devices  21.7 us (14%)
  Pallas kernels  7.12 us (5%)
  local copies, waits for them, and re-layouts  2.85 us (2%)
    all_to_all x5, blocking collectives, swap(): return lax.all_to_all(x, 'krow', 0, 0, tiled=True)  89.4 us
    all_to_all x3, waiting for transfers between devices, swap(): return lax.all_to_all(x, 'krow', 0, 0, tiled=True)  30.5 us
    all_to_all x3, starting transfers between devices, swap(): return lax.all_to_all(x, 'krow', 0, 0, tiled=True)  19.1 us
    pallas_call x9, Pallas kernels, call(): pl.pallas_call(body, out_shape=shapes, in_specs=[vmem] * len(args), out_s...  7.12 us
  transfers between devices with their start and end apart: 5, of which 5 were waited for; matrix products, arithmetic and copies ran while one was open for 0% of the time, Pallas kernels for 0%

profile of v1, /device:TPU:8, one launch (start us, length us, event | category | flops | bytes accessed | tf_op | source)
XLA Modules:
  0.0 154.1 jit_solution(16581745806223036299)
XLA Ops:
  0.6 0.9 copy-done
  1.5 0.9 copy-done.2
  2.4 0.9 copy-done.5
  3.3 0.9 shard_map.95
  4.2 10.3 %all-to-all-start = ((f32[32,8,128]{2,1,0:T(8,128)}), f32[32,8,128]{2,1,0:T(8,128)S(1)}, u32[]{:S(2)}, u32[]{:S(2)}) async-start(f32[32,8,128]{2,1,0:T(8,128)} %bitcast.1), calls=%async_computation | async-start | bytes 262144 | tf_op jit(solution)/shard_map/all_to_all | solution.py:254
  14.6 9.7 %all-to-all-done.y_ref = f32[32,8,128]{2,1,0:T(8,128)S(1)} async-done(((f32[32,8,128]{2,1,0:T(8,128)}), f32[32,8,128]{2,1,0:T(8,128)S(1)}, u32[]{:S(2)}, u32[]{:S(2)}) %all-to-all-start) | async-done | bytes 131104 | tf_op jit(solution)/shard_map/all_to_all | solution.py:254
  24.3 1.2 shard_map.96
  25.6 4.4 %all-to-all-start.1 = ((f32[32,8,128]{2,1,0:T(8,128)}), f32[32,8,128]{2,1,0:T(8,128)S(1)}, u32[]{:S(2)}, u32[]{:S(2)}) async-start(f32[32,8,128]{2,1,0:T(8,128)} %shard_map.96), calls=%async_computation.1 | async-start | bytes 262144 | tf_op jit(solution)/shard_map/all_to_all | solution.py:254
  30.1 9.6 %all-to-all-done.1 = f32[32,8,128]{2,1,0:T(8,128)S(1)} async-done(((f32[32,8,128]{2,1,0:T(8,128)}), f32[32,8,128]{2,1,0:T(8,128)S(1)}, u32[]{:S(2)}, u32[]{:S(2)}) %all-to-all-start.1) | async-done | bytes 131104 | tf_op jit(solution)/shard_map/all_to_all | solution.py:254
  39.7 1.3 shard_map.97
  41.0 4.5 %all-to-all-start.2 = ((f32[32,16,128]{2,1,0:T(8,128)}), f32[32,16,128]{2,1,0:T(8,128)S(1)}, u32[]{:S(2)}, u32[]{:S(2)}) async-start(f32[32,16,128]{2,1,0:T(8,128)} %bitcast.4), calls=%async_computation.2 | async-start | bytes 524288 | tf_op jit(solution)/shard_map/all_to_all | solution.py:254
  45.4 11.1 %all-to-all-done.2.y_ref = f32[32,16,128]{2,1,0:T(8,128)S(1)} async-done(((f32[32,16,128]{2,1,0:T(8,128)}), f32[32,16,128]{2,1,0:T(8,128)S(1)}, u32[]{:S(2)}, u32[]{:S(2)}) %all-to-all-start.2) | async-done | bytes 262176 | tf_op jit(solution)/shard_map/all_to_all | solution.py:254
  56.6 1.3 collective-permute-start
  57.9 0.8 collective-permute-done.carry_ref
  59.3 25.6 %all_to_all.40 = f32[32,16,128]{2,1,0:T(8,128)S(1)} all-to-all(f32[32,16,128]{2,1,0:T(8,128)S(1)} %shard_map.98), channel_id=1, replica_groups=mesh['macro'=16,'krow'=32] {'krow'}, dimensions={0} | all-to-all | bytes 524288 | tf_op jit(solution)/shard_map/all_to_all | solution.py:254
  85.4 14.0 %all_to_all.41.y_ref = f32[32,8,128]{2,1,0:T(8,128)S(1)} all-to-all(f32[32,8,128]{2,1,0:T(8,128)S(1)} %bitcast.22), channel_id=1, replica_groups=mesh['macro'=16,'krow'=32] {'krow'}, dimensions={0} | all-to-all | bytes 262144 | tf_op jit(solution)/shard_map/all_to_all | solution.py:254
  100.0 13.8 %all_to_all.42 = f32[32,8,128]{2,1,0:T(8,128)S(1)} all-to-all(f32[32,8,128]{2,1,0:T(8,128)S(1)} %shard_map.100), channel_id=1, replica_groups=mesh['macro'=16,'krow'=32] {'krow'}, dimensions={0} | all-to-all | bytes 262144 | tf_op jit(solution)/shard_map/all_to_all | solution.py:254
  113.9 0.6 shard_map.101
  114.4 15.2 %all_to_all.43.y_ref = f32[32,16,128]{2,1,0:T(8,128)S(1)} all-to-all(f32[32,16,128]{2,1,0:T(8,128)S(1)} %bitcast.21), channel_id=1, replica_groups=mesh['macro'=16,'krow'=32] {'krow'}, dimensions={0} | all-to-all | bytes 524288 | tf_op jit(solution)/shard_map/all_to_all | solution.py:254
  129.7 1.3 collective-permute-start.1
  131.0 0.8 collective-permute-done.1.carry_ref
  131.8 0.6 shard_map.102
  132.4 20.7 %all_to_all.44 = f32[32,16,128]{2,1,0:T(8,128)S(1)} all-to-all(f32[32,16,128]{2,1,0:T(8,128)S(1)} %shard_map.102), channel_id=1, replica_groups=mesh['macro'=16,'krow'=32] {'krow'}, dimensions={0} | all-to-all | bytes 524288 | tf_op jit(solution)/shard_map/all_to_all | solution.py:254
  153.0 1.0 shard_map.103
  (28 shorter events, 1.9 us)
Async XLA Ops:
  0.6 0.9 copy-start
  1.5 0.9 copy-start.2
  2.4 0.9 copy-start.5
  4.2 10.3 %copy-start.9 = (f32[2,256,128]{2,1,0:T(8,128)S(1)}, f32[2,256,128]{2,1,0:T(8,128)}, u32[]{:S(2)}) copy-start(f32[2,256,128]{2,1,0:T(8,128)} %constant.36.clone) | copy-start | bytes 786436
  4.2 20.1 %all-to-all-start = ((f32[32,8,128]{2,1,0:T(8,128)}), f32[32,8,128]{2,1,0:T(8,128)S(1)}, u32[]{:S(2)}, u32[]{:S(2)}) async-start(f32[32,8,128]{2,1,0:T(8,128)} %bitcast.1), calls=%async_computation | async-start | bytes 262144 | tf_op jit(solution)/shard_map/all_to_all | solution.py:254
  14.5 9.8 %copy-start.1 = (bf16[256,256]{1,0:T(8,128)(2,1)S(1)}, bf16[256,256]{1,0:T(8,128)(2,1)}, u32[]{:S(2)}) copy-start(bf16[256,256]{1,0:T(8,128)(2,1)} %constant.35.clone.low_ref.refs_7_.refs_8_.refs_10_.refs_11_) | copy-start | bytes 393220
  14.6 9.8 %copy-start.3 = (bf16[256,256]{1,0:T(8,128)(2,1)S(1)}, bf16[256,256]{1,0:T(8,128)(2,1)}, u32[]{:S(2)}) copy-start(bf16[256,256]{1,0:T(8,128)(2,1)} %constant.34.clone.high_ref.refs_6_.refs_7_.refs_9_.refs_10_) | copy-start | bytes 393220
  24.3 5.6 %copy-start.10 = (f32[3,2]{0,1:T(2,128)S(1)}, f32[3,2]{0,1:T(2,128)}, u32[]{:S(2)}) copy-start(f32[3,2]{0,1:T(2,128)} %param.12) | copy-start | bytes 76
  24.3 15.4 %copy-start.6 = (f32[1,16,8,256]{3,2,1,0:T(8,128)S(1)}, f32[1,16,8,256]{3,2,1,0:T(8,128)}, u32[]{:S(2)}) copy-start(f32[1,16,8,256]{3,2,1,0:T(8,128)} %param.8) | copy-start | bytes 393220
  24.3 15.4 %copy-start.7 = (f32[4,8,256]{2,1,0:T(8,128)S(1)}, f32[4,8,256]{2,1,0:T(8,128)}, u32[]{:S(2)}) copy-start(f32[4,8,256]{2,1,0:T(8,128)} %refs_5_.6) | copy-start | bytes 98308
  25.6 14.2 %copy-start.4 = (f32[2,16,8,256]{3,2,1,0:T(8,128)S(1)}, f32[2,16,8,256]{3,2,1,0:T(8,128)}, u32[]{:S(2)}) copy-start(f32[2,16,8,256]{3,2,1,0:T(8,128)} %refs_6_.5) | copy-start | bytes 786436
  25.6 14.1 %all-to-all-start.1 = ((f32[32,8,128]{2,1,0:T(8,128)}), f32[32,8,128]{2,1,0:T(8,128)S(1)}, u32[]{:S(2)}, u32[]{:S(2)}) async-start(f32[32,8,128]{2,1,0:T(8,128)} %shard_map.96), calls=%async_computation.1 | async-start | bytes 262144 | tf_op jit(solution)/shard_map/all_to_all | solution.py:254
  30.1 9.7 %copy-start.8 = (f32[1,2]{1,0:T(1,128)S(1)}, f32[1,2]{1,0:T(1,128)}, u32[]{:S(2)}) copy-start(f32[1,2]{1,0:T(1,128)} %refs_7_.4) | copy-start | bytes 28
  41.0 15.6 %all-to-all-start.2 = ((f32[32,16,128]{2,1,0:T(8,128)}), f32[32,16,128]{2,1,0:T(8,128)S(1)}, u32[]{:S(2)}, u32[]{:S(2)}) async-start(f32[32,16,128]{2,1,0:T(8,128)} %bitcast.4), calls=%async_computation.2 | async-start | bytes 524288 | tf_op jit(solution)/shard_map/all_to_all | solution.py:254
  56.6 2.1 %collective-permute-start = (f32[8,128]{1,0:T(8,128)S(1)}, f32[8,128]{1,0:T(8,128)S(1)}, u32[]{:S(2)}, u32[]{:S(2)}) collective-permute-start(f32[8,128]{1,0:T(8,128)S(1)} %broadcast_multiply_fusion.1), channel_id=1, source_target_pairs={{0,0},{32,32},{64,64},{96,96},{128,128},{160,160},{192,192},{224,2... | collective-permute-start | bytes 12296 | tf_op jit(solution)/shard_map/ppermute | solution.py:279
  129.7 2.1 %collective-permute-start.1 = (f32[8,128]{1,0:T(8,128)S(1)}, f32[8,128]{1,0:T(8,128)S(1)}, u32[]{:S(2)}, u32[]{:S(2)}) collective-permute-start(f32[8,128]{1,0:T(8,128)S(1)} %broadcast_multiply_fusion), channel_id=1, source_target_pairs={{0,0},{32,32},{64,64},{96,96},{128,128},{160,160},{192,192},{224,2... | collective-permute-start | bytes 12296 | tf_op jit(solution)/shard_map/ppermute | solution.py:279

commit v2 on v1

--- a/solution.py
+++ b/solution.py
@@ -72,8 +72,40 @@
         )
 
 
-def first_kernel(density_ref, high_ref, low_ref, out_ref):
+def add_currents(currents, key, c, momentum, value):
+    for i in range(2):
+        term = momentum[i] * value
+        term = term if c < BANDS else 2.0 * term
+        currents[key, i] = currents[key, i] + term if (key, i) in currents else term
+
+
+def currents_tile(currents, rows):
+    parts = [jnp.sum(currents[key], axis=0, keepdims=True) for key in sorted(currents)]
+    return jnp.concatenate(
+        parts + [jnp.zeros((rows - len(parts), LANES), jnp.float32)], axis=0
+    )
+
+
+def first_kernel(*refs):
+    sources, (out_ref, tile_ref), fetched, sems = refs[:4], refs[4:6], refs[6:10], refs[10]
+    copies = [
+        pltpu.make_async_copy(source, target, sems.at[n])
+        for n, (source, target) in enumerate(zip(sources, fetched))
+    ]
+    for copy in copies:
+        copy.start()
+    density_ref, high_ref, low_ref, momentum_ref = fetched
+    for copy in copies[:3]:
+        copy.wait()
     send_rows(density_ref[...].reshape(CHANNELS * ROWS, GRID), high_ref, low_ref, out_ref)
+    copies[3].wait()
+    currents = {}
+    for part in range(2):
+        lanes = slice(part * LANES, (part + 1) * LANES)
+        for c in range(CHANNELS):
+            momentum = [momentum_ref[i, c, :, lanes] for i in range(2)]
+            add_currents(currents, 0, c, momentum, density_ref[c, :, lanes])
+    tile_ref[...] = currents_tile(currents, LANES)
 
 
 def column_body(y, high_ref, low_ref, spectrum_ref):
@@ -87,11 +119,15 @@
     out_ref[...] = w.reshape(PEERS, ROWS, LANES)
 
 
-def column_carry_kernel(y_ref, carry_ref, high_ref, low_ref, spectrum_ref, out_ref):
+def column_carry_kernel(y_ref, *refs):
+    *carry_refs, high_ref, low_ref, spectrum_ref, out_ref = refs
     y = y_ref[:, :ROWS, :].reshape(GRID, LANES)
     w = column_body(y, high_ref, low_ref, spectrum_ref)
     out_ref[:, :ROWS, :] = w.reshape(PEERS, ROWS, LANES)
-    out_ref[:, ROWS:, :] = jnp.broadcast_to(carry_ref[...][None], (PEERS, ROWS, LANES))
+    carry = carry_refs[0][...]
+    if len(carry_refs) > 1:
+        carry = jnp.concatenate([carry[:2], carry_refs[1][:2, :], carry[4:]], axis=0)
+    out_ref[:, ROWS:, :] = jnp.broadcast_to(carry[None], (PEERS, ROWS, LANES))
 
 
 def unpack(channels):
@@ -145,42 +181,41 @@
 
 def state_kernel(section, *refs):
     refs = list(refs)
-    back_ref, density_ref = refs.pop(0), refs.pop(0)
-    state_refs = [density_ref] + [refs.pop(0) for _ in range(section)]
+    back_ref = refs.pop(0)
+    state_refs = [refs.pop(0) for _ in range((1, 2, 2, 4)[section])]
+    density_ref, state_ref = state_refs[0], state_refs[-1]
     energies_ref, momentum_ref, emitted_ref, drive_ref = (refs.pop(0) for _ in range(4))
-    sums_ref = refs.pop(0) if section >= 2 else None
+    earlier_refs = [refs.pop(0) for _ in range(2)] if section == 3 else []
     high_ref, low_ref = refs.pop(0), refs.pop(0)
-    out_ref = refs.pop(0)
+    if section == 3:
+        result_ref, emitted_out_ref = refs
+    elif section == 0:
+        out_ref, next_ref, tile_ref = refs
+    elif section == 1:
+        out_ref, next_ref, arrived_ref, tile_ref = refs
+    else:
+        out_ref, next_ref, arrived_ref = refs
     drive_row = (0, 1, 1, 2)[section]
+    fraction = (0.0, 0.5, 0.5, 1.0, None)[section]
     next_fraction = (0.5, 0.5, 1.0, None)[section]
-
-    if section in (1, 3):
+    rate_scale = -coupling / GRID
+
+    if section > 0:
         arrived = jnp.sum(back_ref[:, :, ROWS:, :].reshape(PEERS, ROWS, LANES), axis=0)
         upstream = jnp.sum(arrived, axis=1, keepdims=True)
-    if section >= 2:
-        earlier = jnp.sum(sums_ref[...], axis=1, keepdims=True)
-    rate_scale = -coupling / GRID
-    if section == 0:
-        shift = None
-    elif section == 1:
-        shift = [time_step * 0.5 * rate_scale * upstream[i : i + 1] for i in range(2)]
-    elif section == 2:
-        shift = [time_step * 0.5 * rate_scale * earlier[2 + i : 3 + i] for i in range(2)]
-    else:
-        shift = [time_step * rate_scale * upstream[i : i + 1] for i in range(2)]
     potential = []
     for i in range(2):
         value = drive_ref[drive_row : drive_row + 1, i : i + 1] + emitted_ref[:, i : i + 1]
-        potential.append(value if shift is None else value + shift[i])
+        if section > 0:
+            value = value + (time_step * fraction * rate_scale) * upstream[i : i + 1]
+        potential.append(value)
 
     spectra = jnp.concatenate(
         [back_ref[:, half, :ROWS, :].reshape(CHANNELS * ROWS, LANES) for half in range(2)], axis=1
     )
     sigma = times_table(spectra, high_ref, low_ref)
 
-    state_ref = state_refs[-1]
     currents = {}
-    new_rows = []
     for part in range(2):
         lanes = slice(part * LANES, (part + 1) * LANES)
         rho = [state_ref[c, :, lanes] for c in range(CHANNELS)]
@@ -197,56 +232,52 @@
             rate = rates[c] if c < BANDS else rates[c] - dephasing * rho[c]
             if section < 3:
                 new = density_ref[c, :, lanes] + (time_step * next_fraction) * rate
-                refs[0][c, :, lanes] = new
-                if section in (0, 2):
-                    weight = 1.0 if c < BANDS else 2.0
-                    for i in range(2):
-                        p = momentum_ref[i, c, :, lanes]
-                        p = p if c < BANDS else weight * p
-                        for which, value in ((0, rho[c]), (1, new)):
-                            term = p * value
-                            key = 2 * which + i
-                            currents[key] = currents[key] + term if key in currents else term
+                next_ref[c, :, lanes] = new
+                momentum = [momentum_ref[i, c, :, lanes] for i in range(2)]
+                add_currents(currents, 0, c, momentum, new)
             else:
                 first, second, third, fourth = (r[c, :, lanes] for r in state_refs)
                 base = (second + 2.0 * third + fourth - first) * (1.0 / 3.0)
-                out_ref[c, :, lanes] = base + (time_step / 6.0) * rate
+                result_ref[c, :, lanes] = base + (time_step / 6.0) * rate
 
     if section < 3:
-        state = refs[0][...].reshape(CHANNELS * ROWS, GRID)
+        state = next_ref[...].reshape(CHANNELS * ROWS, GRID)
         send_rows(state, high_ref, low_ref, out_ref)
-    if section in (0, 2):
-        tile = jnp.concatenate(
-            [jnp.sum(currents[key], axis=0, keepdims=True) for key in range(4)]
-            + [jnp.zeros((ROWS - 4, LANES), jnp.float32)],
-            axis=0,
-        )
+    if section in (0, 1):
+        tile_ref[...] = currents_tile(currents, LANES)
+    if section == 2:
+        tile = currents_tile(currents, ROWS)
         out_ref[:, :, ROWS:, :] = jnp.broadcast_to(tile, (CHANNELS, 2, ROWS, LANES))
-    if section == 1:
-        refs[1][...] = arrived
+    if section in (1, 2):
+        arrived_ref[...] = arrived
     if section == 3:
+        first, second = (jnp.sum(r[...], axis=1, keepdims=True) for r in earlier_refs)
         for i in range(2):
             total = (
-                earlier[i : i + 1]
-                + 2.0 * earlier[2 + i : 3 + i]
+                first[i : i + 1]
+                + 2.0 * second[i : i + 1]
                 + 2.0 * upstream[i : i + 1]
                 + upstream[2 + i : 3 + i]
             )
-            refs[0][:, i : i + 1] = emitted_ref[:, i : i + 1] + (
+            emitted_out_ref[:, i : i + 1] = emitted_ref[:, i : i + 1] + (
                 time_step / 6.0 * rate_scale
             ) * total
 
 
-def call(body, outs, *args, flops=2 * 3 * 128 * 256 * 256):
+def call(body, outs, *args, in_hbm=(), scratch=(), vmem_mib=24):
     shapes = [jax.ShapeDtypeStruct(s, jnp.float32) for s in outs]
     vmem = pl.BlockSpec(memory_space=pltpu.VMEM)
+    hbm = pl.BlockSpec(memory_space=pltpu.HBM)
     return pl.pallas_call(
         body,
         out_shape=shapes,
-        in_specs=[vmem] * len(args),
+        in_specs=[hbm if n in in_hbm else vmem for n in range(len(args))],
         out_specs=[vmem] * len(outs),
-        compiler_params=pltpu.CompilerParams(vmem_limit_bytes=24 * 1024 * 1024),
-        cost_estimate=pl.CostEstimate(flops=flops, bytes_accessed=1 << 20, transcendentals=0),
+        scratch_shapes=scratch,
+        compiler_params=pltpu.CompilerParams(vmem_limit_bytes=vmem_mib * 1024 * 1024),
+        cost_estimate=pl.CostEstimate(
+            flops=2 * 3 * 128 * 256 * 256, bytes_accessed=1 << 20, transcendentals=0
+        ),
     )(*args)
 
 
@@ -258,40 +289,81 @@
     high_table, low_table, halves = tables()
     high, low = jnp.asarray(high_table), jnp.asarray(low_table)
     place = lax.axis_index("krow")
+    point = lax.axis_index("macro")
     spectrum = lax.dynamic_index_in_dim(jnp.asarray(halves), place % 2, 0, False)
     density = density.reshape(CHANNELS, ROWS, GRID)
     plain = (CHANNELS, 2, ROWS, LANES)
     carrying = (CHANNELS, 2, 2 * ROWS, LANES)
     state_shape = (CHANNELS, ROWS, GRID)
+    tile = (ROWS, LANES)
+    payload = (LANES, LANES)
     downstream = [
         (m * PEERS + j, (m + j) * PEERS + j) for j in range(POINTS) for m in range(POINTS - j)
     ]
     own = jnp.where(place == 0, 0.5, 1.0)
-
+    upstream_points = jnp.arange(POINTS)[:, None, None]
+    weights = jnp.where(
+        upstream_points < point, 1.0, jnp.where(upstream_points == point, 0.5, 0.0)
+    ) * jnp.ones((1, 1, LANES), jnp.float32)
+
+    out, part = call(
+        first_kernel,
+        [plain, payload],
+        density,
+        high,
+        low,
+        momentum,
+        in_hbm=(0, 1, 2, 3),
+        vmem_mib=58,
+        scratch=[
+            pltpu.VMEM(state_shape, jnp.float32),
+            pltpu.VMEM((GRID, GRID), jnp.bfloat16),
+            pltpu.VMEM((GRID, GRID), jnp.bfloat16),
+            pltpu.VMEM(momentum.shape, jnp.float32),
+            pltpu.SemaphoreType.DMA((4,)),
+        ],
+    )
+    parts = [part]
     states = [density]
     sums = []
-    (out,) = call(first_kernel, [plain], density, high, low)
     for section in range(4):
-        carries = section in (1, 3)
         arrived = swap(out.reshape(PEERS, -1, LANES))
-        if carries:
-            totals = jnp.sum(arrived[:, ROWS:, :], axis=0) * own
-            carry = lax.ppermute(totals, ("macro", "krow"), downstream)
+        tables_in = [high, low, spectrum]
+        if section == 0:
+            (mixed,) = call(column_kernel, [(PEERS, ROWS, LANES)], arrived, *tables_in)
+        else:
+            gathered = lax.all_gather(parts[section - 1], "macro")
+            scale, _ = lax.optimization_barrier((weights, states[section]))
+            carry = [jnp.sum(gathered[:, :ROWS, :] * scale, axis=0)]
+            if section == 3:
+                totals = jnp.sum(arrived[:, ROWS:, :], axis=0) * own
+                carry.append(lax.ppermute(totals, ("macro", "krow"), downstream))
             (mixed,) = call(
-                column_carry_kernel, [arrived.shape], arrived, carry, high, low, spectrum
-            )
-        else:
-            (mixed,) = call(column_kernel, [arrived.shape], arrived, high, low, spectrum)
+                column_carry_kernel, [(PEERS, 2 * ROWS, LANES)], arrived, *carry, *tables_in
+            )
         back = swap(mixed).reshape(CHANNELS, 2, -1, LANES)
         body = functools.partial(state_kernel, section)
-        args = [back, *states, energies, momentum, emitted, drive, *sums, high, low]
-        if section == 0 or section == 2:
-            out, state = call(body, [carrying, state_shape], *args)
+        fields = [energies, momentum, emitted, drive]
+        if section == 0:
+            out, state, part = call(
+                body, [plain, state_shape, payload], back, density, *fields, high, low
+            )
+            parts.append(part)
         elif section == 1:
-            out, state, tile = call(body, [plain, state_shape, (ROWS, LANES)], *args)
-            sums = [tile]
+            out, state, seen, part = call(
+                body, [plain, state_shape, tile, payload], back, density, states[-1], *fields, high, low
+            )
+            parts.append(part)
+            sums.append(seen)
+        elif section == 2:
+            out, state, seen = call(
+                body, [carrying, state_shape, tile], back, density, states[-1], *fields, high, low
+            )
+            sums.append(seen)
         else:
-            density_next, emitted_next = call(body, [state_shape, (1, 2)], *args)
+            density_next, emitted_next = call(
+                body, [state_shape, (1, 2)], back, *states, *fields, *sums, high, low
+            )
         if section < 3:
             states.append(state)
     return density_next.reshape(1, CHANNELS, ROWS, GRID), emitted_next

time: 155 us -> 173 us (1.12)
  blocking collectives: 89.4 us -> 63.6 us
  waiting for transfers between devices: 32.1 us -> 52.9 us
  between operations: 0.81 us -> 13.9 us
  starting transfers between devices: 21.7 us -> 29.7 us
  local copies, waits for them, and re-layouts: 2.85 us -> 0.22 us
  other arithmetic: 0.08 us -> 2.63 us
  Pallas kernels: 7.12 us -> 9.54 us
    all_to_all x5 -> x3, blocking collectives: 89.4 us -> 63.6 us  [swap(): return lax.all_to_all(x, 'krow', 0, 0, tiled=True)]
    all_gather x0 -> x3, waiting for transfers between devices: none -> 18.9 us  [per_device(): gathered = lax.all_gather(parts[section - 1], 'macro')]
    all_to_all x3 -> x5, starting transfers between devices: 19.1 us -> 28.3 us  [swap(): return lax.all_to_all(x, 'krow', 0, 0, tiled=True)]
    all_to_all x3 -> x5, waiting for transfers between devices: 30.5 us -> 33.9 us  [swap(): return lax.all_to_all(x, 'krow', 0, 0, tiled=True)]
    unnamed x23 -> x17, local copies, waits for them, and re-layouts: 2.84 us -> 0.13 us
    reduce_sum x0 -> x3, other arithmetic: none -> 2.59 us  [per_device(): carry = [jnp.sum(gathered[:, :ROWS, :] * scale, axis=0)]]
    pallas_call x9, Pallas kernels: 7.12 us -> 9.54 us  [call(): pl.pallas_call(body, out_shape=shapes, in_specs=[hbm if n in in_hbm else...]
  transfers between devices with their start and end apart: 5 -> 9, of which waited for: 5 -> 6; matrix products, arithmetic and copies ran while one was open for 0% -> 2% of each run, Pallas kernels for 0% -> 3%
where the time goes in v2:
time: 173 us
  blocking collectives  63.6 us (37%)
  waiting for transfers between devices  52.9 us (31%)
  starting transfers between devices  29.7 us (17%)
  between operations  13.9 us (8%)
  Pallas kernels  9.54 us (6%)
  other arithmetic  2.63 us (2%)
    all_to_all x3, blocking collectives, swap(): return lax.all_to_all(x, 'krow', 0, 0, tiled=True)  63.6 us
    all_to_all x5, waiting for transfers between devices, swap(): return lax.all_to_all(x, 'krow', 0, 0, tiled=True)  33.9 us
    all_to_all x5, starting transfers between devices, swap(): return lax.all_to_all(x, 'krow', 0, 0, tiled=True)  28.3 us
    all_gather x3, waiting for transfers between devices, per_device(): gathered = lax.all_gather(parts[section - 1], 'macro')  18.9 us
    pallas_call x9, Pallas kernels, call(): pl.pallas_call(body, out_shape=shapes, in_specs=[hbm if n in in_hbm else...  9.54 us
  transfers between devices with their start and end apart: 9, of which 6 were waited for; matrix products, arithmetic and copies ran while one was open for 2% of the time, Pallas kernels for 3%

profile of v2, /device:TPU:8, one launch (start us, length us, event | category | flops | bytes accessed | tf_op | source)
XLA Modules:
  0.0 172.5 jit_solution(16973799556435743987)
XLA Ops:
  7.2 2.0 %shard_map.95 = (f32[16,2,8,128]{3,2,1,0:T(8,128)}, f32[128,128]{1,0:T(8,128)}) custom-call(f32[16,8,256]{2,1,0:T(8,128)} %bitcast.18, bf16[256,256]{1,0:T(8,128)(2,1)} %constant.39.clone.refs_1_.high_ref.refs_6_.refs_7_.refs_2_.refs_11_, bf16[256,256]{1,0:T(8,128)(2,1)} %constant.40.clone.refs_2_.low_ref.refs_7_.refs_8_.refs_3_.refs_12_, ...), custom_call_target="tpu_custom_call" | custom-call | flops 50331648 | bytes 1048576 | tf_op jit(solution)/shard_map/pallas_call | solution.py:271
  9.2 10.3 %all-to-all-start = ((f32[32,8,128]{2,1,0:T(8,128)}), f32[32,8,128]{2,1,0:T(8,128)S(1)}, u32[]{:S(2)}, u32[]{:S(2)}) async-start(f32[32,8,128]{2,1,0:T(8,128)} %bitcast.30), calls=%async_computation | async-start | bytes 262144 | tf_op jit(solution)/shard_map/all_to_all | solution.py:285
  19.6 9.7 %all-to-all-done.y_ref = f32[32,8,128]{2,1,0:T(8,128)S(1)} async-done(((f32[32,8,128]{2,1,0:T(8,128)}), f32[32,8,128]{2,1,0:T(8,128)S(1)}, u32[]{:S(2)}, u32[]{:S(2)}) %all-to-all-start) | async-done | bytes 131104 | tf_op jit(solution)/shard_map/all_to_all | solution.py:285
  29.3 1.2 shard_map.96
  30.6 4.4 %all-to-all-start.1 = ((f32[32,8,128]{2,1,0:T(8,128)}), f32[32,8,128]{2,1,0:T(8,128)S(1)}, u32[]{:S(2)}, u32[]{:S(2)}) async-start(f32[32,8,128]{2,1,0:T(8,128)} %shard_map.96), calls=%async_computation.1 | async-start | bytes 262144 | tf_op jit(solution)/shard_map/all_to_all | solution.py:285
  35.1 9.6 %all-to-all-done.1 = f32[32,8,128]{2,1,0:T(8,128)S(1)} async-done(((f32[32,8,128]{2,1,0:T(8,128)}), f32[32,8,128]{2,1,0:T(8,128)S(1)}, u32[]{:S(2)}, u32[]{:S(2)}) %all-to-all-start.1) | async-done | bytes 131104 | tf_op jit(solution)/shard_map/all_to_all | solution.py:285
  44.7 1.2 shard_map.97
  46.0 4.5 %all-to-all-start.2 = ((f32[32,8,128]{2,1,0:T(8,128)}), f32[32,8,128]{2,1,0:T(8,128)S(1)}, u32[]{:S(2)}, u32[]{:S(2)}) async-start(f32[32,8,128]{2,1,0:T(8,128)} %bitcast.4), calls=%async_computation.2 | async-start | bytes 262144 | tf_op jit(solution)/shard_map/all_to_all | solution.py:285
  50.6 6.2 %all-gather.7.cloned.1.call-done = f32[2048,128]{1,0:T(8,128)} async-done(((f32[128,128]{1,0:T(8,128)}), f32[2048,128]{1,0:T(8,128)}) %all-gather.7.cloned.1.call-update) | async-done | bytes 1048592 | tf_op jit(solution)/shard_map/all_gather | solution.py:335
  56.7 0.9 fusion.2.refs_0_
  57.6 2.6 %all-to-all-done.2.y_ref = f32[32,8,128]{2,1,0:T(8,128)S(1)} async-done(((f32[32,8,128]{2,1,0:T(8,128)}), f32[32,8,128]{2,1,0:T(8,128)S(1)}, u32[]{:S(2)}, u32[]{:S(2)}) %all-to-all-start.2) | async-done | bytes 131104 | tf_op jit(solution)/shard_map/all_to_all | solution.py:285
  60.8 19.7 %all_to_all.40 = f32[32,16,128]{2,1,0:T(8,128)S(1)} all-to-all(f32[32,16,128]{2,1,0:T(8,128)S(1)} %shard_map.98), channel_id=1, replica_groups=mesh['macro'=16,'krow'=32] {'krow'}, dimensions={0} | all-to-all | bytes 524288 | tf_op jit(solution)/shard_map/all_to_all | solution.py:285
  80.5 1.2 shard_map.99
  81.8 4.6 %all-to-all-start.4 = ((f32[32,8,128]{2,1,0:T(8,128)}), f32[32,8,128]{2,1,0:T(8,128)S(1)}, u32[]{:S(2)}, u32[]{:S(2)}) async-start(f32[32,8,128]{2,1,0:T(8,128)} %bitcast.8), calls=%async_computation.4 | async-start | bytes 262144 | tf_op jit(solution)/shard_map/all_to_all | solution.py:285
  86.3 12.7 %all-gather.9.cloned.1.call-done = f32[2048,128]{1,0:T(8,128)} async-done(((f32[128,128]{1,0:T(8,128)}), f32[2048,128]{1,0:T(8,128)}) %all-gather.9.cloned.1.call-update) | async-done | bytes 1048592 | tf_op jit(solution)/shard_map/all_gather | solution.py:335
  99.0 0.9 fusion.1.refs_0_
  100.5 22.4 %all_to_all.41 = f32[32,16,128]{2,1,0:T(8,128)S(1)} all-to-all(f32[32,16,128]{2,1,0:T(8,128)S(1)} %shard_map.100), channel_id=1, replica_groups=mesh['macro'=16,'krow'=32] {'krow'}, dimensions={0} | all-to-all | bytes 524288 | tf_op jit(solution)/shard_map/all_to_all | solution.py:285
  122.8 1.3 shard_map.101
  124.1 4.6 %all-to-all-start.6 = ((f32[32,16,128]{2,1,0:T(8,128)}), f32[32,16,128]{2,1,0:T(8,128)S(1)}, u32[]{:S(2)}, u32[]{:S(2)}) async-start(f32[32,16,128]{2,1,0:T(8,128)} %bitcast.12), calls=%async_computation.6 | async-start | bytes 524288 | tf_op jit(solution)/shard_map/all_to_all | solution.py:285
  128.7 12.0 %all-to-all-done.6.y_ref = f32[32,16,128]{2,1,0:T(8,128)S(1)} async-done(((f32[32,16,128]{2,1,0:T(8,128)}), f32[32,16,128]{2,1,0:T(8,128)S(1)}, u32[]{:S(2)}, u32[]{:S(2)}) %all-to-all-start.6) | async-done | bytes 262176 | tf_op jit(solution)/shard_map/all_to_all | solution.py:285
  140.7 1.3 collective-permute-start
  142.1 0.9 fusion.refs_0_
  143.5 21.5 %all_to_all.42 = f32[32,16,128]{2,1,0:T(8,128)S(1)} all-to-all(f32[32,16,128]{2,1,0:T(8,128)S(1)} %shard_map.102), channel_id=1, replica_groups=mesh['macro'=16,'krow'=32] {'krow'}, dimensions={0} | all-to-all | bytes 524288 | tf_op jit(solution)/shard_map/all_to_all | solution.py:285
  164.9 1.0 shard_map.103
  (34 shorter events, 2.1 us)
Async XLA Ops:
  7.2 49.6 %all-gather.7.cloned.1.call-start = ((), (), s32[]{:S(2)}) async-start(), calls=%async_computation.8 | async-start | bytes 1114112 | tf_op jit(solution)/shard_map/all_gather | solution.py:335
  9.2 10.4 %copy-start.6 = (f32[2,256,128]{2,1,0:T(8,128)S(1)}, f32[2,256,128]{2,1,0:T(8,128)}, u32[]{:S(2)}) copy-start(f32[2,256,128]{2,1,0:T(8,128)} %constant.41.clone) | copy-start | bytes 786436
  9.2 20.1 %all-to-all-start = ((f32[32,8,128]{2,1,0:T(8,128)}), f32[32,8,128]{2,1,0:T(8,128)S(1)}, u32[]{:S(2)}, u32[]{:S(2)}) async-start(f32[32,8,128]{2,1,0:T(8,128)} %bitcast.30), calls=%async_computation | async-start | bytes 262144 | tf_op jit(solution)/shard_map/all_to_all | solution.py:285
  19.5 9.8 %copy-start = (bf16[256,256]{1,0:T(8,128)(2,1)S(1)}, bf16[256,256]{1,0:T(8,128)(2,1)}, u32[]{:S(2)}) copy-start(bf16[256,256]{1,0:T(8,128)(2,1)} %constant.39.clone.refs_1_.high_ref.refs_6_.refs_7_.refs_2_.refs_11_) | copy-start | bytes 393220
  19.6 9.8 %copy-start.1 = (bf16[256,256]{1,0:T(8,128)(2,1)S(1)}, bf16[256,256]{1,0:T(8,128)(2,1)}, u32[]{:S(2)}) copy-start(bf16[256,256]{1,0:T(8,128)(2,1)} %constant.40.clone.refs_2_.low_ref.refs_7_.refs_8_.refs_3_.refs_12_) | copy-start | bytes 393220
  29.3 5.7 %copy-start.7 = (f32[3,2]{0,1:T(2,128)S(1)}, f32[3,2]{0,1:T(2,128)}, u32[]{:S(2)}) copy-start(f32[3,2]{0,1:T(2,128)} %param.12) | copy-start | bytes 76
  29.3 15.4 %copy-start.3 = (f32[1,16,8,256]{3,2,1,0:T(8,128)S(1)}, f32[1,16,8,256]{3,2,1,0:T(8,128)}, u32[]{:S(2)}) copy-start(f32[1,16,8,256]{3,2,1,0:T(8,128)} %param.8) | copy-start | bytes 393220
  29.3 15.4 %copy-start.4 = (f32[4,8,256]{2,1,0:T(8,128)S(1)}, f32[4,8,256]{2,1,0:T(8,128)}, u32[]{:S(2)}) copy-start(f32[4,8,256]{2,1,0:T(8,128)} %refs_5_.6) | copy-start | bytes 98308
  30.6 14.2 %copy-start.2 = (f32[2,16,8,256]{3,2,1,0:T(8,128)S(1)}, f32[2,16,8,256]{3,2,1,0:T(8,128)}, u32[]{:S(2)}) copy-start(f32[2,16,8,256]{3,2,1,0:T(8,128)} %refs_6_.4) | copy-start | bytes 786436
  30.6 14.1 %all-to-all-start.1 = ((f32[32,8,128]{2,1,0:T(8,128)}), f32[32,8,128]{2,1,0:T(8,128)S(1)}, u32[]{:S(2)}, u32[]{:S(2)}) async-start(f32[32,8,128]{2,1,0:T(8,128)} %shard_map.96), calls=%async_computation.1 | async-start | bytes 262144 | tf_op jit(solution)/shard_map/all_to_all | solution.py:285
  35.0 64.1 %all-gather.9.cloned.1.call-start = ((), (), s32[]{:S(2)}) async-start(), calls=%async_computation.9 | async-start | bytes 1114112 | tf_op jit(solution)/shard_map/all_gather | solution.py:335
  35.1 9.6 %copy-start.5 = (f32[1,2]{1,0:T(1,128)S(1)}, f32[1,2]{1,0:T(1,128)}, u32[]{:S(2)}) copy-start(f32[1,2]{1,0:T(1,128)} %refs_7_.4) | copy-start | bytes 28
  46.0 14.2 %all-to-all-start.2 = ((f32[32,8,128]{2,1,0:T(8,128)}), f32[32,8,128]{2,1,0:T(8,128)S(1)}, u32[]{:S(2)}, u32[]{:S(2)}) async-start(f32[32,8,128]{2,1,0:T(8,128)} %bitcast.4), calls=%async_computation.2 | async-start | bytes 262144 | tf_op jit(solution)/shard_map/all_to_all | solution.py:285
  50.4 91.6 %all-gather.11.cloned.1.call-start = ((), (), s32[]{:S(2)}) async-start(), calls=%async_computation.10 | async-start | bytes 1114112 | tf_op jit(solution)/shard_map/all_gather | solution.py:335
  81.8 18.1 %all-to-all-start.4 = ((f32[32,8,128]{2,1,0:T(8,128)}), f32[32,8,128]{2,1,0:T(8,128)S(1)}, u32[]{:S(2)}, u32[]{:S(2)}) async-start(f32[32,8,128]{2,1,0:T(8,128)} %bitcast.8), calls=%async_computation.4 | async-start | bytes 262144 | tf_op jit(solution)/shard_map/all_to_all | solution.py:285
  124.1 16.6 %all-to-all-start.6 = ((f32[32,16,128]{2,1,0:T(8,128)}), f32[32,16,128]{2,1,0:T(8,128)S(1)}, u32[]{:S(2)}, u32[]{:S(2)}) async-start(f32[32,16,128]{2,1,0:T(8,128)} %bitcast.12), calls=%async_computation.6 | async-start | bytes 524288 | tf_op jit(solution)/shard_map/all_to_all | solution.py:285
  140.7 2.2 %collective-permute-start = (f32[8,128]{1,0:T(8,128)S(1)}, f32[8,128]{1,0:T(8,128)S(1)}, u32[]{:S(2)}, u32[]{:S(2)}) collective-permute-start(f32[8,128]{1,0:T(8,128)S(1)} %broadcast_multiply_fusion), channel_id=1, source_target_pairs={{0,0},{32,32},{64,64},{96,96},{128,128},{160,160},{192,192},{224,2... | collective-permute-start | bytes 12296 | tf_op jit(solution)/shard_map/ppermute | solution.py:340
Sparse Core Ops, SparseCore 0:
  10.1 46.5 all-gather.6
  58.9 40.1 all-gather.8
  101.2 40.0 all-gather.10

commit v3 on v2

v3 whole, which is shorter than its diff:
```python
import functools

import jax
import jax.numpy as jnp
import numpy as np
from jax import lax
from jax.experimental import pallas as pl
from jax.experimental.pallas import tpu as pltpu
from jax.sharding import PartitionSpec as P

BANDS = 4
CHANNELS = 16
GRID = 256
ROWS = 8
LANES = 128
PEERS = 32
POINTS = 16

dephasing = 0.2
coulomb_strength = 0.25
coupling = 2.0
time_step = 0.1
screening_width = 1.0

PAIRS = [(a, b) for a in range(BANDS) for b in range(a + 1, BANDS)]


def coulomb_kernel():
    offsets = np.arange(GRID)
    periodic = np.minimum(offsets, GRID - offsets).astype(np.float64)
    squared = periodic[:, None] ** 2 + periodic[None, :] ** 2 + screening_width**2
    kernel = coulomb_strength / np.sqrt(squared)
    return kernel - np.mean(kernel)


def tables():
    positions = np.arange(GRID)
    angles = (positions[:, None] * positions[None, :] % GRID) * (2.0 * np.pi / GRID)
    basis = ((np.cos(angles) + np.sin(angles)) / np.sqrt(GRID)).astype(np.float32)
    high = basis.astype(jnp.bfloat16)
    low = (basis - high.astype(np.float32)).astype(jnp.bfloat16)
    spectrum = -np.real(np.fft.fft2(coulomb_kernel())).astype(np.float32)
    halves = np.stack([spectrum[:, :LANES], spectrum[:, LANES:]])
    return high, low, halves


def split(x):
    high = x.astype(jnp.bfloat16)
    low = (x - high.astype(jnp.float32)).astype(jnp.bfloat16)
    return high, low


def dot(a, b):
    return jnp.dot(a, b, preferred_element_type=jnp.float32)


def times_table(x, high_ref, low_ref):
    x_high, x_low = split(x)
    return dot(x_high, high_ref[...]) + (dot(x_low, high_ref[...]) + dot(x_high, low_ref[...]))


def table_times(y, high_ref, low_ref):
    y_high, y_low = split(y)
    return dot(high_ref[...], y_high) + (dot(high_ref[...], y_low) + dot(low_ref[...], y_high))


def send_rows(x, high_ref, low_ref, out_ref):
    step = out_ref.shape[0] // PEERS
    spectra = times_table(x, high_ref, low_ref)
    for peer in range(PEERS):
        c, half = peer // 2, peer % 2
        out_ref[peer * step : peer * step + ROWS, :] = spectra[
            c * ROWS : (c + 1) * ROWS, half * LANES : (half + 1) * LANES
        ]


def tiles_of(ref):
    step = ref.shape[0] // PEERS
    return [ref[peer * step : peer * step + ROWS, :] for peer in range(PEERS)]


def rows_of(ref):
    return jnp.sum(ref[pl.ds(ROWS, PEERS, stride=ROWS + 1), :], axis=0, keepdims=True)


def send_row(row, out_ref):
    out_ref[pl.ds(ROWS, PEERS, stride=ROWS + 1), :] = jnp.broadcast_to(row, (PEERS, LANES))


def first_kernel(*refs):
    sources, out_ref, fetched, sems = refs[:3], refs[3], refs[4:7], refs[7]
    copies = [
        pltpu.make_async_copy(source, target, sems.at[n])
        for n, (source, target) in enumerate(zip(sources, fetched))
    ]
    for copy in copies:
        copy.start()
    for copy in copies:
        copy.wait()
    density_ref, high_ref, low_ref = fetched
    send_rows(density_ref[...].reshape(CHANNELS * ROWS, GRID), high_ref, low_ref, out_ref)


def total_kernel(y_ref, out_ref):
    out_ref[...] = rows_of(y_ref)


def column_kernel(y_ref, *refs):
    *carry_ref, high_ref, low_ref, spectrum_ref, out_ref = refs
    place = lax.axis_index("krow")
    y = jnp.concatenate(tiles_of(y_ref), axis=0)
    z = table_times(y, high_ref, low_ref) * spectrum_ref[place % 2]
    w = table_times(z, high_ref, low_ref)
    step = out_ref.shape[0] // PEERS
    for peer in range(PEERS):
        out_ref[peer * step : peer * step + ROWS, :] = w[peer * ROWS : (peer + 1) * ROWS]
    if carry_ref:
        point = lax.axis_index("macro")
        upstream = jnp.logical_and(place < POINTS, (point ^ place) < point)
        weight = jnp.where(place == 0, 0.5, jnp.where(upstream, 1.0, 0.0))
        send_row(carry_ref[0][...] * weight, out_ref)


def unpack(channels):
    real = [[None] * BANDS for _ in range(BANDS)]
    imag = [[None] * BANDS for _ in range(BANDS)]
    for band in range(BANDS):
        real[band][band] = channels[band]
    for position, (a, b) in enumerate(PAIRS):
        real[a][b] = real[b][a] = channels[BANDS + position]
        value = channels[BANDS + len(PAIRS) + position]
        imag[a][b] = (value, 1)
        imag[b][a] = (value, -1)
    return real, imag


def signed_product(total, x, y, sign):
    term = x * y
    if total is None:
        return term if sign > 0 else -term
    return total + term if sign > 0 else total - term


def commute(hamilton, channels):
    hr, hi = unpack(hamilton)
    rr, ri = unpack(channels)

    def product(a, b):
        real = imag = None
        for m in range(BANDS):
            real = signed_product(real, hr[a][m], rr[m][b], 1)
            if hi[a][m] is not None and ri[m][b] is not None:
                real = signed_product(
                    real, hi[a][m][0], ri[m][b][0], -hi[a][m][1] * ri[m][b][1]
                )
            if ri[m][b] is not None:
                imag = signed_product(imag, hr[a][m], ri[m][b][0], ri[m][b][1])
            if hi[a][m] is not None:
                imag = signed_product(imag, hi[a][m][0], rr[m][b], hi[a][m][1])
        return real, imag

    diagonal = [2.0 * product(a, a)[1] for a in range(BANDS)]
    upper_real = []
    upper_imag = []
    for a, b in PAIRS:
        real_ab, imag_ab = product(a, b)
        real_ba, imag_ba = product(b, a)
        upper_real.append(imag_ab + imag_ba)
        upper_imag.append(real_ba - real_ab)
    return diagonal + upper_real + upper_imag


def add_currents(currents, key, c, momentum, value):
    for i in range(2):
        term = momentum[i] * value
        term = term if c < BANDS else 2.0 * term
        currents[key, i] = currents[key, i] + term if (key, i) in currents else term


def currents_row(currents):
    lane = lax.broadcasted_iota(jnp.int32, (1, LANES), 1)
    row = jnp.zeros((1, LANES), jnp.float32)
    for place, key in enumerate(sorted(currents)):
        total = jnp.sum(jnp.sum(currents[key], axis=0, keepdims=True), axis=1, keepdims=True)
        row = jnp.where(lane == place, total, row)
    return row


def state_kernel(section, *refs):
    refs = list(refs)
    back_ref = refs.pop(0)
    state_refs = [refs.pop(0) for _ in range((1, 2, 2, 4)[section])]
    density_ref, state_ref = state_refs[0], state_refs[-1]
    energies_ref, momentum_ref, emitted_ref, drive_ref = (refs.pop(0) for _ in range(4))
    earlier_ref = refs.pop(0) if section >= 2 else None
    high_ref, low_ref = refs.pop(0), refs.pop(0)
    if section == 3:
        result_ref, emitted_out_ref = refs
    elif section == 1:
        out_ref, next_ref, arrived_ref = refs
    else:
        out_ref, next_ref = refs
    drive_row = (0, 1, 1, 2)[section]
    fraction = (0.0, 0.5, 0.5, 1.0, None)[section]
    next_fraction = (0.5, 0.5, 1.0, None)[section]
    rate_scale = -coupling / GRID

    if section in (1, 3):
        arrived = rows_of(back_ref)
    if section == 1:
        arrived_ref[...] = arrived
    upstream = None if section == 0 else earlier_ref[...] if section == 2 else arrived
    potential = []
    for i in range(2):
        value = drive_ref[i : i + 1, drive_row : drive_row + 1] + emitted_ref[:, i : i + 1]
        if section > 0:
            lane = 2 + i if section == 2 else i
            value = value + (time_step * fraction * rate_scale) * upstream[:, lane : lane + 1]
        potential.append(value)

    tiles = tiles_of(back_ref)
    spectra = jnp.concatenate(
        [jnp.concatenate(tiles[half::2], axis=0) for half in range(2)], axis=1
    )
    sigma = times_table(spectra, high_ref, low_ref)

    currents = {}
    for part in range(2):
        lanes = slice(part * LANES, (part + 1) * LANES)
        rho = [state_ref[c, :, lanes] for c in range(CHANNELS)]
        hamilton = []
        for c in range(CHANNELS):
            value = sigma[c * ROWS : (c + 1) * ROWS, lanes]
            value = value + potential[0] * momentum_ref[0, c, :, lanes]
            value = value + potential[1] * momentum_ref[1, c, :, lanes]
            if c < BANDS:
                value = value + energies_ref[c, :, lanes]
            hamilton.append(value)
        rates = commute(hamilton, rho)
        for c in range(CHANNELS):
            rate = rates[c] if c < BANDS else rates[c] - dephasing * rho[c]
            if section < 3:
                new = density_ref[c, :, lanes] + (time_step * next_fraction) * rate
                next_ref[c, :, lanes] = new
                if section in (0, 2):
                    momentum = [momentum_ref[i, c, :, lanes] for i in range(2)]
                    add_currents(currents, 0, c, momentum, rho[c])
                    add_currents(currents, 1, c, momentum, new)
            else:
                first, second, third, fourth = (r[c, :, lanes] for r in state_refs)
                base = (second + 2.0 * third + fourth - first) * (1.0 / 3.0)
                result_ref[c, :, lanes] = base + (time_step / 6.0) * rate

    if section < 3:
        state = next_ref[...].reshape(CHANNELS * ROWS, GRID)
        send_rows(state, high_ref, low_ref, out_ref)
    if section in (0, 2):
        send_row(currents_row(currents), out_ref)
    if section == 3:
        early = earlier_ref[...]
        for i in range(2):
            total = (
                early[:, i : i + 1]
                + 2.0 * early[:, 2 + i : 3 + i]
                + 2.0 * arrived[:, i : i + 1]
                + arrived[:, 2 + i : 3 + i]
            )
            emitted_out_ref[:, i : i + 1] = emitted_ref[:, i : i + 1] + (
                time_step / 6.0 * rate_scale
            ) * total


def call(body, outs, *args, in_hbm=(), scratch=(), vmem_mib=24):
    shapes = [jax.ShapeDtypeStruct(s, jnp.float32) for s in outs]
    vmem = pl.BlockSpec(memory_space=pltpu.VMEM)
    hbm = pl.BlockSpec(memory_space=pltpu.HBM)
    return pl.pallas_call(
        body,
        out_shape=shapes,
        in_specs=[hbm if n in in_hbm else vmem for n in range(len(args))],
        out_specs=[vmem] * len(outs),
        scratch_shapes=scratch,
        compiler_params=pltpu.CompilerParams(vmem_limit_bytes=vmem_mib * 1024 * 1024),
        cost_estimate=pl.CostEstimate(
            flops=2 * 3 * 128 * 256 * 256, bytes_accessed=1 << 20, transcendentals=0
        ),
    )(*args)


def swap(x):
    blocks = x.reshape(PEERS, 1, x.shape[0] // PEERS * LANES)
    return lax.all_to_all(blocks, "krow", 0, 0, tiled=True).reshape(x.shape)


def per_device(density, energies, momentum, emitted, drive):
    high, low, spectrum = (jnp.asarray(table) for table in tables())
    density = density.reshape(CHANNELS, ROWS, GRID)
    drive = drive.T
    plain = (PEERS * ROWS, LANES)
    carrying = (PEERS * (ROWS + 1), LANES)
    state_shape = (CHANNELS, ROWS, GRID)
    exchange = [(m * PEERS + j, (m ^ j) * PEERS + j) for j in range(POINTS) for m in range(POINTS)]

    (out,) = call(
        first_kernel,
        [plain],
        density,
        high,
        low,
        in_hbm=(0, 1, 2),
        vmem_mib=58,
        scratch=[
            pltpu.VMEM(state_shape, jnp.float32),
            pltpu.VMEM((GRID, GRID), jnp.bfloat16),
            pltpu.VMEM((GRID, GRID), jnp.bfloat16),
            pltpu.SemaphoreType.DMA((3,)),
        ],
    )
    states = [density]
    earlier = []
    for section in range(4):
        arrived = swap(out)
        carry = []
        if section in (1, 3):
            (total,) = call(total_kernel, [(1, LANES)], arrived)
            carry = [lax.ppermute(total, ("macro", "krow"), exchange)]
        (mixed,) = call(
            column_kernel, [carrying if carry else plain], arrived, *carry, high, low, spectrum
        )
        back = swap(mixed)
        body = functools.partial(state_kernel, section)
        used = states if section == 3 else states[:1] if section == 0 else [density, states[-1]]
        args = [back, *used, energies, momentum, emitted, drive, *earlier, high, low]
        if section in (0, 2):
            out, state = call(body, [carrying, state_shape], *args)
        elif section == 1:
            out, state, seen = call(body, [plain, state_shape, (1, LANES)], *args)
            earlier = [seen]
        else:
            density_next, emitted_next = call(body, [state_shape, (1, 2)], *args)
        if section < 3:
            states.append(state)
    return density_next.reshape(1, CHANNELS, ROWS, GRID), emitted_next


def solution(mesh):
    in_specs = (
        P("macro", None, "krow", None),
        P(None, "krow", None),
        P(None, None, "krow", None),
        P("macro", None),
        P(),
    )
    out_specs = (P("macro", None, "krow", None), P("macro", None))
    return jax.shard_map(
        per_device, mesh=mesh, in_specs=in_specs, out_specs=out_specs, check_vma=False
    )
```

time: 173 us -> 147 us (0.85)
  blocking collectives: 63.6 us -> 132 us
  waiting for transfers between devices: 52.9 us -> 2.17 us
  starting transfers between devices: 29.7 us -> 3.82 us
  between operations: 13.9 us -> 0.77 us
  other arithmetic: 2.63 us -> 0 us
  Pallas kernels: 9.54 us -> 6.97 us
    all_to_all x3 -> x8, blocking collectives: 63.6 us -> 132 us  [swap(): return lax.all_to_all(blocks, 'krow', 0, 0, tiled=True).reshape(x.shape)]
    all_to_all x5 -> x0, waiting for transfers between devices: 33.9 us -> none  [swap(): return lax.all_to_all(x, 'krow', 0, 0, tiled=True)]
    all_to_all x5 -> x0, starting transfers between devices: 28.3 us -> none  [swap(): return lax.all_to_all(x, 'krow', 0, 0, tiled=True)]
    all_gather x3 -> x0, waiting for transfers between devices: 18.9 us -> none  [per_device(): gathered = lax.all_gather(parts[section - 1], 'macro')]
    reduce_sum x4 -> x0, other arithmetic: 2.62 us -> none  [the longest x3 2.59 us: per_device(): carry = [jnp.sum(gathered[:, :ROWS, :] * scale, axis=0)]]
    pallas_call x9 -> x11, Pallas kernels: 9.54 us -> 6.97 us  [call(): pl.pallas_call(body, out_shape=shapes, in_specs=[hbm if n in in_hbm else...]
    ppermute x1 -> x2, starting transfers between devices: 1.29 us -> 3.82 us  [per_device(): carry = [lax.ppermute(total, ('macro', 'krow'), exchange)]]
    ppermute x1 -> x2, waiting for transfers between devices: 0.01 us -> 2.17 us  [per_device(): carry = [lax.ppermute(total, ('macro', 'krow'), exchange)]]
  transfers between devices with their start and end apart: 9 -> 2, of which waited for: 6 -> 2; matrix products, arithmetic and copies ran while one was open for 2% -> 0% of each run, Pallas kernels for 3% -> 0%
where the time goes in v3:
time: 147 us; the launch traced here: 146 us
  blocking collectives  132 us (90%)
  Pallas kernels  6.97 us (5%)
  starting transfers between devices  3.82 us (3%)
  waiting for transfers between devices  2.17 us (1%)
    all_to_all x8, blocking collectives, swap(): return lax.all_to_all(blocks, 'krow', 0, 0, tiled=True).reshape(x.shape)  132 us
    pallas_call x11, Pallas kernels, call(): pl.pallas_call(body, out_shape=shapes, in_specs=[hbm if n in in_hbm else...  6.97 us
    ppermute x2, starting transfers between devices, per_device(): carry = [lax.ppermute(total, ('macro', 'krow'), exchange)]  3.82 us
  transfers between devices with their start and end apart: 2, of which 2 were waited for; matrix products, arithmetic and copies ran while one was open for 0% of the time, Pallas kernels for 0%

profile of v3, /device:TPU:8, one launch (start us, length us, event | category | flops | bytes accessed | tf_op | source)
XLA Modules:
  0.0 146.1 jit_solution(13813002135967219152)
XLA Ops:
  0.6 0.0 copy-start.2
  0.6 2.0 %shard_map.95 = f32[256,128]{1,0:T(8,128)} custom-call(f32[16,8,256]{2,1,0:T(8,128)} %bitcast.19, bf16[256,256]{1,0:T(8,128)(2,1)} %constant.6.clone.refs_1_.refs_0_.refs_6_.refs_7_.refs_8_.refs_10_, bf16[256,256]{1,0:T(8,128)(2,1)} %constant.7.clone.refs_2_.refs_1_.refs_7_.refs_8_.refs_9_.refs_11_), custom_call_target="tpu_custom_call" | custom-call | flops 50331648 | bytes 1048576 | tf_op jit(solution)/shard_map/pallas_call | solution.py:277
  2.6 0.0 copy-start
  2.6 20.1 %all_to_all.40 = f32[32,1,1024]{2,1,0:T(1,128)S(1)} all-to-all(f32[32,1,1024]{2,1,0:T(1,128)} %bitcast.45), channel_id=1, replica_groups=mesh['macro'=16,'krow'=32] {'krow'}, dimensions={0} | all-to-all | bytes 262144 | tf_op jit(solution)/shard_map/all_to_all | solution.py:292
  22.8 0.6 shard_map.96
  23.3 13.9 %all_to_all.41 = f32[32,1,1024]{2,1,0:T(1,128)S(1)} all-to-all(f32[32,1,1024]{2,1,0:T(1,128)S(1)} %bitcast.34), channel_id=1, replica_groups=mesh['macro'=16,'krow'=32] {'krow'}, dimensions={0} | all-to-all | bytes 262144 | tf_op jit(solution)/shard_map/all_to_all | solution.py:292
  37.2 0.7 copy-done.6
  37.9 0.6 shard_map.97
  38.5 14.0 %all_to_all.42 = f32[32,1,1152]{2,1,0:T(1,128)S(1)} all-to-all(f32[32,1,1152]{2,1,0:T(1,128)S(1)} %bitcast.38), channel_id=1, replica_groups=mesh['macro'=16,'krow'=32] {'krow'}, dimensions={0} | all-to-all | bytes 294912 | tf_op jit(solution)/shard_map/all_to_all | solution.py:292
  52.5 1.9 %collective-permute-start = (f32[1,128]{1,0:T(1,128)S(1)}, f32[1,128]{1,0:T(1,128)S(1)}, u32[]{:S(2)}, u32[]{:S(2)}) collective-permute-start(f32[1,128]{1,0:T(1,128)S(1)} %shard_map.98), channel_id=1, source_target_pairs={{0,0},{32,32},{64,64},{96,96},{128,128},{160,160},{192,192},{224,2... | collective-permute-start | bytes 1544 | tf_op jit(solution)/shard_map/ppermute | solution.py:326
  54.5 1.1 collective-permute-done.refs_0_
  55.5 0.5 shard_map.99
  56.1 22.9 %all_to_all.43 = f32[32,1,1152]{2,1,0:T(1,128)S(1)} all-to-all(f32[32,1,1152]{2,1,0:T(1,128)S(1)} %bitcast.31), channel_id=1, replica_groups=mesh['macro'=16,'krow'=32] {'krow'}, dimensions={0} | all-to-all | bytes 294912 | tf_op jit(solution)/shard_map/all_to_all | solution.py:292
  79.0 0.5 shard_map.100
  79.6 13.8 %all_to_all.44 = f32[32,1,1024]{2,1,0:T(1,128)S(1)} all-to-all(f32[32,1,1024]{2,1,0:T(1,128)S(1)} %bitcast.40), channel_id=1, replica_groups=mesh['macro'=16,'krow'=32] {'krow'}, dimensions={0} | all-to-all | bytes 262144 | tf_op jit(solution)/shard_map/all_to_all | solution.py:292
  93.4 0.6 shard_map.101
  94.0 13.9 %all_to_all.45 = f32[32,1,1024]{2,1,0:T(1,128)S(1)} all-to-all(f32[32,1,1024]{2,1,0:T(1,128)S(1)} %bitcast.36), channel_id=1, replica_groups=mesh['macro'=16,'krow'=32] {'krow'}, dimensions={0} | all-to-all | bytes 262144 | tf_op jit(solution)/shard_map/all_to_all | solution.py:292
  107.8 0.6 shard_map.102
  108.4 14.0 %all_to_all.46 = f32[32,1,1152]{2,1,0:T(1,128)S(1)} all-to-all(f32[32,1,1152]{2,1,0:T(1,128)S(1)} %bitcast.39), channel_id=1, replica_groups=mesh['macro'=16,'krow'=32] {'krow'}, dimensions={0} | all-to-all | bytes 294912 | tf_op jit(solution)/shard_map/all_to_all | solution.py:292
  122.5 1.9 %collective-permute-start.1 = (f32[1,128]{1,0:T(1,128)S(1)}, f32[1,128]{1,0:T(1,128)S(1)}, u32[]{:S(2)}, u32[]{:S(2)}) collective-permute-start(f32[1,128]{1,0:T(1,128)S(1)} %shard_map.103), channel_id=1, source_target_pairs={{0,0},{32,32},{64,64},{96,96},{128,128},{160,160},{192,192},{224,2... | collective-permute-start | bytes 1544 | tf_op jit(solution)/shard_map/ppermute | solution.py:326
  124.4 1.1 collective-permute-done.1.refs_0_
  125.5 0.6 shard_map.104
  126.0 19.0 %all_to_all.47 = f32[32,1,1152]{2,1,0:T(1,128)S(1)} all-to-all(f32[32,1,1152]{2,1,0:T(1,128)S(1)} %bitcast.30), channel_id=1, replica_groups=mesh['macro'=16,'krow'=32] {'krow'}, dimensions={0} | all-to-all | bytes 294912 | tf_op jit(solution)/shard_map/all_to_all | solution.py:292
  145.0 1.1 shard_map.105
  (15 shorter events, 0.1 us)
Async XLA Ops:
  0.6 22.1 %copy-start.2 = (f32[2,256,128]{2,1,0:T(8,128)S(1)}, f32[2,256,128]{2,1,0:T(8,128)}, u32[]{:S(2)}) copy-start(f32[2,256,128]{2,1,0:T(8,128)} %constant.8.clone.refs_2_.refs_3_) | copy-start | bytes 786436
  2.6 20.1 %copy-start = (bf16[256,256]{1,0:T(8,128)(2,1)S(1)}, bf16[256,256]{1,0:T(8,128)(2,1)}, u32[]{:S(2)}) copy-start(bf16[256,256]{1,0:T(8,128)(2,1)} %constant.7.clone.refs_2_.refs_1_.refs_7_.refs_8_.refs_9_.refs_11_) | copy-start | bytes 393220
  2.6 20.1 %copy-start.1 = (bf16[256,256]{1,0:T(8,128)(2,1)S(1)}, bf16[256,256]{1,0:T(8,128)(2,1)}, u32[]{:S(2)}) copy-start(bf16[256,256]{1,0:T(8,128)(2,1)} %constant.6.clone.refs_1_.refs_0_.refs_6_.refs_7_.refs_8_.refs_10_) | copy-start | bytes 393220
  22.7 14.5 %copy-start.4 = (f32[1,16,8,256]{3,2,1,0:T(8,128)S(1)}, f32[1,16,8,256]{3,2,1,0:T(8,128)}, u32[]{:S(2)}) copy-start(f32[1,16,8,256]{3,2,1,0:T(8,128)} %param.8) | copy-start | bytes 393220
  22.8 14.5 %copy-start.5 = (f32[4,8,256]{2,1,0:T(8,128)S(1)}, f32[4,8,256]{2,1,0:T(8,128)}, u32[]{:S(2)}) copy-start(f32[4,8,256]{2,1,0:T(8,128)} %refs_5_.5) | copy-start | bytes 98308
  23.3 13.9 %copy-start.3 = (f32[2,16,8,256]{3,2,1,0:T(8,128)S(1)}, f32[2,16,8,256]{3,2,1,0:T(8,128)}, u32[]{:S(2)}) copy-start(f32[2,16,8,256]{3,2,1,0:T(8,128)} %refs_6_.2) | copy-start | bytes 786436
  37.2 0.7 copy-start.6
  37.2 0.7 copy-start.7
  52.5 3.0 %collective-permute-start = (f32[1,128]{1,0:T(1,128)S(1)}, f32[1,128]{1,0:T(1,128)S(1)}, u32[]{:S(2)}, u32[]{:S(2)}) collective-permute-start(f32[1,128]{1,0:T(1,128)S(1)} %shard_map.98), channel_id=1, source_target_pairs={{0,0},{32,32},{64,64},{96,96},{128,128},{160,160},{192,192},{224,2... | collective-permute-start | bytes 1544 | tf_op jit(solution)/shard_map/ppermute | solution.py:326
  122.5 3.0 %collective-permute-start.1 = (f32[1,128]{1,0:T(1,128)S(1)}, f32[1,128]{1,0:T(1,128)S(1)}, u32[]{:S(2)}, u32[]{:S(2)}) collective-permute-start(f32[1,128]{1,0:T(1,128)S(1)} %shard_map.103), channel_id=1, source_target_pairs={{0,0},{32,32},{64,64},{96,96},{128,128},{160,160},{192,192},{224,2... | collective-permute-start | bytes 1544 | tf_op jit(solution)/shard_map/ppermute | solution.py:326

commit v4 on v3

--- a/solution.py
+++ b/solution.py
@@ -14,6 +14,8 @@
 ROWS = 8
 LANES = 128
 PEERS = 32
+SEATS = 16
+BLOCK = 16
 POINTS = 16
 
 dephasing = 0.2
@@ -40,8 +42,11 @@
     high = basis.astype(jnp.bfloat16)
     low = (basis - high.astype(np.float32)).astype(jnp.bfloat16)
     spectrum = -np.real(np.fft.fft2(coulomb_kernel())).astype(np.float32)
-    halves = np.stack([spectrum[:, :LANES], spectrum[:, LANES:]])
-    return high, low, halves
+    return high, low, spectrum
+
+
+def seat(place):
+    return place % 8 // 4, place // 8 * 4 + place % 4
 
 
 def split(x):
@@ -59,32 +64,41 @@
     return dot(x_high, high_ref[...]) + (dot(x_low, high_ref[...]) + dot(x_high, low_ref[...]))
 
 
-def table_times(y, high_ref, low_ref):
+def table_times(y, high, low):
     y_high, y_low = split(y)
-    return dot(high_ref[...], y_high) + (dot(high_ref[...], y_low) + dot(low_ref[...], y_high))
+    return dot(high, y_high) + (dot(high, y_low) + dot(low, y_high))
+
+
+def put(out_ref, start, tile):
+    for half in range(2):
+        out_ref[start + half * ROWS : start + (half + 1) * ROWS, :] = tile[
+            :, half * LANES : (half + 1) * LANES
+        ]
+
+
+def take(ref, blocks):
+    step = ref.shape[0] // blocks
+    halves = [
+        [ref[n * step + half * ROWS : n * step + (half + 1) * ROWS, :] for n in range(blocks)]
+        for half in range(2)
+    ]
+    return jnp.concatenate([jnp.concatenate(tiles, axis=0) for tiles in halves], axis=1)
 
 
 def send_rows(x, high_ref, low_ref, out_ref):
     step = out_ref.shape[0] // PEERS
     spectra = times_table(x, high_ref, low_ref)
     for peer in range(PEERS):
-        c, half = peer // 2, peer % 2
-        out_ref[peer * step : peer * step + ROWS, :] = spectra[
-            c * ROWS : (c + 1) * ROWS, half * LANES : (half + 1) * LANES
-        ]
-
-
-def tiles_of(ref):
-    step = ref.shape[0] // PEERS
-    return [ref[peer * step : peer * step + ROWS, :] for peer in range(PEERS)]
-
-
-def rows_of(ref):
-    return jnp.sum(ref[pl.ds(ROWS, PEERS, stride=ROWS + 1), :], axis=0, keepdims=True)
-
-
-def send_row(row, out_ref):
-    out_ref[pl.ds(ROWS, PEERS, stride=ROWS + 1), :] = jnp.broadcast_to(row, (PEERS, LANES))
+        c = seat(peer)[1]
+        put(out_ref, peer * step, spectra[c * ROWS : (c + 1) * ROWS])
+
+
+def rows_of(ref, blocks):
+    return jnp.sum(ref[pl.ds(BLOCK, blocks, stride=BLOCK + 1), :], axis=0, keepdims=True)
+
+
+def send_row(row, out_ref, blocks):
+    out_ref[pl.ds(BLOCK, blocks, stride=BLOCK + 1), :] = jnp.broadcast_to(row, (blocks, LANES))
 
 
 def first_kernel(*refs):
@@ -102,23 +116,23 @@
 
 
 def total_kernel(y_ref, out_ref):
-    out_ref[...] = rows_of(y_ref)
+    out_ref[...] = rows_of(y_ref, PEERS)
 
 
 def column_kernel(y_ref, *refs):
     *carry_ref, high_ref, low_ref, spectrum_ref, out_ref = refs
-    place = lax.axis_index("krow")
-    y = jnp.concatenate(tiles_of(y_ref), axis=0)
-    z = table_times(y, high_ref, low_ref) * spectrum_ref[place % 2]
-    w = table_times(z, high_ref, low_ref)
-    step = out_ref.shape[0] // PEERS
-    for peer in range(PEERS):
-        out_ref[peer * step : peer * step + ROWS, :] = w[peer * ROWS : (peer + 1) * ROWS]
+    half, place = seat(lax.axis_index("krow"))
+    z = table_times(take(y_ref, PEERS), high_ref[...], low_ref[...]) * spectrum_ref[...]
+    rows = [pl.ds(pl.multiple_of(x * 64 + half * 32, 32), 32) for x in range(4)]
+    high, low = (jnp.concatenate([r[at, :] for at in rows], axis=0) for r in (high_ref, low_ref))
+    w = table_times(z, high, low)
+    step = out_ref.shape[0] // SEATS
+    for n in range(SEATS):
+        put(out_ref, n * step, w[n * ROWS : (n + 1) * ROWS])
     if carry_ref:
         point = lax.axis_index("macro")
-        upstream = jnp.logical_and(place < POINTS, (point ^ place) < point)
-        weight = jnp.where(place == 0, 0.5, jnp.where(upstream, 1.0, 0.0))
-        send_row(carry_ref[0][...] * weight, out_ref)
+        weight = jnp.where(place == 0, 0.5, jnp.where((point ^ place) < point, 1.0, 0.0))
+        send_row(carry_ref[0][...] * weight, out_ref, SEATS)
 
 
 def unpack(channels):
@@ -206,7 +220,7 @@
     rate_scale = -coupling / GRID
 
     if section in (1, 3):
-        arrived = rows_of(back_ref)
+        arrived = rows_of(back_ref, SEATS)
     if section == 1:
         arrived_ref[...] = arrived
     upstream = None if section == 0 else earlier_ref[...] if section == 2 else arrived
@@ -218,11 +232,7 @@
             value = value + (time_step * fraction * rate_scale) * upstream[:, lane : lane + 1]
         potential.append(value)
 
-    tiles = tiles_of(back_ref)
-    spectra = jnp.concatenate(
-        [jnp.concatenate(tiles[half::2], axis=0) for half in range(2)], axis=1
-    )
-    sigma = times_table(spectra, high_ref, low_ref)
+    sigma = times_table(take(back_ref, SEATS), high_ref, low_ref)
 
     currents = {}
     for part in range(2):
@@ -255,7 +265,7 @@
         state = next_ref[...].reshape(CHANNELS * ROWS, GRID)
         send_rows(state, high_ref, low_ref, out_ref)
     if section in (0, 2):
-        send_row(currents_row(currents), out_ref)
+        send_row(currents_row(currents), out_ref, PEERS)
     if section == 3:
         early = earlier_ref[...]
         for i in range(2):
@@ -287,23 +297,29 @@
     )(*args)
 
 
-def swap(x):
-    blocks = x.reshape(PEERS, 1, x.shape[0] // PEERS * LANES)
-    return lax.all_to_all(blocks, "krow", 0, 0, tiled=True).reshape(x.shape)
+def swap(x, blocks, groups=None):
+    flat = x.reshape(blocks, 1, x.shape[0] // blocks * LANES)
+    flat = lax.all_to_all(flat, "krow", 0, 0, tiled=True, axis_index_groups=groups)
+    return flat.reshape(x.shape)
 
 
 def per_device(density, energies, momentum, emitted, drive):
     high, low, spectrum = (jnp.asarray(table) for table in tables())
     density = density.reshape(CHANNELS, ROWS, GRID)
     drive = drive.T
-    plain = (PEERS * ROWS, LANES)
-    carrying = (PEERS * (ROWS + 1), LANES)
+    there = (PEERS * BLOCK, LANES)
+    there_carrying = (PEERS * (BLOCK + 1), LANES)
+    back_shape = (SEATS * BLOCK, LANES)
+    back_carrying = (SEATS * (BLOCK + 1), LANES)
     state_shape = (CHANNELS, ROWS, GRID)
-    exchange = [(m * PEERS + j, (m ^ j) * PEERS + j) for j in range(POINTS) for m in range(POINTS)]
+    halves = [[n for n in range(PEERS) if seat(n)[0] == half] for half in range(2)]
+    exchange = [
+        (m * PEERS + n, (m ^ seat(n)[1]) * PEERS + n) for n in range(PEERS) for m in range(POINTS)
+    ]
 
     (out,) = call(
         first_kernel,
-        [plain],
+        [there],
         density,
         high,
         low,
@@ -319,22 +335,28 @@
     states = [density]
     earlier = []
     for section in range(4):
-        arrived = swap(out)
+        arrived = swap(out, PEERS)
         carry = []
         if section in (1, 3):
             (total,) = call(total_kernel, [(1, LANES)], arrived)
             carry = [lax.ppermute(total, ("macro", "krow"), exchange)]
         (mixed,) = call(
-            column_kernel, [carrying if carry else plain], arrived, *carry, high, low, spectrum
+            column_kernel,
+            [back_carrying if carry else back_shape],
+            arrived,
+            *carry,
+            high,
+            low,
+            spectrum,
         )
-        back = swap(mixed)
+        back = swap(mixed, SEATS, halves)
         body = functools.partial(state_kernel, section)
         used = states if section == 3 else states[:1] if section == 0 else [density, states[-1]]
         args = [back, *used, energies, momentum, emitted, drive, *earlier, high, low]
         if section in (0, 2):
-            out, state = call(body, [carrying, state_shape], *args)
+            out, state = call(body, [there_carrying, state_shape], *args)
         elif section == 1:
-            out, state, seen = call(body, [plain, state_shape, (1, LANES)], *args)
+            out, state, seen = call(body, [there, state_shape, (1, LANES)], *args)
             earlier = [seen]
         else:
             density_next, emitted_next = call(body, [state_shape, (1, 2)], *args)

time: 147 us -> 149 us (1.014)
  blocking collectives: 132 us -> 134 us
    all_to_all x8, blocking collectives: 132 us -> 134 us  [swap(): lax.all_to_all(flat, 'krow', 0, 0, tiled=True, axis_index_groups=groups)]
where the time goes in v4:
time: 149 us
  blocking collectives  134 us (90%)
  Pallas kernels  6.98 us (5%)
  starting transfers between devices  3.82 us (3%)
  waiting for transfers between devices  2.17 us (1%)
    all_to_all x8, blocking collectives, swap(): lax.all_to_all(flat, 'krow', 0, 0, tiled=True, axis_index_groups=groups)  134 us
    pallas_call x11, Pallas kernels, call(): pl.pallas_call(body, out_shape=shapes, in_specs=[hbm if n in in_hbm else...  6.98 us
    ppermute x2, starting transfers between devices, per_device(): carry = [lax.ppermute(total, ('macro', 'krow'), exchange)]  3.82 us
  transfers between devices with their start and end apart: 2, of which 2 were waited for; matrix products, arithmetic and copies ran while one was open for 0% of the time, Pallas kernels for 0%

profile of v4, /device:TPU:8, one launch (start us, length us, event | category | flops | bytes accessed | tf_op | source)
XLA Modules:
  0.0 148.9 jit_solution(17204583999797710098)
XLA Ops:
  0.6 2.0 %shard_map.95 = f32[512,128]{1,0:T(8,128)} custom-call(f32[16,8,256]{2,1,0:T(8,128)} %bitcast.19, bf16[256,256]{1,0:T(8,128)(2,1)} %constant.6.clone.refs_1_.refs_0_.refs_6_.refs_7_.refs_8_.refs_10_, bf16[256,256]{1,0:T(8,128)(2,1)} %constant.7.clone.refs_2_.refs_1_.refs_7_.refs_8_.refs_9_.refs_11_), custom_call_target="tpu_custom_call" | custom-call | flops 50331648 | bytes 1048576 | tf_op jit(solution)/shard_map/pallas_call | solution.py:287
  2.6 0.0 copy-start
  2.6 0.0 copy-start.1
  2.6 22.6 %all_to_all.40 = f32[32,1,2048]{2,1,0:T(1,128)S(1)} all-to-all(f32[32,1,2048]{2,1,0:T(1,128)} %bitcast.45), channel_id=1, replica_groups=mesh['macro'=16,'krow'=32] {'krow'}, dimensions={0} | all-to-all | bytes 524288 | tf_op jit(solution)/shard_map/all_to_all | solution.py:302
  25.3 0.6 shard_map.96
  25.9 11.6 %all_to_all.41 = f32[16,1,2048]{2,1,0:T(1,128)S(1)} all-to-all(f32[16,1,2048]{2,1,0:T(1,128)S(1)} %bitcast.34), channel_id=1, replica_groups={{0,1,2,3,8,9,10,11,16,17,18,19,24,25,26,27},{4,5,6,7,12,13,14,15,20,21,..., dimensions={0} | all-to-all | bytes 262144 | tf_op jit(solution)/shard_map/all_to_all | solution.py:302
  37.5 0.7 copy-done.6
  38.2 0.6 shard_map.97
  38.8 17.1 %all_to_all.42 = f32[32,1,2176]{2,1,0:T(1,128)S(1)} all-to-all(f32[32,1,2176]{2,1,0:T(1,128)S(1)} %bitcast.38), channel_id=1, replica_groups=mesh['macro'=16,'krow'=32] {'krow'}, dimensions={0} | all-to-all | bytes 557056 | tf_op jit(solution)/shard_map/all_to_all | solution.py:302
  55.8 1.9 %collective-permute-start = (f32[1,128]{1,0:T(1,128)S(1)}, f32[1,128]{1,0:T(1,128)S(1)}, u32[]{:S(2)}, u32[]{:S(2)}) collective-permute-start(f32[1,128]{1,0:T(1,128)S(1)} %shard_map.98), channel_id=1, source_target_pairs={{0,0},{32,32},{64,64},{96,96},{128,128},{160,160},{192,192},{224,2... | collective-permute-start | bytes 1544 | tf_op jit(solution)/shard_map/ppermute | solution.py:342
  57.7 1.1 collective-permute-done.refs_0_
  58.8 0.6 shard_map.99
  59.4 20.7 %all_to_all.43 = f32[16,1,2176]{2,1,0:T(1,128)S(1)} all-to-all(f32[16,1,2176]{2,1,0:T(1,128)S(1)} %bitcast.32), channel_id=1, replica_groups={{0,1,2,3,8,9,10,11,16,17,18,19,24,25,26,27},{4,5,6,7,12,13,14,15,20,21,..., dimensions={0} | all-to-all | bytes 278528 | tf_op jit(solution)/shard_map/all_to_all | solution.py:302
  80.1 0.5 shard_map.100
  80.7 16.9 %all_to_all.44 = f32[32,1,2048]{2,1,0:T(1,128)S(1)} all-to-all(f32[32,1,2048]{2,1,0:T(1,128)S(1)} %bitcast.40), channel_id=1, replica_groups=mesh['macro'=16,'krow'=32] {'krow'}, dimensions={0} | all-to-all | bytes 524288 | tf_op jit(solution)/shard_map/all_to_all | solution.py:302
  97.5 0.6 shard_map.101
  98.1 11.5 %all_to_all.45 = f32[16,1,2048]{2,1,0:T(1,128)S(1)} all-to-all(f32[16,1,2048]{2,1,0:T(1,128)S(1)} %bitcast.35), channel_id=1, replica_groups={{0,1,2,3,8,9,10,11,16,17,18,19,24,25,26,27},{4,5,6,7,12,13,14,15,20,21,..., dimensions={0} | all-to-all | bytes 262144 | tf_op jit(solution)/shard_map/all_to_all | solution.py:302
  109.6 0.6 shard_map.102
  110.2 17.0 %all_to_all.46 = f32[32,1,2176]{2,1,0:T(1,128)S(1)} all-to-all(f32[32,1,2176]{2,1,0:T(1,128)S(1)} %bitcast.39), channel_id=1, replica_groups=mesh['macro'=16,'krow'=32] {'krow'}, dimensions={0} | all-to-all | bytes 557056 | tf_op jit(solution)/shard_map/all_to_all | solution.py:302
  127.2 1.9 %collective-permute-start.1 = (f32[1,128]{1,0:T(1,128)S(1)}, f32[1,128]{1,0:T(1,128)S(1)}, u32[]{:S(2)}, u32[]{:S(2)}) collective-permute-start(f32[1,128]{1,0:T(1,128)S(1)} %shard_map.103), channel_id=1, source_target_pairs={{0,0},{32,32},{64,64},{96,96},{128,128},{160,160},{192,192},{224,2... | collective-permute-start | bytes 1544 | tf_op jit(solution)/shard_map/ppermute | solution.py:342
  129.1 1.1 collective-permute-done.1.refs_0_
  130.2 0.6 shard_map.104
  130.7 17.1 %all_to_all.47 = f32[16,1,2176]{2,1,0:T(1,128)S(1)} all-to-all(f32[16,1,2176]{2,1,0:T(1,128)S(1)} %bitcast.31), channel_id=1, replica_groups={{0,1,2,3,8,9,10,11,16,17,18,19,24,25,26,27},{4,5,6,7,12,13,14,15,20,21,..., dimensions={0} | all-to-all | bytes 278528 | tf_op jit(solution)/shard_map/all_to_all | solution.py:302
  147.8 1.1 shard_map.105
  (15 shorter events, 0.1 us)
Async XLA Ops:
  2.6 22.6 %copy-start = (bf16[256,256]{1,0:T(8,128)(2,1)S(1)}, bf16[256,256]{1,0:T(8,128)(2,1)}, u32[]{:S(2)}) copy-start(bf16[256,256]{1,0:T(8,128)(2,1)} %constant.7.clone.refs_2_.refs_1_.refs_7_.refs_8_.refs_9_.refs_11_) | copy-start | bytes 393220
  2.6 22.6 %copy-start.1 = (bf16[256,256]{1,0:T(8,128)(2,1)S(1)}, bf16[256,256]{1,0:T(8,128)(2,1)}, u32[]{:S(2)}) copy-start(bf16[256,256]{1,0:T(8,128)(2,1)} %constant.6.clone.refs_1_.refs_0_.refs_6_.refs_7_.refs_8_.refs_10_) | copy-start | bytes 393220
  2.6 22.6 %copy-start.2 = (f32[256,256]{1,0:T(8,128)S(1)}, f32[256,256]{1,0:T(8,128)}, u32[]{:S(2)}) copy-start(f32[256,256]{1,0:T(8,128)} %constant.8.clone.refs_2_.refs_3_) | copy-start | bytes 786436
  25.3 12.2 %copy-start.4 = (f32[1,16,8,256]{3,2,1,0:T(8,128)S(1)}, f32[1,16,8,256]{3,2,1,0:T(8,128)}, u32[]{:S(2)}) copy-start(f32[1,16,8,256]{3,2,1,0:T(8,128)} %param.8) | copy-start | bytes 393220
  25.3 12.2 %copy-start.5 = (f32[4,8,256]{2,1,0:T(8,128)S(1)}, f32[4,8,256]{2,1,0:T(8,128)}, u32[]{:S(2)}) copy-start(f32[4,8,256]{2,1,0:T(8,128)} %refs_5_.5) | copy-start | bytes 98308
  25.8 11.6 %copy-start.3 = (f32[2,16,8,256]{3,2,1,0:T(8,128)S(1)}, f32[2,16,8,256]{3,2,1,0:T(8,128)}, u32[]{:S(2)}) copy-start(f32[2,16,8,256]{3,2,1,0:T(8,128)} %refs_6_.2) | copy-start | bytes 786436
  37.5 0.7 copy-start.6
  37.5 0.7 copy-start.7
  55.8 3.0 %collective-permute-start = (f32[1,128]{1,0:T(1,128)S(1)}, f32[1,128]{1,0:T(1,128)S(1)}, u32[]{:S(2)}, u32[]{:S(2)}) collective-permute-start(f32[1,128]{1,0:T(1,128)S(1)} %shard_map.98), channel_id=1, source_target_pairs={{0,0},{32,32},{64,64},{96,96},{128,128},{160,160},{192,192},{224,2... | collective-permute-start | bytes 1544 | tf_op jit(solution)/shard_map/ppermute | solution.py:342
  127.2 3.0 %collective-permute-start.1 = (f32[1,128]{1,0:T(1,128)S(1)}, f32[1,128]{1,0:T(1,128)S(1)}, u32[]{:S(2)}, u32[]{:S(2)}) collective-permute-start(f32[1,128]{1,0:T(1,128)S(1)} %shard_map.103), channel_id=1, source_target_pairs={{0,0},{32,32},{64,64},{96,96},{128,128},{160,160},{192,192},{224,2... | collective-permute-start | bytes 1544 | tf_op jit(solution)/shard_map/ppermute | solution.py:342

commit v5 on v3

--- a/solution.py
+++ b/solution.py
@@ -87,38 +87,79 @@
     out_ref[pl.ds(ROWS, PEERS, stride=ROWS + 1), :] = jnp.broadcast_to(row, (PEERS, LANES))
 
 
+def add_currents(currents, key, c, momentum, value):
+    for i in range(2):
+        term = momentum[i] * value
+        term = term if c < BANDS else 2.0 * term
+        currents[key, i] = currents[key, i] + term if (key, i) in currents else term
+
+
+def currents_row(currents):
+    lane = lax.broadcasted_iota(jnp.int32, (1, LANES), 1)
+    row = jnp.zeros((1, LANES), jnp.float32)
+    for place, key in enumerate(sorted(currents)):
+        total = jnp.sum(jnp.sum(currents[key], axis=0, keepdims=True), axis=1, keepdims=True)
+        row = jnp.where(lane == place, total, row)
+    return row
+
+
 def first_kernel(*refs):
-    sources, out_ref, fetched, sems = refs[:3], refs[3], refs[4:7], refs[7]
+    sources, (out_ref, fields_ref), fetched, sems = refs[:7], refs[7:9], refs[9:16], refs[16]
     copies = [
         pltpu.make_async_copy(source, target, sems.at[n])
         for n, (source, target) in enumerate(zip(sources, fetched))
     ]
     for copy in copies:
         copy.start()
-    for copy in copies:
+    density_ref, high_ref, low_ref, momentum_ref, energies_ref, emitted_ref, drive_ref = fetched
+    for copy in copies[:3]:
         copy.wait()
-    density_ref, high_ref, low_ref = fetched
     send_rows(density_ref[...].reshape(CHANNELS * ROWS, GRID), high_ref, low_ref, out_ref)
+    for copy in copies[3:]:
+        copy.wait()
+    currents = {}
+    for part in range(2):
+        lanes = slice(part * LANES, (part + 1) * LANES)
+        for c in range(CHANNELS):
+            momentum = [momentum_ref[i, c, :, lanes] for i in range(2)]
+            add_currents(currents, 0, c, momentum, density_ref[c, :, lanes])
+    send_row(currents_row(currents), out_ref)
+    fields_ref[:BANDS] = energies_ref[...]
+    lane = lax.broadcasted_iota(jnp.int32, (1, LANES), 1)
+    row = jnp.zeros((1, LANES), jnp.float32)
+    for i in range(2):
+        emitted = emitted_ref[:, i : i + 1]
+        row = jnp.where(lane == 6 + i, emitted, row)
+        for n in range(3):
+            row = jnp.where(lane == 3 * i + n, drive_ref[i : i + 1, n : n + 1] + emitted, row)
+    fields_ref[BANDS, :, :LANES] = jnp.broadcast_to(row, (ROWS, LANES))
+    fields_ref[BANDS, :, LANES:] = jnp.zeros((ROWS, LANES), jnp.float32)
+
+
+def prefix_weight():
+    place, point = lax.axis_index("krow"), lax.axis_index("macro")
+    upstream = jnp.logical_and(place < POINTS, (point ^ place) < point)
+    return jnp.where(place == 0, 0.5, jnp.where(upstream, 1.0, 0.0))
 
 
 def total_kernel(y_ref, out_ref):
     out_ref[...] = rows_of(y_ref)
 
 
-def column_kernel(y_ref, *refs):
-    *carry_ref, high_ref, low_ref, spectrum_ref, out_ref = refs
-    place = lax.axis_index("krow")
+def column_kernel(carries, y_ref, *refs):
+    refs = list(refs)
+    carry_ref = refs.pop(0) if carries else None
+    high_ref, low_ref, spectrum_ref, out_ref = refs[:4]
     y = jnp.concatenate(tiles_of(y_ref), axis=0)
-    z = table_times(y, high_ref, low_ref) * spectrum_ref[place % 2]
+    z = table_times(y, high_ref, low_ref) * spectrum_ref[lax.axis_index("krow") % 2]
     w = table_times(z, high_ref, low_ref)
     step = out_ref.shape[0] // PEERS
     for peer in range(PEERS):
         out_ref[peer * step : peer * step + ROWS, :] = w[peer * ROWS : (peer + 1) * ROWS]
-    if carry_ref:
-        point = lax.axis_index("macro")
-        upstream = jnp.logical_and(place < POINTS, (point ^ place) < point)
-        weight = jnp.where(place == 0, 0.5, jnp.where(upstream, 1.0, 0.0))
-        send_row(carry_ref[0][...] * weight, out_ref)
+    if carries:
+        send_row(carry_ref[...] * prefix_weight(), out_ref)
+    else:
+        refs[4][...] = rows_of(y_ref)
 
 
 def unpack(channels):
@@ -170,51 +211,34 @@
     return diagonal + upper_real + upper_imag
 
 
-def add_currents(currents, key, c, momentum, value):
-    for i in range(2):
-        term = momentum[i] * value
-        term = term if c < BANDS else 2.0 * term
-        currents[key, i] = currents[key, i] + term if (key, i) in currents else term
-
-
-def currents_row(currents):
-    lane = lax.broadcasted_iota(jnp.int32, (1, LANES), 1)
-    row = jnp.zeros((1, LANES), jnp.float32)
-    for place, key in enumerate(sorted(currents)):
-        total = jnp.sum(jnp.sum(currents[key], axis=0, keepdims=True), axis=1, keepdims=True)
-        row = jnp.where(lane == place, total, row)
-    return row
-
-
 def state_kernel(section, *refs):
     refs = list(refs)
     back_ref = refs.pop(0)
     state_refs = [refs.pop(0) for _ in range((1, 2, 2, 4)[section])]
     density_ref, state_ref = state_refs[0], state_refs[-1]
-    energies_ref, momentum_ref, emitted_ref, drive_ref = (refs.pop(0) for _ in range(4))
-    earlier_ref = refs.pop(0) if section >= 2 else None
+    fields_ref, momentum_ref = refs.pop(0), refs.pop(0)
+    sums_ref = refs.pop(0) if section in (1, 2) else None
+    permuted_ref = refs.pop(0) if section in (0, 1) else None
+    earlier_refs = [refs.pop(0) for _ in range(2)] if section == 3 else None
     high_ref, low_ref = refs.pop(0), refs.pop(0)
     if section == 3:
         result_ref, emitted_out_ref = refs
-    elif section == 1:
-        out_ref, next_ref, arrived_ref = refs
     else:
         out_ref, next_ref = refs
     drive_row = (0, 1, 1, 2)[section]
-    fraction = (0.0, 0.5, 0.5, 1.0, None)[section]
+    fraction = (0.0, 0.5, 0.5, 1.0)[section]
     next_fraction = (0.5, 0.5, 1.0, None)[section]
     rate_scale = -coupling / GRID
 
-    if section in (1, 3):
+    if section == 3:
         arrived = rows_of(back_ref)
-    if section == 1:
-        arrived_ref[...] = arrived
-    upstream = None if section == 0 else earlier_ref[...] if section == 2 else arrived
+    upstream = None if section == 0 else arrived if section == 3 else sums_ref[...]
     potential = []
     for i in range(2):
-        value = drive_ref[i : i + 1, drive_row : drive_row + 1] + emitted_ref[:, i : i + 1]
+        lane = 3 * i + drive_row
+        value = fields_ref[BANDS, 0:1, lane : lane + 1]
         if section > 0:
-            lane = 2 + i if section == 2 else i
+            lane = i if section == 3 else 2 + i
             value = value + (time_step * fraction * rate_scale) * upstream[:, lane : lane + 1]
         potential.append(value)
 
@@ -234,7 +258,7 @@
             value = value + potential[0] * momentum_ref[0, c, :, lanes]
             value = value + potential[1] * momentum_ref[1, c, :, lanes]
             if c < BANDS:
-                value = value + energies_ref[c, :, lanes]
+                value = value + fields_ref[c, :, lanes]
             hamilton.append(value)
         rates = commute(hamilton, rho)
         for c in range(CHANNELS):
@@ -242,8 +266,10 @@
             if section < 3:
                 new = density_ref[c, :, lanes] + (time_step * next_fraction) * rate
                 next_ref[c, :, lanes] = new
-                if section in (0, 2):
-                    momentum = [momentum_ref[i, c, :, lanes] for i in range(2)]
+                momentum = [momentum_ref[i, c, :, lanes] for i in range(2)]
+                if section == 0:
+                    add_currents(currents, 0, c, momentum, new)
+                elif section == 2:
                     add_currents(currents, 0, c, momentum, rho[c])
                     add_currents(currents, 1, c, momentum, new)
             else:
@@ -254,20 +280,25 @@
     if section < 3:
         state = next_ref[...].reshape(CHANNELS * ROWS, GRID)
         send_rows(state, high_ref, low_ref, out_ref)
-    if section in (0, 2):
-        send_row(currents_row(currents), out_ref)
-    if section == 3:
-        early = earlier_ref[...]
+        row = currents_row(currents)
+        if section < 2:
+            lane = lax.broadcasted_iota(jnp.int32, (1, LANES), 1)
+            permuted = permuted_ref[...] * prefix_weight()
+            for i in range(2):
+                row = jnp.where(lane == 2 + i, permuted[:, i : i + 1], row)
+        send_row(row, out_ref)
+    else:
+        first, second = (r[...] for r in earlier_refs)
         for i in range(2):
             total = (
-                early[:, i : i + 1]
-                + 2.0 * early[:, 2 + i : 3 + i]
+                first[:, 2 + i : 3 + i]
+                + 2.0 * second[:, 2 + i : 3 + i]
                 + 2.0 * arrived[:, i : i + 1]
                 + arrived[:, 2 + i : 3 + i]
             )
-            emitted_out_ref[:, i : i + 1] = emitted_ref[:, i : i + 1] + (
-                time_step / 6.0 * rate_scale
-            ) * total
+            lane = 6 + i
+            emitted = fields_ref[BANDS, 0:1, lane : lane + 1]
+            emitted_out_ref[:, i : i + 1] = emitted + (time_step / 6.0 * rate_scale) * total
 
 
 def call(body, outs, *args, in_hbm=(), scratch=(), vmem_mib=24):
@@ -301,45 +332,55 @@
     state_shape = (CHANNELS, ROWS, GRID)
     exchange = [(m * PEERS + j, (m ^ j) * PEERS + j) for j in range(POINTS) for m in range(POINTS)]
 
-    (out,) = call(
+    out, fields = call(
         first_kernel,
-        [plain],
+        [carrying, (BANDS + 1, ROWS, GRID)],
         density,
         high,
         low,
-        in_hbm=(0, 1, 2),
+        momentum,
+        energies,
+        emitted,
+        drive,
+        in_hbm=range(7),
         vmem_mib=58,
         scratch=[
             pltpu.VMEM(state_shape, jnp.float32),
             pltpu.VMEM((GRID, GRID), jnp.bfloat16),
             pltpu.VMEM((GRID, GRID), jnp.bfloat16),
-            pltpu.SemaphoreType.DMA((3,)),
+            pltpu.VMEM(momentum.shape, jnp.float32),
+            pltpu.VMEM(energies.shape, jnp.float32),
+            pltpu.VMEM(emitted.shape, jnp.float32),
+            pltpu.VMEM(drive.shape, jnp.float32),
+            pltpu.SemaphoreType.DMA((7,)),
         ],
     )
+    row = (1, LANES)
     states = [density]
-    earlier = []
+    sums = []
     for section in range(4):
         arrived = swap(out)
-        carry = []
-        if section in (1, 3):
-            (total,) = call(total_kernel, [(1, LANES)], arrived)
-            carry = [lax.ppermute(total, ("macro", "krow"), exchange)]
-        (mixed,) = call(
-            column_kernel, [carrying if carry else plain], arrived, *carry, high, low, spectrum
-        )
+        column = functools.partial(column_kernel, section == 3)
+        if section < 3:
+            mixed, total = call(column, [plain, row], arrived, high, low, spectrum)
+        else:
+            (total,) = call(total_kernel, [row], arrived)
+            carry = lax.ppermute(total, ("macro", "krow"), exchange)
+            (mixed,) = call(column, [carrying], arrived, carry, high, low, spectrum)
+        extra = [total] if section in (1, 2) else []
+        sums += extra
+        if section in (0, 1):
+            extra = extra + [lax.ppermute(total, ("macro", "krow"), exchange)]
         back = swap(mixed)
         body = functools.partial(state_kernel, section)
         used = states if section == 3 else states[:1] if section == 0 else [density, states[-1]]
-        args = [back, *used, energies, momentum, emitted, drive, *earlier, high, low]
-        if section in (0, 2):
+        extra = sums if section == 3 else extra
+        args = [back, *used, fields, momentum, *extra, high, low]
+        if section < 3:
             out, state = call(body, [carrying, state_shape], *args)
-        elif section == 1:
-            out, state, seen = call(body, [plain, state_shape, (1, LANES)], *args)
-            earlier = [seen]
+            states.append(state)
         else:
             density_next, emitted_next = call(body, [state_shape, (1, 2)], *args)
-        if section < 3:
-            states.append(state)
     return density_next.reshape(1, CHANNELS, ROWS, GRID), emitted_next
 
 

time: 147 us -> 145 us (0.986)
  blocking collectives: 132 us -> 104 us
  waiting for transfers between devices: 2.17 us -> 16.6 us
  starting transfers between devices: 3.82 us -> 14.7 us
    all_to_all x8 -> x6, blocking collectives: 132 us -> 104 us  [swap(): return lax.all_to_all(blocks, 'krow', 0, 0, tiled=True).reshape(x.shape)]
    all_to_all x0 -> x2, waiting for transfers between devices: none -> 13.4 us  [swap(): return lax.all_to_all(blocks, 'krow', 0, 0, tiled=True).reshape(x.shape)]
    all_to_all x0 -> x2, starting transfers between devices: none -> 8.91 us  [swap(): return lax.all_to_all(blocks, 'krow', 0, 0, tiled=True).reshape(x.shape)]
    ppermute x2 -> x3, starting transfers between devices: 3.82 us -> 5.75 us  [the longest x2 3.84 us: per_device(): extra = extra + [lax.ppermute(total, ('macro', 'krow'), exchange)]]
    pallas_call x11 -> x10, Pallas kernels: 6.97 us -> 8.37 us  [call(): pl.pallas_call(body, out_shape=shapes, in_specs=[hbm if n in in_hbm else...]
    ppermute x2 -> x3, waiting for transfers between devices: 2.17 us -> 3.26 us  [the longest x2 2.17 us: per_device(): extra = extra + [lax.ppermute(total, ('macro', 'krow'), exchange)]]
  transfers between devices with their start and end apart: 2 -> 5, of which waited for: 2 -> 5; matrix products, arithmetic and copies ran while one was open for 0% -> 0% of each run, Pallas kernels for 0% -> 0%
where the time goes in v5:
time: 145 us; the launch traced here: 144 us
  blocking collectives  104 us (72%)
  waiting for transfers between devices  16.6 us (11%)
  starting transfers between devices  14.7 us (10%)
  Pallas kernels  8.37 us (6%)
    all_to_all x6, blocking collectives, swap(): return lax.all_to_all(blocks, 'krow', 0, 0, tiled=True).reshape(x.shape)  104 us
    all_to_all x2, waiting for transfers between devices, swap(): return lax.all_to_all(blocks, 'krow', 0, 0, tiled=True).reshape(x.shape)  13.4 us
    all_to_all x2, starting transfers between devices, swap(): return lax.all_to_all(blocks, 'krow', 0, 0, tiled=True).reshape(x.shape)  8.91 us
    pallas_call x10, Pallas kernels, call(): pl.pallas_call(body, out_shape=shapes, in_specs=[hbm if n in in_hbm else...  8.37 us
    ppermute x2, starting transfers between devices, per_device(): extra = extra + [lax.ppermute(total, ('macro', 'krow'), exchange)]  3.84 us
  transfers between devices with their start and end apart: 5, of which 5 were waited for; matrix products, arithmetic and copies ran while one was open for 0% of the time, Pallas kernels for 0%

profile of v5, /device:TPU:8, one launch (start us, length us, event | category | flops | bytes accessed | tf_op | source)
XLA Modules:
  0.0 144.1 jit_solution(3710129322191188960)
XLA Ops:
  0.6 2.2 %shard_map.95 = (f32[288,128]{1,0:T(8,128)}, f32[5,8,256]{2,1,0:T(8,128)}) custom-call(f32[16,8,256]{2,1,0:T(8,128)} %bitcast.19, bf16[256,256]{1,0:T(8,128)(2,1)} %constant.6.clone.refs_1_.refs_0_.refs_5_.refs_7_.refs_6_.refs_9_, bf16[256,256]{1,0:T(8,128)(2,1)} %constant.7.clone.refs_2_.refs_1_.refs_6_.refs_8_.refs_7_.refs_10_, f32[2,16,8,256]{3,2,1,0:T(8,128)} %refs_6_.3, ...), custom_call_target="tpu_custom_call" | custom-call | flops 50331648 | bytes 1048576 | tf_op jit(solution)/shard_map/pallas_call | solution.py:308
  2.8 20.3 %all_to_all.40 = f32[32,1,1152]{2,1,0:T(1,128)S(1)} all-to-all(f32[32,1,1152]{2,1,0:T(1,128)} %bitcast.38), channel_id=1, replica_groups=mesh['macro'=16,'krow'=32] {'krow'}, dimensions={0} | all-to-all | bytes 294912 | tf_op jit(solution)/shard_map/all_to_all | solution.py:323
  23.2 1.2 shard_map.96
  24.4 4.5 %all-to-all-start.1 = ((f32[32,1,1024]{2,1,0:T(1,128)}), f32[32,1,1024]{2,1,0:T(1,128)S(1)}, u32[]{:S(2)}, u32[]{:S(2)}) async-start(f32[32,1,1024]{2,1,0:T(1,128)} %bitcast.4), calls=%async_computation.1 | async-start | bytes 262144 | tf_op jit(solution)/shard_map/all_to_all | solution.py:323
  28.9 1.9 %collective-permute-start = (f32[1,128]{1,0:T(1,128)S(1)}, f32[1,128]{1,0:T(1,128)S(1)}, u32[]{:S(2)}, u32[]{:S(2)}) collective-permute-start(f32[1,128]{1,0:T(1,128)S(1)} %get-tuple-element.21), channel_id=1, source_target_pairs={{0,0},{32,32},{64,64},{96,96},{128,128},{160,160},{192,192},{224,2... | collective-permute-start | bytes 1544 | tf_op jit(solution)/shard_map/ppermute | solution.py:373
  30.8 1.1 collective-permute-done.refs_4_
  31.9 6.7 %all-to-all-done.1 = f32[32,1,1024]{2,1,0:T(1,128)S(1)} async-done(((f32[32,1,1024]{2,1,0:T(1,128)}), f32[32,1,1024]{2,1,0:T(1,128)S(1)}, u32[]{:S(2)}, u32[]{:S(2)}) %all-to-all-start.1) | async-done | bytes 131104 | tf_op jit(solution)/shard_map/all_to_all | solution.py:323
  38.6 0.5 shard_map.97
  39.1 20.7 %all_to_all.41 = f32[32,1,1152]{2,1,0:T(1,128)S(1)} all-to-all(f32[32,1,1152]{2,1,0:T(1,128)S(1)} %bitcast.34), channel_id=1, replica_groups=mesh['macro'=16,'krow'=32] {'krow'}, dimensions={0} | all-to-all | bytes 294912 | tf_op jit(solution)/shard_map/all_to_all | solution.py:323
  59.8 1.2 shard_map.98
  61.0 4.4 %all-to-all-start.3 = ((f32[32,1,1024]{2,1,0:T(1,128)}), f32[32,1,1024]{2,1,0:T(1,128)S(1)}, u32[]{:S(2)}, u32[]{:S(2)}) async-start(f32[32,1,1024]{2,1,0:T(1,128)} %bitcast.8), calls=%async_computation.3 | async-start | bytes 262144 | tf_op jit(solution)/shard_map/all_to_all | solution.py:323
  65.4 1.9 %collective-permute-start.1 = (f32[1,128]{1,0:T(1,128)S(1)}, f32[1,128]{1,0:T(1,128)S(1)}, u32[]{:S(2)}, u32[]{:S(2)}) collective-permute-start(f32[1,128]{1,0:T(1,128)S(1)} %get-tuple-element.25.refs_5_.refs_7_), channel_id=1, source_target_pairs={{0,0},{32,32},{64,64},{96,96},{128,128},{160,160},{192,192},{224,2... | collective-permute-start | bytes 1544 | tf_op jit(solution)/shard_map/ppermute | solution.py:373
  67.4 1.1 collective-permute-done.1.refs_6_
  68.5 6.7 %all-to-all-done.3 = f32[32,1,1024]{2,1,0:T(1,128)S(1)} async-done(((f32[32,1,1024]{2,1,0:T(1,128)}), f32[32,1,1024]{2,1,0:T(1,128)S(1)}, u32[]{:S(2)}, u32[]{:S(2)}) %all-to-all-start.3) | async-done | bytes 131104 | tf_op jit(solution)/shard_map/all_to_all | solution.py:323
  75.7 15.7 %all_to_all.42 = f32[32,1,1152]{2,1,0:T(1,128)S(1)} all-to-all(f32[32,1,1152]{2,1,0:T(1,128)S(1)} %bitcast.35), channel_id=1, replica_groups=mesh['macro'=16,'krow'=32] {'krow'}, dimensions={0} | all-to-all | bytes 294912 | tf_op jit(solution)/shard_map/all_to_all | solution.py:323
  91.5 0.6 shard_map.100
  92.0 13.9 %all_to_all.43 = f32[32,1,1024]{2,1,0:T(1,128)S(1)} all-to-all(f32[32,1,1024]{2,1,0:T(1,128)S(1)} %bitcast.37), channel_id=1, replica_groups=mesh['macro'=16,'krow'=32] {'krow'}, dimensions={0} | all-to-all | bytes 262144 | tf_op jit(solution)/shard_map/all_to_all | solution.py:323
  105.9 0.6 shard_map.101
  106.5 14.0 %all_to_all.44 = f32[32,1,1152]{2,1,0:T(1,128)S(1)} all-to-all(f32[32,1,1152]{2,1,0:T(1,128)S(1)} %bitcast.36), channel_id=1, replica_groups=mesh['macro'=16,'krow'=32] {'krow'}, dimensions={0} | all-to-all | bytes 294912 | tf_op jit(solution)/shard_map/all_to_all | solution.py:323
  120.5 1.9 %collective-permute-start.2 = (f32[1,128]{1,0:T(1,128)S(1)}, f32[1,128]{1,0:T(1,128)S(1)}, u32[]{:S(2)}, u32[]{:S(2)}) collective-permute-start(f32[1,128]{1,0:T(1,128)S(1)} %shard_map.102), channel_id=1, source_target_pairs={{0,0},{32,32},{64,64},{96,96},{128,128},{160,160},{192,192},{224,2... | collective-permute-start | bytes 1544 | tf_op jit(solution)/shard_map/ppermute | solution.py:368
  122.4 1.1 collective-permute-done.2.refs_0_
  123.5 0.6 shard_map.103
  124.1 18.9 %all_to_all.45 = f32[32,1,1152]{2,1,0:T(1,128)S(1)} all-to-all(f32[32,1,1152]{2,1,0:T(1,128)S(1)} %bitcast.30), channel_id=1, replica_groups=mesh['macro'=16,'krow'=32] {'krow'}, dimensions={0} | all-to-all | bytes 294912 | tf_op jit(solution)/shard_map/all_to_all | solution.py:323
  143.0 1.1 shard_map.104
  (14 shorter events, 0.6 us)
Async XLA Ops:
  0.6 22.5 %copy-start.3 = (f32[2,256,128]{2,1,0:T(8,128)S(1)}, f32[2,256,128]{2,1,0:T(8,128)}, u32[]{:S(2)}) copy-start(f32[2,256,128]{2,1,0:T(8,128)} %constant.8.clone.refs_2_.refs_3_) | copy-start | bytes 786436
  2.8 20.4 %copy-start = (bf16[256,256]{1,0:T(8,128)(2,1)S(1)}, bf16[256,256]{1,0:T(8,128)(2,1)}, u32[]{:S(2)}) copy-start(bf16[256,256]{1,0:T(8,128)(2,1)} %constant.7.clone.refs_2_.refs_1_.refs_6_.refs_8_.refs_7_.refs_10_) | copy-start | bytes 393220
  2.8 20.4 %copy-start.1 = (bf16[256,256]{1,0:T(8,128)(2,1)S(1)}, bf16[256,256]{1,0:T(8,128)(2,1)}, u32[]{:S(2)}) copy-start(bf16[256,256]{1,0:T(8,128)(2,1)} %constant.6.clone.refs_1_.refs_0_.refs_5_.refs_7_.refs_6_.refs_9_) | copy-start | bytes 393220
  23.2 15.4 %copy-start.4 = (f32[1,16,8,256]{3,2,1,0:T(8,128)S(1)}, f32[1,16,8,256]{3,2,1,0:T(8,128)}, u32[]{:S(2)}) copy-start(f32[1,16,8,256]{3,2,1,0:T(8,128)} %param.8) | copy-start | bytes 393220
  23.2 15.4 %copy-start.5 = (f32[5,8,256]{2,1,0:T(8,128)S(1)}, f32[5,8,256]{2,1,0:T(8,128)}, u32[]{:S(2)}) copy-start(f32[5,8,256]{2,1,0:T(8,128)} %get-tuple-element.20.refs_2_.refs_3_.refs_5_) | copy-start | bytes 122884
  24.4 14.2 %copy-start.2 = (f32[2,16,8,256]{3,2,1,0:T(8,128)S(1)}, f32[2,16,8,256]{3,2,1,0:T(8,128)}, u32[]{:S(2)}) copy-start(f32[2,16,8,256]{3,2,1,0:T(8,128)} %refs_6_.3) | copy-start | bytes 786436
  24.4 14.2 %all-to-all-start.1 = ((f32[32,1,1024]{2,1,0:T(1,128)}), f32[32,1,1024]{2,1,0:T(1,128)S(1)}, u32[]{:S(2)}, u32[]{:S(2)}) async-start(f32[32,1,1024]{2,1,0:T(1,128)} %bitcast.4), calls=%async_computation.1 | async-start | bytes 262144 | tf_op jit(solution)/shard_map/all_to_all | solution.py:323
  28.9 3.0 %collective-permute-start = (f32[1,128]{1,0:T(1,128)S(1)}, f32[1,128]{1,0:T(1,128)S(1)}, u32[]{:S(2)}, u32[]{:S(2)}) collective-permute-start(f32[1,128]{1,0:T(1,128)S(1)} %get-tuple-element.21), channel_id=1, source_target_pairs={{0,0},{32,32},{64,64},{96,96},{128,128},{160,160},{192,192},{224,2... | collective-permute-start | bytes 1544 | tf_op jit(solution)/shard_map/ppermute | solution.py:373
  61.0 14.2 %all-to-all-start.3 = ((f32[32,1,1024]{2,1,0:T(1,128)}), f32[32,1,1024]{2,1,0:T(1,128)S(1)}, u32[]{:S(2)}, u32[]{:S(2)}) async-start(f32[32,1,1024]{2,1,0:T(1,128)} %bitcast.8), calls=%async_computation.3 | async-start | bytes 262144 | tf_op jit(solution)/shard_map/all_to_all | solution.py:323
  65.4 3.0 %collective-permute-start.1 = (f32[1,128]{1,0:T(1,128)S(1)}, f32[1,128]{1,0:T(1,128)S(1)}, u32[]{:S(2)}, u32[]{:S(2)}) collective-permute-start(f32[1,128]{1,0:T(1,128)S(1)} %get-tuple-element.25.refs_5_.refs_7_), channel_id=1, source_target_pairs={{0,0},{32,32},{64,64},{96,96},{128,128},{160,160},{192,192},{224,2... | collective-permute-start | bytes 1544 | tf_op jit(solution)/shard_map/ppermute | solution.py:373
  120.5 3.0 %collective-permute-start.2 = (f32[1,128]{1,0:T(1,128)S(1)}, f32[1,128]{1,0:T(1,128)S(1)}, u32[]{:S(2)}, u32[]{:S(2)}) collective-permute-start(f32[1,128]{1,0:T(1,128)S(1)} %shard_map.102), channel_id=1, source_target_pairs={{0,0},{32,32},{64,64},{96,96},{128,128},{160,160},{192,192},{224,2... | collective-permute-start | bytes 1544 | tf_op jit(solution)/shard_map/ppermute | solution.py:368

commit v6 on v5

--- a/solution.py
+++ b/solution.py
@@ -56,12 +56,14 @@
 
 def times_table(x, high_ref, low_ref):
     x_high, x_low = split(x)
-    return dot(x_high, high_ref[...]) + (dot(x_low, high_ref[...]) + dot(x_high, low_ref[...]))
+    both = dot(jnp.concatenate([x_high, x_low], axis=0), high_ref[...])
+    return both[: x.shape[0]] + (both[x.shape[0] :] + dot(x_high, low_ref[...]))
 
 
 def table_times(y, high_ref, low_ref):
     y_high, y_low = split(y)
-    return dot(high_ref[...], y_high) + (dot(high_ref[...], y_low) + dot(low_ref[...], y_high))
+    both = dot(high_ref[...], jnp.concatenate([y_high, y_low], axis=1))
+    return both[:, : y.shape[1]] + (both[:, y.shape[1] :] + dot(low_ref[...], y_high))
 
 
 def send_rows(x, high_ref, low_ref, out_ref):

time: 145 us -> 144 us (level)
  no operation moved by 1% of the time
where the time goes in v6:
time: 144 us
  blocking collectives  104 us (72%)
  waiting for transfers between devices  16.6 us (12%)
  starting transfers between devices  14.7 us (10%)
  Pallas kernels  7.89 us (5%)
    all_to_all x6, blocking collectives, swap(): return lax.all_to_all(blocks, 'krow', 0, 0, tiled=True).reshape(x.shape)  104 us
    all_to_all x2, waiting for transfers between devices, swap(): return lax.all_to_all(blocks, 'krow', 0, 0, tiled=True).reshape(x.shape)  13.4 us
    all_to_all x2, starting transfers between devices, swap(): return lax.all_to_all(blocks, 'krow', 0, 0, tiled=True).reshape(x.shape)  8.91 us
    pallas_call x10, Pallas kernels, call(): pl.pallas_call(body, out_shape=shapes, in_specs=[hbm if n in in_hbm else...  7.89 us
    ppermute x2, starting transfers between devices, per_device(): extra = extra + [lax.ppermute(total, ('macro', 'krow'), exchange)]  3.84 us
  transfers between devices with their start and end apart: 5, of which 5 were waited for; matrix products, arithmetic and copies ran while one was open for 0% of the time, Pallas kernels for 0%

profile of v6, /device:TPU:8, one launch (start us, length us, event | category | flops | bytes accessed | tf_op | source)
XLA Modules:
  0.0 143.6 jit_solution(10551813789121323563)
XLA Ops:
  0.6 2.2 %shard_map.95 = (f32[288,128]{1,0:T(8,128)}, f32[5,8,256]{2,1,0:T(8,128)}) custom-call(f32[16,8,256]{2,1,0:T(8,128)} %bitcast.19, bf16[256,256]{1,0:T(8,128)(2,1)} %constant.6.clone.refs_1_.refs_0_.refs_5_.refs_7_.refs_6_.refs_9_, bf16[256,256]{1,0:T(8,128)(2,1)} %constant.7.clone.refs_2_.refs_1_.refs_6_.refs_8_.refs_7_.refs_10_, f32[2,16,8,256]{3,2,1,0:T(8,128)} %refs_6_.3, ...), custom_call_target="tpu_custom_call" | custom-call | flops 50331648 | bytes 1048576 | tf_op jit(solution)/shard_map/pallas_call | solution.py:310
  2.8 20.3 %all_to_all.40 = f32[32,1,1152]{2,1,0:T(1,128)S(1)} all-to-all(f32[32,1,1152]{2,1,0:T(1,128)} %bitcast.38), channel_id=1, replica_groups=mesh['macro'=16,'krow'=32] {'krow'}, dimensions={0} | all-to-all | bytes 294912 | tf_op jit(solution)/shard_map/all_to_all | solution.py:325
  23.2 1.1 shard_map.96
  24.3 4.5 %all-to-all-start.1 = ((f32[32,1,1024]{2,1,0:T(1,128)}), f32[32,1,1024]{2,1,0:T(1,128)S(1)}, u32[]{:S(2)}, u32[]{:S(2)}) async-start(f32[32,1,1024]{2,1,0:T(1,128)} %bitcast.4), calls=%async_computation.1 | async-start | bytes 262144 | tf_op jit(solution)/shard_map/all_to_all | solution.py:325
  28.8 1.9 %collective-permute-start = (f32[1,128]{1,0:T(1,128)S(1)}, f32[1,128]{1,0:T(1,128)S(1)}, u32[]{:S(2)}, u32[]{:S(2)}) collective-permute-start(f32[1,128]{1,0:T(1,128)S(1)} %get-tuple-element.21), channel_id=1, source_target_pairs={{0,0},{32,32},{64,64},{96,96},{128,128},{160,160},{192,192},{224,2... | collective-permute-start | bytes 1544 | tf_op jit(solution)/shard_map/ppermute | solution.py:375
  30.7 1.1 collective-permute-done.refs_4_
  31.8 6.7 %all-to-all-done.1 = f32[32,1,1024]{2,1,0:T(1,128)S(1)} async-done(((f32[32,1,1024]{2,1,0:T(1,128)}), f32[32,1,1024]{2,1,0:T(1,128)S(1)}, u32[]{:S(2)}, u32[]{:S(2)}) %all-to-all-start.1) | async-done | bytes 131104 | tf_op jit(solution)/shard_map/all_to_all | solution.py:325
  38.5 0.5 shard_map.97
  39.0 20.7 %all_to_all.41 = f32[32,1,1152]{2,1,0:T(1,128)S(1)} all-to-all(f32[32,1,1152]{2,1,0:T(1,128)S(1)} %bitcast.34), channel_id=1, replica_groups=mesh['macro'=16,'krow'=32] {'krow'}, dimensions={0} | all-to-all | bytes 294912 | tf_op jit(solution)/shard_map/all_to_all | solution.py:325
  59.7 1.1 shard_map.98
  60.8 4.4 %all-to-all-start.3 = ((f32[32,1,1024]{2,1,0:T(1,128)}), f32[32,1,1024]{2,1,0:T(1,128)S(1)}, u32[]{:S(2)}, u32[]{:S(2)}) async-start(f32[32,1,1024]{2,1,0:T(1,128)} %bitcast.8), calls=%async_computation.3 | async-start | bytes 262144 | tf_op jit(solution)/shard_map/all_to_all | solution.py:325
  65.2 1.9 %collective-permute-start.1 = (f32[1,128]{1,0:T(1,128)S(1)}, f32[1,128]{1,0:T(1,128)S(1)}, u32[]{:S(2)}, u32[]{:S(2)}) collective-permute-start(f32[1,128]{1,0:T(1,128)S(1)} %get-tuple-element.25.refs_5_.refs_7_), channel_id=1, source_target_pairs={{0,0},{32,32},{64,64},{96,96},{128,128},{160,160},{192,192},{224,2... | collective-permute-start | bytes 1544 | tf_op jit(solution)/shard_map/ppermute | solution.py:375
  67.1 1.1 collective-permute-done.1.refs_6_
  68.2 6.7 %all-to-all-done.3 = f32[32,1,1024]{2,1,0:T(1,128)S(1)} async-done(((f32[32,1,1024]{2,1,0:T(1,128)}), f32[32,1,1024]{2,1,0:T(1,128)S(1)}, u32[]{:S(2)}, u32[]{:S(2)}) %all-to-all-start.3) | async-done | bytes 131104 | tf_op jit(solution)/shard_map/all_to_all | solution.py:325
  75.0 0.5 shard_map.99
  75.5 15.7 %all_to_all.42 = f32[32,1,1152]{2,1,0:T(1,128)S(1)} all-to-all(f32[32,1,1152]{2,1,0:T(1,128)S(1)} %bitcast.35), channel_id=1, replica_groups=mesh['macro'=16,'krow'=32] {'krow'}, dimensions={0} | all-to-all | bytes 294912 | tf_op jit(solution)/shard_map/all_to_all | solution.py:325
  91.2 0.4 shard_map.100
  91.7 13.9 %all_to_all.43 = f32[32,1,1024]{2,1,0:T(1,128)S(1)} all-to-all(f32[32,1,1024]{2,1,0:T(1,128)S(1)} %bitcast.37), channel_id=1, replica_groups=mesh['macro'=16,'krow'=32] {'krow'}, dimensions={0} | all-to-all | bytes 262144 | tf_op jit(solution)/shard_map/all_to_all | solution.py:325
  105.5 0.6 shard_map.101
  106.1 14.0 %all_to_all.44 = f32[32,1,1152]{2,1,0:T(1,128)S(1)} all-to-all(f32[32,1,1152]{2,1,0:T(1,128)S(1)} %bitcast.36), channel_id=1, replica_groups=mesh['macro'=16,'krow'=32] {'krow'}, dimensions={0} | all-to-all | bytes 294912 | tf_op jit(solution)/shard_map/all_to_all | solution.py:325
  120.2 1.9 %collective-permute-start.2 = (f32[1,128]{1,0:T(1,128)S(1)}, f32[1,128]{1,0:T(1,128)S(1)}, u32[]{:S(2)}, u32[]{:S(2)}) collective-permute-start(f32[1,128]{1,0:T(1,128)S(1)} %shard_map.102), channel_id=1, source_target_pairs={{0,0},{32,32},{64,64},{96,96},{128,128},{160,160},{192,192},{224,2... | collective-permute-start | bytes 1544 | tf_op jit(solution)/shard_map/ppermute | solution.py:370
  122.1 1.1 collective-permute-done.2.refs_0_
  123.6 18.9 %all_to_all.45 = f32[32,1,1152]{2,1,0:T(1,128)S(1)} all-to-all(f32[32,1,1152]{2,1,0:T(1,128)S(1)} %bitcast.30), channel_id=1, replica_groups=mesh['macro'=16,'krow'=32] {'krow'}, dimensions={0} | all-to-all | bytes 294912 | tf_op jit(solution)/shard_map/all_to_all | solution.py:325
  142.5 1.0 shard_map.104
  (14 shorter events, 0.5 us)
Async XLA Ops:
  0.6 22.5 %copy-start.3 = (f32[2,256,128]{2,1,0:T(8,128)S(1)}, f32[2,256,128]{2,1,0:T(8,128)}, u32[]{:S(2)}) copy-start(f32[2,256,128]{2,1,0:T(8,128)} %constant.8.clone.refs_2_.refs_3_) | copy-start | bytes 786436
  2.8 20.4 %copy-start = (bf16[256,256]{1,0:T(8,128)(2,1)S(1)}, bf16[256,256]{1,0:T(8,128)(2,1)}, u32[]{:S(2)}) copy-start(bf16[256,256]{1,0:T(8,128)(2,1)} %constant.7.clone.refs_2_.refs_1_.refs_6_.refs_8_.refs_7_.refs_10_) | copy-start | bytes 393220
  2.8 20.4 %copy-start.1 = (bf16[256,256]{1,0:T(8,128)(2,1)S(1)}, bf16[256,256]{1,0:T(8,128)(2,1)}, u32[]{:S(2)}) copy-start(bf16[256,256]{1,0:T(8,128)(2,1)} %constant.6.clone.refs_1_.refs_0_.refs_5_.refs_7_.refs_6_.refs_9_) | copy-start | bytes 393220
  23.2 15.3 %copy-start.4 = (f32[1,16,8,256]{3,2,1,0:T(8,128)S(1)}, f32[1,16,8,256]{3,2,1,0:T(8,128)}, u32[]{:S(2)}) copy-start(f32[1,16,8,256]{3,2,1,0:T(8,128)} %param.8) | copy-start | bytes 393220
  23.2 15.3 %copy-start.5 = (f32[5,8,256]{2,1,0:T(8,128)S(1)}, f32[5,8,256]{2,1,0:T(8,128)}, u32[]{:S(2)}) copy-start(f32[5,8,256]{2,1,0:T(8,128)} %get-tuple-element.20.refs_2_.refs_3_.refs_5_) | copy-start | bytes 122884
  24.3 14.2 %copy-start.2 = (f32[2,16,8,256]{3,2,1,0:T(8,128)S(1)}, f32[2,16,8,256]{3,2,1,0:T(8,128)}, u32[]{:S(2)}) copy-start(f32[2,16,8,256]{3,2,1,0:T(8,128)} %refs_6_.3) | copy-start | bytes 786436
  24.3 14.2 %all-to-all-start.1 = ((f32[32,1,1024]{2,1,0:T(1,128)}), f32[32,1,1024]{2,1,0:T(1,128)S(1)}, u32[]{:S(2)}, u32[]{:S(2)}) async-start(f32[32,1,1024]{2,1,0:T(1,128)} %bitcast.4), calls=%async_computation.1 | async-start | bytes 262144 | tf_op jit(solution)/shard_map/all_to_all | solution.py:325
  28.8 3.0 %collective-permute-start = (f32[1,128]{1,0:T(1,128)S(1)}, f32[1,128]{1,0:T(1,128)S(1)}, u32[]{:S(2)}, u32[]{:S(2)}) collective-permute-start(f32[1,128]{1,0:T(1,128)S(1)} %get-tuple-element.21), channel_id=1, source_target_pairs={{0,0},{32,32},{64,64},{96,96},{128,128},{160,160},{192,192},{224,2... | collective-permute-start | bytes 1544 | tf_op jit(solution)/shard_map/ppermute | solution.py:375
  60.8 14.2 %all-to-all-start.3 = ((f32[32,1,1024]{2,1,0:T(1,128)}), f32[32,1,1024]{2,1,0:T(1,128)S(1)}, u32[]{:S(2)}, u32[]{:S(2)}) async-start(f32[32,1,1024]{2,1,0:T(1,128)} %bitcast.8), calls=%async_computation.3 | async-start | bytes 262144 | tf_op jit(solution)/shard_map/all_to_all | solution.py:325
  65.2 3.0 %collective-permute-start.1 = (f32[1,128]{1,0:T(1,128)S(1)}, f32[1,128]{1,0:T(1,128)S(1)}, u32[]{:S(2)}, u32[]{:S(2)}) collective-permute-start(f32[1,128]{1,0:T(1,128)S(1)} %get-tuple-element.25.refs_5_.refs_7_), channel_id=1, source_target_pairs={{0,0},{32,32},{64,64},{96,96},{128,128},{160,160},{192,192},{224,2... | collective-permute-start | bytes 1544 | tf_op jit(solution)/shard_map/ppermute | solution.py:375
  120.2 3.0 %collective-permute-start.2 = (f32[1,128]{1,0:T(1,128)S(1)}, f32[1,128]{1,0:T(1,128)S(1)}, u32[]{:S(2)}, u32[]{:S(2)}) collective-permute-start(f32[1,128]{1,0:T(1,128)S(1)} %shard_map.102), channel_id=1, source_target_pairs={{0,0},{32,32},{64,64},{96,96},{128,128},{160,160},{192,192},{224,2... | collective-permute-start | bytes 1544 | tf_op jit(solution)/shard_map/ppermute | solution.py:370

commit v7 on v6

--- a/solution.py
+++ b/solution.py
@@ -15,6 +15,7 @@
 LANES = 128
 PEERS = 32
 POINTS = 16
+LONG = 1 << 36
 
 dephasing = 0.2
 coulomb_strength = 0.25
@@ -148,7 +149,11 @@
     out_ref[...] = rows_of(y_ref)
 
 
-def column_kernel(carries, y_ref, *refs):
+def weight_kernel(row_ref, out_ref):
+    out_ref[...] = row_ref[...] * prefix_weight()
+
+
+def column_kernel(carries, totals, y_ref, *refs):
     refs = list(refs)
     carry_ref = refs.pop(0) if carries else None
     high_ref, low_ref, spectrum_ref, out_ref = refs[:4]
@@ -159,8 +164,9 @@
     for peer in range(PEERS):
         out_ref[peer * step : peer * step + ROWS, :] = w[peer * ROWS : (peer + 1) * ROWS]
     if carries:
-        send_row(carry_ref[...] * prefix_weight(), out_ref)
-    else:
+        row = carry_ref[...]
+        send_row(row if totals is not None else row * prefix_weight(), out_ref)
+    if totals:
         refs[4][...] = rows_of(y_ref)
 
 
@@ -219,12 +225,12 @@
     state_refs = [refs.pop(0) for _ in range((1, 2, 2, 4)[section])]
     density_ref, state_ref = state_refs[0], state_refs[-1]
     fields_ref, momentum_ref = refs.pop(0), refs.pop(0)
-    sums_ref = refs.pop(0) if section in (1, 2) else None
-    permuted_ref = refs.pop(0) if section in (0, 1) else None
     earlier_refs = [refs.pop(0) for _ in range(2)] if section == 3 else None
     high_ref, low_ref = refs.pop(0), refs.pop(0)
     if section == 3:
         result_ref, emitted_out_ref = refs
+    elif section > 0:
+        out_ref, next_ref, arrived_ref = refs
     else:
         out_ref, next_ref = refs
     drive_row = (0, 1, 1, 2)[section]
@@ -232,16 +238,16 @@
     next_fraction = (0.5, 0.5, 1.0, None)[section]
     rate_scale = -coupling / GRID
 
-    if section == 3:
+    if section > 0:
         arrived = rows_of(back_ref)
-    upstream = None if section == 0 else arrived if section == 3 else sums_ref[...]
+    if section in (1, 2):
+        arrived_ref[...] = arrived
     potential = []
     for i in range(2):
         lane = 3 * i + drive_row
         value = fields_ref[BANDS, 0:1, lane : lane + 1]
         if section > 0:
-            lane = i if section == 3 else 2 + i
-            value = value + (time_step * fraction * rate_scale) * upstream[:, lane : lane + 1]
+            value = value + (time_step * fraction * rate_scale) * arrived[:, i : i + 1]
         potential.append(value)
 
     tiles = tiles_of(back_ref)
@@ -282,19 +288,14 @@
     if section < 3:
         state = next_ref[...].reshape(CHANNELS * ROWS, GRID)
         send_rows(state, high_ref, low_ref, out_ref)
-        row = currents_row(currents)
-        if section < 2:
-            lane = lax.broadcasted_iota(jnp.int32, (1, LANES), 1)
-            permuted = permuted_ref[...] * prefix_weight()
-            for i in range(2):
-                row = jnp.where(lane == 2 + i, permuted[:, i : i + 1], row)
-        send_row(row, out_ref)
+        if currents:
+            send_row(currents_row(currents), out_ref)
     else:
         first, second = (r[...] for r in earlier_refs)
         for i in range(2):
             total = (
-                first[:, 2 + i : 3 + i]
-                + 2.0 * second[:, 2 + i : 3 + i]
+                first[:, i : i + 1]
+                + 2.0 * second[:, i : i + 1]
                 + 2.0 * arrived[:, i : i + 1]
                 + arrived[:, 2 + i : 3 + i]
             )
@@ -303,7 +304,7 @@
             emitted_out_ref[:, i : i + 1] = emitted + (time_step / 6.0 * rate_scale) * total
 
 
-def call(body, outs, *args, in_hbm=(), scratch=(), vmem_mib=24):
+def call(body, outs, *args, in_hbm=(), scratch=(), vmem_mib=24, flops=1 << 26):
     shapes = [jax.ShapeDtypeStruct(s, jnp.float32) for s in outs]
     vmem = pl.BlockSpec(memory_space=pltpu.VMEM)
     hbm = pl.BlockSpec(memory_space=pltpu.HBM)
@@ -315,7 +316,7 @@
         scratch_shapes=scratch,
         compiler_params=pltpu.CompilerParams(vmem_limit_bytes=vmem_mib * 1024 * 1024),
         cost_estimate=pl.CostEstimate(
-            flops=2 * 3 * 128 * 256 * 256, bytes_accessed=1 << 20, transcendentals=0
+            flops=flops, bytes_accessed=1 << 20, transcendentals=0
         ),
     )(*args)
 
@@ -359,28 +360,36 @@
     )
     row = (1, LANES)
     states = [density]
-    sums = []
+    seen = []
+    carry = []
     for section in range(4):
         arrived = swap(out)
-        column = functools.partial(column_kernel, section == 3)
-        if section < 3:
-            mixed, total = call(column, [plain, row], arrived, high, low, spectrum)
-        else:
+        if section == 3:
             (total,) = call(total_kernel, [row], arrived)
-            carry = lax.ppermute(total, ("macro", "krow"), exchange)
-            (mixed,) = call(column, [carrying], arrived, carry, high, low, spectrum)
-        extra = [total] if section in (1, 2) else []
-        sums += extra
-        if section in (0, 1):
-            extra = extra + [lax.ppermute(total, ("macro", "krow"), exchange)]
+            carry = [lax.ppermute(total, ("macro", "krow"), exchange)]
+        totals = None if section == 3 else section < 2
+        mixed, *total = call(
+            functools.partial(column_kernel, bool(carry), totals),
+            [carrying if carry else plain] + [row] * bool(totals),
+            arrived,
+            *carry,
+            high,
+            low,
+            spectrum,
+        )
+        carry = []
+        if section < 2:
+            permuted = lax.ppermute(total[0], ("macro", "krow"), exchange)
+            carry = call(weight_kernel, [row], permuted, flops=LONG)
         back = swap(mixed)
         body = functools.partial(state_kernel, section)
         used = states if section == 3 else states[:1] if section == 0 else [density, states[-1]]
-        extra = sums if section == 3 else extra
-        args = [back, *used, fields, momentum, *extra, high, low]
+        args = [back, *used, fields, momentum, *(seen if section == 3 else []), high, low]
         if section < 3:
-            out, state = call(body, [carrying, state_shape], *args)
+            shape = plain if section == 1 else carrying
+            out, state, *rows = call(body, [shape, state_shape] + [row] * (section > 0), *args)
             states.append(state)
+            seen += rows
         else:
             density_next, emitted_next = call(body, [state_shape, (1, 2)], *args)
     return density_next.reshape(1, CHANNELS, ROWS, GRID), emitted_next

time: 144 us -> 143 us (level)
  blocking collectives: 104 us -> 67.2 us
  waiting for transfers between devices: 16.6 us -> 36.5 us
  starting transfers between devices: 14.7 us -> 28.6 us
    all_to_all x6 -> x4, blocking collectives: 104 us -> 67.2 us  [swap(): return lax.all_to_all(blocks, 'krow', 0, 0, tiled=True).reshape(x.shape)]
    all_to_all x2 -> x4, waiting for transfers between devices: 13.4 us -> 35.4 us  [swap(): return lax.all_to_all(blocks, 'krow', 0, 0, tiled=True).reshape(x.shape)]
    all_to_all x2 -> x4, starting transfers between devices: 8.91 us -> 22.9 us  [swap(): return lax.all_to_all(blocks, 'krow', 0, 0, tiled=True).reshape(x.shape)]
    ppermute x3, waiting for transfers between devices: 3.26 us -> 1.09 us  [the longest x1 1.09 us: per_device(): carry = [lax.ppermute(total, ('macro', 'krow'), exchange)]]
    pallas_call x10 -> x12, Pallas kernels: 7.89 us -> 9.25 us  [call(): pl.pallas_call(body, out_shape=shapes, in_specs=[hbm if n in in_hbm else...]
  transfers between devices with their start and end apart: 5 -> 7, of which waited for: 5 -> 5; matrix products, arithmetic and copies ran while one was open for 0% -> 0% of each run, Pallas kernels for 0% -> 2%
where the time goes in v7:
time: 143 us; the launch traced here: 142 us
  blocking collectives  67.2 us (47%)
  waiting for transfers between devices  36.5 us (26%)
  starting transfers between devices  28.6 us (20%)
  Pallas kernels  9.25 us (6%)
    all_to_all x4, blocking collectives, swap(): return lax.all_to_all(blocks, 'krow', 0, 0, tiled=True).reshape(x.shape)  67.2 us
    all_to_all x4, waiting for transfers between devices, swap(): return lax.all_to_all(blocks, 'krow', 0, 0, tiled=True).reshape(x.shape)  35.4 us
    all_to_all x4, starting transfers between devices, swap(): return lax.all_to_all(blocks, 'krow', 0, 0, tiled=True).reshape(x.shape)  22.9 us
    pallas_call x12, Pallas kernels, call(): pl.pallas_call(body, out_shape=shapes, in_specs=[hbm if n in in_hbm else...  9.25 us
    ppermute x2, starting transfers between devices, per_device(): permuted = lax.ppermute(total[0], ('macro', 'krow'), exchange)  3.84 us
  transfers between devices with their start and end apart: 7, of which 5 were waited for; matrix products, arithmetic and copies ran while one was open for 0% of the time, Pallas kernels for 2%

profile of v7, /device:TPU:8, one launch (start us, length us, event | category | flops | bytes accessed | tf_op | source)
XLA Modules:
  0.0 142.5 jit_solution(1582839274085924283)
XLA Ops:
  0.6 2.2 %shard_map.95 = (f32[288,128]{1,0:T(8,128)}, f32[5,8,256]{2,1,0:T(8,128)}) custom-call(f32[16,8,256]{2,1,0:T(8,128)} %bitcast.19, bf16[256,256]{1,0:T(8,128)(2,1)} %constant.6.clone.refs_1_.refs_0_.refs_4_.refs_5_.refs_9_, bf16[256,256]{1,0:T(8,128)(2,1)} %constant.7.clone.refs_2_.refs_1_.refs_5_.refs_6_.refs_10_, f32[2,16,8,256]{3,2,1,0:T(8,128)} %refs_6_.3, ...), custom_call_target="tpu_custom_call" | custom-call | flops 67108864 | bytes 1048576 | tf_op jit(solution)/shard_map/pallas_call | solution.py:311
  2.8 20.3 %all_to_all.40 = f32[32,1,1152]{2,1,0:T(1,128)S(1)} all-to-all(f32[32,1,1152]{2,1,0:T(1,128)} %bitcast.36), channel_id=1, replica_groups=mesh['macro'=16,'krow'=32] {'krow'}, dimensions={0} | all-to-all | bytes 294912 | tf_op jit(solution)/shard_map/all_to_all | solution.py:326
  23.2 1.1 shard_map.96
  24.3 4.5 %all-to-all-start.1 = ((f32[32,1,1024]{2,1,0:T(1,128)}), f32[32,1,1024]{2,1,0:T(1,128)S(1)}, u32[]{:S(2)}, u32[]{:S(2)}) async-start(f32[32,1,1024]{2,1,0:T(1,128)} %bitcast.4), calls=%async_computation.1 | async-start | bytes 262144 | tf_op jit(solution)/shard_map/all_to_all | solution.py:326
  28.8 1.9 %collective-permute-start = (f32[1,128]{1,0:T(1,128)S(1)}, f32[1,128]{1,0:T(1,128)S(1)}, u32[]{:S(2)}, u32[]{:S(2)}) collective-permute-start(f32[1,128]{1,0:T(1,128)S(1)} %get-tuple-element.22), channel_id=1, source_target_pairs={{0,0},{32,32},{64,64},{96,96},{128,128},{160,160},{192,192},{224,2... | collective-permute-start | bytes 1544 | tf_op jit(solution)/shard_map/ppermute | solution.py:382
  30.7 7.7 %all-to-all-done.1 = f32[32,1,1024]{2,1,0:T(1,128)S(1)} async-done(((f32[32,1,1024]{2,1,0:T(1,128)}), f32[32,1,1024]{2,1,0:T(1,128)S(1)}, u32[]{:S(2)}, u32[]{:S(2)}) %all-to-all-start.1) | async-done | bytes 131104 | tf_op jit(solution)/shard_map/all_to_all | solution.py:326
  38.5 1.2 shard_map.97
  39.7 9.6 %all-to-all-start.2 = ((f32[32,1,1152]{2,1,0:T(1,128)}), f32[32,1,1152]{2,1,0:T(1,128)S(1)}, u32[]{:S(2)}, u32[]{:S(2)}) async-start(f32[32,1,1152]{2,1,0:T(1,128)} %bitcast.6), calls=%async_computation.2 | async-start | bytes 294912 | tf_op jit(solution)/shard_map/all_to_all | solution.py:326
  49.3 9.8 %all-to-all-done.2 = f32[32,1,1152]{2,1,0:T(1,128)S(1)} async-done(((f32[32,1,1152]{2,1,0:T(1,128)}), f32[32,1,1152]{2,1,0:T(1,128)S(1)}, u32[]{:S(2)}, u32[]{:S(2)}) %all-to-all-start.2) | async-done | bytes 147488 | tf_op jit(solution)/shard_map/all_to_all | solution.py:326
  59.1 1.1 shard_map.99
  60.2 4.5 %all-to-all-start.3 = ((f32[32,1,1152]{2,1,0:T(1,128)}), f32[32,1,1152]{2,1,0:T(1,128)S(1)}, u32[]{:S(2)}, u32[]{:S(2)}) async-start(f32[32,1,1152]{2,1,0:T(1,128)} %bitcast.8), calls=%async_computation.3 | async-start | bytes 294912 | tf_op jit(solution)/shard_map/all_to_all | solution.py:326
  64.7 1.9 %collective-permute-start.1 = (f32[1,128]{1,0:T(1,128)S(1)}, f32[1,128]{1,0:T(1,128)S(1)}, u32[]{:S(2)}, u32[]{:S(2)}) collective-permute-start(f32[1,128]{1,0:T(1,128)S(1)} %get-tuple-element.26), channel_id=1, source_target_pairs={{0,0},{32,32},{64,64},{96,96},{128,128},{160,160},{192,192},{224,2... | collective-permute-start | bytes 1544 | tf_op jit(solution)/shard_map/ppermute | solution.py:382
  66.6 8.0 %all-to-all-done.3 = f32[32,1,1152]{2,1,0:T(1,128)S(1)} async-done(((f32[32,1,1152]{2,1,0:T(1,128)}), f32[32,1,1152]{2,1,0:T(1,128)S(1)}, u32[]{:S(2)}, u32[]{:S(2)}) %all-to-all-start.3) | async-done | bytes 147488 | tf_op jit(solution)/shard_map/all_to_all | solution.py:326
  74.6 1.2 shard_map.100
  75.8 4.4 %all-to-all-start.4 = ((f32[32,1,1024]{2,1,0:T(1,128)}), f32[32,1,1024]{2,1,0:T(1,128)S(1)}, u32[]{:S(2)}, u32[]{:S(2)}) async-start(f32[32,1,1024]{2,1,0:T(1,128)} %bitcast.10), calls=%async_computation.4 | async-start | bytes 262144 | tf_op jit(solution)/shard_map/all_to_all | solution.py:326
  80.2 9.8 %all-to-all-done.4 = f32[32,1,1024]{2,1,0:T(1,128)S(1)} async-done(((f32[32,1,1024]{2,1,0:T(1,128)}), f32[32,1,1024]{2,1,0:T(1,128)S(1)}, u32[]{:S(2)}, u32[]{:S(2)}) %all-to-all-start.4) | async-done | bytes 131104 | tf_op jit(solution)/shard_map/all_to_all | solution.py:326
  90.1 0.4 shard_map.102
  90.5 14.0 %all_to_all.41 = f32[32,1,1152]{2,1,0:T(1,128)S(1)} all-to-all(f32[32,1,1152]{2,1,0:T(1,128)S(1)} %bitcast.30), channel_id=1, replica_groups=mesh['macro'=16,'krow'=32] {'krow'}, dimensions={0} | all-to-all | bytes 294912 | tf_op jit(solution)/shard_map/all_to_all | solution.py:326
  104.5 0.6 shard_map.103
  105.0 14.0 %all_to_all.42 = f32[32,1,1152]{2,1,0:T(1,128)S(1)} all-to-all(f32[32,1,1152]{2,1,0:T(1,128)S(1)} %bitcast.35), channel_id=1, replica_groups=mesh['macro'=16,'krow'=32] {'krow'}, dimensions={0} | all-to-all | bytes 294912 | tf_op jit(solution)/shard_map/all_to_all | solution.py:326
  119.1 1.9 %collective-permute-start.2 = (f32[1,128]{1,0:T(1,128)S(1)}, f32[1,128]{1,0:T(1,128)S(1)}, u32[]{:S(2)}, u32[]{:S(2)}) collective-permute-start(f32[1,128]{1,0:T(1,128)S(1)} %shard_map.104), channel_id=1, source_target_pairs={{0,0},{32,32},{64,64},{96,96},{128,128},{160,160},{192,192},{224,2... | collective-permute-start | bytes 1544 | tf_op jit(solution)/shard_map/ppermute | solution.py:369
  121.0 1.1 collective-permute-done.2.refs_0_
  122.5 18.9 %all_to_all.43 = f32[32,1,1152]{2,1,0:T(1,128)S(1)} all-to-all(f32[32,1,1152]{2,1,0:T(1,128)S(1)} %bitcast.29), channel_id=1, replica_groups=mesh['macro'=16,'krow'=32] {'krow'}, dimensions={0} | all-to-all | bytes 294912 | tf_op jit(solution)/shard_map/all_to_all | solution.py:326
  141.4 1.0 shard_map.106
  (18 shorter events, 0.5 us)
Async XLA Ops:
  0.6 22.6 %copy-start.3 = (f32[2,256,128]{2,1,0:T(8,128)S(1)}, f32[2,256,128]{2,1,0:T(8,128)}, u32[]{:S(2)}) copy-start(f32[2,256,128]{2,1,0:T(8,128)} %constant.8.clone.refs_2_.refs_3_) | copy-start | bytes 786436
  2.8 20.4 %copy-start = (bf16[256,256]{1,0:T(8,128)(2,1)S(1)}, bf16[256,256]{1,0:T(8,128)(2,1)}, u32[]{:S(2)}) copy-start(bf16[256,256]{1,0:T(8,128)(2,1)} %constant.7.clone.refs_2_.refs_1_.refs_5_.refs_6_.refs_10_) | copy-start | bytes 393220
  2.8 20.4 %copy-start.1 = (bf16[256,256]{1,0:T(8,128)(2,1)S(1)}, bf16[256,256]{1,0:T(8,128)(2,1)}, u32[]{:S(2)}) copy-start(bf16[256,256]{1,0:T(8,128)(2,1)} %constant.6.clone.refs_1_.refs_0_.refs_4_.refs_5_.refs_9_) | copy-start | bytes 393220
  23.2 15.3 %copy-start.4 = (f32[1,16,8,256]{3,2,1,0:T(8,128)S(1)}, f32[1,16,8,256]{3,2,1,0:T(8,128)}, u32[]{:S(2)}) copy-start(f32[1,16,8,256]{3,2,1,0:T(8,128)} %param.8) | copy-start | bytes 393220
  23.2 15.3 %copy-start.5 = (f32[5,8,256]{2,1,0:T(8,128)S(1)}, f32[5,8,256]{2,1,0:T(8,128)}, u32[]{:S(2)}) copy-start(f32[5,8,256]{2,1,0:T(8,128)} %get-tuple-element.20.refs_2_.refs_3_.refs_5_) | copy-start | bytes 122884
  24.3 14.2 %copy-start.2 = (f32[2,16,8,256]{3,2,1,0:T(8,128)S(1)}, f32[2,16,8,256]{3,2,1,0:T(8,128)}, u32[]{:S(2)}) copy-start(f32[2,16,8,256]{3,2,1,0:T(8,128)} %refs_6_.3) | copy-start | bytes 786436
  24.3 14.2 %all-to-all-start.1 = ((f32[32,1,1024]{2,1,0:T(1,128)}), f32[32,1,1024]{2,1,0:T(1,128)S(1)}, u32[]{:S(2)}, u32[]{:S(2)}) async-start(f32[32,1,1024]{2,1,0:T(1,128)} %bitcast.4), calls=%async_computation.1 | async-start | bytes 262144 | tf_op jit(solution)/shard_map/all_to_all | solution.py:326
  28.8 20.5 %collective-permute-start = (f32[1,128]{1,0:T(1,128)S(1)}, f32[1,128]{1,0:T(1,128)S(1)}, u32[]{:S(2)}, u32[]{:S(2)}) collective-permute-start(f32[1,128]{1,0:T(1,128)S(1)} %get-tuple-element.22), channel_id=1, source_target_pairs={{0,0},{32,32},{64,64},{96,96},{128,128},{160,160},{192,192},{224,2... | collective-permute-start | bytes 1544 | tf_op jit(solution)/shard_map/ppermute | solution.py:382
  39.7 19.4 %all-to-all-start.2 = ((f32[32,1,1152]{2,1,0:T(1,128)}), f32[32,1,1152]{2,1,0:T(1,128)S(1)}, u32[]{:S(2)}, u32[]{:S(2)}) async-start(f32[32,1,1152]{2,1,0:T(1,128)} %bitcast.6), calls=%async_computation.2 | async-start | bytes 294912 | tf_op jit(solution)/shard_map/all_to_all | solution.py:326
  60.2 14.4 %all-to-all-start.3 = ((f32[32,1,1152]{2,1,0:T(1,128)}), f32[32,1,1152]{2,1,0:T(1,128)S(1)}, u32[]{:S(2)}, u32[]{:S(2)}) async-start(f32[32,1,1152]{2,1,0:T(1,128)} %bitcast.8), calls=%async_computation.3 | async-start | bytes 294912 | tf_op jit(solution)/shard_map/all_to_all | solution.py:326
  64.7 15.6 %collective-permute-start.1 = (f32[1,128]{1,0:T(1,128)S(1)}, f32[1,128]{1,0:T(1,128)S(1)}, u32[]{:S(2)}, u32[]{:S(2)}) collective-permute-start(f32[1,128]{1,0:T(1,128)S(1)} %get-tuple-element.26), channel_id=1, source_target_pairs={{0,0},{32,32},{64,64},{96,96},{128,128},{160,160},{192,192},{224,2... | collective-permute-start | bytes 1544 | tf_op jit(solution)/shard_map/ppermute | solution.py:382
  75.8 14.3 %all-to-all-start.4 = ((f32[32,1,1024]{2,1,0:T(1,128)}), f32[32,1,1024]{2,1,0:T(1,128)S(1)}, u32[]{:S(2)}, u32[]{:S(2)}) async-start(f32[32,1,1024]{2,1,0:T(1,128)} %bitcast.10), calls=%async_computation.4 | async-start | bytes 262144 | tf_op jit(solution)/shard_map/all_to_all | solution.py:326
  119.1 3.0 %collective-permute-start.2 = (f32[1,128]{1,0:T(1,128)S(1)}, f32[1,128]{1,0:T(1,128)S(1)}, u32[]{:S(2)}, u32[]{:S(2)}) collective-permute-start(f32[1,128]{1,0:T(1,128)S(1)} %shard_map.104), channel_id=1, source_target_pairs={{0,0},{32,32},{64,64},{96,96},{128,128},{160,160},{192,192},{224,2... | collective-permute-start | bytes 1544 | tf_op jit(solution)/shard_map/ppermute | solution.py:369

commit v8 on v6

--- a/solution.py
+++ b/solution.py
@@ -21,6 +21,13 @@
 coupling = 2.0
 time_step = 0.1
 screening_width = 1.0
+
+SEATS = dict(
+    zip(
+        (0, 1, 8, 2, 9, 16, 24, 3, 10, 25, 17, 6, 7, 18, 26, 11),
+        (8, 9, 10, 11, 14, 15, 12, 13, 6, 7, 4, 5, 2, 3, 1, 0),
+    )
+)
 
 PAIRS = [(a, b) for a in range(BANDS) for b in range(a + 1, BANDS)]
 
@@ -140,8 +147,11 @@
 
 def prefix_weight():
     place, point = lax.axis_index("krow"), lax.axis_index("macro")
-    upstream = jnp.logical_and(place < POINTS, (point ^ place) < point)
-    return jnp.where(place == 0, 0.5, jnp.where(upstream, 1.0, 0.0))
+    shift = jnp.int32(-1)
+    for seat, value in SEATS.items():
+        shift = jnp.where(place == seat, value, shift)
+    upstream = jnp.logical_and(shift > 0, (point ^ shift) < point)
+    return jnp.where(shift == 0, 0.5, jnp.where(upstream, 1.0, 0.0))
 
 
 def total_kernel(y_ref, out_ref):
@@ -332,7 +342,11 @@
     plain = (PEERS * ROWS, LANES)
     carrying = (PEERS * (ROWS + 1), LANES)
     state_shape = (CHANNELS, ROWS, GRID)
-    exchange = [(m * PEERS + j, (m ^ j) * PEERS + j) for j in range(POINTS) for m in range(POINTS)]
+    exchange = [
+        (m * PEERS + seat, (m ^ shift) * PEERS + seat)
+        for seat, shift in SEATS.items()
+        for m in range(POINTS)
+    ]
 
     out, fields = call(
         first_kernel,

time: 144 us -> 140 us (0.972)
  blocking collectives: 104 us -> 93.6 us
  starting transfers between devices: 14.7 us -> 23 us
  waiting for transfers between devices: 16.6 us -> 14.4 us
    all_to_all x2, waiting for transfers between devices: 13.4 us -> 0.91 us  [swap(): return lax.all_to_all(blocks, 'krow', 0, 0, tiled=True).reshape(x.shape)]
    all_to_all x6, blocking collectives: 104 us -> 93.6 us  [swap(): return lax.all_to_all(blocks, 'krow', 0, 0, tiled=True).reshape(x.shape)]
    ppermute x2, starting transfers between devices: 3.84 us -> 12.3 us  [per_device(): extra = extra + [lax.ppermute(total, ('macro', 'krow'), exchange)]]
    ppermute x1, waiting for transfers between devices: 1.09 us -> 6.84 us  [per_device(): carry = lax.ppermute(total, ('macro', 'krow'), exchange)]
    ppermute x2, waiting for transfers between devices: 2.17 us -> 6.69 us  [per_device(): extra = extra + [lax.ppermute(total, ('macro', 'krow'), exchange)]]
  transfers between devices with their start and end apart: 5 -> 5, of which waited for: 5 -> 4; matrix products, arithmetic and copies ran while one was open for 0% -> 0% of each run, Pallas kernels for 0% -> 0%
where the time goes in v8:
time: 140 us
  blocking collectives  93.6 us (67%)
  starting transfers between devices  23 us (16%)
  waiting for transfers between devices  14.4 us (10%)
  Pallas kernels  7.9 us (6%)
    all_to_all x6, blocking collectives, swap(): return lax.all_to_all(blocks, 'krow', 0, 0, tiled=True).reshape(x.shape)  93.6 us
    ppermute x2, starting transfers between devices, per_device(): extra = extra + [lax.ppermute(total, ('macro', 'krow'), exchange)]  12.3 us
    all_to_all x2, starting transfers between devices, swap(): return lax.all_to_all(blocks, 'krow', 0, 0, tiled=True).reshape(x.shape)  8.77 us
    pallas_call x10, Pallas kernels, call(): pl.pallas_call(body, out_shape=shapes, in_specs=[hbm if n in in_hbm else...  7.9 us
    ppermute x1, waiting for transfers between devices, per_device(): carry = lax.ppermute(total, ('macro', 'krow'), exchange)  6.84 us
    ppermute x2, waiting for transfers between devices, per_device(): extra = extra + [lax.ppermute(total, ('macro', 'krow'), exchange)]  6.69 us
  transfers between devices with their start and end apart: 5, of which 4 were waited for; matrix products, arithmetic and copies ran while one was open for 0% of the time, Pallas kernels for 0%

profile of v8, /device:TPU:8, one launch (start us, length us, event | category | flops | bytes accessed | tf_op | source)
XLA Modules:
  0.0 139.7 jit_solution(4564101784053474440)
XLA Ops:
  0.6 2.2 %shard_map.95 = (f32[288,128]{1,0:T(8,128)}, f32[5,8,256]{2,1,0:T(8,128)}) custom-call(f32[16,8,256]{2,1,0:T(8,128)} %bitcast.19, bf16[256,256]{1,0:T(8,128)(2,1)} %constant.6.clone.refs_1_.refs_0_.refs_5_.refs_7_.refs_6_.refs_9_, bf16[256,256]{1,0:T(8,128)(2,1)} %constant.7.clone.refs_2_.refs_1_.refs_6_.refs_8_.refs_7_.refs_10_, f32[2,16,8,256]{3,2,1,0:T(8,128)} %refs_6_.3, ...), custom_call_target="tpu_custom_call" | custom-call | flops 50331648 | bytes 1048576 | tf_op jit(solution)/shard_map/pallas_call | solution.py:320
  2.8 20.3 %all_to_all.40 = f32[32,1,1152]{2,1,0:T(1,128)S(1)} all-to-all(f32[32,1,1152]{2,1,0:T(1,128)} %bitcast.38), channel_id=1, replica_groups=mesh['macro'=16,'krow'=32] {'krow'}, dimensions={0} | all-to-all | bytes 294912 | tf_op jit(solution)/shard_map/all_to_all | solution.py:335
  23.2 1.1 shard_map.96
  24.3 4.5 %all-to-all-start.1 = ((f32[32,1,1024]{2,1,0:T(1,128)}), f32[32,1,1024]{2,1,0:T(1,128)S(1)}, u32[]{:S(2)}, u32[]{:S(2)}) async-start(f32[32,1,1024]{2,1,0:T(1,128)} %bitcast.4), calls=%async_computation.1 | async-start | bytes 262144 | tf_op jit(solution)/shard_map/all_to_all | solution.py:335
  28.8 9.0 %collective-permute-start = (f32[1,128]{1,0:T(1,128)S(1)}, f32[1,128]{1,0:T(1,128)S(1)}, u32[]{:S(2)}, u32[]{:S(2)}) collective-permute-start(f32[1,128]{1,0:T(1,128)S(1)} %get-tuple-element.21), channel_id=1, source_target_pairs={{0,256},{32,288},{64,320},{96,352},{128,384},{160,416},{192,448},{... | collective-permute-start | bytes 1544 | tf_op jit(solution)/shard_map/ppermute | solution.py:389
  37.8 1.3 collective-permute-done.refs_4_
  39.1 0.5 shard_map.97
  39.6 17.4 %all_to_all.41 = f32[32,1,1152]{2,1,0:T(1,128)S(1)} all-to-all(f32[32,1,1152]{2,1,0:T(1,128)S(1)} %bitcast.34), channel_id=1, replica_groups=mesh['macro'=16,'krow'=32] {'krow'}, dimensions={0} | all-to-all | bytes 294912 | tf_op jit(solution)/shard_map/all_to_all | solution.py:335
  57.0 1.1 shard_map.98
  58.1 4.3 %all-to-all-start.3 = ((f32[32,1,1024]{2,1,0:T(1,128)}), f32[32,1,1024]{2,1,0:T(1,128)S(1)}, u32[]{:S(2)}, u32[]{:S(2)}) async-start(f32[32,1,1024]{2,1,0:T(1,128)} %bitcast.8), calls=%async_computation.3 | async-start | bytes 262144 | tf_op jit(solution)/shard_map/all_to_all | solution.py:335
  62.4 3.3 %collective-permute-start.1 = (f32[1,128]{1,0:T(1,128)S(1)}, f32[1,128]{1,0:T(1,128)S(1)}, u32[]{:S(2)}, u32[]{:S(2)}) collective-permute-start(f32[1,128]{1,0:T(1,128)S(1)} %get-tuple-element.25.refs_5_.refs_7_), channel_id=1, source_target_pairs={{0,256},{32,288},{64,320},{96,352},{128,384},{160,416},{192,448},{... | collective-permute-start | bytes 1544 | tf_op jit(solution)/shard_map/ppermute | solution.py:389
  65.7 5.4 %collective-permute-done.1.refs_6_ = f32[1,128]{1,0:T(1,128)S(1)} collective-permute-done((f32[1,128]{1,0:T(1,128)S(1)}, f32[1,128]{1,0:T(1,128)S(1)}, u32[]{:S(2)}, u32[]{:S(2)}) %collective-permute-start.1) | collective-permute-done | bytes 544 | tf_op jit(solution)/shard_map/ppermute | solution.py:389
  71.1 0.9 all-to-all-done.3
  72.0 0.5 shard_map.99
  72.6 14.1 %all_to_all.42 = f32[32,1,1152]{2,1,0:T(1,128)S(1)} all-to-all(f32[32,1,1152]{2,1,0:T(1,128)S(1)} %bitcast.35), channel_id=1, replica_groups=mesh['macro'=16,'krow'=32] {'krow'}, dimensions={0} | all-to-all | bytes 294912 | tf_op jit(solution)/shard_map/all_to_all | solution.py:335
  86.6 0.4 shard_map.100
  87.1 13.8 %all_to_all.43 = f32[32,1,1024]{2,1,0:T(1,128)S(1)} all-to-all(f32[32,1,1024]{2,1,0:T(1,128)S(1)} %bitcast.37), channel_id=1, replica_groups=mesh['macro'=16,'krow'=32] {'krow'}, dimensions={0} | all-to-all | bytes 262144 | tf_op jit(solution)/shard_map/all_to_all | solution.py:335
  100.9 0.6 shard_map.101
  101.4 14.0 %all_to_all.44 = f32[32,1,1152]{2,1,0:T(1,128)S(1)} all-to-all(f32[32,1,1152]{2,1,0:T(1,128)S(1)} %bitcast.36), channel_id=1, replica_groups=mesh['macro'=16,'krow'=32] {'krow'}, dimensions={0} | all-to-all | bytes 294912 | tf_op jit(solution)/shard_map/all_to_all | solution.py:335
  115.5 1.9 %collective-permute-start.2 = (f32[1,128]{1,0:T(1,128)S(1)}, f32[1,128]{1,0:T(1,128)S(1)}, u32[]{:S(2)}, u32[]{:S(2)}) collective-permute-start(f32[1,128]{1,0:T(1,128)S(1)} %shard_map.102), channel_id=1, source_target_pairs={{0,256},{32,288},{64,320},{96,352},{128,384},{160,416},{192,448},{... | collective-permute-start | bytes 1544 | tf_op jit(solution)/shard_map/ppermute | solution.py:384
  117.4 6.8 %collective-permute-done.2.refs_0_ = f32[1,128]{1,0:T(1,128)S(1)} collective-permute-done((f32[1,128]{1,0:T(1,128)S(1)}, f32[1,128]{1,0:T(1,128)S(1)}, u32[]{:S(2)}, u32[]{:S(2)}) %collective-permute-start.2) | collective-permute-done | bytes 544 | tf_op jit(solution)/shard_map/ppermute | solution.py:384
  124.3 0.4 shard_map.103
  124.7 13.9 %all_to_all.45 = f32[32,1,1152]{2,1,0:T(1,128)S(1)} all-to-all(f32[32,1,1152]{2,1,0:T(1,128)S(1)} %bitcast.30), channel_id=1, replica_groups=mesh['macro'=16,'krow'=32] {'krow'}, dimensions={0} | all-to-all | bytes 294912 | tf_op jit(solution)/shard_map/all_to_all | solution.py:335
  138.6 1.0 shard_map.104
  (14 shorter events, 0.0 us)
Async XLA Ops:
  0.6 22.5 %copy-start.3 = (f32[2,256,128]{2,1,0:T(8,128)S(1)}, f32[2,256,128]{2,1,0:T(8,128)}, u32[]{:S(2)}) copy-start(f32[2,256,128]{2,1,0:T(8,128)} %constant.8.clone.refs_2_.refs_3_) | copy-start | bytes 786436
  2.8 20.4 %copy-start = (bf16[256,256]{1,0:T(8,128)(2,1)S(1)}, bf16[256,256]{1,0:T(8,128)(2,1)}, u32[]{:S(2)}) copy-start(bf16[256,256]{1,0:T(8,128)(2,1)} %constant.7.clone.refs_2_.refs_1_.refs_6_.refs_8_.refs_7_.refs_10_) | copy-start | bytes 393220
  2.8 20.4 %copy-start.1 = (bf16[256,256]{1,0:T(8,128)(2,1)S(1)}, bf16[256,256]{1,0:T(8,128)(2,1)}, u32[]{:S(2)}) copy-start(bf16[256,256]{1,0:T(8,128)(2,1)} %constant.6.clone.refs_1_.refs_0_.refs_5_.refs_7_.refs_6_.refs_9_) | copy-start | bytes 393220
  23.2 15.9 %copy-start.4 = (f32[1,16,8,256]{3,2,1,0:T(8,128)S(1)}, f32[1,16,8,256]{3,2,1,0:T(8,128)}, u32[]{:S(2)}) copy-start(f32[1,16,8,256]{3,2,1,0:T(8,128)} %param.8) | copy-start | bytes 393220
  23.2 15.9 %copy-start.5 = (f32[5,8,256]{2,1,0:T(8,128)S(1)}, f32[5,8,256]{2,1,0:T(8,128)}, u32[]{:S(2)}) copy-start(f32[5,8,256]{2,1,0:T(8,128)} %get-tuple-element.20.refs_2_.refs_3_.refs_5_) | copy-start | bytes 122884
  24.3 14.8 %copy-start.2 = (f32[2,16,8,256]{3,2,1,0:T(8,128)S(1)}, f32[2,16,8,256]{3,2,1,0:T(8,128)}, u32[]{:S(2)}) copy-start(f32[2,16,8,256]{3,2,1,0:T(8,128)} %refs_6_.3) | copy-start | bytes 786436
  24.3 14.7 %all-to-all-start.1 = ((f32[32,1,1024]{2,1,0:T(1,128)}), f32[32,1,1024]{2,1,0:T(1,128)S(1)}, u32[]{:S(2)}, u32[]{:S(2)}) async-start(f32[32,1,1024]{2,1,0:T(1,128)} %bitcast.4), calls=%async_computation.1 | async-start | bytes 262144 | tf_op jit(solution)/shard_map/all_to_all | solution.py:335
  28.8 10.2 %collective-permute-start = (f32[1,128]{1,0:T(1,128)S(1)}, f32[1,128]{1,0:T(1,128)S(1)}, u32[]{:S(2)}, u32[]{:S(2)}) collective-permute-start(f32[1,128]{1,0:T(1,128)S(1)} %get-tuple-element.21), channel_id=1, source_target_pairs={{0,256},{32,288},{64,320},{96,352},{128,384},{160,416},{192,448},{... | collective-permute-start | bytes 1544 | tf_op jit(solution)/shard_map/ppermute | solution.py:389
  58.1 14.0 %all-to-all-start.3 = ((f32[32,1,1024]{2,1,0:T(1,128)}), f32[32,1,1024]{2,1,0:T(1,128)S(1)}, u32[]{:S(2)}, u32[]{:S(2)}) async-start(f32[32,1,1024]{2,1,0:T(1,128)} %bitcast.8), calls=%async_computation.3 | async-start | bytes 262144 | tf_op jit(solution)/shard_map/all_to_all | solution.py:335
  62.4 8.8 %collective-permute-start.1 = (f32[1,128]{1,0:T(1,128)S(1)}, f32[1,128]{1,0:T(1,128)S(1)}, u32[]{:S(2)}, u32[]{:S(2)}) collective-permute-start(f32[1,128]{1,0:T(1,128)S(1)} %get-tuple-element.25.refs_5_.refs_7_), channel_id=1, source_target_pairs={{0,256},{32,288},{64,320},{96,352},{128,384},{160,416},{192,448},{... | collective-permute-start | bytes 1544 | tf_op jit(solution)/shard_map/ppermute | solution.py:389
  115.5 8.8 %collective-permute-start.2 = (f32[1,128]{1,0:T(1,128)S(1)}, f32[1,128]{1,0:T(1,128)S(1)}, u32[]{:S(2)}, u32[]{:S(2)}) collective-permute-start(f32[1,128]{1,0:T(1,128)S(1)} %shard_map.102), channel_id=1, source_target_pairs={{0,256},{32,288},{64,320},{96,352},{128,384},{160,416},{192,448},{... | collective-permute-start | bytes 1544 | tf_op jit(solution)/shard_map/ppermute | solution.py:384

commit v9 on v8

--- a/solution.py
+++ b/solution.py
@@ -43,39 +43,50 @@
 def tables():
     positions = np.arange(GRID)
     angles = (positions[:, None] * positions[None, :] % GRID) * (2.0 * np.pi / GRID)
-    basis = ((np.cos(angles) + np.sin(angles)) / np.sqrt(GRID)).astype(np.float32)
+    basis = (np.cos(angles) + np.sin(angles)) / np.sqrt(GRID)
     high = basis.astype(jnp.bfloat16)
-    low = (basis - high.astype(np.float32)).astype(jnp.bfloat16)
+    rest = basis - high.astype(np.float64)
+    middle = rest.astype(jnp.bfloat16)
+    low = (rest - middle.astype(np.float64)).astype(jnp.bfloat16)
     spectrum = -np.real(np.fft.fft2(coulomb_kernel())).astype(np.float32)
     halves = np.stack([spectrum[:, :LANES], spectrum[:, LANES:]])
-    return high, low, halves
+    return np.stack([high, middle, low]), halves
 
 
 def split(x):
     high = x.astype(jnp.bfloat16)
-    low = (x - high.astype(jnp.float32)).astype(jnp.bfloat16)
-    return high, low
+    rest = x - high.astype(jnp.float32)
+    middle = rest.astype(jnp.bfloat16)
+    return high, middle, (rest - middle.astype(jnp.float32)).astype(jnp.bfloat16)
 
 
 def dot(a, b):
     return jnp.dot(a, b, preferred_element_type=jnp.float32)
 
 
-def times_table(x, high_ref, low_ref):
-    x_high, x_low = split(x)
-    both = dot(jnp.concatenate([x_high, x_low], axis=0), high_ref[...])
-    return both[: x.shape[0]] + (both[x.shape[0] :] + dot(x_high, low_ref[...]))
-
-
-def table_times(y, high_ref, low_ref):
-    y_high, y_low = split(y)
-    both = dot(high_ref[...], jnp.concatenate([y_high, y_low], axis=1))
-    return both[:, : y.shape[1]] + (both[:, y.shape[1] :] + dot(low_ref[...], y_high))
-
-
-def send_rows(x, high_ref, low_ref, out_ref):
+def times_table(x, table_ref):
+    n = x.shape[0]
+    parts = split(x)
+    high = dot(jnp.concatenate(parts, axis=0), table_ref[0])
+    middle = dot(jnp.concatenate(parts[:2], axis=0), table_ref[1])
+    low = dot(parts[0], table_ref[2])
+    return high[:n] + ((high[n : 2 * n] + middle[:n]) + (high[2 * n :] + (middle[n:] + low)))
+
+
+def table_times(y, table_ref):
+    n = y.shape[1]
+    parts = split(y)
+    high = dot(table_ref[0], jnp.concatenate(parts, axis=1))
+    middle = dot(table_ref[1], jnp.concatenate(parts[:2], axis=1))
+    low = dot(table_ref[2], parts[0])
+    return high[:, :n] + (
+        (high[:, n : 2 * n] + middle[:, :n]) + (high[:, 2 * n :] + (middle[:, n:] + low))
+    )
+
+
+def send_rows(x, table_ref, out_ref):
     step = out_ref.shape[0] // PEERS
-    spectra = times_table(x, high_ref, low_ref)
+    spectra = times_table(x, table_ref)
     for peer in range(PEERS):
         c, half = peer // 2, peer % 2
         out_ref[peer * step : peer * step + ROWS, :] = spectra[
@@ -113,18 +124,18 @@
 
 
 def first_kernel(*refs):
-    sources, (out_ref, fields_ref), fetched, sems = refs[:7], refs[7:9], refs[9:16], refs[16]
+    sources, (out_ref, fields_ref), fetched, sems = refs[:6], refs[6:8], refs[8:14], refs[14]
     copies = [
         pltpu.make_async_copy(source, target, sems.at[n])
         for n, (source, target) in enumerate(zip(sources, fetched))
     ]
     for copy in copies:
         copy.start()
-    density_ref, high_ref, low_ref, momentum_ref, energies_ref, emitted_ref, drive_ref = fetched
-    for copy in copies[:3]:
+    density_ref, table_ref, momentum_ref, energies_ref, emitted_ref, drive_ref = fetched
+    for copy in copies[:2]:
         copy.wait()
-    send_rows(density_ref[...].reshape(CHANNELS * ROWS, GRID), high_ref, low_ref, out_ref)
-    for copy in copies[3:]:
+    send_rows(density_ref[...].reshape(CHANNELS * ROWS, GRID), table_ref, out_ref)
+    for copy in copies[2:]:
         copy.wait()
     currents = {}
     for part in range(2):
@@ -161,17 +172,17 @@
 def column_kernel(carries, y_ref, *refs):
     refs = list(refs)
     carry_ref = refs.pop(0) if carries else None
-    high_ref, low_ref, spectrum_ref, out_ref = refs[:4]
+    table_ref, spectrum_ref, out_ref = refs[:3]
     y = jnp.concatenate(tiles_of(y_ref), axis=0)
-    z = table_times(y, high_ref, low_ref) * spectrum_ref[lax.axis_index("krow") % 2]
-    w = table_times(z, high_ref, low_ref)
+    z = table_times(y, table_ref) * spectrum_ref[lax.axis_index("krow") % 2]
+    w = table_times(z, table_ref)
     step = out_ref.shape[0] // PEERS
     for peer in range(PEERS):
         out_ref[peer * step : peer * step + ROWS, :] = w[peer * ROWS : (peer + 1) * ROWS]
     if carries:
         send_row(carry_ref[...] * prefix_weight(), out_ref)
     else:
-        refs[4][...] = rows_of(y_ref)
+        refs[3][...] = rows_of(y_ref)
 
 
 def unpack(channels):
@@ -232,7 +243,7 @@
     sums_ref = refs.pop(0) if section in (1, 2) else None
     permuted_ref = refs.pop(0) if section in (0, 1) else None
     earlier_refs = [refs.pop(0) for _ in range(2)] if section == 3 else None
-    high_ref, low_ref = refs.pop(0), refs.pop(0)
+    table_ref = refs.pop(0)
     if section == 3:
         result_ref, emitted_out_ref = refs
     else:
@@ -258,7 +269,7 @@
     spectra = jnp.concatenate(
         [jnp.concatenate(tiles[half::2], axis=0) for half in range(2)], axis=1
     )
-    sigma = times_table(spectra, high_ref, low_ref)
+    sigma = times_table(spectra, table_ref)
 
     currents = {}
     for part in range(2):
@@ -291,7 +302,7 @@
 
     if section < 3:
         state = next_ref[...].reshape(CHANNELS * ROWS, GRID)
-        send_rows(state, high_ref, low_ref, out_ref)
+        send_rows(state, table_ref, out_ref)
         row = currents_row(currents)
         if section < 2:
             lane = lax.broadcasted_iota(jnp.int32, (1, LANES), 1)
@@ -336,7 +347,7 @@
 
 
 def per_device(density, energies, momentum, emitted, drive):
-    high, low, spectrum = (jnp.asarray(table) for table in tables())
+    table, spectrum = (jnp.asarray(t) for t in tables())
     density = density.reshape(CHANNELS, ROWS, GRID)
     drive = drive.T
     plain = (PEERS * ROWS, LANES)
@@ -352,23 +363,21 @@
         first_kernel,
         [carrying, (BANDS + 1, ROWS, GRID)],
         density,
-        high,
-        low,
+        table,
         momentum,
         energies,
         emitted,
         drive,
-        in_hbm=range(7),
+        in_hbm=range(6),
         vmem_mib=58,
         scratch=[
             pltpu.VMEM(state_shape, jnp.float32),
-            pltpu.VMEM((GRID, GRID), jnp.bfloat16),
-            pltpu.VMEM((GRID, GRID), jnp.bfloat16),
+            pltpu.VMEM(table.shape, jnp.bfloat16),
             pltpu.VMEM(momentum.shape, jnp.float32),
             pltpu.VMEM(energies.shape, jnp.float32),
             pltpu.VMEM(emitted.shape, jnp.float32),
             pltpu.VMEM(drive.shape, jnp.float32),
-            pltpu.SemaphoreType.DMA((7,)),
+            pltpu.SemaphoreType.DMA((6,)),
         ],
     )
     row = (1, LANES)
@@ -378,11 +387,11 @@
         arrived = swap(out)
         column = functools.partial(column_kernel, section == 3)
         if section < 3:
-            mixed, total = call(column, [plain, row], arrived, high, low, spectrum)
+            mixed, total = call(column, [plain, row], arrived, table, spectrum)
         else:
             (total,) = call(total_kernel, [row], arrived)
             carry = lax.ppermute(total, ("macro", "krow"), exchange)
-            (mixed,) = call(column, [carrying], arrived, carry, high, low, spectrum)
+            (mixed,) = call(column, [carrying], arrived, carry, table, spectrum)
         extra = [total] if section in (1, 2) else []
         sums += extra
         if section in (0, 1):
@@ -391,7 +400,7 @@
         body = functools.partial(state_kernel, section)
         used = states if section == 3 else states[:1] if section == 0 else [density, states[-1]]
         extra = sums if section == 3 else extra
-        args = [back, *used, fields, momentum, *extra, high, low]
+        args = [back, *used, fields, momentum, *extra, table]
         if section < 3:
             out, state = call(body, [carrying, state_shape], *args)
             states.append(state)

time: 140 us -> 142 us (1.014)
  no operation moved by 1% of the time
where the time goes in v9:
time: 142 us; the launch traced here: 141 us
  blocking collectives  93.6 us (66%)
  starting transfers between devices  23 us (16%)
  waiting for transfers between devices  14.4 us (10%)
  Pallas kernels  9.27 us (7%)
    all_to_all x6, blocking collectives, swap(): return lax.all_to_all(blocks, 'krow', 0, 0, tiled=True).reshape(x.shape)  93.6 us
    ppermute x2, starting transfers between devices, per_device(): extra = extra + [lax.ppermute(total, ('macro', 'krow'), exchange)]  12.3 us
    pallas_call x10, Pallas kernels, call(): pl.pallas_call(body, out_shape=shapes, in_specs=[hbm if n in in_hbm else...  9.27 us
    all_to_all x2, starting transfers between devices, swap(): return lax.all_to_all(blocks, 'krow', 0, 0, tiled=True).reshape(x.shape)  8.79 us
    ppermute x1, waiting for transfers between devices, per_device(): carry = lax.ppermute(total, ('macro', 'krow'), exchange)  6.84 us
    ppermute x2, waiting for transfers between devices, per_device(): extra = extra + [lax.ppermute(total, ('macro', 'krow'), exchange)]  6.7 us
  transfers between devices with their start and end apart: 5, of which 4 were waited for; matrix products, arithmetic and copies ran while one was open for 0% of the time, Pallas kernels for 0%

profile of v9, /device:TPU:8, one launch (start us, length us, event | category | flops | bytes accessed | tf_op | source)
XLA Modules:
  0.0 141.0 jit_solution(16312168960586338172)
XLA Ops:
  0.6 2.2 %shard_map.86 = (f32[288,128]{1,0:T(8,128)}, f32[5,8,256]{2,1,0:T(8,128)}) custom-call(f32[16,8,256]{2,1,0:T(8,128)} %bitcast.19, bf16[3,256,256]{2,1,0:T(8,128)(2,1)} %constant.4.clone.refs_1_.refs_0_.refs_5_.refs_7_.refs_6_.refs_9_, f32[2,16,8,256]{3,2,1,0:T(8,128)} %refs_6_.2, f32[4,8,256]{2,1,0:T(8,128)} %refs_3_.2, f32[1,2]{1,0:T(1,128)} %refs_4_.3, ...), custom_call_target="tpu_custom_call" | custom-call | flops 50331648 | bytes 1048576 | tf_op jit(solution)/shard_map/pallas_call | solution.py:331
  2.9 20.3 %all_to_all.40 = f32[32,1,1152]{2,1,0:T(1,128)S(1)} all-to-all(f32[32,1,1152]{2,1,0:T(1,128)} %bitcast.38), channel_id=1, replica_groups=mesh['macro'=16,'krow'=32] {'krow'}, dimensions={0} | all-to-all | bytes 294912 | tf_op jit(solution)/shard_map/all_to_all | solution.py:346
  23.3 1.3 shard_map.87
  24.5 4.5 %all-to-all-start.1 = ((f32[32,1,1024]{2,1,0:T(1,128)}), f32[32,1,1024]{2,1,0:T(1,128)S(1)}, u32[]{:S(2)}, u32[]{:S(2)}) async-start(f32[32,1,1024]{2,1,0:T(1,128)} %bitcast.4), calls=%async_computation.1 | async-start | bytes 262144 | tf_op jit(solution)/shard_map/all_to_all | solution.py:346
  29.0 9.0 %collective-permute-start = (f32[1,128]{1,0:T(1,128)S(1)}, f32[1,128]{1,0:T(1,128)S(1)}, u32[]{:S(2)}, u32[]{:S(2)}) collective-permute-start(f32[1,128]{1,0:T(1,128)S(1)} %get-tuple-element.21), channel_id=1, source_target_pairs={{0,256},{32,288},{64,320},{96,352},{128,384},{160,416},{192,448},{... | collective-permute-start | bytes 1544 | tf_op jit(solution)/shard_map/ppermute | solution.py:398
  38.0 1.3 collective-permute-done.refs_4_
  39.3 0.7 shard_map.88
  40.0 17.4 %all_to_all.41 = f32[32,1,1152]{2,1,0:T(1,128)S(1)} all-to-all(f32[32,1,1152]{2,1,0:T(1,128)S(1)} %bitcast.34), channel_id=1, replica_groups=mesh['macro'=16,'krow'=32] {'krow'}, dimensions={0} | all-to-all | bytes 294912 | tf_op jit(solution)/shard_map/all_to_all | solution.py:346
  57.4 1.2 shard_map.89
  58.6 4.3 %all-to-all-start.3 = ((f32[32,1,1024]{2,1,0:T(1,128)}), f32[32,1,1024]{2,1,0:T(1,128)S(1)}, u32[]{:S(2)}, u32[]{:S(2)}) async-start(f32[32,1,1024]{2,1,0:T(1,128)} %bitcast.8), calls=%async_computation.3 | async-start | bytes 262144 | tf_op jit(solution)/shard_map/all_to_all | solution.py:346
  62.9 3.3 %collective-permute-start.1 = (f32[1,128]{1,0:T(1,128)S(1)}, f32[1,128]{1,0:T(1,128)S(1)}, u32[]{:S(2)}, u32[]{:S(2)}) collective-permute-start(f32[1,128]{1,0:T(1,128)S(1)} %get-tuple-element.25.refs_5_.refs_7_), channel_id=1, source_target_pairs={{0,256},{32,288},{64,320},{96,352},{128,384},{160,416},{192,448},{... | collective-permute-start | bytes 1544 | tf_op jit(solution)/shard_map/ppermute | solution.py:398
  66.3 5.4 %collective-permute-done.1.refs_6_ = f32[1,128]{1,0:T(1,128)S(1)} collective-permute-done((f32[1,128]{1,0:T(1,128)S(1)}, f32[1,128]{1,0:T(1,128)S(1)}, u32[]{:S(2)}, u32[]{:S(2)}) %collective-permute-start.1) | collective-permute-done | bytes 544 | tf_op jit(solution)/shard_map/ppermute | solution.py:398
  71.7 0.9 all-to-all-done.3
  72.6 0.7 shard_map.90
  73.3 14.1 %all_to_all.42 = f32[32,1,1152]{2,1,0:T(1,128)S(1)} all-to-all(f32[32,1,1152]{2,1,0:T(1,128)S(1)} %bitcast.35), channel_id=1, replica_groups=mesh['macro'=16,'krow'=32] {'krow'}, dimensions={0} | all-to-all | bytes 294912 | tf_op jit(solution)/shard_map/all_to_all | solution.py:346
  87.4 0.6 shard_map.91
  88.0 13.8 %all_to_all.43 = f32[32,1,1024]{2,1,0:T(1,128)S(1)} all-to-all(f32[32,1,1024]{2,1,0:T(1,128)S(1)} %bitcast.37), channel_id=1, replica_groups=mesh['macro'=16,'krow'=32] {'krow'}, dimensions={0} | all-to-all | bytes 262144 | tf_op jit(solution)/shard_map/all_to_all | solution.py:346
  101.8 0.8 shard_map.92
  102.6 14.0 %all_to_all.44 = f32[32,1,1152]{2,1,0:T(1,128)S(1)} all-to-all(f32[32,1,1152]{2,1,0:T(1,128)S(1)} %bitcast.36), channel_id=1, replica_groups=mesh['macro'=16,'krow'=32] {'krow'}, dimensions={0} | all-to-all | bytes 294912 | tf_op jit(solution)/shard_map/all_to_all | solution.py:346
  116.7 1.9 %collective-permute-start.2 = (f32[1,128]{1,0:T(1,128)S(1)}, f32[1,128]{1,0:T(1,128)S(1)}, u32[]{:S(2)}, u32[]{:S(2)}) collective-permute-start(f32[1,128]{1,0:T(1,128)S(1)} %shard_map.93), channel_id=1, source_target_pairs={{0,256},{32,288},{64,320},{96,352},{128,384},{160,416},{192,448},{... | collective-permute-start | bytes 1544 | tf_op jit(solution)/shard_map/ppermute | solution.py:393
  118.6 6.8 %collective-permute-done.2.refs_0_ = f32[1,128]{1,0:T(1,128)S(1)} collective-permute-done((f32[1,128]{1,0:T(1,128)S(1)}, f32[1,128]{1,0:T(1,128)S(1)}, u32[]{:S(2)}, u32[]{:S(2)}) %collective-permute-start.2) | collective-permute-done | bytes 544 | tf_op jit(solution)/shard_map/ppermute | solution.py:393
  125.4 0.6 shard_map.94
  126.0 13.9 %all_to_all.45 = f32[32,1,1152]{2,1,0:T(1,128)S(1)} all-to-all(f32[32,1,1152]{2,1,0:T(1,128)S(1)} %bitcast.27), channel_id=1, replica_groups=mesh['macro'=16,'krow'=32] {'krow'}, dimensions={0} | all-to-all | bytes 294912 | tf_op jit(solution)/shard_map/all_to_all | solution.py:346
  140.0 1.1 shard_map.95
  (12 shorter events, 0.0 us)
Async XLA Ops:
  0.6 22.6 %copy-start = (bf16[3,256,256]{2,1,0:T(8,128)(2,1)S(1)}, bf16[3,256,256]{2,1,0:T(8,128)(2,1)}, u32[]{:S(2)}) copy-start(bf16[3,256,256]{2,1,0:T(8,128)(2,1)} %constant.4.clone.refs_1_.refs_0_.refs_5_.refs_7_.refs_6_.refs_9_) | copy-start | bytes 1179652
  2.9 20.4 %copy-start.2 = (f32[2,256,128]{2,1,0:T(8,128)S(1)}, f32[2,256,128]{2,1,0:T(8,128)}, u32[]{:S(2)}) copy-start(f32[2,256,128]{2,1,0:T(8,128)} %constant.5.clone.refs_1_.refs_2_) | copy-start | bytes 786436
  23.2 16.0 %copy-start.3 = (f32[1,16,8,256]{3,2,1,0:T(8,128)S(1)}, f32[1,16,8,256]{3,2,1,0:T(8,128)}, u32[]{:S(2)}) copy-start(f32[1,16,8,256]{3,2,1,0:T(8,128)} %param.7) | copy-start | bytes 393220
  23.2 16.0 %copy-start.4 = (f32[5,8,256]{2,1,0:T(8,128)S(1)}, f32[5,8,256]{2,1,0:T(8,128)}, u32[]{:S(2)}) copy-start(f32[5,8,256]{2,1,0:T(8,128)} %get-tuple-element.20.refs_2_.refs_3_.refs_5_) | copy-start | bytes 122884
  24.5 14.8 %copy-start.1 = (f32[2,16,8,256]{3,2,1,0:T(8,128)S(1)}, f32[2,16,8,256]{3,2,1,0:T(8,128)}, u32[]{:S(2)}) copy-start(f32[2,16,8,256]{3,2,1,0:T(8,128)} %refs_6_.2) | copy-start | bytes 786436
  24.5 14.8 %all-to-all-start.1 = ((f32[32,1,1024]{2,1,0:T(1,128)}), f32[32,1,1024]{2,1,0:T(1,128)S(1)}, u32[]{:S(2)}, u32[]{:S(2)}) async-start(f32[32,1,1024]{2,1,0:T(1,128)} %bitcast.4), calls=%async_computation.1 | async-start | bytes 262144 | tf_op jit(solution)/shard_map/all_to_all | solution.py:346
  29.0 10.2 %collective-permute-start = (f32[1,128]{1,0:T(1,128)S(1)}, f32[1,128]{1,0:T(1,128)S(1)}, u32[]{:S(2)}, u32[]{:S(2)}) collective-permute-start(f32[1,128]{1,0:T(1,128)S(1)} %get-tuple-element.21), channel_id=1, source_target_pairs={{0,256},{32,288},{64,320},{96,352},{128,384},{160,416},{192,448},{... | collective-permute-start | bytes 1544 | tf_op jit(solution)/shard_map/ppermute | solution.py:398
  58.6 14.0 %all-to-all-start.3 = ((f32[32,1,1024]{2,1,0:T(1,128)}), f32[32,1,1024]{2,1,0:T(1,128)S(1)}, u32[]{:S(2)}, u32[]{:S(2)}) async-start(f32[32,1,1024]{2,1,0:T(1,128)} %bitcast.8), calls=%async_computation.3 | async-start | bytes 262144 | tf_op jit(solution)/shard_map/all_to_all | solution.py:346
  62.9 8.8 %collective-permute-start.1 = (f32[1,128]{1,0:T(1,128)S(1)}, f32[1,128]{1,0:T(1,128)S(1)}, u32[]{:S(2)}, u32[]{:S(2)}) collective-permute-start(f32[1,128]{1,0:T(1,128)S(1)} %get-tuple-element.25.refs_5_.refs_7_), channel_id=1, source_target_pairs={{0,256},{32,288},{64,320},{96,352},{128,384},{160,416},{192,448},{... | collective-permute-start | bytes 1544 | tf_op jit(solution)/shard_map/ppermute | solution.py:398
  116.7 8.8 %collective-permute-start.2 = (f32[1,128]{1,0:T(1,128)S(1)}, f32[1,128]{1,0:T(1,128)S(1)}, u32[]{:S(2)}, u32[]{:S(2)}) collective-permute-start(f32[1,128]{1,0:T(1,128)S(1)} %shard_map.93), channel_id=1, source_target_pairs={{0,256},{32,288},{64,320},{96,352},{128,384},{160,416},{192,448},{... | collective-permute-start | bytes 1544 | tf_op jit(solution)/shard_map/ppermute | solution.py:393

commit v10 on v8

--- a/solution.py
+++ b/solution.py
@@ -40,47 +40,72 @@
     return kernel - np.mean(kernel)
 
 
+def parts_of(table):
+    high = table.astype(jnp.bfloat16)
+    rest = table - high.astype(np.float64)
+    middle = rest.astype(jnp.bfloat16)
+    return high, middle, (rest - middle.astype(np.float64)).astype(jnp.bfloat16)
+
+
 def tables():
-    positions = np.arange(GRID)
-    angles = (positions[:, None] * positions[None, :] % GRID) * (2.0 * np.pi / GRID)
-    basis = ((np.cos(angles) + np.sin(angles)) / np.sqrt(GRID)).astype(np.float32)
-    high = basis.astype(jnp.bfloat16)
-    low = (basis - high.astype(np.float32)).astype(jnp.bfloat16)
+    half = GRID // 2
+    positions = np.arange(half)
+    wide, narrow, left = [], [], []
+    frequencies = np.concatenate([2 * positions, 2 * positions + 1])
+    angles = (frequencies[:, None] * positions[None, :] % GRID) * (2.0 * np.pi / GRID)
+    basis = (np.cos(angles) + np.sin(angles)) / np.sqrt(GRID)
+    even, odd = basis[:half], basis[half:]
+    for table in (even, odd.T, odd):
+        high, middle, low = parts_of(table)
+        wide.append(np.block([[high, middle], [high, middle]]))
+        narrow.append(np.concatenate([high, low], axis=0))
+        left.append(
+            [np.concatenate([high, middle], axis=1), np.concatenate([high, low], axis=1)]
+        )
     spectrum = -np.real(np.fft.fft2(coulomb_kernel())).astype(np.float32)
+    spectrum = spectrum[frequencies][:, frequencies]
     halves = np.stack([spectrum[:, :LANES], spectrum[:, LANES:]])
-    return high, low, halves
+    return np.stack(wide), np.stack(narrow), np.stack(left), halves
 
 
 def split(x):
     high = x.astype(jnp.bfloat16)
-    low = (x - high.astype(jnp.float32)).astype(jnp.bfloat16)
-    return high, low
+    rest = x - high.astype(jnp.float32)
+    middle = rest.astype(jnp.bfloat16)
+    return high, middle, (rest - middle.astype(jnp.float32)).astype(jnp.bfloat16)
 
 
 def dot(a, b):
     return jnp.dot(a, b, preferred_element_type=jnp.float32)
 
 
-def times_table(x, high_ref, low_ref):
-    x_high, x_low = split(x)
-    both = dot(jnp.concatenate([x_high, x_low], axis=0), high_ref[...])
-    return both[: x.shape[0]] + (both[x.shape[0] :] + dot(x_high, low_ref[...]))
-
-
-def table_times(y, high_ref, low_ref):
-    y_high, y_low = split(y)
-    both = dot(high_ref[...], jnp.concatenate([y_high, y_low], axis=1))
-    return both[:, : y.shape[1]] + (both[:, y.shape[1] :] + dot(low_ref[...], y_high))
-
-
-def send_rows(x, high_ref, low_ref, out_ref):
+EVEN, ODD, ODD_BACK = 0, 1, 2
+
+
+def times_table(x, wide, narrow):
+    high, middle, low = split(x)
+    most = dot(jnp.concatenate([high, middle], axis=1), wide)
+    rest = dot(jnp.concatenate([low, high], axis=1), narrow)
+    return most[:, :LANES] + (most[:, LANES:] + rest)
+
+
+def table_times(left, y):
+    n = y.shape[1]
+    high, middle, low = split(y)
+    both = jnp.concatenate([high, middle], axis=1)
+    most = dot(left[0], jnp.concatenate([both, both], axis=0))
+    rest = dot(left[1], jnp.concatenate([low, high], axis=0))
+    return most[:, :n] + (most[:, n:] + rest)
+
+
+def send_rows(x, wide_ref, narrow_ref, out_ref):
     step = out_ref.shape[0] // PEERS
-    spectra = times_table(x, high_ref, low_ref)
-    for peer in range(PEERS):
-        c, half = peer // 2, peer % 2
-        out_ref[peer * step : peer * step + ROWS, :] = spectra[
-            c * ROWS : (c + 1) * ROWS, half * LANES : (half + 1) * LANES
-        ]
+    first, second = x[:, :LANES], x[:, LANES:]
+    for half, value in ((EVEN, first + second), (ODD, first - second)):
+        spectra = times_table(value, wide_ref[half], narrow_ref[half])
+        for c in range(CHANNELS):
+            start = (2 * c + half) * step
+            out_ref[start : start + ROWS, :] = spectra[c * ROWS : (c + 1) * ROWS]
 
 
 def tiles_of(ref):
@@ -115,15 +140,17 @@
 def first_kernel(*refs):
     sources, (out_ref, fields_ref), fetched, sems = refs[:7], refs[7:9], refs[9:16], refs[16]
     copies = [
-        pltpu.make_async_copy(source, target, sems.at[n])
+        pltpu.make_async_copy(
+            source.at[pl.ds(0, 2)] if n in (1, 2) else source, target, sems.at[n]
+        )
         for n, (source, target) in enumerate(zip(sources, fetched))
     ]
     for copy in copies:
         copy.start()
-    density_ref, high_ref, low_ref, momentum_ref, energies_ref, emitted_ref, drive_ref = fetched
+    density_ref, wide_ref, narrow_ref, momentum_ref, energies_ref, emitted_ref, drive_ref = fetched
     for copy in copies[:3]:
         copy.wait()
-    send_rows(density_ref[...].reshape(CHANNELS * ROWS, GRID), high_ref, low_ref, out_ref)
+    send_rows(density_ref[...].reshape(CHANNELS * ROWS, GRID), wide_ref, narrow_ref, out_ref)
     for copy in copies[3:]:
         copy.wait()
     currents = {}
@@ -161,17 +188,22 @@
 def column_kernel(carries, y_ref, *refs):
     refs = list(refs)
     carry_ref = refs.pop(0) if carries else None
-    high_ref, low_ref, spectrum_ref, out_ref = refs[:4]
-    y = jnp.concatenate(tiles_of(y_ref), axis=0)
-    z = table_times(y, high_ref, low_ref) * spectrum_ref[lax.axis_index("krow") % 2]
-    w = table_times(z, high_ref, low_ref)
+    left_ref, spectrum_ref, out_ref = refs[:3]
+    tiles = tiles_of(y_ref)
+    first, second = (jnp.concatenate(t, axis=0) for t in (tiles[: PEERS // 2], tiles[PEERS // 2 :]))
+    spectrum = spectrum_ref[lax.axis_index("krow") % 2]
+    even = table_times(left_ref[EVEN], first + second) * spectrum[:LANES]
+    odd = table_times(left_ref[ODD_BACK], first - second) * spectrum[LANES:]
+    even = table_times(left_ref[EVEN], even)
+    odd = table_times(left_ref[ODD], odd)
+    w = jnp.concatenate([even + odd, even - odd], axis=0)
     step = out_ref.shape[0] // PEERS
     for peer in range(PEERS):
         out_ref[peer * step : peer * step + ROWS, :] = w[peer * ROWS : (peer + 1) * ROWS]
     if carries:
         send_row(carry_ref[...] * prefix_weight(), out_ref)
     else:
-        refs[4][...] = rows_of(y_ref)
+        refs[3][...] = rows_of(y_ref)
 
 
 def unpack(channels):
@@ -232,7 +264,7 @@
     sums_ref = refs.pop(0) if section in (1, 2) else None
     permuted_ref = refs.pop(0) if section in (0, 1) else None
     earlier_refs = [refs.pop(0) for _ in range(2)] if section == 3 else None
-    high_ref, low_ref = refs.pop(0), refs.pop(0)
+    wide_ref, narrow_ref = refs.pop(0), refs.pop(0)
     if section == 3:
         result_ref, emitted_out_ref = refs
     else:
@@ -255,10 +287,11 @@
         potential.append(value)
 
     tiles = tiles_of(back_ref)
-    spectra = jnp.concatenate(
-        [jnp.concatenate(tiles[half::2], axis=0) for half in range(2)], axis=1
+    even, odd = (
+        times_table(jnp.concatenate(tiles[half::2], axis=0), wide_ref[table], narrow_ref[table])
+        for half, table in ((0, EVEN), (1, ODD_BACK))
     )
-    sigma = times_table(spectra, high_ref, low_ref)
+    sigma = (even + odd, even - odd)
 
     currents = {}
     for part in range(2):
@@ -266,7 +299,7 @@
         rho = [state_ref[c, :, lanes] for c in range(CHANNELS)]
         hamilton = []
         for c in range(CHANNELS):
-            value = sigma[c * ROWS : (c + 1) * ROWS, lanes]
+            value = sigma[part][c * ROWS : (c + 1) * ROWS]
             value = value + potential[0] * momentum_ref[0, c, :, lanes]
             value = value + potential[1] * momentum_ref[1, c, :, lanes]
             if c < BANDS:
@@ -291,7 +324,7 @@
 
     if section < 3:
         state = next_ref[...].reshape(CHANNELS * ROWS, GRID)
-        send_rows(state, high_ref, low_ref, out_ref)
+        send_rows(state, wide_ref, narrow_ref, out_ref)
         row = currents_row(currents)
         if section < 2:
             lane = lax.broadcasted_iota(jnp.int32, (1, LANES), 1)
@@ -336,7 +369,7 @@
 
 
 def per_device(density, energies, momentum, emitted, drive):
-    high, low, spectrum = (jnp.asarray(table) for table in tables())
+    wide, narrow, left, spectrum = (jnp.asarray(t) for t in tables())
     density = density.reshape(CHANNELS, ROWS, GRID)
     drive = drive.T
     plain = (PEERS * ROWS, LANES)
@@ -352,8 +385,8 @@
         first_kernel,
         [carrying, (BANDS + 1, ROWS, GRID)],
         density,
-        high,
-        low,
+        wide,
+        narrow,
         momentum,
         energies,
         emitted,
@@ -362,8 +395,8 @@
         vmem_mib=58,
         scratch=[
             pltpu.VMEM(state_shape, jnp.float32),
-            pltpu.VMEM((GRID, GRID), jnp.bfloat16),
-            pltpu.VMEM((GRID, GRID), jnp.bfloat16),
+            pltpu.VMEM((2, GRID, GRID), jnp.bfloat16),
+            pltpu.VMEM((2, GRID, LANES), jnp.bfloat16),
             pltpu.VMEM(momentum.shape, jnp.float32),
             pltpu.VMEM(energies.shape, jnp.float32),
             pltpu.VMEM(emitted.shape, jnp.float32),
@@ -378,11 +411,11 @@
         arrived = swap(out)
         column = functools.partial(column_kernel, section == 3)
         if section < 3:
-            mixed, total = call(column, [plain, row], arrived, high, low, spectrum)
+            mixed, total = call(column, [plain, row], arrived, left, spectrum)
         else:
             (total,) = call(total_kernel, [row], arrived)
             carry = lax.ppermute(total, ("macro", "krow"), exchange)
-            (mixed,) = call(column, [carrying], arrived, carry, high, low, spectrum)
+            (mixed,) = call(column, [carrying], arrived, carry, left, spectrum)
         extra = [total] if section in (1, 2) else []
         sums += extra
         if section in (0, 1):
@@ -391,7 +424,7 @@
         body = functools.partial(state_kernel, section)
         used = states if section == 3 else states[:1] if section == 0 else [density, states[-1]]
         extra = sums if section == 3 else extra
-        args = [back, *used, fields, momentum, *extra, high, low]
+        args = [back, *used, fields, momentum, *extra, wide, narrow]
         if section < 3:
             out, state = call(body, [carrying, state_shape], *args)
             states.append(state)

time: 140 us -> 140 us (level)
  no operation moved by 1% of the time
where the time goes in v10:
time: 140 us
  blocking collectives  93.6 us (67%)
  starting transfers between devices  23 us (16%)
  waiting for transfers between devices  14.4 us (10%)
  Pallas kernels  7.9 us (6%)
    all_to_all x6, blocking collectives, swap(): return lax.all_to_all(blocks, 'krow', 0, 0, tiled=True).reshape(x.shape)  93.6 us
    ppermute x2, starting transfers between devices, per_device(): extra = extra + [lax.ppermute(total, ('macro', 'krow'), exchange)]  12.3 us
    all_to_all x2, starting transfers between devices, swap(): return lax.all_to_all(blocks, 'krow', 0, 0, tiled=True).reshape(x.shape)  8.79 us
    pallas_call x10, Pallas kernels, call(): pl.pallas_call(body, out_shape=shapes, in_specs=[hbm if n in in_hbm else...  7.9 us
    ppermute x1, waiting for transfers between devices, per_device(): carry = lax.ppermute(total, ('macro', 'krow'), exchange)  6.84 us
    ppermute x2, waiting for transfers between devices, per_device(): extra = extra + [lax.ppermute(total, ('macro', 'krow'), exchange)]  6.7 us
  transfers between devices with their start and end apart: 5, of which 4 were waited for; matrix products, arithmetic and copies ran while one was open for 0% of the time, Pallas kernels for 0%

profile of v10, /device:TPU:8, one launch (start us, length us, event | category | flops | bytes accessed | tf_op | source)
XLA Modules:
  0.0 139.7 jit_solution(4561427074435665972)
XLA Ops:
  0.6 2.2 %shard_map.104 = (f32[288,128]{1,0:T(8,128)}, f32[5,8,256]{2,1,0:T(8,128)}) custom-call(f32[16,8,256]{2,1,0:T(8,128)} %bitcast.19, bf16[3,256,256]{2,1,0:T(8,128)(2,1)} %constant.8.clone.refs_1_.refs_5_.refs_7_.refs_6_.refs_9_, bf16[3,256,128]{2,1,0:T(8,128)(2,1)} %constant.9.clone.refs_2_.refs_6_.refs_8_.refs_7_.refs_10_, f32[2,16,8,256]{3,2,1,0:T(8,128)} %refs_6_.3, ...), custom_call_target="tpu_custom_call" | custom-call | flops 50331648 | bytes 1048576 | tf_op jit(solution)/shard_map/pallas_call | solution.py:353
  2.8 20.3 %all_to_all.40 = f32[32,1,1152]{2,1,0:T(1,128)S(1)} all-to-all(f32[32,1,1152]{2,1,0:T(1,128)} %bitcast.38), channel_id=1, replica_groups=mesh['macro'=16,'krow'=32] {'krow'}, dimensions={0} | all-to-all | bytes 294912 | tf_op jit(solution)/shard_map/all_to_all | solution.py:368
  23.2 1.1 shard_map.105
  24.3 4.5 %all-to-all-start.1 = ((f32[32,1,1024]{2,1,0:T(1,128)}), f32[32,1,1024]{2,1,0:T(1,128)S(1)}, u32[]{:S(2)}, u32[]{:S(2)}) async-start(f32[32,1,1024]{2,1,0:T(1,128)} %bitcast.4), calls=%async_computation.1 | async-start | bytes 262144 | tf_op jit(solution)/shard_map/all_to_all | solution.py:368
  28.8 9.0 %collective-permute-start = (f32[1,128]{1,0:T(1,128)S(1)}, f32[1,128]{1,0:T(1,128)S(1)}, u32[]{:S(2)}, u32[]{:S(2)}) collective-permute-start(f32[1,128]{1,0:T(1,128)S(1)} %get-tuple-element.21), channel_id=1, source_target_pairs={{0,256},{32,288},{64,320},{96,352},{128,384},{160,416},{192,448},{... | collective-permute-start | bytes 1544 | tf_op jit(solution)/shard_map/ppermute | solution.py:422
  37.8 1.3 collective-permute-done.refs_4_
  39.1 0.5 shard_map.106
  39.6 17.4 %all_to_all.41 = f32[32,1,1152]{2,1,0:T(1,128)S(1)} all-to-all(f32[32,1,1152]{2,1,0:T(1,128)S(1)} %bitcast.34), channel_id=1, replica_groups=mesh['macro'=16,'krow'=32] {'krow'}, dimensions={0} | all-to-all | bytes 294912 | tf_op jit(solution)/shard_map/all_to_all | solution.py:368
  57.0 1.1 shard_map.107
  58.1 4.3 %all-to-all-start.3 = ((f32[32,1,1024]{2,1,0:T(1,128)}), f32[32,1,1024]{2,1,0:T(1,128)S(1)}, u32[]{:S(2)}, u32[]{:S(2)}) async-start(f32[32,1,1024]{2,1,0:T(1,128)} %bitcast.8), calls=%async_computation.3 | async-start | bytes 262144 | tf_op jit(solution)/shard_map/all_to_all | solution.py:368
  62.4 3.3 %collective-permute-start.1 = (f32[1,128]{1,0:T(1,128)S(1)}, f32[1,128]{1,0:T(1,128)S(1)}, u32[]{:S(2)}, u32[]{:S(2)}) collective-permute-start(f32[1,128]{1,0:T(1,128)S(1)} %get-tuple-element.25.refs_5_.refs_7_), channel_id=1, source_target_pairs={{0,256},{32,288},{64,320},{96,352},{128,384},{160,416},{192,448},{... | collective-permute-start | bytes 1544 | tf_op jit(solution)/shard_map/ppermute | solution.py:422
  65.7 5.4 %collective-permute-done.1.refs_6_ = f32[1,128]{1,0:T(1,128)S(1)} collective-permute-done((f32[1,128]{1,0:T(1,128)S(1)}, f32[1,128]{1,0:T(1,128)S(1)}, u32[]{:S(2)}, u32[]{:S(2)}) %collective-permute-start.1) | collective-permute-done | bytes 544 | tf_op jit(solution)/shard_map/ppermute | solution.py:422
  71.1 0.9 all-to-all-done.3
  72.0 0.5 shard_map.108
  72.6 14.1 %all_to_all.42 = f32[32,1,1152]{2,1,0:T(1,128)S(1)} all-to-all(f32[32,1,1152]{2,1,0:T(1,128)S(1)} %bitcast.35), channel_id=1, replica_groups=mesh['macro'=16,'krow'=32] {'krow'}, dimensions={0} | all-to-all | bytes 294912 | tf_op jit(solution)/shard_map/all_to_all | solution.py:368
  86.7 0.4 shard_map.109
  87.1 13.8 %all_to_all.43 = f32[32,1,1024]{2,1,0:T(1,128)S(1)} all-to-all(f32[32,1,1024]{2,1,0:T(1,128)S(1)} %bitcast.37), channel_id=1, replica_groups=mesh['macro'=16,'krow'=32] {'krow'}, dimensions={0} | all-to-all | bytes 262144 | tf_op jit(solution)/shard_map/all_to_all | solution.py:368
  100.9 0.6 shard_map.110
  101.5 14.0 %all_to_all.44 = f32[32,1,1152]{2,1,0:T(1,128)S(1)} all-to-all(f32[32,1,1152]{2,1,0:T(1,128)S(1)} %bitcast.36), channel_id=1, replica_groups=mesh['macro'=16,'krow'=32] {'krow'}, dimensions={0} | all-to-all | bytes 294912 | tf_op jit(solution)/shard_map/all_to_all | solution.py:368
  115.5 1.9 %collective-permute-start.2 = (f32[1,128]{1,0:T(1,128)S(1)}, f32[1,128]{1,0:T(1,128)S(1)}, u32[]{:S(2)}, u32[]{:S(2)}) collective-permute-start(f32[1,128]{1,0:T(1,128)S(1)} %shard_map.111), channel_id=1, source_target_pairs={{0,256},{32,288},{64,320},{96,352},{128,384},{160,416},{192,448},{... | collective-permute-start | bytes 1544 | tf_op jit(solution)/shard_map/ppermute | solution.py:417
  117.4 6.8 %collective-permute-done.2.refs_0_ = f32[1,128]{1,0:T(1,128)S(1)} collective-permute-done((f32[1,128]{1,0:T(1,128)S(1)}, f32[1,128]{1,0:T(1,128)S(1)}, u32[]{:S(2)}, u32[]{:S(2)}) %collective-permute-start.2) | collective-permute-done | bytes 544 | tf_op jit(solution)/shard_map/ppermute | solution.py:417
  124.3 0.4 shard_map.112
  124.7 13.9 %all_to_all.45 = f32[32,1,1152]{2,1,0:T(1,128)S(1)} all-to-all(f32[32,1,1152]{2,1,0:T(1,128)S(1)} %bitcast.26), channel_id=1, replica_groups=mesh['macro'=16,'krow'=32] {'krow'}, dimensions={0} | all-to-all | bytes 294912 | tf_op jit(solution)/shard_map/all_to_all | solution.py:368
  138.6 1.1 shard_map.113
  (16 shorter events, 0.0 us)
Async XLA Ops:
  0.6 22.5 %copy-start.2 = (bf16[3,2,128,256]{3,2,1,0:T(8,128)(2,1)S(1)}, bf16[3,2,128,256]{3,2,1,0:T(8,128)(2,1)}, u32[]{:S(2)}) copy-start(bf16[3,2,128,256]{3,2,1,0:T(8,128)(2,1)} %constant.10.clone.refs_0_.refs_1_) | copy-start | bytes 1179652
  2.8 20.4 %copy-start.4 = (f32[2,256,128]{2,1,0:T(8,128)S(1)}, f32[2,256,128]{2,1,0:T(8,128)}, u32[]{:S(2)}) copy-start(f32[2,256,128]{2,1,0:T(8,128)} %constant.11.clone.refs_1_.refs_2_) | copy-start | bytes 786436
  23.2 15.9 %copy-start = (bf16[3,256,256]{2,1,0:T(8,128)(2,1)S(1)}, bf16[3,256,256]{2,1,0:T(8,128)(2,1)}, u32[]{:S(2)}) copy-start(bf16[3,256,256]{2,1,0:T(8,128)(2,1)} %constant.8.clone.refs_1_.refs_5_.refs_7_.refs_6_.refs_9_) | copy-start | bytes 1179652
  23.2 15.9 %copy-start.3 = (bf16[3,256,128]{2,1,0:T(8,128)(2,1)S(1)}, bf16[3,256,128]{2,1,0:T(8,128)(2,1)}, u32[]{:S(2)}) copy-start(bf16[3,256,128]{2,1,0:T(8,128)(2,1)} %constant.9.clone.refs_2_.refs_6_.refs_8_.refs_7_.refs_10_) | copy-start | bytes 589828
  23.2 15.9 %copy-start.5 = (f32[1,16,8,256]{3,2,1,0:T(8,128)S(1)}, f32[1,16,8,256]{3,2,1,0:T(8,128)}, u32[]{:S(2)}) copy-start(f32[1,16,8,256]{3,2,1,0:T(8,128)} %param.9) | copy-start | bytes 393220
  23.2 15.9 %copy-start.6 = (f32[5,8,256]{2,1,0:T(8,128)S(1)}, f32[5,8,256]{2,1,0:T(8,128)}, u32[]{:S(2)}) copy-start(f32[5,8,256]{2,1,0:T(8,128)} %get-tuple-element.20.refs_2_.refs_3_.refs_5_) | copy-start | bytes 122884
  24.3 14.8 %copy-start.1 = (f32[2,16,8,256]{3,2,1,0:T(8,128)S(1)}, f32[2,16,8,256]{3,2,1,0:T(8,128)}, u32[]{:S(2)}) copy-start(f32[2,16,8,256]{3,2,1,0:T(8,128)} %refs_6_.3) | copy-start | bytes 786436
  24.3 14.8 %all-to-all-start.1 = ((f32[32,1,1024]{2,1,0:T(1,128)}), f32[32,1,1024]{2,1,0:T(1,128)S(1)}, u32[]{:S(2)}, u32[]{:S(2)}) async-start(f32[32,1,1024]{2,1,0:T(1,128)} %bitcast.4), calls=%async_computation.1 | async-start | bytes 262144 | tf_op jit(solution)/shard_map/all_to_all | solution.py:368
  28.8 10.2 %collective-permute-start = (f32[1,128]{1,0:T(1,128)S(1)}, f32[1,128]{1,0:T(1,128)S(1)}, u32[]{:S(2)}, u32[]{:S(2)}) collective-permute-start(f32[1,128]{1,0:T(1,128)S(1)} %get-tuple-element.21), channel_id=1, source_target_pairs={{0,256},{32,288},{64,320},{96,352},{128,384},{160,416},{192,448},{... | collective-permute-start | bytes 1544 | tf_op jit(solution)/shard_map/ppermute | solution.py:422
  58.1 14.0 %all-to-all-start.3 = ((f32[32,1,1024]{2,1,0:T(1,128)}), f32[32,1,1024]{2,1,0:T(1,128)S(1)}, u32[]{:S(2)}, u32[]{:S(2)}) async-start(f32[32,1,1024]{2,1,0:T(1,128)} %bitcast.8), calls=%async_computation.3 | async-start | bytes 262144 | tf_op jit(solution)/shard_map/all_to_all | solution.py:368
  62.4 8.8 %collective-permute-start.1 = (f32[1,128]{1,0:T(1,128)S(1)}, f32[1,128]{1,0:T(1,128)S(1)}, u32[]{:S(2)}, u32[]{:S(2)}) collective-permute-start(f32[1,128]{1,0:T(1,128)S(1)} %get-tuple-element.25.refs_5_.refs_7_), channel_id=1, source_target_pairs={{0,256},{32,288},{64,320},{96,352},{128,384},{160,416},{192,448},{... | collective-permute-start | bytes 1544 | tf_op jit(solution)/shard_map/ppermute | solution.py:422
  115.5 8.8 %collective-permute-start.2 = (f32[1,128]{1,0:T(1,128)S(1)}, f32[1,128]{1,0:T(1,128)S(1)}, u32[]{:S(2)}, u32[]{:S(2)}) collective-permute-start(f32[1,128]{1,0:T(1,128)S(1)} %shard_map.111), channel_id=1, source_target_pairs={{0,256},{32,288},{64,320},{96,352},{128,384},{160,416},{192,448},{... | collective-permute-start | bytes 1544 | tf_op jit(solution)/shard_map/ppermute | solution.py:417

commit v11 on v10

--- a/solution.py
+++ b/solution.py
@@ -185,25 +185,37 @@
     out_ref[...] = rows_of(y_ref)
 
 
-def column_kernel(carries, y_ref, *refs):
+def column_kernel(carries, chunks, y_ref, *refs):
     refs = list(refs)
     carry_ref = refs.pop(0) if carries else None
     left_ref, spectrum_ref, out_ref = refs[:3]
+    target, sems = refs[4:6] if chunks > 1 else (out_ref, None)
     tiles = tiles_of(y_ref)
     first, second = (jnp.concatenate(t, axis=0) for t in (tiles[: PEERS // 2], tiles[PEERS // 2 :]))
     spectrum = spectrum_ref[lax.axis_index("krow") % 2]
     even = table_times(left_ref[EVEN], first + second) * spectrum[:LANES]
     odd = table_times(left_ref[ODD_BACK], first - second) * spectrum[LANES:]
-    even = table_times(left_ref[EVEN], even)
-    odd = table_times(left_ref[ODD], odd)
-    w = jnp.concatenate([even + odd, even - odd], axis=0)
     step = out_ref.shape[0] // PEERS
-    for peer in range(PEERS):
-        out_ref[peer * step : peer * step + ROWS, :] = w[peer * ROWS : (peer + 1) * ROWS]
+    leaving = []
+    for chunk in range(chunks):
+        rows = slice(chunk * LANES // chunks, (chunk + 1) * LANES // chunks)
+        e = table_times(left_ref[EVEN, :, rows], even)
+        o = table_times(left_ref[ODD, :, rows], odd)
+        for side, w in enumerate((e + o, e - o)):
+            first = side * PEERS // 2 + chunk * PEERS // 2 // chunks
+            for n in range(PEERS // 2 // chunks):
+                peer = first + n
+                target[peer * step : peer * step + ROWS, :] = w[n * ROWS : (n + 1) * ROWS]
+            if chunks > 1:
+                at = pl.ds(first * step, PEERS // 2 // chunks * step)
+                leaving.append(pltpu.make_async_copy(target.at[at], out_ref.at[at], sems.at[len(leaving)]))
+                leaving[-1].start()
     if carries:
         send_row(carry_ref[...] * prefix_weight(), out_ref)
     else:
         refs[3][...] = rows_of(y_ref)
+    for copy in leaving:
+        copy.wait()
 
 
 def unpack(channels):
@@ -346,7 +358,7 @@
             emitted_out_ref[:, i : i + 1] = emitted + (time_step / 6.0 * rate_scale) * total
 
 
-def call(body, outs, *args, in_hbm=(), scratch=(), vmem_mib=24):
+def call(body, outs, *args, in_hbm=(), out_hbm=(), scratch=(), vmem_mib=24):
     shapes = [jax.ShapeDtypeStruct(s, jnp.float32) for s in outs]
     vmem = pl.BlockSpec(memory_space=pltpu.VMEM)
     hbm = pl.BlockSpec(memory_space=pltpu.HBM)
@@ -354,7 +366,7 @@
         body,
         out_shape=shapes,
         in_specs=[hbm if n in in_hbm else vmem for n in range(len(args))],
-        out_specs=[vmem] * len(outs),
+        out_specs=[hbm if n in out_hbm else vmem for n in range(len(outs))],
         scratch_shapes=scratch,
         compiler_params=pltpu.CompilerParams(vmem_limit_bytes=vmem_mib * 1024 * 1024),
         cost_estimate=pl.CostEstimate(
@@ -409,9 +421,19 @@
     sums = []
     for section in range(4):
         arrived = swap(out)
-        column = functools.partial(column_kernel, section == 3)
+        chunks = 2 if section < 2 else 1
+        column = functools.partial(column_kernel, section == 3, chunks)
         if section < 3:
-            mixed, total = call(column, [plain, row], arrived, left, spectrum)
+            scratch = [pltpu.VMEM(plain, jnp.float32), pltpu.SemaphoreType.DMA((4,))]
+            mixed, total = call(
+                column,
+                [plain, row],
+                arrived,
+                left,
+                spectrum,
+                out_hbm=(0,) if chunks > 1 else (),
+                scratch=scratch if chunks > 1 else (),
+            )
         else:
             (total,) = call(total_kernel, [row], arrived)
             carry = lax.ppermute(total, ("macro", "krow"), exchange)

time: 140 us -> 140 us (level)
  no operation moved by 1% of the time
where the time goes in v11:
time: 140 us
  blocking collectives  93.5 us (67%)
  starting transfers between devices  23 us (16%)
  waiting for transfers between devices  14.4 us (10%)
  Pallas kernels  7.94 us (6%)
    all_to_all x6, blocking collectives, swap(): return lax.all_to_all(blocks, 'krow', 0, 0, tiled=True).reshape(x.shape)  93.5 us
    ppermute x2, starting transfers between devices, per_device(): extra = extra + [lax.ppermute(total, ('macro', 'krow'), exchange)]  12.3 us
    all_to_all x2, starting transfers between devices, swap(): return lax.all_to_all(blocks, 'krow', 0, 0, tiled=True).reshape(x.shape)  8.81 us
    pallas_call x10, Pallas kernels, call(): pl.pallas_call(body, out_shape=shapes, in_specs=[hbm if n in in_hbm else...  7.94 us
    ppermute x1, waiting for transfers between devices, per_device(): carry = lax.ppermute(total, ('macro', 'krow'), exchange)  6.84 us
    ppermute x2, waiting for transfers between devices, per_device(): extra = extra + [lax.ppermute(total, ('macro', 'krow'), exchange)]  6.7 us
  transfers between devices with their start and end apart: 5, of which 4 were waited for; matrix products, arithmetic and copies ran while one was open for 0% of the time, Pallas kernels for 0%

profile of v11, /device:TPU:8, one launch (start us, length us, event | category | flops | bytes accessed | tf_op | source)
XLA Modules:
  0.0 139.7 jit_solution(5730153895539344494)
XLA Ops:
  0.6 2.2 %shard_map.104 = (f32[288,128]{1,0:T(8,128)}, f32[5,8,256]{2,1,0:T(8,128)}) custom-call(f32[16,8,256]{2,1,0:T(8,128)} %bitcast.19, bf16[3,256,256]{2,1,0:T(8,128)(2,1)} %constant.8.clone.refs_1_.refs_5_.refs_7_.refs_6_.refs_9_, bf16[3,256,128]{2,1,0:T(8,128)(2,1)} %constant.9.clone.refs_2_.refs_6_.refs_8_.refs_7_.refs_10_, f32[2,16,8,256]{3,2,1,0:T(8,128)} %refs_6_.3, ...), custom_call_target="tpu_custom_call" | custom-call | flops 50331648 | bytes 1048576 | tf_op jit(solution)/shard_map/pallas_call | solution.py:365
  2.8 20.3 %all_to_all.40 = f32[32,1,1152]{2,1,0:T(1,128)S(1)} all-to-all(f32[32,1,1152]{2,1,0:T(1,128)} %bitcast.38), channel_id=1, replica_groups=mesh['macro'=16,'krow'=32] {'krow'}, dimensions={0} | all-to-all | bytes 294912 | tf_op jit(solution)/shard_map/all_to_all | solution.py:380
  23.2 1.1 shard_map.105
  24.3 4.5 %all-to-all-start.1 = ((f32[32,1,1024]{2,1,0:T(1,128)}), f32[32,1,1024]{2,1,0:T(1,128)S(1)}, u32[]{:S(2)}, u32[]{:S(2)}) async-start(f32[32,1,1024]{2,1,0:T(1,128)} %bitcast.4), calls=%async_computation.1 | async-start | bytes 262144 | tf_op jit(solution)/shard_map/all_to_all | solution.py:380
  28.9 9.0 %collective-permute-start = (f32[1,128]{1,0:T(1,128)S(1)}, f32[1,128]{1,0:T(1,128)S(1)}, u32[]{:S(2)}, u32[]{:S(2)}) collective-permute-start(f32[1,128]{1,0:T(1,128)S(1)} %get-tuple-element.21), channel_id=1, source_target_pairs={{0,256},{32,288},{64,320},{96,352},{128,384},{160,416},{192,448},{... | collective-permute-start | bytes 1544 | tf_op jit(solution)/shard_map/ppermute | solution.py:444
  37.8 1.3 collective-permute-done.refs_4_
  39.1 0.5 shard_map.106
  39.7 17.4 %all_to_all.41 = f32[32,1,1152]{2,1,0:T(1,128)S(1)} all-to-all(f32[32,1,1152]{2,1,0:T(1,128)S(1)} %bitcast.34), channel_id=1, replica_groups=mesh['macro'=16,'krow'=32] {'krow'}, dimensions={0} | all-to-all | bytes 294912 | tf_op jit(solution)/shard_map/all_to_all | solution.py:380
  57.0 1.1 shard_map.107
  58.1 4.3 %all-to-all-start.3 = ((f32[32,1,1024]{2,1,0:T(1,128)}), f32[32,1,1024]{2,1,0:T(1,128)S(1)}, u32[]{:S(2)}, u32[]{:S(2)}) async-start(f32[32,1,1024]{2,1,0:T(1,128)} %bitcast.8), calls=%async_computation.3 | async-start | bytes 262144 | tf_op jit(solution)/shard_map/all_to_all | solution.py:380
  62.5 3.3 %collective-permute-start.1 = (f32[1,128]{1,0:T(1,128)S(1)}, f32[1,128]{1,0:T(1,128)S(1)}, u32[]{:S(2)}, u32[]{:S(2)}) collective-permute-start(f32[1,128]{1,0:T(1,128)S(1)} %get-tuple-element.25.refs_5_.refs_7_), channel_id=1, source_target_pairs={{0,256},{32,288},{64,320},{96,352},{128,384},{160,416},{192,448},{... | collective-permute-start | bytes 1544 | tf_op jit(solution)/shard_map/ppermute | solution.py:444
  65.8 5.4 %collective-permute-done.1.refs_6_ = f32[1,128]{1,0:T(1,128)S(1)} collective-permute-done((f32[1,128]{1,0:T(1,128)S(1)}, f32[1,128]{1,0:T(1,128)S(1)}, u32[]{:S(2)}, u32[]{:S(2)}) %collective-permute-start.1) | collective-permute-done | bytes 544 | tf_op jit(solution)/shard_map/ppermute | solution.py:444
  71.2 0.9 all-to-all-done.3
  72.1 0.5 shard_map.108
  72.7 14.1 %all_to_all.42 = f32[32,1,1152]{2,1,0:T(1,128)S(1)} all-to-all(f32[32,1,1152]{2,1,0:T(1,128)S(1)} %bitcast.35), channel_id=1, replica_groups=mesh['macro'=16,'krow'=32] {'krow'}, dimensions={0} | all-to-all | bytes 294912 | tf_op jit(solution)/shard_map/all_to_all | solution.py:380
  86.7 0.4 shard_map.109
  87.2 13.8 %all_to_all.43 = f32[32,1,1024]{2,1,0:T(1,128)S(1)} all-to-all(f32[32,1,1024]{2,1,0:T(1,128)S(1)} %bitcast.37), channel_id=1, replica_groups=mesh['macro'=16,'krow'=32] {'krow'}, dimensions={0} | all-to-all | bytes 262144 | tf_op jit(solution)/shard_map/all_to_all | solution.py:380
  101.0 0.6 shard_map.110
  101.5 14.0 %all_to_all.44 = f32[32,1,1152]{2,1,0:T(1,128)S(1)} all-to-all(f32[32,1,1152]{2,1,0:T(1,128)S(1)} %bitcast.36), channel_id=1, replica_groups=mesh['macro'=16,'krow'=32] {'krow'}, dimensions={0} | all-to-all | bytes 294912 | tf_op jit(solution)/shard_map/all_to_all | solution.py:380
  115.6 1.9 %collective-permute-start.2 = (f32[1,128]{1,0:T(1,128)S(1)}, f32[1,128]{1,0:T(1,128)S(1)}, u32[]{:S(2)}, u32[]{:S(2)}) collective-permute-start(f32[1,128]{1,0:T(1,128)S(1)} %shard_map.111), channel_id=1, source_target_pairs={{0,256},{32,288},{64,320},{96,352},{128,384},{160,416},{192,448},{... | collective-permute-start | bytes 1544 | tf_op jit(solution)/shard_map/ppermute | solution.py:439
  117.5 6.8 %collective-permute-done.2.refs_0_ = f32[1,128]{1,0:T(1,128)S(1)} collective-permute-done((f32[1,128]{1,0:T(1,128)S(1)}, f32[1,128]{1,0:T(1,128)S(1)}, u32[]{:S(2)}, u32[]{:S(2)}) %collective-permute-start.2) | collective-permute-done | bytes 544 | tf_op jit(solution)/shard_map/ppermute | solution.py:439
  124.4 0.4 shard_map.112
  124.8 13.9 %all_to_all.45 = f32[32,1,1152]{2,1,0:T(1,128)S(1)} all-to-all(f32[32,1,1152]{2,1,0:T(1,128)S(1)} %bitcast.26), channel_id=1, replica_groups=mesh['macro'=16,'krow'=32] {'krow'}, dimensions={0} | all-to-all | bytes 294912 | tf_op jit(solution)/shard_map/all_to_all | solution.py:380
  138.7 1.1 shard_map.113
  (16 shorter events, 0.1 us)
Async XLA Ops:
  0.6 22.5 %copy-start.2 = (bf16[3,2,128,256]{3,2,1,0:T(8,128)(2,1)S(1)}, bf16[3,2,128,256]{3,2,1,0:T(8,128)(2,1)}, u32[]{:S(2)}) copy-start(bf16[3,2,128,256]{3,2,1,0:T(8,128)(2,1)} %constant.10.clone.refs_0_.refs_1_) | copy-start | bytes 1179652
  2.8 20.4 %copy-start.4 = (f32[2,256,128]{2,1,0:T(8,128)S(1)}, f32[2,256,128]{2,1,0:T(8,128)}, u32[]{:S(2)}) copy-start(f32[2,256,128]{2,1,0:T(8,128)} %constant.11.clone.refs_1_.refs_2_) | copy-start | bytes 786436
  23.2 15.9 %copy-start = (bf16[3,256,256]{2,1,0:T(8,128)(2,1)S(1)}, bf16[3,256,256]{2,1,0:T(8,128)(2,1)}, u32[]{:S(2)}) copy-start(bf16[3,256,256]{2,1,0:T(8,128)(2,1)} %constant.8.clone.refs_1_.refs_5_.refs_7_.refs_6_.refs_9_) | copy-start | bytes 1179652
  23.2 15.9 %copy-start.3 = (bf16[3,256,128]{2,1,0:T(8,128)(2,1)S(1)}, bf16[3,256,128]{2,1,0:T(8,128)(2,1)}, u32[]{:S(2)}) copy-start(bf16[3,256,128]{2,1,0:T(8,128)(2,1)} %constant.9.clone.refs_2_.refs_6_.refs_8_.refs_7_.refs_10_) | copy-start | bytes 589828
  23.2 15.9 %copy-start.5 = (f32[1,16,8,256]{3,2,1,0:T(8,128)S(1)}, f32[1,16,8,256]{3,2,1,0:T(8,128)}, u32[]{:S(2)}) copy-start(f32[1,16,8,256]{3,2,1,0:T(8,128)} %param.9) | copy-start | bytes 393220
  23.2 15.9 %copy-start.6 = (f32[5,8,256]{2,1,0:T(8,128)S(1)}, f32[5,8,256]{2,1,0:T(8,128)}, u32[]{:S(2)}) copy-start(f32[5,8,256]{2,1,0:T(8,128)} %get-tuple-element.20.refs_2_.refs_3_.refs_5_) | copy-start | bytes 122884
  24.3 14.8 %copy-start.1 = (f32[2,16,8,256]{3,2,1,0:T(8,128)S(1)}, f32[2,16,8,256]{3,2,1,0:T(8,128)}, u32[]{:S(2)}) copy-start(f32[2,16,8,256]{3,2,1,0:T(8,128)} %refs_6_.3) | copy-start | bytes 786436
  24.3 14.8 %all-to-all-start.1 = ((f32[32,1,1024]{2,1,0:T(1,128)}), f32[32,1,1024]{2,1,0:T(1,128)S(1)}, u32[]{:S(2)}, u32[]{:S(2)}) async-start(f32[32,1,1024]{2,1,0:T(1,128)} %bitcast.4), calls=%async_computation.1 | async-start | bytes 262144 | tf_op jit(solution)/shard_map/all_to_all | solution.py:380
  28.9 10.2 %collective-permute-start = (f32[1,128]{1,0:T(1,128)S(1)}, f32[1,128]{1,0:T(1,128)S(1)}, u32[]{:S(2)}, u32[]{:S(2)}) collective-permute-start(f32[1,128]{1,0:T(1,128)S(1)} %get-tuple-element.21), channel_id=1, source_target_pairs={{0,256},{32,288},{64,320},{96,352},{128,384},{160,416},{192,448},{... | collective-permute-start | bytes 1544 | tf_op jit(solution)/shard_map/ppermute | solution.py:444
  58.1 14.0 %all-to-all-start.3 = ((f32[32,1,1024]{2,1,0:T(1,128)}), f32[32,1,1024]{2,1,0:T(1,128)S(1)}, u32[]{:S(2)}, u32[]{:S(2)}) async-start(f32[32,1,1024]{2,1,0:T(1,128)} %bitcast.8), calls=%async_computation.3 | async-start | bytes 262144 | tf_op jit(solution)/shard_map/all_to_all | solution.py:380
  62.5 8.8 %collective-permute-start.1 = (f32[1,128]{1,0:T(1,128)S(1)}, f32[1,128]{1,0:T(1,128)S(1)}, u32[]{:S(2)}, u32[]{:S(2)}) collective-permute-start(f32[1,128]{1,0:T(1,128)S(1)} %get-tuple-element.25.refs_5_.refs_7_), channel_id=1, source_target_pairs={{0,256},{32,288},{64,320},{96,352},{128,384},{160,416},{192,448},{... | collective-permute-start | bytes 1544 | tf_op jit(solution)/shard_map/ppermute | solution.py:444
  115.6 8.8 %collective-permute-start.2 = (f32[1,128]{1,0:T(1,128)S(1)}, f32[1,128]{1,0:T(1,128)S(1)}, u32[]{:S(2)}, u32[]{:S(2)}) collective-permute-start(f32[1,128]{1,0:T(1,128)S(1)} %shard_map.111), channel_id=1, source_target_pairs={{0,256},{32,288},{64,320},{96,352},{128,384},{160,416},{192,448},{... | collective-permute-start | bytes 1544 | tf_op jit(solution)/shard_map/ppermute | solution.py:439

commit v12 on v10

--- a/solution.py
+++ b/solution.py
@@ -185,10 +185,7 @@
     out_ref[...] = rows_of(y_ref)
 
 
-def column_kernel(carries, y_ref, *refs):
-    refs = list(refs)
-    carry_ref = refs.pop(0) if carries else None
-    left_ref, spectrum_ref, out_ref = refs[:3]
+def column_kernel(totals, y_ref, left_ref, spectrum_ref, out_ref, *total_ref):
     tiles = tiles_of(y_ref)
     first, second = (jnp.concatenate(t, axis=0) for t in (tiles[: PEERS // 2], tiles[PEERS // 2 :]))
     spectrum = spectrum_ref[lax.axis_index("krow") % 2]
@@ -200,10 +197,13 @@
     step = out_ref.shape[0] // PEERS
     for peer in range(PEERS):
         out_ref[peer * step : peer * step + ROWS, :] = w[peer * ROWS : (peer + 1) * ROWS]
-    if carries:
-        send_row(carry_ref[...] * prefix_weight(), out_ref)
-    else:
-        refs[3][...] = rows_of(y_ref)
+    if totals:
+        total_ref[0][...] = rows_of(y_ref)
+
+
+def carry_kernel(blocks_ref, row_ref, out_ref):
+    out_ref[...] = blocks_ref[...]
+    send_row(row_ref[...] * prefix_weight(), out_ref)
 
 
 def unpack(channels):
@@ -409,13 +409,14 @@
     sums = []
     for section in range(4):
         arrived = swap(out)
-        column = functools.partial(column_kernel, section == 3)
+        column = functools.partial(column_kernel, section < 3)
         if section < 3:
             mixed, total = call(column, [plain, row], arrived, left, spectrum)
         else:
             (total,) = call(total_kernel, [row], arrived)
             carry = lax.ppermute(total, ("macro", "krow"), exchange)
-            (mixed,) = call(column, [carrying], arrived, carry, left, spectrum)
+            (mixed,) = call(column, [carrying], arrived, left, spectrum)
+            (mixed,) = call(carry_kernel, [carrying], mixed, carry)
         extra = [total] if section in (1, 2) else []
         sums += extra
         if section in (0, 1):

time: 140 us -> 140 us (level)
    pallas_call x10 -> x11, Pallas kernels: 7.9 us -> 7.93 us  [call(): pl.pallas_call(body, out_shape=shapes, in_specs=[hbm if n in in_hbm else...]
where the time goes in v12:
time: 140 us; the launch traced here: 139 us
  blocking collectives  93.6 us (67%)
  starting transfers between devices  23 us (16%)
  waiting for transfers between devices  14 us (10%)
  Pallas kernels  7.93 us (6%)
    all_to_all x6, blocking collectives, swap(): return lax.all_to_all(blocks, 'krow', 0, 0, tiled=True).reshape(x.shape)  93.6 us
    ppermute x2, starting transfers between devices, per_device(): extra = extra + [lax.ppermute(total, ('macro', 'krow'), exchange)]  12.3 us
    all_to_all x2, starting transfers between devices, swap(): return lax.all_to_all(blocks, 'krow', 0, 0, tiled=True).reshape(x.shape)  8.79 us
    pallas_call x11, Pallas kernels, call(): pl.pallas_call(body, out_shape=shapes, in_specs=[hbm if n in in_hbm else...  7.93 us
    ppermute x2, waiting for transfers between devices, per_device(): extra = extra + [lax.ppermute(total, ('macro', 'krow'), exchange)]  6.7 us
    ppermute x1, waiting for transfers between devices, per_device(): carry = lax.ppermute(total, ('macro', 'krow'), exchange)  6.41 us
  transfers between devices with their start and end apart: 5, of which 4 were waited for; matrix products, arithmetic and copies ran while one was open for 0% of the time, Pallas kernels for 0%

profile of v12, /device:TPU:8, one launch (start us, length us, event | category | flops | bytes accessed | tf_op | source)
XLA Modules:
  0.0 139.3 jit_solution(678666413876383268)
XLA Ops:
  0.6 2.2 %shard_map.104 = (f32[288,128]{1,0:T(8,128)}, f32[5,8,256]{2,1,0:T(8,128)}) custom-call(f32[16,8,256]{2,1,0:T(8,128)} %bitcast.19, bf16[3,256,256]{2,1,0:T(8,128)(2,1)} %constant.8.clone.refs_1_.refs_5_.refs_7_.refs_6_.refs_9_, bf16[3,256,128]{2,1,0:T(8,128)(2,1)} %constant.9.clone.refs_2_.refs_6_.refs_8_.refs_7_.refs_10_, f32[2,16,8,256]{3,2,1,0:T(8,128)} %refs_6_.3, ...), custom_call_target="tpu_custom_call" | custom-call | flops 50331648 | bytes 1048576 | tf_op jit(solution)/shard_map/pallas_call | solution.py:353
  2.8 20.3 %all_to_all.40 = f32[32,1,1152]{2,1,0:T(1,128)S(1)} all-to-all(f32[32,1,1152]{2,1,0:T(1,128)} %bitcast.38), channel_id=1, replica_groups=mesh['macro'=16,'krow'=32] {'krow'}, dimensions={0} | all-to-all | bytes 294912 | tf_op jit(solution)/shard_map/all_to_all | solution.py:368
  23.2 1.1 shard_map.105
  24.3 4.5 %all-to-all-start.1 = ((f32[32,1,1024]{2,1,0:T(1,128)}), f32[32,1,1024]{2,1,0:T(1,128)S(1)}, u32[]{:S(2)}, u32[]{:S(2)}) async-start(f32[32,1,1024]{2,1,0:T(1,128)} %bitcast.4), calls=%async_computation.1 | async-start | bytes 262144 | tf_op jit(solution)/shard_map/all_to_all | solution.py:368
  28.8 9.0 %collective-permute-start = (f32[1,128]{1,0:T(1,128)S(1)}, f32[1,128]{1,0:T(1,128)S(1)}, u32[]{:S(2)}, u32[]{:S(2)}) collective-permute-start(f32[1,128]{1,0:T(1,128)S(1)} %get-tuple-element.21), channel_id=1, source_target_pairs={{0,256},{32,288},{64,320},{96,352},{128,384},{160,416},{192,448},{... | collective-permute-start | bytes 1544 | tf_op jit(solution)/shard_map/ppermute | solution.py:423
  37.8 1.3 collective-permute-done.refs_4_
  39.1 0.5 shard_map.106
  39.6 17.4 %all_to_all.41 = f32[32,1,1152]{2,1,0:T(1,128)S(1)} all-to-all(f32[32,1,1152]{2,1,0:T(1,128)S(1)} %bitcast.34), channel_id=1, replica_groups=mesh['macro'=16,'krow'=32] {'krow'}, dimensions={0} | all-to-all | bytes 294912 | tf_op jit(solution)/shard_map/all_to_all | solution.py:368
  57.0 1.1 shard_map.107
  58.1 4.3 %all-to-all-start.3 = ((f32[32,1,1024]{2,1,0:T(1,128)}), f32[32,1,1024]{2,1,0:T(1,128)S(1)}, u32[]{:S(2)}, u32[]{:S(2)}) async-start(f32[32,1,1024]{2,1,0:T(1,128)} %bitcast.8), calls=%async_computation.3 | async-start | bytes 262144 | tf_op jit(solution)/shard_map/all_to_all | solution.py:368
  62.4 3.3 %collective-permute-start.1 = (f32[1,128]{1,0:T(1,128)S(1)}, f32[1,128]{1,0:T(1,128)S(1)}, u32[]{:S(2)}, u32[]{:S(2)}) collective-permute-start(f32[1,128]{1,0:T(1,128)S(1)} %get-tuple-element.25.refs_5_.refs_7_), channel_id=1, source_target_pairs={{0,256},{32,288},{64,320},{96,352},{128,384},{160,416},{192,448},{... | collective-permute-start | bytes 1544 | tf_op jit(solution)/shard_map/ppermute | solution.py:423
  65.7 5.4 %collective-permute-done.1.refs_6_ = f32[1,128]{1,0:T(1,128)S(1)} collective-permute-done((f32[1,128]{1,0:T(1,128)S(1)}, f32[1,128]{1,0:T(1,128)S(1)}, u32[]{:S(2)}, u32[]{:S(2)}) %collective-permute-start.1) | collective-permute-done | bytes 544 | tf_op jit(solution)/shard_map/ppermute | solution.py:423
  71.1 0.9 all-to-all-done.3
  72.0 0.5 shard_map.108
  72.6 14.1 %all_to_all.42 = f32[32,1,1152]{2,1,0:T(1,128)S(1)} all-to-all(f32[32,1,1152]{2,1,0:T(1,128)S(1)} %bitcast.35), channel_id=1, replica_groups=mesh['macro'=16,'krow'=32] {'krow'}, dimensions={0} | all-to-all | bytes 294912 | tf_op jit(solution)/shard_map/all_to_all | solution.py:368
  86.7 0.4 shard_map.109
  87.1 13.8 %all_to_all.43 = f32[32,1,1024]{2,1,0:T(1,128)S(1)} all-to-all(f32[32,1,1024]{2,1,0:T(1,128)S(1)} %bitcast.37), channel_id=1, replica_groups=mesh['macro'=16,'krow'=32] {'krow'}, dimensions={0} | all-to-all | bytes 262144 | tf_op jit(solution)/shard_map/all_to_all | solution.py:368
  100.9 0.6 shard_map.110
  101.5 14.0 %all_to_all.44 = f32[32,1,1152]{2,1,0:T(1,128)S(1)} all-to-all(f32[32,1,1152]{2,1,0:T(1,128)S(1)} %bitcast.36), channel_id=1, replica_groups=mesh['macro'=16,'krow'=32] {'krow'}, dimensions={0} | all-to-all | bytes 294912 | tf_op jit(solution)/shard_map/all_to_all | solution.py:368
  115.5 1.9 %collective-permute-start.2 = (f32[1,128]{1,0:T(1,128)S(1)}, f32[1,128]{1,0:T(1,128)S(1)}, u32[]{:S(2)}, u32[]{:S(2)}) collective-permute-start(f32[1,128]{1,0:T(1,128)S(1)} %shard_map.112), channel_id=1, source_target_pairs={{0,256},{32,288},{64,320},{96,352},{128,384},{160,416},{192,448},{... | collective-permute-start | bytes 1544 | tf_op jit(solution)/shard_map/ppermute | solution.py:417
  117.4 0.4 shard_map.111.blocks_ref
  117.9 6.4 %collective-permute-done.2.row_ref = f32[1,128]{1,0:T(1,128)S(1)} collective-permute-done((f32[1,128]{1,0:T(1,128)S(1)}, f32[1,128]{1,0:T(1,128)S(1)}, u32[]{:S(2)}, u32[]{:S(2)}) %collective-permute-start.2) | collective-permute-done | bytes 544 | tf_op jit(solution)/shard_map/ppermute | solution.py:417
  124.3 13.9 %all_to_all.45 = f32[32,1,1152]{2,1,0:T(1,128)S(1)} all-to-all(f32[32,1,1152]{2,1,0:T(1,128)S(1)} %bitcast.24), channel_id=1, replica_groups=mesh['macro'=16,'krow'=32] {'krow'}, dimensions={0} | all-to-all | bytes 294912 | tf_op jit(solution)/shard_map/all_to_all | solution.py:368
  138.3 1.1 shard_map.114
  (17 shorter events, 0.1 us)
Async XLA Ops:
  0.6 22.5 %copy-start.2 = (bf16[3,2,128,256]{3,2,1,0:T(8,128)(2,1)S(1)}, bf16[3,2,128,256]{3,2,1,0:T(8,128)(2,1)}, u32[]{:S(2)}) copy-start(bf16[3,2,128,256]{3,2,1,0:T(8,128)(2,1)} %constant.10.clone.left_ref) | copy-start | bytes 1179652
  2.8 20.4 %copy-start.4 = (f32[2,256,128]{2,1,0:T(8,128)S(1)}, f32[2,256,128]{2,1,0:T(8,128)}, u32[]{:S(2)}) copy-start(f32[2,256,128]{2,1,0:T(8,128)} %constant.11.clone.spectrum_ref) | copy-start | bytes 786436
  23.2 15.9 %copy-start = (bf16[3,256,256]{2,1,0:T(8,128)(2,1)S(1)}, bf16[3,256,256]{2,1,0:T(8,128)(2,1)}, u32[]{:S(2)}) copy-start(bf16[3,256,256]{2,1,0:T(8,128)(2,1)} %constant.8.clone.refs_1_.refs_5_.refs_7_.refs_6_.refs_9_) | copy-start | bytes 1179652
  23.2 15.9 %copy-start.3 = (bf16[3,256,128]{2,1,0:T(8,128)(2,1)S(1)}, bf16[3,256,128]{2,1,0:T(8,128)(2,1)}, u32[]{:S(2)}) copy-start(bf16[3,256,128]{2,1,0:T(8,128)(2,1)} %constant.9.clone.refs_2_.refs_6_.refs_8_.refs_7_.refs_10_) | copy-start | bytes 589828
  23.2 15.9 %copy-start.5 = (f32[1,16,8,256]{3,2,1,0:T(8,128)S(1)}, f32[1,16,8,256]{3,2,1,0:T(8,128)}, u32[]{:S(2)}) copy-start(f32[1,16,8,256]{3,2,1,0:T(8,128)} %param.9) | copy-start | bytes 393220
  23.2 15.9 %copy-start.6 = (f32[5,8,256]{2,1,0:T(8,128)S(1)}, f32[5,8,256]{2,1,0:T(8,128)}, u32[]{:S(2)}) copy-start(f32[5,8,256]{2,1,0:T(8,128)} %get-tuple-element.20.refs_2_.refs_3_.refs_5_) | copy-start | bytes 122884
  24.3 14.8 %copy-start.1 = (f32[2,16,8,256]{3,2,1,0:T(8,128)S(1)}, f32[2,16,8,256]{3,2,1,0:T(8,128)}, u32[]{:S(2)}) copy-start(f32[2,16,8,256]{3,2,1,0:T(8,128)} %refs_6_.3) | copy-start | bytes 786436
  24.3 14.8 %all-to-all-start.1 = ((f32[32,1,1024]{2,1,0:T(1,128)}), f32[32,1,1024]{2,1,0:T(1,128)S(1)}, u32[]{:S(2)}, u32[]{:S(2)}) async-start(f32[32,1,1024]{2,1,0:T(1,128)} %bitcast.4), calls=%async_computation.1 | async-start | bytes 262144 | tf_op jit(solution)/shard_map/all_to_all | solution.py:368
  28.8 10.2 %collective-permute-start = (f32[1,128]{1,0:T(1,128)S(1)}, f32[1,128]{1,0:T(1,128)S(1)}, u32[]{:S(2)}, u32[]{:S(2)}) collective-permute-start(f32[1,128]{1,0:T(1,128)S(1)} %get-tuple-element.21), channel_id=1, source_target_pairs={{0,256},{32,288},{64,320},{96,352},{128,384},{160,416},{192,448},{... | collective-permute-start | bytes 1544 | tf_op jit(solution)/shard_map/ppermute | solution.py:423
  58.1 14.0 %all-to-all-start.3 = ((f32[32,1,1024]{2,1,0:T(1,128)}), f32[32,1,1024]{2,1,0:T(1,128)S(1)}, u32[]{:S(2)}, u32[]{:S(2)}) async-start(f32[32,1,1024]{2,1,0:T(1,128)} %bitcast.8), calls=%async_computation.3 | async-start | bytes 262144 | tf_op jit(solution)/shard_map/all_to_all | solution.py:368
  62.4 8.8 %collective-permute-start.1 = (f32[1,128]{1,0:T(1,128)S(1)}, f32[1,128]{1,0:T(1,128)S(1)}, u32[]{:S(2)}, u32[]{:S(2)}) collective-permute-start(f32[1,128]{1,0:T(1,128)S(1)} %get-tuple-element.25.refs_5_.refs_7_), channel_id=1, source_target_pairs={{0,256},{32,288},{64,320},{96,352},{128,384},{160,416},{192,448},{... | collective-permute-start | bytes 1544 | tf_op jit(solution)/shard_map/ppermute | solution.py:423
  115.5 8.8 %collective-permute-start.2 = (f32[1,128]{1,0:T(1,128)S(1)}, f32[1,128]{1,0:T(1,128)S(1)}, u32[]{:S(2)}, u32[]{:S(2)}) collective-permute-start(f32[1,128]{1,0:T(1,128)S(1)} %shard_map.112), channel_id=1, source_target_pairs={{0,256},{32,288},{64,320},{96,352},{128,384},{160,416},{192,448},{... | collective-permute-start | bytes 1544 | tf_op jit(solution)/shard_map/ppermute | solution.py:417

commit v13 on v12

--- a/solution.py
+++ b/solution.py
@@ -379,6 +379,7 @@
         (m * PEERS + seat, (m ^ shift) * PEERS + seat)
         for seat, shift in SEATS.items()
         for m in range(POINTS)
+        if m <= m ^ shift
     ]
 
     out, fields = call(

time: 140 us -> 139 us (level)
  waiting for transfers between devices: 14 us -> 8.51 us
  blocking collectives: 93.6 us -> 98.7 us
    ppermute x1, waiting for transfers between devices: 6.41 us -> 0.85 us  [per_device(): carry = lax.ppermute(total, ('macro', 'krow'), exchange)]
    all_to_all x6, blocking collectives: 93.6 us -> 98.7 us  [swap(): return lax.all_to_all(blocks, 'krow', 0, 0, tiled=True).reshape(x.shape)]
    all_to_all x2, waiting for transfers between devices: 0.9 us -> 5.1 us  [swap(): return lax.all_to_all(blocks, 'krow', 0, 0, tiled=True).reshape(x.shape)]
    ppermute x2, waiting for transfers between devices: 6.7 us -> 2.55 us  [per_device(): extra = extra + [lax.ppermute(total, ('macro', 'krow'), exchange)]]
where the time goes in v13:
time: 139 us; the launch traced here: 138 us
  blocking collectives  98.7 us (71%)
  starting transfers between devices  22.4 us (16%)
  waiting for transfers between devices  8.51 us (6%)
  Pallas kernels  7.92 us (6%)
    all_to_all x6, blocking collectives, swap(): return lax.all_to_all(blocks, 'krow', 0, 0, tiled=True).reshape(x.shape)  98.7 us
    ppermute x2, starting transfers between devices, per_device(): extra = extra + [lax.ppermute(total, ('macro', 'krow'), exchange)]  12.4 us
    all_to_all x2, starting transfers between devices, swap(): return lax.all_to_all(blocks, 'krow', 0, 0, tiled=True).reshape(x.shape)  8.78 us
    pallas_call x11, Pallas kernels, call(): pl.pallas_call(body, out_shape=shapes, in_specs=[hbm if n in in_hbm else...  7.92 us
    all_to_all x2, waiting for transfers between devices, swap(): return lax.all_to_all(blocks, 'krow', 0, 0, tiled=True).reshape(x.shape)  5.1 us
  transfers between devices with their start and end apart: 5, of which 4 were waited for; matrix products, arithmetic and copies ran while one was open for 0% of the time, Pallas kernels for 0%

profile of v13, /device:TPU:8, one launch (start us, length us, event | category | flops | bytes accessed | tf_op | source)
XLA Modules:
  0.0 138.3 jit_solution(2636389636255794549)
XLA Ops:
  0.6 2.2 %shard_map.104 = (f32[288,128]{1,0:T(8,128)}, f32[5,8,256]{2,1,0:T(8,128)}) custom-call(f32[16,8,256]{2,1,0:T(8,128)} %bitcast.19, bf16[3,256,256]{2,1,0:T(8,128)(2,1)} %constant.8.clone.refs_1_.refs_5_.refs_7_.refs_6_.refs_9_, bf16[3,256,128]{2,1,0:T(8,128)(2,1)} %constant.9.clone.refs_2_.refs_6_.refs_8_.refs_7_.refs_10_, f32[2,16,8,256]{3,2,1,0:T(8,128)} %refs_6_.3, ...), custom_call_target="tpu_custom_call" | custom-call | flops 50331648 | bytes 1048576 | tf_op jit(solution)/shard_map/pallas_call | solution.py:353
  2.8 20.3 %all_to_all.40 = f32[32,1,1152]{2,1,0:T(1,128)S(1)} all-to-all(f32[32,1,1152]{2,1,0:T(1,128)} %bitcast.38), channel_id=1, replica_groups=mesh['macro'=16,'krow'=32] {'krow'}, dimensions={0} | all-to-all | bytes 294912 | tf_op jit(solution)/shard_map/all_to_all | solution.py:368
  23.2 1.1 shard_map.105
  24.3 4.5 %all-to-all-start.1 = ((f32[32,1,1024]{2,1,0:T(1,128)}), f32[32,1,1024]{2,1,0:T(1,128)S(1)}, u32[]{:S(2)}, u32[]{:S(2)}) async-start(f32[32,1,1024]{2,1,0:T(1,128)} %bitcast.4), calls=%async_computation.1 | async-start | bytes 262144 | tf_op jit(solution)/shard_map/all_to_all | solution.py:368
  28.8 9.0 %collective-permute-start = (f32[1,128]{1,0:T(1,128)S(1)}, f32[1,128]{1,0:T(1,128)S(1)}, u32[]{:S(2)}, u32[]{:S(2)}) collective-permute-start(f32[1,128]{1,0:T(1,128)S(1)} %get-tuple-element.21), channel_id=1, source_target_pairs={{0,256},{32,288},{64,320},{96,352},{128,384},{160,416},{192,448},{... | collective-permute-start | bytes 1544 | tf_op jit(solution)/shard_map/ppermute | solution.py:424
  37.8 1.3 collective-permute-done.refs_4_
  39.1 0.5 shard_map.106
  39.6 16.8 %all_to_all.41 = f32[32,1,1152]{2,1,0:T(1,128)S(1)} all-to-all(f32[32,1,1152]{2,1,0:T(1,128)S(1)} %bitcast.34), channel_id=1, replica_groups=mesh['macro'=16,'krow'=32] {'krow'}, dimensions={0} | all-to-all | bytes 294912 | tf_op jit(solution)/shard_map/all_to_all | solution.py:368
  56.5 1.1 shard_map.107
  57.5 4.3 %all-to-all-start.3 = ((f32[32,1,1024]{2,1,0:T(1,128)}), f32[32,1,1024]{2,1,0:T(1,128)S(1)}, u32[]{:S(2)}, u32[]{:S(2)}) async-start(f32[32,1,1024]{2,1,0:T(1,128)} %bitcast.8), calls=%async_computation.3 | async-start | bytes 262144 | tf_op jit(solution)/shard_map/all_to_all | solution.py:368
  61.8 3.4 %collective-permute-start.1 = (f32[1,128]{1,0:T(1,128)S(1)}, f32[1,128]{1,0:T(1,128)S(1)}, u32[]{:S(2)}, u32[]{:S(2)}) collective-permute-start(f32[1,128]{1,0:T(1,128)S(1)} %get-tuple-element.25.refs_5_.refs_7_), channel_id=1, source_target_pairs={{0,256},{32,288},{64,320},{96,352},{128,384},{160,416},{192,448},{... | collective-permute-start | bytes 1544 | tf_op jit(solution)/shard_map/ppermute | solution.py:424
  65.2 1.3 collective-permute-done.1.refs_6_
  66.5 5.1 %all-to-all-done.3 = f32[32,1,1024]{2,1,0:T(1,128)S(1)} async-done(((f32[32,1,1024]{2,1,0:T(1,128)}), f32[32,1,1024]{2,1,0:T(1,128)S(1)}, u32[]{:S(2)}, u32[]{:S(2)}) %all-to-all-start.3) | async-done | bytes 131104 | tf_op jit(solution)/shard_map/all_to_all | solution.py:368
  71.6 0.5 shard_map.108
  72.2 14.0 %all_to_all.42 = f32[32,1,1152]{2,1,0:T(1,128)S(1)} all-to-all(f32[32,1,1152]{2,1,0:T(1,128)S(1)} %bitcast.35), channel_id=1, replica_groups=mesh['macro'=16,'krow'=32] {'krow'}, dimensions={0} | all-to-all | bytes 294912 | tf_op jit(solution)/shard_map/all_to_all | solution.py:368
  86.1 0.4 shard_map.109
  86.6 13.8 %all_to_all.43 = f32[32,1,1024]{2,1,0:T(1,128)S(1)} all-to-all(f32[32,1,1024]{2,1,0:T(1,128)S(1)} %bitcast.37), channel_id=1, replica_groups=mesh['macro'=16,'krow'=32] {'krow'}, dimensions={0} | all-to-all | bytes 262144 | tf_op jit(solution)/shard_map/all_to_all | solution.py:368
  100.4 0.6 shard_map.110
  101.0 14.0 %all_to_all.44 = f32[32,1,1152]{2,1,0:T(1,128)S(1)} all-to-all(f32[32,1,1152]{2,1,0:T(1,128)S(1)} %bitcast.36), channel_id=1, replica_groups=mesh['macro'=16,'krow'=32] {'krow'}, dimensions={0} | all-to-all | bytes 294912 | tf_op jit(solution)/shard_map/all_to_all | solution.py:368
  115.0 1.3 collective-permute-start.2
  116.3 0.4 shard_map.111.blocks_ref
  116.7 0.8 collective-permute-done.2.row_ref
  117.6 19.6 %all_to_all.45 = f32[32,1,1152]{2,1,0:T(1,128)S(1)} all-to-all(f32[32,1,1152]{2,1,0:T(1,128)S(1)} %bitcast.24), channel_id=1, replica_groups=mesh['macro'=16,'krow'=32] {'krow'}, dimensions={0} | all-to-all | bytes 294912 | tf_op jit(solution)/shard_map/all_to_all | solution.py:368
  137.3 1.1 shard_map.114
  (17 shorter events, 0.1 us)
Async XLA Ops:
  0.6 22.5 %copy-start.2 = (bf16[3,2,128,256]{3,2,1,0:T(8,128)(2,1)S(1)}, bf16[3,2,128,256]{3,2,1,0:T(8,128)(2,1)}, u32[]{:S(2)}) copy-start(bf16[3,2,128,256]{3,2,1,0:T(8,128)(2,1)} %constant.10.clone.left_ref) | copy-start | bytes 1179652
  2.8 20.4 %copy-start.4 = (f32[2,256,128]{2,1,0:T(8,128)S(1)}, f32[2,256,128]{2,1,0:T(8,128)}, u32[]{:S(2)}) copy-start(f32[2,256,128]{2,1,0:T(8,128)} %constant.11.clone.spectrum_ref) | copy-start | bytes 786436
  23.2 15.9 %copy-start = (bf16[3,256,256]{2,1,0:T(8,128)(2,1)S(1)}, bf16[3,256,256]{2,1,0:T(8,128)(2,1)}, u32[]{:S(2)}) copy-start(bf16[3,256,256]{2,1,0:T(8,128)(2,1)} %constant.8.clone.refs_1_.refs_5_.refs_7_.refs_6_.refs_9_) | copy-start | bytes 1179652
  23.2 15.9 %copy-start.3 = (bf16[3,256,128]{2,1,0:T(8,128)(2,1)S(1)}, bf16[3,256,128]{2,1,0:T(8,128)(2,1)}, u32[]{:S(2)}) copy-start(bf16[3,256,128]{2,1,0:T(8,128)(2,1)} %constant.9.clone.refs_2_.refs_6_.refs_8_.refs_7_.refs_10_) | copy-start | bytes 589828
  23.2 15.9 %copy-start.5 = (f32[1,16,8,256]{3,2,1,0:T(8,128)S(1)}, f32[1,16,8,256]{3,2,1,0:T(8,128)}, u32[]{:S(2)}) copy-start(f32[1,16,8,256]{3,2,1,0:T(8,128)} %param.9) | copy-start | bytes 393220
  23.2 15.9 %copy-start.6 = (f32[5,8,256]{2,1,0:T(8,128)S(1)}, f32[5,8,256]{2,1,0:T(8,128)}, u32[]{:S(2)}) copy-start(f32[5,8,256]{2,1,0:T(8,128)} %get-tuple-element.20.refs_2_.refs_3_.refs_5_) | copy-start | bytes 122884
  24.3 14.8 %copy-start.1 = (f32[2,16,8,256]{3,2,1,0:T(8,128)S(1)}, f32[2,16,8,256]{3,2,1,0:T(8,128)}, u32[]{:S(2)}) copy-start(f32[2,16,8,256]{3,2,1,0:T(8,128)} %refs_6_.3) | copy-start | bytes 786436
  24.3 14.8 %all-to-all-start.1 = ((f32[32,1,1024]{2,1,0:T(1,128)}), f32[32,1,1024]{2,1,0:T(1,128)S(1)}, u32[]{:S(2)}, u32[]{:S(2)}) async-start(f32[32,1,1024]{2,1,0:T(1,128)} %bitcast.4), calls=%async_computation.1 | async-start | bytes 262144 | tf_op jit(solution)/shard_map/all_to_all | solution.py:368
  28.8 10.2 %collective-permute-start = (f32[1,128]{1,0:T(1,128)S(1)}, f32[1,128]{1,0:T(1,128)S(1)}, u32[]{:S(2)}, u32[]{:S(2)}) collective-permute-start(f32[1,128]{1,0:T(1,128)S(1)} %get-tuple-element.21), channel_id=1, source_target_pairs={{0,256},{32,288},{64,320},{96,352},{128,384},{160,416},{192,448},{... | collective-permute-start | bytes 1544 | tf_op jit(solution)/shard_map/ppermute | solution.py:424
  57.5 14.1 %all-to-all-start.3 = ((f32[32,1,1024]{2,1,0:T(1,128)}), f32[32,1,1024]{2,1,0:T(1,128)S(1)}, u32[]{:S(2)}, u32[]{:S(2)}) async-start(f32[32,1,1024]{2,1,0:T(1,128)} %bitcast.8), calls=%async_computation.3 | async-start | bytes 262144 | tf_op jit(solution)/shard_map/all_to_all | solution.py:368
  61.8 4.7 %collective-permute-start.1 = (f32[1,128]{1,0:T(1,128)S(1)}, f32[1,128]{1,0:T(1,128)S(1)}, u32[]{:S(2)}, u32[]{:S(2)}) collective-permute-start(f32[1,128]{1,0:T(1,128)S(1)} %get-tuple-element.25.refs_5_.refs_7_), channel_id=1, source_target_pairs={{0,256},{32,288},{64,320},{96,352},{128,384},{160,416},{192,448},{... | collective-permute-start | bytes 1544 | tf_op jit(solution)/shard_map/ppermute | solution.py:424
  115.0 2.6 %collective-permute-start.2 = (f32[1,128]{1,0:T(1,128)S(1)}, f32[1,128]{1,0:T(1,128)S(1)}, u32[]{:S(2)}, u32[]{:S(2)}) collective-permute-start(f32[1,128]{1,0:T(1,128)S(1)} %shard_map.112), channel_id=1, source_target_pairs={{0,256},{32,288},{64,320},{96,352},{128,384},{160,416},{192,448},{... | collective-permute-start | bytes 1544 | tf_op jit(solution)/shard_map/ppermute | solution.py:418

commit v14 on v13

--- a/solution.py
+++ b/solution.py
@@ -138,7 +138,7 @@
 
 
 def first_kernel(*refs):
-    sources, (out_ref, fields_ref), fetched, sems = refs[:7], refs[7:9], refs[9:16], refs[16]
+    sources, out_ref, fetched, sems = refs[:4], refs[4], refs[5:9], refs[9]
     copies = [
         pltpu.make_async_copy(
             source.at[pl.ds(0, 2)] if n in (1, 2) else source, target, sems.at[n]
@@ -147,7 +147,7 @@
     ]
     for copy in copies:
         copy.start()
-    density_ref, wide_ref, narrow_ref, momentum_ref, energies_ref, emitted_ref, drive_ref = fetched
+    density_ref, wide_ref, narrow_ref, momentum_ref = fetched
     for copy in copies[:3]:
         copy.wait()
     send_rows(density_ref[...].reshape(CHANNELS * ROWS, GRID), wide_ref, narrow_ref, out_ref)
@@ -160,6 +160,9 @@
             momentum = [momentum_ref[i, c, :, lanes] for i in range(2)]
             add_currents(currents, 0, c, momentum, density_ref[c, :, lanes])
     send_row(currents_row(currents), out_ref)
+
+
+def pack_kernel(energies_ref, emitted_ref, drive_ref, fields_ref):
     fields_ref[:BANDS] = energies_ref[...]
     lane = lax.broadcasted_iota(jnp.int32, (1, LANES), 1)
     row = jnp.zeros((1, LANES), jnp.float32)
@@ -255,10 +258,35 @@
     return diagonal + upper_real + upper_imag
 
 
+def last_kernel(first_ref, second_ref, third_ref, fourth_ref, fields_ref, momentum_ref, out_ref):
+    for part in range(2):
+        lanes = slice(part * LANES, (part + 1) * LANES)
+        rho = [fourth_ref[c, :, lanes] for c in range(CHANNELS)]
+        hamilton = []
+        for c in range(CHANNELS):
+            value = fields_ref[c, :, lanes] if c < BANDS else 0.0
+            for i in range(2):
+                lane = 3 * i + 2
+                value = value + fields_ref[BANDS, 0:1, lane : lane + 1] * momentum_ref[i, c, :, lanes]
+            hamilton.append(value)
+        rates = commute(hamilton, rho)
+        for c in range(CHANNELS):
+            rate = rates[c] if c < BANDS else rates[c] - dephasing * rho[c]
+            base = second_ref[c, :, lanes] + 2.0 * third_ref[c, :, lanes] + rho[c]
+            base = (base - first_ref[c, :, lanes]) * (1.0 / 3.0)
+            out_ref[c, :, lanes] = base + (time_step / 6.0) * rate
+
+
+def last_column_kernel(y_ref, left_ref, spectrum_ref, *refs):
+    *state_refs, out_ref, base_ref = refs
+    column_kernel(False, y_ref, left_ref, spectrum_ref, out_ref)
+    last_kernel(*state_refs, base_ref)
+
+
 def state_kernel(section, *refs):
     refs = list(refs)
     back_ref = refs.pop(0)
-    state_refs = [refs.pop(0) for _ in range((1, 2, 2, 4)[section])]
+    state_refs = [refs.pop(0) for _ in range((1, 2, 2, 2)[section])]
     density_ref, state_ref = state_refs[0], state_refs[-1]
     fields_ref, momentum_ref = refs.pop(0), refs.pop(0)
     sums_ref = refs.pop(0) if section in (1, 2) else None
@@ -280,7 +308,7 @@
     potential = []
     for i in range(2):
         lane = 3 * i + drive_row
-        value = fields_ref[BANDS, 0:1, lane : lane + 1]
+        value = fields_ref[BANDS, 0:1, lane : lane + 1] if section < 3 else 0.0
         if section > 0:
             lane = i if section == 3 else 2 + i
             value = value + (time_step * fraction * rate_scale) * upstream[:, lane : lane + 1]
@@ -302,13 +330,13 @@
             value = sigma[part][c * ROWS : (c + 1) * ROWS]
             value = value + potential[0] * momentum_ref[0, c, :, lanes]
             value = value + potential[1] * momentum_ref[1, c, :, lanes]
-            if c < BANDS:
+            if c < BANDS and section < 3:
                 value = value + fields_ref[c, :, lanes]
             hamilton.append(value)
         rates = commute(hamilton, rho)
         for c in range(CHANNELS):
-            rate = rates[c] if c < BANDS else rates[c] - dephasing * rho[c]
             if section < 3:
+                rate = rates[c] if c < BANDS else rates[c] - dephasing * rho[c]
                 new = density_ref[c, :, lanes] + (time_step * next_fraction) * rate
                 next_ref[c, :, lanes] = new
                 momentum = [momentum_ref[i, c, :, lanes] for i in range(2)]
@@ -318,9 +346,7 @@
                     add_currents(currents, 0, c, momentum, rho[c])
                     add_currents(currents, 1, c, momentum, new)
             else:
-                first, second, third, fourth = (r[c, :, lanes] for r in state_refs)
-                base = (second + 2.0 * third + fourth - first) * (1.0 / 3.0)
-                result_ref[c, :, lanes] = base + (time_step / 6.0) * rate
+                result_ref[c, :, lanes] = density_ref[c, :, lanes] + (time_step / 6.0) * rates[c]
 
     if section < 3:
         state = next_ref[...].reshape(CHANNELS * ROWS, GRID)
@@ -382,29 +408,24 @@
         if m <= m ^ shift
     ]
 
-    out, fields = call(
+    (out,) = call(
         first_kernel,
-        [carrying, (BANDS + 1, ROWS, GRID)],
+        [carrying],
         density,
         wide,
         narrow,
         momentum,
-        energies,
-        emitted,
-        drive,
-        in_hbm=range(7),
+        in_hbm=range(4),
         vmem_mib=58,
         scratch=[
             pltpu.VMEM(state_shape, jnp.float32),
             pltpu.VMEM((2, GRID, GRID), jnp.bfloat16),
             pltpu.VMEM((2, GRID, LANES), jnp.bfloat16),
             pltpu.VMEM(momentum.shape, jnp.float32),
-            pltpu.VMEM(energies.shape, jnp.float32),
-            pltpu.VMEM(emitted.shape, jnp.float32),
-            pltpu.VMEM(drive.shape, jnp.float32),
-            pltpu.SemaphoreType.DMA((7,)),
+            pltpu.SemaphoreType.DMA((4,)),
         ],
     )
+    (fields,) = call(pack_kernel, [(BANDS + 1, ROWS, GRID)], energies, emitted, drive)
     row = (1, LANES)
     states = [density]
     sums = []
@@ -416,7 +437,16 @@
         else:
             (total,) = call(total_kernel, [row], arrived)
             carry = lax.ppermute(total, ("macro", "krow"), exchange)
-            (mixed,) = call(column, [carrying], arrived, left, spectrum)
+            mixed, base = call(
+                last_column_kernel,
+                [carrying, state_shape],
+                arrived,
+                left,
+                spectrum,
+                *states,
+                fields,
+                momentum,
+            )
             (mixed,) = call(carry_kernel, [carrying], mixed, carry)
         extra = [total] if section in (1, 2) else []
         sums += extra
@@ -424,7 +454,9 @@
             extra = extra + [lax.ppermute(total, ("macro", "krow"), exchange)]
         back = swap(mixed)
         body = functools.partial(state_kernel, section)
-        used = states if section == 3 else states[:1] if section == 0 else [density, states[-1]]
+        used = states[:1] if section == 0 else [density, states[-1]]
+        if section == 3:
+            used = [base, states[-1]]
         extra = sums if section == 3 else extra
         args = [back, *used, fields, momentum, *extra, wide, narrow]
         if section < 3:

time: 139 us -> 139 us (level)
    pallas_call x11 -> x12, Pallas kernels: 7.92 us -> 8.04 us  [call(): pl.pallas_call(body, out_shape=shapes, in_specs=[hbm if n in in_hbm else...]
where the time goes in v14:
time: 139 us; the launch traced here: 138 us
  blocking collectives  98.7 us (71%)
  starting transfers between devices  22.4 us (16%)
  waiting for transfers between devices  8.25 us (6%)
  Pallas kernels  8.04 us (6%)
    all_to_all x6, blocking collectives, swap(): return lax.all_to_all(blocks, 'krow', 0, 0, tiled=True).reshape(x.shape)  98.7 us
    ppermute x2, starting transfers between devices, per_device(): extra = extra + [lax.ppermute(total, ('macro', 'krow'), exchange)]  12.3 us
    all_to_all x2, starting transfers between devices, swap(): return lax.all_to_all(blocks, 'krow', 0, 0, tiled=True).reshape(x.shape)  8.78 us
    pallas_call x12, Pallas kernels, call(): pl.pallas_call(body, out_shape=shapes, in_specs=[hbm if n in in_hbm else...  8.04 us
    all_to_all x2, waiting for transfers between devices, swap(): return lax.all_to_all(blocks, 'krow', 0, 0, tiled=True).reshape(x.shape)  5.1 us
  transfers between devices with their start and end apart: 5, of which 4 were waited for; matrix products, arithmetic and copies ran while one was open for 0% of the time, Pallas kernels for 0%

profile of v14, /device:TPU:8, one launch (start us, length us, event | category | flops | bytes accessed | tf_op | source)
XLA Modules:
  0.0 138.2 jit_solution(15348981739283705087)
XLA Ops:
  0.6 2.1 %shard_map.104 = f32[288,128]{1,0:T(8,128)} custom-call(f32[16,8,256]{2,1,0:T(8,128)} %bitcast.19, bf16[3,256,256]{2,1,0:T(8,128)(2,1)} %constant.8.clone.refs_1_.refs_5_.refs_7_.refs_6_, bf16[3,256,128]{2,1,0:T(8,128)(2,1)} %constant.9.clone.refs_2_.refs_6_.refs_8_.refs_7_, f32[2,16,8,256]{3,2,1,0:T(8,128)} %refs_4_.5), custom_call_target="tpu_custom_call" | custom-call | flops 50331648 | bytes 1048576 | tf_op jit(solution)/shard_map/pallas_call | solution.py:379
  2.8 20.3 %all_to_all.40 = f32[32,1,1152]{2,1,0:T(1,128)S(1)} all-to-all(f32[32,1,1152]{2,1,0:T(1,128)} %bitcast.39), channel_id=1, replica_groups=mesh['macro'=16,'krow'=32] {'krow'}, dimensions={0} | all-to-all | bytes 294912 | tf_op jit(solution)/shard_map/all_to_all | solution.py:394
  23.2 1.1 shard_map.105
  24.3 4.5 %all-to-all-start.1 = ((f32[32,1,1024]{2,1,0:T(1,128)}), f32[32,1,1024]{2,1,0:T(1,128)S(1)}, u32[]{:S(2)}, u32[]{:S(2)}) async-start(f32[32,1,1024]{2,1,0:T(1,128)} %bitcast.3), calls=%async_computation.1 | async-start | bytes 262144 | tf_op jit(solution)/shard_map/all_to_all | solution.py:394
  28.8 9.0 %collective-permute-start = (f32[1,128]{1,0:T(1,128)S(1)}, f32[1,128]{1,0:T(1,128)S(1)}, u32[]{:S(2)}, u32[]{:S(2)}) collective-permute-start(f32[1,128]{1,0:T(1,128)S(1)} %get-tuple-element.19), channel_id=1, source_target_pairs={{0,256},{32,288},{64,320},{96,352},{128,384},{160,416},{192,448},{... | collective-permute-start | bytes 1544 | tf_op jit(solution)/shard_map/ppermute | solution.py:454
  37.9 1.1 collective-permute-done.refs_4_
  39.0 0.5 shard_map.107
  39.6 16.8 %all_to_all.41 = f32[32,1,1152]{2,1,0:T(1,128)S(1)} all-to-all(f32[32,1,1152]{2,1,0:T(1,128)S(1)} %bitcast.34), channel_id=1, replica_groups=mesh['macro'=16,'krow'=32] {'krow'}, dimensions={0} | all-to-all | bytes 294912 | tf_op jit(solution)/shard_map/all_to_all | solution.py:394
  56.4 1.1 shard_map.108
  57.5 4.3 %all-to-all-start.3 = ((f32[32,1,1024]{2,1,0:T(1,128)}), f32[32,1,1024]{2,1,0:T(1,128)S(1)}, u32[]{:S(2)}, u32[]{:S(2)}) async-start(f32[32,1,1024]{2,1,0:T(1,128)} %bitcast.8), calls=%async_computation.3 | async-start | bytes 262144 | tf_op jit(solution)/shard_map/all_to_all | solution.py:394
  61.8 3.4 %collective-permute-start.1 = (f32[1,128]{1,0:T(1,128)S(1)}, f32[1,128]{1,0:T(1,128)S(1)}, u32[]{:S(2)}, u32[]{:S(2)}) collective-permute-start(f32[1,128]{1,0:T(1,128)S(1)} %get-tuple-element.23.refs_5_), channel_id=1, source_target_pairs={{0,256},{32,288},{64,320},{96,352},{128,384},{160,416},{192,448},{... | collective-permute-start | bytes 1544 | tf_op jit(solution)/shard_map/ppermute | solution.py:454
  65.2 1.3 collective-permute-done.1.refs_6_
  66.5 5.1 %all-to-all-done.3 = f32[32,1,1024]{2,1,0:T(1,128)S(1)} async-done(((f32[32,1,1024]{2,1,0:T(1,128)}), f32[32,1,1024]{2,1,0:T(1,128)S(1)}, u32[]{:S(2)}, u32[]{:S(2)}) %all-to-all-start.3) | async-done | bytes 131104 | tf_op jit(solution)/shard_map/all_to_all | solution.py:394
  71.6 0.5 shard_map.109
  72.1 14.0 %all_to_all.42 = f32[32,1,1152]{2,1,0:T(1,128)S(1)} all-to-all(f32[32,1,1152]{2,1,0:T(1,128)S(1)} %bitcast.35), channel_id=1, replica_groups=mesh['macro'=16,'krow'=32] {'krow'}, dimensions={0} | all-to-all | bytes 294912 | tf_op jit(solution)/shard_map/all_to_all | solution.py:394
  86.1 0.4 shard_map.110
  86.5 13.8 %all_to_all.43 = f32[32,1,1024]{2,1,0:T(1,128)S(1)} all-to-all(f32[32,1,1024]{2,1,0:T(1,128)S(1)} %bitcast.37), channel_id=1, replica_groups=mesh['macro'=16,'krow'=32] {'krow'}, dimensions={0} | all-to-all | bytes 262144 | tf_op jit(solution)/shard_map/all_to_all | solution.py:394
  100.3 0.6 shard_map.111
  100.9 14.0 %all_to_all.44 = f32[32,1,1152]{2,1,0:T(1,128)S(1)} all-to-all(f32[32,1,1152]{2,1,0:T(1,128)S(1)} %bitcast.36), channel_id=1, replica_groups=mesh['macro'=16,'krow'=32] {'krow'}, dimensions={0} | all-to-all | bytes 294912 | tf_op jit(solution)/shard_map/all_to_all | solution.py:394
  115.0 1.3 collective-permute-start.2
  116.3 0.5 shard_map.112
  116.8 0.8 collective-permute-done.2.row_ref
  117.6 19.6 %all_to_all.45 = f32[32,1,1152]{2,1,0:T(1,128)S(1)} all-to-all(f32[32,1,1152]{2,1,0:T(1,128)S(1)} %bitcast.27), channel_id=1, replica_groups=mesh['macro'=16,'krow'=32] {'krow'}, dimensions={0} | all-to-all | bytes 294912 | tf_op jit(solution)/shard_map/all_to_all | solution.py:394
  137.2 1.0 shard_map.115
  (22 shorter events, 0.2 us)
Async XLA Ops:
  0.6 22.5 %copy-start.2 = (bf16[3,2,128,256]{3,2,1,0:T(8,128)(2,1)S(1)}, bf16[3,2,128,256]{3,2,1,0:T(8,128)(2,1)}, u32[]{:S(2)}) copy-start(bf16[3,2,128,256]{3,2,1,0:T(8,128)(2,1)} %constant.10.clone.left_ref) | copy-start | bytes 1179652
  2.8 20.4 %copy-start.4 = (f32[2,256,128]{2,1,0:T(8,128)S(1)}, f32[2,256,128]{2,1,0:T(8,128)}, u32[]{:S(2)}) copy-start(f32[2,256,128]{2,1,0:T(8,128)} %constant.11.clone.spectrum_ref) | copy-start | bytes 786436
  23.1 14.6 %copy-start.6 = (f32[4,8,256]{2,1,0:T(8,128)S(1)}, f32[4,8,256]{2,1,0:T(8,128)}, u32[]{:S(2)}) copy-start(f32[4,8,256]{2,1,0:T(8,128)} %energies_ref.1) | copy-start | bytes 98308
  23.1 14.6 %copy-start.7 = (f32[3,2]{0,1:T(2,128)S(1)}, f32[3,2]{0,1:T(2,128)}, u32[]{:S(2)}) copy-start(f32[3,2]{0,1:T(2,128)} %param.13) | copy-start | bytes 76
  23.1 14.6 %copy-start.8 = (f32[1,2]{1,0:T(1,128)S(1)}, f32[1,2]{1,0:T(1,128)}, u32[]{:S(2)}) copy-start(f32[1,2]{1,0:T(1,128)} %emitted_ref.1) | copy-start | bytes 28
  23.2 15.9 %copy-start.1 = (f32[2,16,8,256]{3,2,1,0:T(8,128)S(1)}, f32[2,16,8,256]{3,2,1,0:T(8,128)}, u32[]{:S(2)}) copy-start(f32[2,16,8,256]{3,2,1,0:T(8,128)} %refs_4_.5) | copy-start | bytes 786436
  23.2 15.9 %copy-start.3 = (bf16[3,256,128]{2,1,0:T(8,128)(2,1)S(1)}, bf16[3,256,128]{2,1,0:T(8,128)(2,1)}, u32[]{:S(2)}) copy-start(bf16[3,256,128]{2,1,0:T(8,128)(2,1)} %constant.9.clone.refs_2_.refs_6_.refs_8_.refs_7_) | copy-start | bytes 589828
  23.2 15.9 %copy-start.5 = (f32[1,16,8,256]{3,2,1,0:T(8,128)S(1)}, f32[1,16,8,256]{3,2,1,0:T(8,128)}, u32[]{:S(2)}) copy-start(f32[1,16,8,256]{3,2,1,0:T(8,128)} %param.9) | copy-start | bytes 393220
  24.3 14.8 %copy-start = (bf16[3,256,256]{2,1,0:T(8,128)(2,1)S(1)}, bf16[3,256,256]{2,1,0:T(8,128)(2,1)}, u32[]{:S(2)}) copy-start(bf16[3,256,256]{2,1,0:T(8,128)(2,1)} %constant.8.clone.refs_1_.refs_5_.refs_7_.refs_6_) | copy-start | bytes 1179652
  24.3 14.7 %all-to-all-start.1 = ((f32[32,1,1024]{2,1,0:T(1,128)}), f32[32,1,1024]{2,1,0:T(1,128)S(1)}, u32[]{:S(2)}, u32[]{:S(2)}) async-start(f32[32,1,1024]{2,1,0:T(1,128)} %bitcast.3), calls=%async_computation.1 | async-start | bytes 262144 | tf_op jit(solution)/shard_map/all_to_all | solution.py:394
  28.8 10.2 %collective-permute-start = (f32[1,128]{1,0:T(1,128)S(1)}, f32[1,128]{1,0:T(1,128)S(1)}, u32[]{:S(2)}, u32[]{:S(2)}) collective-permute-start(f32[1,128]{1,0:T(1,128)S(1)} %get-tuple-element.19), channel_id=1, source_target_pairs={{0,256},{32,288},{64,320},{96,352},{128,384},{160,416},{192,448},{... | collective-permute-start | bytes 1544 | tf_op jit(solution)/shard_map/ppermute | solution.py:454
  57.5 14.1 %all-to-all-start.3 = ((f32[32,1,1024]{2,1,0:T(1,128)}), f32[32,1,1024]{2,1,0:T(1,128)S(1)}, u32[]{:S(2)}, u32[]{:S(2)}) async-start(f32[32,1,1024]{2,1,0:T(1,128)} %bitcast.8), calls=%async_computation.3 | async-start | bytes 262144 | tf_op jit(solution)/shard_map/all_to_all | solution.py:394
  61.8 4.7 %collective-permute-start.1 = (f32[1,128]{1,0:T(1,128)S(1)}, f32[1,128]{1,0:T(1,128)S(1)}, u32[]{:S(2)}, u32[]{:S(2)}) collective-permute-start(f32[1,128]{1,0:T(1,128)S(1)} %get-tuple-element.23.refs_5_), channel_id=1, source_target_pairs={{0,256},{32,288},{64,320},{96,352},{128,384},{160,416},{192,448},{... | collective-permute-start | bytes 1544 | tf_op jit(solution)/shard_map/ppermute | solution.py:454
  115.0 2.6 %collective-permute-start.2 = (f32[1,128]{1,0:T(1,128)S(1)}, f32[1,128]{1,0:T(1,128)S(1)}, u32[]{:S(2)}, u32[]{:S(2)}) collective-permute-start(f32[1,128]{1,0:T(1,128)S(1)} %shard_map.113), channel_id=1, source_target_pairs={{0,256},{32,288},{64,320},{96,352},{128,384},{160,416},{192,448},{... | collective-permute-start | bytes 1544 | tf_op jit(solution)/shard_map/ppermute | solution.py:439

commit v15 on v14

--- a/solution.py
+++ b/solution.py
@@ -277,6 +277,30 @@
             out_ref[c, :, lanes] = base + (time_step / 6.0) * rate
 
 
+def local_kernel(section, *refs):
+    density_ref, state_ref, fields_ref, momentum_ref, *sums_ref, out_ref = refs
+    potential = []
+    for i in range(2):
+        lane = 3 * i + section
+        value = fields_ref[BANDS, 0:1, lane : lane + 1]
+        if section > 0:
+            scale = time_step * 0.5 * -coupling / GRID
+            value = value + scale * sums_ref[0][:, 2 + i : 3 + i]
+        potential.append(value)
+    for part in range(2):
+        lanes = slice(part * LANES, (part + 1) * LANES)
+        rho = [state_ref[c, :, lanes] for c in range(CHANNELS)]
+        hamilton = []
+        for c in range(CHANNELS):
+            value = potential[0] * momentum_ref[0, c, :, lanes]
+            value = value + potential[1] * momentum_ref[1, c, :, lanes]
+            hamilton.append(value + fields_ref[c, :, lanes] if c < BANDS else value)
+        rates = commute(hamilton, rho)
+        for c in range(CHANNELS):
+            rate = rates[c] if c < BANDS else rates[c] - dephasing * rho[c]
+            out_ref[c, :, lanes] = density_ref[c, :, lanes] + (time_step * 0.5) * rate
+
+
 def last_column_kernel(y_ref, left_ref, spectrum_ref, *refs):
     *state_refs, out_ref, base_ref = refs
     column_kernel(False, y_ref, left_ref, spectrum_ref, out_ref)
@@ -286,10 +310,10 @@
 def state_kernel(section, *refs):
     refs = list(refs)
     back_ref = refs.pop(0)
-    state_refs = [refs.pop(0) for _ in range((1, 2, 2, 2)[section])]
+    state_refs = [refs.pop(0) for _ in range(2)]
     density_ref, state_ref = state_refs[0], state_refs[-1]
     fields_ref, momentum_ref = refs.pop(0), refs.pop(0)
-    sums_ref = refs.pop(0) if section in (1, 2) else None
+    sums_ref = refs.pop(0) if section == 2 else None
     permuted_ref = refs.pop(0) if section in (0, 1) else None
     earlier_refs = [refs.pop(0) for _ in range(2)] if section == 3 else None
     wide_ref, narrow_ref = refs.pop(0), refs.pop(0)
@@ -304,9 +328,9 @@
 
     if section == 3:
         arrived = rows_of(back_ref)
-    upstream = None if section == 0 else arrived if section == 3 else sums_ref[...]
+    upstream = arrived if section == 3 else sums_ref[...] if section == 2 else None
     potential = []
-    for i in range(2):
+    for i in range(2 if section > 1 else 0):
         lane = 3 * i + drive_row
         value = fields_ref[BANDS, 0:1, lane : lane + 1] if section < 3 else 0.0
         if section > 0:
@@ -328,15 +352,16 @@
         hamilton = []
         for c in range(CHANNELS):
             value = sigma[part][c * ROWS : (c + 1) * ROWS]
-            value = value + potential[0] * momentum_ref[0, c, :, lanes]
-            value = value + potential[1] * momentum_ref[1, c, :, lanes]
-            if c < BANDS and section < 3:
+            if section > 1:
+                value = value + potential[0] * momentum_ref[0, c, :, lanes]
+                value = value + potential[1] * momentum_ref[1, c, :, lanes]
+            if c < BANDS and section == 2:
                 value = value + fields_ref[c, :, lanes]
             hamilton.append(value)
         rates = commute(hamilton, rho)
         for c in range(CHANNELS):
             if section < 3:
-                rate = rates[c] if c < BANDS else rates[c] - dephasing * rho[c]
+                rate = rates[c] if c < BANDS or section < 2 else rates[c] - dephasing * rho[c]
                 new = density_ref[c, :, lanes] + (time_step * next_fraction) * rate
                 next_ref[c, :, lanes] = new
                 momentum = [momentum_ref[i, c, :, lanes] for i in range(2)]
@@ -454,10 +479,14 @@
             extra = extra + [lax.ppermute(total, ("macro", "krow"), exchange)]
         back = swap(mixed)
         body = functools.partial(state_kernel, section)
-        used = states[:1] if section == 0 else [density, states[-1]]
+        used = [density, states[-1]]
+        if section < 2:
+            local = functools.partial(local_kernel, section)
+            given = [density, states[-1], fields, momentum] + sums
+            used = [*call(local, [state_shape], *given), states[-1]]
         if section == 3:
             used = [base, states[-1]]
-        extra = sums if section == 3 else extra
+        extra = sums if section == 3 else extra[section == 1 :]
         args = [back, *used, fields, momentum, *extra, wide, narrow]
         if section < 3:
             out, state = call(body, [carrying, state_shape], *args)

time: 139 us -> 139 us (level)
    pallas_call x12 -> x14, Pallas kernels: 8.04 us -> 8.48 us  [call(): pl.pallas_call(body, out_shape=shapes, in_specs=[hbm if n in in_hbm else...]
  transfers between devices with their start and end apart: 5 -> 5, of which waited for: 4 -> 4; matrix products, arithmetic and copies ran while one was open for 0% -> 0% of each run, Pallas kernels for 0% -> 1%
where the time goes in v15:
time: 139 us; the launch traced here: 138 us
  blocking collectives  98.3 us (71%)
  starting transfers between devices  22.3 us (16%)
  Pallas kernels  8.48 us (6%)
  waiting for transfers between devices  8.19 us (6%)
    all_to_all x6, blocking collectives, swap(): return lax.all_to_all(blocks, 'krow', 0, 0, tiled=True).reshape(x.shape)  98.3 us
    ppermute x2, starting transfers between devices, per_device(): extra = extra + [lax.ppermute(total, ('macro', 'krow'), exchange)]  12.2 us
    all_to_all x2, starting transfers between devices, swap(): return lax.all_to_all(blocks, 'krow', 0, 0, tiled=True).reshape(x.shape)  8.78 us
    pallas_call x14, Pallas kernels, call(): pl.pallas_call(body, out_shape=shapes, in_specs=[hbm if n in in_hbm else...  8.48 us
    all_to_all x2, waiting for transfers between devices, swap(): return lax.all_to_all(blocks, 'krow', 0, 0, tiled=True).reshape(x.shape)  5.37 us
  transfers between devices with their start and end apart: 5, of which 4 were waited for; matrix products, arithmetic and copies ran while one was open for 0% of the time, Pallas kernels for 1%

profile of v15, /device:TPU:8, one launch (start us, length us, event | category | flops | bytes accessed | tf_op | source)
XLA Modules:
  0.0 138.1 jit_solution(11812759749792733012)
XLA Ops:
  0.6 2.1 %shard_map.104 = f32[288,128]{1,0:T(8,128)} custom-call(f32[16,8,256]{2,1,0:T(8,128)} %bitcast.19, bf16[3,256,256]{2,1,0:T(8,128)(2,1)} %constant.8.clone.refs_1_.refs_6_.refs_7_, bf16[3,256,128]{2,1,0:T(8,128)(2,1)} %constant.9.clone.refs_2_.refs_7_.refs_8_, f32[2,16,8,256]{3,2,1,0:T(8,128)} %refs_4_.7), custom_call_target="tpu_custom_call" | custom-call | flops 50331648 | bytes 1048576 | tf_op jit(solution)/shard_map/pallas_call | solution.py:404
  2.8 20.3 %all_to_all.40 = f32[32,1,1152]{2,1,0:T(1,128)S(1)} all-to-all(f32[32,1,1152]{2,1,0:T(1,128)} %bitcast.41), channel_id=1, replica_groups=mesh['macro'=16,'krow'=32] {'krow'}, dimensions={0} | all-to-all | bytes 294912 | tf_op jit(solution)/shard_map/all_to_all | solution.py:419
  23.1 1.1 shard_map.105
  24.2 4.5 %all-to-all-start.1 = ((f32[32,1,1024]{2,1,0:T(1,128)}), f32[32,1,1024]{2,1,0:T(1,128)S(1)}, u32[]{:S(2)}, u32[]{:S(2)}) async-start(f32[32,1,1024]{2,1,0:T(1,128)} %bitcast.3), calls=%async_computation.1 | async-start | bytes 262144 | tf_op jit(solution)/shard_map/all_to_all | solution.py:419
  28.9 9.1 %collective-permute-start = (f32[1,128]{1,0:T(1,128)S(1)}, f32[1,128]{1,0:T(1,128)S(1)}, u32[]{:S(2)}, u32[]{:S(2)}) collective-permute-start(f32[1,128]{1,0:T(1,128)S(1)} %get-tuple-element.19), channel_id=1, source_target_pairs={{0,256},{32,288},{64,320},{96,352},{128,384},{160,416},{192,448},{... | collective-permute-start | bytes 1544 | tf_op jit(solution)/shard_map/ppermute | solution.py:479
  38.2 1.1 collective-permute-done.refs_5_
  39.3 0.5 shard_map.108
  39.8 16.8 %all_to_all.41 = f32[32,1,1152]{2,1,0:T(1,128)S(1)} all-to-all(f32[32,1,1152]{2,1,0:T(1,128)S(1)} %bitcast.36), channel_id=1, replica_groups=mesh['macro'=16,'krow'=32] {'krow'}, dimensions={0} | all-to-all | bytes 294912 | tf_op jit(solution)/shard_map/all_to_all | solution.py:419
  56.7 1.1 shard_map.109
  57.8 4.3 %all-to-all-start.3 = ((f32[32,1,1024]{2,1,0:T(1,128)}), f32[32,1,1024]{2,1,0:T(1,128)S(1)}, u32[]{:S(2)}, u32[]{:S(2)}) async-start(f32[32,1,1024]{2,1,0:T(1,128)} %bitcast.8), calls=%async_computation.3 | async-start | bytes 262144 | tf_op jit(solution)/shard_map/all_to_all | solution.py:419
  62.0 3.1 %collective-permute-start.1 = (f32[1,128]{1,0:T(1,128)S(1)}, f32[1,128]{1,0:T(1,128)S(1)}, u32[]{:S(2)}, u32[]{:S(2)}) collective-permute-start(f32[1,128]{1,0:T(1,128)S(1)} %get-tuple-element.23.refs_4_.refs_5_), channel_id=1, source_target_pairs={{0,256},{32,288},{64,320},{96,352},{128,384},{160,416},{192,448},{... | collective-permute-start | bytes 1544 | tf_op jit(solution)/shard_map/ppermute | solution.py:479
  65.5 1.0 collective-permute-done.1.refs_5_
  66.5 5.4 %all-to-all-done.3 = f32[32,1,1024]{2,1,0:T(1,128)S(1)} async-done(((f32[32,1,1024]{2,1,0:T(1,128)}), f32[32,1,1024]{2,1,0:T(1,128)S(1)}, u32[]{:S(2)}, u32[]{:S(2)}) %all-to-all-start.3) | async-done | bytes 131104 | tf_op jit(solution)/shard_map/all_to_all | solution.py:419
  71.8 0.5 shard_map.111
  72.4 13.9 %all_to_all.42 = f32[32,1,1152]{2,1,0:T(1,128)S(1)} all-to-all(f32[32,1,1152]{2,1,0:T(1,128)S(1)} %bitcast.37), channel_id=1, replica_groups=mesh['macro'=16,'krow'=32] {'krow'}, dimensions={0} | all-to-all | bytes 294912 | tf_op jit(solution)/shard_map/all_to_all | solution.py:419
  86.3 0.4 shard_map.112
  86.7 13.9 %all_to_all.43 = f32[32,1,1024]{2,1,0:T(1,128)S(1)} all-to-all(f32[32,1,1024]{2,1,0:T(1,128)S(1)} %bitcast.39), channel_id=1, replica_groups=mesh['macro'=16,'krow'=32] {'krow'}, dimensions={0} | all-to-all | bytes 262144 | tf_op jit(solution)/shard_map/all_to_all | solution.py:419
  100.6 0.6 shard_map.113
  101.2 14.0 %all_to_all.44 = f32[32,1,1152]{2,1,0:T(1,128)S(1)} all-to-all(f32[32,1,1152]{2,1,0:T(1,128)S(1)} %bitcast.38), channel_id=1, replica_groups=mesh['macro'=16,'krow'=32] {'krow'}, dimensions={0} | all-to-all | bytes 294912 | tf_op jit(solution)/shard_map/all_to_all | solution.py:419
  115.2 1.3 collective-permute-start.2
  116.5 0.5 shard_map.114
  117.0 0.8 collective-permute-done.2.row_ref
  117.8 19.3 %all_to_all.45 = f32[32,1,1152]{2,1,0:T(1,128)S(1)} all-to-all(f32[32,1,1152]{2,1,0:T(1,128)S(1)} %bitcast.29), channel_id=1, replica_groups=mesh['macro'=16,'krow'=32] {'krow'}, dimensions={0} | all-to-all | bytes 294912 | tf_op jit(solution)/shard_map/all_to_all | solution.py:419
  137.1 1.0 shard_map.117
  (24 shorter events, 0.7 us)
Async XLA Ops:
  0.6 22.5 %copy-start.3 = (bf16[3,2,128,256]{3,2,1,0:T(8,128)(2,1)S(1)}, bf16[3,2,128,256]{3,2,1,0:T(8,128)(2,1)}, u32[]{:S(2)}) copy-start(bf16[3,2,128,256]{3,2,1,0:T(8,128)(2,1)} %constant.10.clone.left_ref) | copy-start | bytes 1179652
  2.8 20.4 %copy-start.5 = (f32[2,256,128]{2,1,0:T(8,128)S(1)}, f32[2,256,128]{2,1,0:T(8,128)}, u32[]{:S(2)}) copy-start(f32[2,256,128]{2,1,0:T(8,128)} %constant.11.clone.spectrum_ref) | copy-start | bytes 786436
  23.1 5.6 %copy-start.6 = (f32[4,8,256]{2,1,0:T(8,128)S(1)}, f32[4,8,256]{2,1,0:T(8,128)}, u32[]{:S(2)}) copy-start(f32[4,8,256]{2,1,0:T(8,128)} %energies_ref.1) | copy-start | bytes 98308
  24.2 13.8 %copy-start = (f32[2,16,8,256]{3,2,1,0:T(8,128)S(1)}, f32[2,16,8,256]{3,2,1,0:T(8,128)}, u32[]{:S(2)}) copy-start(f32[2,16,8,256]{3,2,1,0:T(8,128)} %refs_4_.7) | copy-start | bytes 786436
  24.2 4.5 %copy-start.7 = (f32[3,2]{0,1:T(2,128)S(1)}, f32[3,2]{0,1:T(2,128)}, u32[]{:S(2)}) copy-start(f32[3,2]{0,1:T(2,128)} %param.13) | copy-start | bytes 76
  24.2 4.5 %copy-start.8 = (f32[1,2]{1,0:T(1,128)S(1)}, f32[1,2]{1,0:T(1,128)}, u32[]{:S(2)}) copy-start(f32[1,2]{1,0:T(1,128)} %emitted_ref.1) | copy-start | bytes 28
  24.2 15.1 %all-to-all-start.1 = ((f32[32,1,1024]{2,1,0:T(1,128)}), f32[32,1,1024]{2,1,0:T(1,128)S(1)}, u32[]{:S(2)}, u32[]{:S(2)}) async-start(f32[32,1,1024]{2,1,0:T(1,128)} %bitcast.3), calls=%async_computation.1 | async-start | bytes 262144 | tf_op jit(solution)/shard_map/all_to_all | solution.py:419
  28.7 9.3 %copy-start.2 = (f32[1,16,8,256]{3,2,1,0:T(8,128)S(1)}, f32[1,16,8,256]{3,2,1,0:T(8,128)}, u32[]{:S(2)}) copy-start(f32[1,16,8,256]{3,2,1,0:T(8,128)} %param.9) | copy-start | bytes 393220
  28.9 10.4 %copy-start.1 = (bf16[3,256,256]{2,1,0:T(8,128)(2,1)S(1)}, bf16[3,256,256]{2,1,0:T(8,128)(2,1)}, u32[]{:S(2)}) copy-start(bf16[3,256,256]{2,1,0:T(8,128)(2,1)} %constant.8.clone.refs_1_.refs_6_.refs_7_) | copy-start | bytes 1179652
  28.9 10.4 %copy-start.4 = (bf16[3,256,128]{2,1,0:T(8,128)(2,1)S(1)}, bf16[3,256,128]{2,1,0:T(8,128)(2,1)}, u32[]{:S(2)}) copy-start(bf16[3,256,128]{2,1,0:T(8,128)(2,1)} %constant.9.clone.refs_2_.refs_7_.refs_8_) | copy-start | bytes 589828
  28.9 10.4 %collective-permute-start = (f32[1,128]{1,0:T(1,128)S(1)}, f32[1,128]{1,0:T(1,128)S(1)}, u32[]{:S(2)}, u32[]{:S(2)}) collective-permute-start(f32[1,128]{1,0:T(1,128)S(1)} %get-tuple-element.19), channel_id=1, source_target_pairs={{0,256},{32,288},{64,320},{96,352},{128,384},{160,416},{192,448},{... | collective-permute-start | bytes 1544 | tf_op jit(solution)/shard_map/ppermute | solution.py:479
  57.8 14.1 %all-to-all-start.3 = ((f32[32,1,1024]{2,1,0:T(1,128)}), f32[32,1,1024]{2,1,0:T(1,128)S(1)}, u32[]{:S(2)}, u32[]{:S(2)}) async-start(f32[32,1,1024]{2,1,0:T(1,128)} %bitcast.8), calls=%async_computation.3 | async-start | bytes 262144 | tf_op jit(solution)/shard_map/all_to_all | solution.py:419
  62.0 4.4 %collective-permute-start.1 = (f32[1,128]{1,0:T(1,128)S(1)}, f32[1,128]{1,0:T(1,128)S(1)}, u32[]{:S(2)}, u32[]{:S(2)}) collective-permute-start(f32[1,128]{1,0:T(1,128)S(1)} %get-tuple-element.23.refs_4_.refs_5_), channel_id=1, source_target_pairs={{0,256},{32,288},{64,320},{96,352},{128,384},{160,416},{192,448},{... | collective-permute-start | bytes 1544 | tf_op jit(solution)/shard_map/ppermute | solution.py:479
  115.2 2.6 %collective-permute-start.2 = (f32[1,128]{1,0:T(1,128)S(1)}, f32[1,128]{1,0:T(1,128)S(1)}, u32[]{:S(2)}, u32[]{:S(2)}) collective-permute-start(f32[1,128]{1,0:T(1,128)S(1)} %shard_map.115), channel_id=1, source_target_pairs={{0,256},{32,288},{64,320},{96,352},{128,384},{160,416},{192,448},{... | collective-permute-start | bytes 1544 | tf_op jit(solution)/shard_map/ppermute | solution.py:464

commit v16 on v14

--- a/solution.py
+++ b/solution.py
@@ -138,7 +138,7 @@
 
 
 def first_kernel(*refs):
-    sources, out_ref, fetched, sems = refs[:4], refs[4], refs[5:9], refs[9]
+    sources, (out_ref, fields_ref), fetched, sems = refs[:7], refs[7:9], refs[9:16], refs[16]
     copies = [
         pltpu.make_async_copy(
             source.at[pl.ds(0, 2)] if n in (1, 2) else source, target, sems.at[n]
@@ -147,7 +147,7 @@
     ]
     for copy in copies:
         copy.start()
-    density_ref, wide_ref, narrow_ref, momentum_ref = fetched
+    density_ref, wide_ref, narrow_ref, momentum_ref, energies_ref, emitted_ref, drive_ref = fetched
     for copy in copies[:3]:
         copy.wait()
     send_rows(density_ref[...].reshape(CHANNELS * ROWS, GRID), wide_ref, narrow_ref, out_ref)
@@ -160,9 +160,6 @@
             momentum = [momentum_ref[i, c, :, lanes] for i in range(2)]
             add_currents(currents, 0, c, momentum, density_ref[c, :, lanes])
     send_row(currents_row(currents), out_ref)
-
-
-def pack_kernel(energies_ref, emitted_ref, drive_ref, fields_ref):
     fields_ref[:BANDS] = energies_ref[...]
     lane = lax.broadcasted_iota(jnp.int32, (1, LANES), 1)
     row = jnp.zeros((1, LANES), jnp.float32)
@@ -408,24 +405,29 @@
         if m <= m ^ shift
     ]
 
-    (out,) = call(
+    out, fields = call(
         first_kernel,
-        [carrying],
+        [carrying, (BANDS + 1, ROWS, GRID)],
         density,
         wide,
         narrow,
         momentum,
-        in_hbm=range(4),
+        energies,
+        emitted,
+        drive,
+        in_hbm=range(7),
         vmem_mib=58,
         scratch=[
             pltpu.VMEM(state_shape, jnp.float32),
             pltpu.VMEM((2, GRID, GRID), jnp.bfloat16),
             pltpu.VMEM((2, GRID, LANES), jnp.bfloat16),
             pltpu.VMEM(momentum.shape, jnp.float32),
-            pltpu.SemaphoreType.DMA((4,)),
+            pltpu.VMEM(energies.shape, jnp.float32),
+            pltpu.VMEM(emitted.shape, jnp.float32),
+            pltpu.VMEM(drive.shape, jnp.float32),
+            pltpu.SemaphoreType.DMA((7,)),
         ],
     )
-    (fields,) = call(pack_kernel, [(BANDS + 1, ROWS, GRID)], energies, emitted, drive)
     row = (1, LANES)
     states = [density]
     sums = []

time: 139 us -> 139 us (level)
    pallas_call x12 -> x11, Pallas kernels: 8.04 us -> 7.94 us  [call(): pl.pallas_call(body, out_shape=shapes, in_specs=[hbm if n in in_hbm else...]
where the time goes in v16:
time: 139 us; the launch traced here: 138 us
  blocking collectives  98.7 us (71%)
  starting transfers between devices  22.4 us (16%)
  waiting for transfers between devices  8.43 us (6%)
  Pallas kernels  7.94 us (6%)
    all_to_all x6, blocking collectives, swap(): return lax.all_to_all(blocks, 'krow', 0, 0, tiled=True).reshape(x.shape)  98.7 us
    ppermute x2, starting transfers between devices, per_device(): extra = extra + [lax.ppermute(total, ('macro', 'krow'), exchange)]  12.4 us
    all_to_all x2, starting transfers between devices, swap(): return lax.all_to_all(blocks, 'krow', 0, 0, tiled=True).reshape(x.shape)  8.79 us
    pallas_call x11, Pallas kernels, call(): pl.pallas_call(body, out_shape=shapes, in_specs=[hbm if n in in_hbm else...  7.94 us
    all_to_all x2, waiting for transfers between devices, swap(): return lax.all_to_all(blocks, 'krow', 0, 0, tiled=True).reshape(x.shape)  5.1 us
  transfers between devices with their start and end apart: 5, of which 4 were waited for; matrix products, arithmetic and copies ran while one was open for 0% of the time, Pallas kernels for 0%

profile of v16, /device:TPU:8, one launch (start us, length us, event | category | flops | bytes accessed | tf_op | source)
XLA Modules:
  0.0 138.3 jit_solution(1334620422868429689)
XLA Ops:
  0.6 2.2 %shard_map.104 = (f32[288,128]{1,0:T(8,128)}, f32[5,8,256]{2,1,0:T(8,128)}) custom-call(f32[16,8,256]{2,1,0:T(8,128)} %bitcast.19, bf16[3,256,256]{2,1,0:T(8,128)(2,1)} %constant.8.clone.refs_1_.refs_5_.refs_7_.refs_6_, bf16[3,256,128]{2,1,0:T(8,128)(2,1)} %constant.9.clone.refs_2_.refs_6_.refs_8_.refs_7_, f32[2,16,8,256]{3,2,1,0:T(8,128)} %refs_4_.7, ...), custom_call_target="tpu_custom_call" | custom-call | flops 50331648 | bytes 1048576 | tf_op jit(solution)/shard_map/pallas_call | solution.py:376
  2.8 20.3 %all_to_all.40 = f32[32,1,1152]{2,1,0:T(1,128)S(1)} all-to-all(f32[32,1,1152]{2,1,0:T(1,128)} %bitcast.38), channel_id=1, replica_groups=mesh['macro'=16,'krow'=32] {'krow'}, dimensions={0} | all-to-all | bytes 294912 | tf_op jit(solution)/shard_map/all_to_all | solution.py:391
  23.2 1.1 shard_map.105
  24.3 4.5 %all-to-all-start.1 = ((f32[32,1,1024]{2,1,0:T(1,128)}), f32[32,1,1024]{2,1,0:T(1,128)S(1)}, u32[]{:S(2)}, u32[]{:S(2)}) async-start(f32[32,1,1024]{2,1,0:T(1,128)} %bitcast.4), calls=%async_computation.1 | async-start | bytes 262144 | tf_op jit(solution)/shard_map/all_to_all | solution.py:391
  28.8 9.0 %collective-permute-start = (f32[1,128]{1,0:T(1,128)S(1)}, f32[1,128]{1,0:T(1,128)S(1)}, u32[]{:S(2)}, u32[]{:S(2)}) collective-permute-start(f32[1,128]{1,0:T(1,128)S(1)} %get-tuple-element.23), channel_id=1, source_target_pairs={{0,256},{32,288},{64,320},{96,352},{128,384},{160,416},{192,448},{... | collective-permute-start | bytes 1544 | tf_op jit(solution)/shard_map/ppermute | solution.py:456
  37.8 1.3 collective-permute-done.refs_4_
  39.1 0.5 shard_map.106
  39.6 16.8 %all_to_all.41 = f32[32,1,1152]{2,1,0:T(1,128)S(1)} all-to-all(f32[32,1,1152]{2,1,0:T(1,128)S(1)} %bitcast.34), channel_id=1, replica_groups=mesh['macro'=16,'krow'=32] {'krow'}, dimensions={0} | all-to-all | bytes 294912 | tf_op jit(solution)/shard_map/all_to_all | solution.py:391
  56.5 1.1 shard_map.107
  57.6 4.3 %all-to-all-start.3 = ((f32[32,1,1024]{2,1,0:T(1,128)}), f32[32,1,1024]{2,1,0:T(1,128)S(1)}, u32[]{:S(2)}, u32[]{:S(2)}) async-start(f32[32,1,1024]{2,1,0:T(1,128)} %bitcast.8), calls=%async_computation.3 | async-start | bytes 262144 | tf_op jit(solution)/shard_map/all_to_all | solution.py:391
  61.9 3.4 %collective-permute-start.1 = (f32[1,128]{1,0:T(1,128)S(1)}, f32[1,128]{1,0:T(1,128)S(1)}, u32[]{:S(2)}, u32[]{:S(2)}) collective-permute-start(f32[1,128]{1,0:T(1,128)S(1)} %get-tuple-element.27.refs_5_), channel_id=1, source_target_pairs={{0,256},{32,288},{64,320},{96,352},{128,384},{160,416},{192,448},{... | collective-permute-start | bytes 1544 | tf_op jit(solution)/shard_map/ppermute | solution.py:456
  65.3 1.3 collective-permute-done.1.refs_6_
  66.5 5.1 %all-to-all-done.3 = f32[32,1,1024]{2,1,0:T(1,128)S(1)} async-done(((f32[32,1,1024]{2,1,0:T(1,128)}), f32[32,1,1024]{2,1,0:T(1,128)S(1)}, u32[]{:S(2)}, u32[]{:S(2)}) %all-to-all-start.3) | async-done | bytes 131104 | tf_op jit(solution)/shard_map/all_to_all | solution.py:391
  71.6 0.5 shard_map.108
  72.2 14.0 %all_to_all.42 = f32[32,1,1152]{2,1,0:T(1,128)S(1)} all-to-all(f32[32,1,1152]{2,1,0:T(1,128)S(1)} %bitcast.35), channel_id=1, replica_groups=mesh['macro'=16,'krow'=32] {'krow'}, dimensions={0} | all-to-all | bytes 294912 | tf_op jit(solution)/shard_map/all_to_all | solution.py:391
  86.2 0.4 shard_map.109
  86.6 13.8 %all_to_all.43 = f32[32,1,1024]{2,1,0:T(1,128)S(1)} all-to-all(f32[32,1,1024]{2,1,0:T(1,128)S(1)} %bitcast.37), channel_id=1, replica_groups=mesh['macro'=16,'krow'=32] {'krow'}, dimensions={0} | all-to-all | bytes 262144 | tf_op jit(solution)/shard_map/all_to_all | solution.py:391
  100.4 0.6 shard_map.110
  101.0 14.0 %all_to_all.44 = f32[32,1,1152]{2,1,0:T(1,128)S(1)} all-to-all(f32[32,1,1152]{2,1,0:T(1,128)S(1)} %bitcast.36), channel_id=1, replica_groups=mesh['macro'=16,'krow'=32] {'krow'}, dimensions={0} | all-to-all | bytes 294912 | tf_op jit(solution)/shard_map/all_to_all | solution.py:391
  115.0 1.3 collective-permute-start.2
  116.3 0.5 shard_map.111
  116.8 0.8 collective-permute-done.2.row_ref
  117.6 19.6 %all_to_all.45 = f32[32,1,1152]{2,1,0:T(1,128)S(1)} all-to-all(f32[32,1,1152]{2,1,0:T(1,128)S(1)} %bitcast.27), channel_id=1, replica_groups=mesh['macro'=16,'krow'=32] {'krow'}, dimensions={0} | all-to-all | bytes 294912 | tf_op jit(solution)/shard_map/all_to_all | solution.py:391
  137.3 1.0 shard_map.114
  (17 shorter events, 0.1 us)
Async XLA Ops:
  0.6 22.6 %copy-start.2 = (bf16[3,2,128,256]{3,2,1,0:T(8,128)(2,1)S(1)}, bf16[3,2,128,256]{3,2,1,0:T(8,128)(2,1)}, u32[]{:S(2)}) copy-start(bf16[3,2,128,256]{3,2,1,0:T(8,128)(2,1)} %constant.10.clone.left_ref) | copy-start | bytes 1179652
  2.8 20.4 %copy-start.4 = (f32[2,256,128]{2,1,0:T(8,128)S(1)}, f32[2,256,128]{2,1,0:T(8,128)}, u32[]{:S(2)}) copy-start(f32[2,256,128]{2,1,0:T(8,128)} %constant.11.clone.spectrum_ref) | copy-start | bytes 786436
  23.2 15.9 %copy-start = (bf16[3,256,256]{2,1,0:T(8,128)(2,1)S(1)}, bf16[3,256,256]{2,1,0:T(8,128)(2,1)}, u32[]{:S(2)}) copy-start(bf16[3,256,256]{2,1,0:T(8,128)(2,1)} %constant.8.clone.refs_1_.refs_5_.refs_7_.refs_6_) | copy-start | bytes 1179652
  23.2 15.9 %copy-start.3 = (bf16[3,256,128]{2,1,0:T(8,128)(2,1)S(1)}, bf16[3,256,128]{2,1,0:T(8,128)(2,1)}, u32[]{:S(2)}) copy-start(bf16[3,256,128]{2,1,0:T(8,128)(2,1)} %constant.9.clone.refs_2_.refs_6_.refs_8_.refs_7_) | copy-start | bytes 589828
  23.2 15.9 %copy-start.5 = (f32[1,16,8,256]{3,2,1,0:T(8,128)S(1)}, f32[1,16,8,256]{3,2,1,0:T(8,128)}, u32[]{:S(2)}) copy-start(f32[1,16,8,256]{3,2,1,0:T(8,128)} %param.9) | copy-start | bytes 393220
  23.2 15.9 %copy-start.6 = (f32[5,8,256]{2,1,0:T(8,128)S(1)}, f32[5,8,256]{2,1,0:T(8,128)}, u32[]{:S(2)}) copy-start(f32[5,8,256]{2,1,0:T(8,128)} %get-tuple-element.22.refs_2_.refs_3_.refs_4_) | copy-start | bytes 122884
  24.3 14.8 %copy-start.1 = (f32[2,16,8,256]{3,2,1,0:T(8,128)S(1)}, f32[2,16,8,256]{3,2,1,0:T(8,128)}, u32[]{:S(2)}) copy-start(f32[2,16,8,256]{3,2,1,0:T(8,128)} %refs_4_.7) | copy-start | bytes 786436
  24.3 14.8 %all-to-all-start.1 = ((f32[32,1,1024]{2,1,0:T(1,128)}), f32[32,1,1024]{2,1,0:T(1,128)S(1)}, u32[]{:S(2)}, u32[]{:S(2)}) async-start(f32[32,1,1024]{2,1,0:T(1,128)} %bitcast.4), calls=%async_computation.1 | async-start | bytes 262144 | tf_op jit(solution)/shard_map/all_to_all | solution.py:391
  28.8 10.2 %collective-permute-start = (f32[1,128]{1,0:T(1,128)S(1)}, f32[1,128]{1,0:T(1,128)S(1)}, u32[]{:S(2)}, u32[]{:S(2)}) collective-permute-start(f32[1,128]{1,0:T(1,128)S(1)} %get-tuple-element.23), channel_id=1, source_target_pairs={{0,256},{32,288},{64,320},{96,352},{128,384},{160,416},{192,448},{... | collective-permute-start | bytes 1544 | tf_op jit(solution)/shard_map/ppermute | solution.py:456
  57.6 14.1 %all-to-all-start.3 = ((f32[32,1,1024]{2,1,0:T(1,128)}), f32[32,1,1024]{2,1,0:T(1,128)S(1)}, u32[]{:S(2)}, u32[]{:S(2)}) async-start(f32[32,1,1024]{2,1,0:T(1,128)} %bitcast.8), calls=%async_computation.3 | async-start | bytes 262144 | tf_op jit(solution)/shard_map/all_to_all | solution.py:391
  61.9 4.7 %collective-permute-start.1 = (f32[1,128]{1,0:T(1,128)S(1)}, f32[1,128]{1,0:T(1,128)S(1)}, u32[]{:S(2)}, u32[]{:S(2)}) collective-permute-start(f32[1,128]{1,0:T(1,128)S(1)} %get-tuple-element.27.refs_5_), channel_id=1, source_target_pairs={{0,256},{32,288},{64,320},{96,352},{128,384},{160,416},{192,448},{... | collective-permute-start | bytes 1544 | tf_op jit(solution)/shard_map/ppermute | solution.py:456
  115.0 2.6 %collective-permute-start.2 = (f32[1,128]{1,0:T(1,128)S(1)}, f32[1,128]{1,0:T(1,128)S(1)}, u32[]{:S(2)}, u32[]{:S(2)}) collective-permute-start(f32[1,128]{1,0:T(1,128)S(1)} %shard_map.112), channel_id=1, source_target_pairs={{0,256},{32,288},{64,320},{96,352},{128,384},{160,416},{192,448},{... | collective-permute-start | bytes 1544 | tf_op jit(solution)/shard_map/ppermute | solution.py:441

commit v17 on v13

--- a/solution.py
+++ b/solution.py
@@ -219,40 +219,39 @@
     return real, imag
 
 
-def signed_product(total, x, y, sign):
-    term = x * y
-    if total is None:
-        return term if sign > 0 else -term
-    return total + term if sign > 0 else total - term
-
-
 def commute(hamilton, channels):
     hr, hi = unpack(hamilton)
     rr, ri = unpack(channels)
 
-    def product(a, b):
-        real = imag = None
-        for m in range(BANDS):
-            real = signed_product(real, hr[a][m], rr[m][b], 1)
-            if hi[a][m] is not None and ri[m][b] is not None:
-                real = signed_product(
-                    real, hi[a][m][0], ri[m][b][0], -hi[a][m][1] * ri[m][b][1]
-                )
-            if ri[m][b] is not None:
-                imag = signed_product(imag, hr[a][m], ri[m][b][0], ri[m][b][1])
-            if hi[a][m] is not None:
-                imag = signed_product(imag, hi[a][m][0], rr[m][b], hi[a][m][1])
+    def add_product(real, imag, left, right, a, m, b, sign):
+        (lr, li), (qr, qi) = left, right
+        x, p = li[a][m]
+        y, q = qi[m][b]
+        for term, s in ((lr[a][m] * qr[m][b], sign), (x * y, -sign * p * q)):
+            real = real + term if s > 0 else real - term
+        for term, s in ((lr[a][m] * y, sign * q), (x * qr[m][b], sign * p)):
+            imag = imag + term if s > 0 else imag - term
         return real, imag
 
-    diagonal = [2.0 * product(a, a)[1] for a in range(BANDS)]
+    diagonal = [None] * BANDS
     upper_real = []
     upper_imag = []
     for a, b in PAIRS:
-        real_ab, imag_ab = product(a, b)
-        real_ba, imag_ba = product(b, a)
-        upper_real.append(imag_ab + imag_ba)
-        upper_imag.append(real_ba - real_ab)
-    return diagonal + upper_real + upper_imag
+        own, other = hi[a][b][0], ri[a][b][0]
+        flow = own * rr[a][b] - hr[a][b] * other
+        diagonal[a] = flow if diagonal[a] is None else diagonal[a] + flow
+        diagonal[b] = -flow if diagonal[b] is None else diagonal[b] - flow
+        gap = hr[a][a] - hr[b][b]
+        filling = rr[b][b] - rr[a][a]
+        real = gap * rr[a][b] + filling * hr[a][b]
+        imag = gap * other + filling * own
+        for m in range(BANDS):
+            if m not in (a, b):
+                real, imag = add_product(real, imag, (hr, hi), (rr, ri), a, m, b, 1)
+                real, imag = add_product(real, imag, (rr, ri), (hr, hi), a, m, b, -1)
+        upper_real.append(imag)
+        upper_imag.append(-real)
+    return [2.0 * value for value in diagonal] + upper_real + upper_imag
 
 
 def state_kernel(section, *refs):

time: 139 us -> 139 us (level)
  no operation moved by 1% of the time
where the time goes in v17:
time: 139 us; the launch traced here: 138 us
  blocking collectives  98.7 us (71%)
  starting transfers between devices  22.4 us (16%)
  waiting for transfers between devices  8.5 us (6%)
  Pallas kernels  7.85 us (6%)
    all_to_all x6, blocking collectives, swap(): return lax.all_to_all(blocks, 'krow', 0, 0, tiled=True).reshape(x.shape)  98.7 us
    ppermute x2, starting transfers between devices, per_device(): extra = extra + [lax.ppermute(total, ('macro', 'krow'), exchange)]  12.4 us
    all_to_all x2, starting transfers between devices, swap(): return lax.all_to_all(blocks, 'krow', 0, 0, tiled=True).reshape(x.shape)  8.79 us
    pallas_call x11, Pallas kernels, call(): pl.pallas_call(body, out_shape=shapes, in_specs=[hbm if n in in_hbm else...  7.85 us
    all_to_all x2, waiting for transfers between devices, swap(): return lax.all_to_all(blocks, 'krow', 0, 0, tiled=True).reshape(x.shape)  5.1 us
  transfers between devices with their start and end apart: 5, of which 4 were waited for; matrix products, arithmetic and copies ran while one was open for 0% of the time, Pallas kernels for 0%

profile of v17, /device:TPU:8, one launch (start us, length us, event | category | flops | bytes accessed | tf_op | source)
XLA Modules:
  0.0 138.3 jit_solution(13528656333934552436)
XLA Ops:
  0.6 2.2 %shard_map.104 = (f32[288,128]{1,0:T(8,128)}, f32[5,8,256]{2,1,0:T(8,128)}) custom-call(f32[16,8,256]{2,1,0:T(8,128)} %bitcast.19, bf16[3,256,256]{2,1,0:T(8,128)(2,1)} %constant.8.clone.refs_1_.refs_5_.refs_7_.refs_6_.refs_9_, bf16[3,256,128]{2,1,0:T(8,128)(2,1)} %constant.9.clone.refs_2_.refs_6_.refs_8_.refs_7_.refs_10_, f32[2,16,8,256]{3,2,1,0:T(8,128)} %refs_6_.3, ...), custom_call_target="tpu_custom_call" | custom-call | flops 50331648 | bytes 1048576 | tf_op jit(solution)/shard_map/pallas_call | solution.py:352
  2.8 20.3 %all_to_all.40 = f32[32,1,1152]{2,1,0:T(1,128)S(1)} all-to-all(f32[32,1,1152]{2,1,0:T(1,128)} %bitcast.38), channel_id=1, replica_groups=mesh['macro'=16,'krow'=32] {'krow'}, dimensions={0} | all-to-all | bytes 294912 | tf_op jit(solution)/shard_map/all_to_all | solution.py:367
  23.2 1.1 shard_map.105
  24.3 4.5 %all-to-all-start.1 = ((f32[32,1,1024]{2,1,0:T(1,128)}), f32[32,1,1024]{2,1,0:T(1,128)S(1)}, u32[]{:S(2)}, u32[]{:S(2)}) async-start(f32[32,1,1024]{2,1,0:T(1,128)} %bitcast.4), calls=%async_computation.1 | async-start | bytes 262144 | tf_op jit(solution)/shard_map/all_to_all | solution.py:367
  28.8 9.0 %collective-permute-start = (f32[1,128]{1,0:T(1,128)S(1)}, f32[1,128]{1,0:T(1,128)S(1)}, u32[]{:S(2)}, u32[]{:S(2)}) collective-permute-start(f32[1,128]{1,0:T(1,128)S(1)} %get-tuple-element.21), channel_id=1, source_target_pairs={{0,256},{32,288},{64,320},{96,352},{128,384},{160,416},{192,448},{... | collective-permute-start | bytes 1544 | tf_op jit(solution)/shard_map/ppermute | solution.py:423
  37.8 1.3 collective-permute-done.refs_4_
  39.1 0.5 shard_map.106
  39.6 16.8 %all_to_all.41 = f32[32,1,1152]{2,1,0:T(1,128)S(1)} all-to-all(f32[32,1,1152]{2,1,0:T(1,128)S(1)} %bitcast.34), channel_id=1, replica_groups=mesh['macro'=16,'krow'=32] {'krow'}, dimensions={0} | all-to-all | bytes 294912 | tf_op jit(solution)/shard_map/all_to_all | solution.py:367
  56.5 1.1 shard_map.107
  57.5 4.3 %all-to-all-start.3 = ((f32[32,1,1024]{2,1,0:T(1,128)}), f32[32,1,1024]{2,1,0:T(1,128)S(1)}, u32[]{:S(2)}, u32[]{:S(2)}) async-start(f32[32,1,1024]{2,1,0:T(1,128)} %bitcast.8), calls=%async_computation.3 | async-start | bytes 262144 | tf_op jit(solution)/shard_map/all_to_all | solution.py:367
  61.8 3.4 %collective-permute-start.1 = (f32[1,128]{1,0:T(1,128)S(1)}, f32[1,128]{1,0:T(1,128)S(1)}, u32[]{:S(2)}, u32[]{:S(2)}) collective-permute-start(f32[1,128]{1,0:T(1,128)S(1)} %get-tuple-element.25.refs_5_.refs_7_), channel_id=1, source_target_pairs={{0,256},{32,288},{64,320},{96,352},{128,384},{160,416},{192,448},{... | collective-permute-start | bytes 1544 | tf_op jit(solution)/shard_map/ppermute | solution.py:423
  65.2 1.3 collective-permute-done.1.refs_6_
  66.5 5.1 %all-to-all-done.3 = f32[32,1,1024]{2,1,0:T(1,128)S(1)} async-done(((f32[32,1,1024]{2,1,0:T(1,128)}), f32[32,1,1024]{2,1,0:T(1,128)S(1)}, u32[]{:S(2)}, u32[]{:S(2)}) %all-to-all-start.3) | async-done | bytes 131104 | tf_op jit(solution)/shard_map/all_to_all | solution.py:367
  71.6 0.5 shard_map.108
  72.1 14.0 %all_to_all.42 = f32[32,1,1152]{2,1,0:T(1,128)S(1)} all-to-all(f32[32,1,1152]{2,1,0:T(1,128)S(1)} %bitcast.35), channel_id=1, replica_groups=mesh['macro'=16,'krow'=32] {'krow'}, dimensions={0} | all-to-all | bytes 294912 | tf_op jit(solution)/shard_map/all_to_all | solution.py:367
  86.1 0.4 shard_map.109
  86.6 13.8 %all_to_all.43 = f32[32,1,1024]{2,1,0:T(1,128)S(1)} all-to-all(f32[32,1,1024]{2,1,0:T(1,128)S(1)} %bitcast.37), channel_id=1, replica_groups=mesh['macro'=16,'krow'=32] {'krow'}, dimensions={0} | all-to-all | bytes 262144 | tf_op jit(solution)/shard_map/all_to_all | solution.py:367
  100.4 0.5 shard_map.110
  100.9 14.0 %all_to_all.44 = f32[32,1,1152]{2,1,0:T(1,128)S(1)} all-to-all(f32[32,1,1152]{2,1,0:T(1,128)S(1)} %bitcast.36), channel_id=1, replica_groups=mesh['macro'=16,'krow'=32] {'krow'}, dimensions={0} | all-to-all | bytes 294912 | tf_op jit(solution)/shard_map/all_to_all | solution.py:367
  115.0 1.3 collective-permute-start.2
  116.3 0.4 shard_map.111.blocks_ref
  116.7 0.8 collective-permute-done.2.row_ref
  117.6 19.6 %all_to_all.45 = f32[32,1,1152]{2,1,0:T(1,128)S(1)} all-to-all(f32[32,1,1152]{2,1,0:T(1,128)S(1)} %bitcast.24), channel_id=1, replica_groups=mesh['macro'=16,'krow'=32] {'krow'}, dimensions={0} | all-to-all | bytes 294912 | tf_op jit(solution)/shard_map/all_to_all | solution.py:367
  137.2 1.0 shard_map.114
  (17 shorter events, 0.1 us)
Async XLA Ops:
  0.6 22.5 %copy-start.2 = (bf16[3,2,128,256]{3,2,1,0:T(8,128)(2,1)S(1)}, bf16[3,2,128,256]{3,2,1,0:T(8,128)(2,1)}, u32[]{:S(2)}) copy-start(bf16[3,2,128,256]{3,2,1,0:T(8,128)(2,1)} %constant.10.clone.left_ref) | copy-start | bytes 1179652
  2.8 20.4 %copy-start.4 = (f32[2,256,128]{2,1,0:T(8,128)S(1)}, f32[2,256,128]{2,1,0:T(8,128)}, u32[]{:S(2)}) copy-start(f32[2,256,128]{2,1,0:T(8,128)} %constant.11.clone.spectrum_ref) | copy-start | bytes 786436
  23.2 15.9 %copy-start = (bf16[3,256,256]{2,1,0:T(8,128)(2,1)S(1)}, bf16[3,256,256]{2,1,0:T(8,128)(2,1)}, u32[]{:S(2)}) copy-start(bf16[3,256,256]{2,1,0:T(8,128)(2,1)} %constant.8.clone.refs_1_.refs_5_.refs_7_.refs_6_.refs_9_) | copy-start | bytes 1179652
  23.2 15.9 %copy-start.3 = (bf16[3,256,128]{2,1,0:T(8,128)(2,1)S(1)}, bf16[3,256,128]{2,1,0:T(8,128)(2,1)}, u32[]{:S(2)}) copy-start(bf16[3,256,128]{2,1,0:T(8,128)(2,1)} %constant.9.clone.refs_2_.refs_6_.refs_8_.refs_7_.refs_10_) | copy-start | bytes 589828
  23.2 15.9 %copy-start.5 = (f32[1,16,8,256]{3,2,1,0:T(8,128)S(1)}, f32[1,16,8,256]{3,2,1,0:T(8,128)}, u32[]{:S(2)}) copy-start(f32[1,16,8,256]{3,2,1,0:T(8,128)} %param.9) | copy-start | bytes 393220
  23.2 15.9 %copy-start.6 = (f32[5,8,256]{2,1,0:T(8,128)S(1)}, f32[5,8,256]{2,1,0:T(8,128)}, u32[]{:S(2)}) copy-start(f32[5,8,256]{2,1,0:T(8,128)} %get-tuple-element.20.refs_2_.refs_3_.refs_5_) | copy-start | bytes 122884
  24.3 14.8 %copy-start.1 = (f32[2,16,8,256]{3,2,1,0:T(8,128)S(1)}, f32[2,16,8,256]{3,2,1,0:T(8,128)}, u32[]{:S(2)}) copy-start(f32[2,16,8,256]{3,2,1,0:T(8,128)} %refs_6_.3) | copy-start | bytes 786436
  24.3 14.8 %all-to-all-start.1 = ((f32[32,1,1024]{2,1,0:T(1,128)}), f32[32,1,1024]{2,1,0:T(1,128)S(1)}, u32[]{:S(2)}, u32[]{:S(2)}) async-start(f32[32,1,1024]{2,1,0:T(1,128)} %bitcast.4), calls=%async_computation.1 | async-start | bytes 262144 | tf_op jit(solution)/shard_map/all_to_all | solution.py:367
  28.8 10.2 %collective-permute-start = (f32[1,128]{1,0:T(1,128)S(1)}, f32[1,128]{1,0:T(1,128)S(1)}, u32[]{:S(2)}, u32[]{:S(2)}) collective-permute-start(f32[1,128]{1,0:T(1,128)S(1)} %get-tuple-element.21), channel_id=1, source_target_pairs={{0,256},{32,288},{64,320},{96,352},{128,384},{160,416},{192,448},{... | collective-permute-start | bytes 1544 | tf_op jit(solution)/shard_map/ppermute | solution.py:423
  57.5 14.1 %all-to-all-start.3 = ((f32[32,1,1024]{2,1,0:T(1,128)}), f32[32,1,1024]{2,1,0:T(1,128)S(1)}, u32[]{:S(2)}, u32[]{:S(2)}) async-start(f32[32,1,1024]{2,1,0:T(1,128)} %bitcast.8), calls=%async_computation.3 | async-start | bytes 262144 | tf_op jit(solution)/shard_map/all_to_all | solution.py:367
  61.8 4.7 %collective-permute-start.1 = (f32[1,128]{1,0:T(1,128)S(1)}, f32[1,128]{1,0:T(1,128)S(1)}, u32[]{:S(2)}, u32[]{:S(2)}) collective-permute-start(f32[1,128]{1,0:T(1,128)S(1)} %get-tuple-element.25.refs_5_.refs_7_), channel_id=1, source_target_pairs={{0,256},{32,288},{64,320},{96,352},{128,384},{160,416},{192,448},{... | collective-permute-start | bytes 1544 | tf_op jit(solution)/shard_map/ppermute | solution.py:423
  115.0 2.6 %collective-permute-start.2 = (f32[1,128]{1,0:T(1,128)S(1)}, f32[1,128]{1,0:T(1,128)S(1)}, u32[]{:S(2)}, u32[]{:S(2)}) collective-permute-start(f32[1,128]{1,0:T(1,128)S(1)} %shard_map.112), channel_id=1, source_target_pairs={{0,256},{32,288},{64,320},{96,352},{128,384},{160,416},{192,448},{... | collective-permute-start | bytes 1544 | tf_op jit(solution)/shard_map/ppermute | solution.py:417

commit v18 on v17

--- a/solution.py
+++ b/solution.py
@@ -124,15 +124,16 @@
 def add_currents(currents, key, c, momentum, value):
     for i in range(2):
         term = momentum[i] * value
-        term = term if c < BANDS else 2.0 * term
-        currents[key, i] = currents[key, i] + term if (key, i) in currents else term
+        place = (key, i, c < BANDS)
+        currents[place] = currents[place] + term if place in currents else term
 
 
 def currents_row(currents):
     lane = lax.broadcasted_iota(jnp.int32, (1, LANES), 1)
     row = jnp.zeros((1, LANES), jnp.float32)
-    for place, key in enumerate(sorted(currents)):
-        total = jnp.sum(jnp.sum(currents[key], axis=0, keepdims=True), axis=1, keepdims=True)
+    for place, (key, i) in enumerate(sorted({k[:2] for k in currents})):
+        both = currents[key, i, True] + 2.0 * currents[key, i, False]
+        total = jnp.sum(jnp.sum(both, axis=0, keepdims=True), axis=1, keepdims=True)
         row = jnp.where(lane == place, total, row)
     return row
 

time: 139 us -> 139 us (level)
  no operation moved by 1% of the time
where the time goes in v18:
time: 139 us; the launch traced here: 138 us
  blocking collectives  98.7 us (71%)
  starting transfers between devices  22.4 us (16%)
  waiting for transfers between devices  8.5 us (6%)
  Pallas kernels  7.86 us (6%)
    all_to_all x6, blocking collectives, swap(): return lax.all_to_all(blocks, 'krow', 0, 0, tiled=True).reshape(x.shape)  98.7 us
    ppermute x2, starting transfers between devices, per_device(): extra = extra + [lax.ppermute(total, ('macro', 'krow'), exchange)]  12.4 us
    all_to_all x2, starting transfers between devices, swap(): return lax.all_to_all(blocks, 'krow', 0, 0, tiled=True).reshape(x.shape)  8.78 us
    pallas_call x11, Pallas kernels, call(): pl.pallas_call(body, out_shape=shapes, in_specs=[hbm if n in in_hbm else...  7.86 us
    all_to_all x2, waiting for transfers between devices, swap(): return lax.all_to_all(blocks, 'krow', 0, 0, tiled=True).reshape(x.shape)  5.1 us
  transfers between devices with their start and end apart: 5, of which 4 were waited for; matrix products, arithmetic and copies ran while one was open for 0% of the time, Pallas kernels for 0%

profile of v18, /device:TPU:8, one launch (start us, length us, event | category | flops | bytes accessed | tf_op | source)
XLA Modules:
  0.0 138.3 jit_solution(9233006577602036205)
XLA Ops:
  0.6 2.2 %shard_map.104 = (f32[288,128]{1,0:T(8,128)}, f32[5,8,256]{2,1,0:T(8,128)}) custom-call(f32[16,8,256]{2,1,0:T(8,128)} %bitcast.19, bf16[3,256,256]{2,1,0:T(8,128)(2,1)} %constant.8.clone.refs_1_.refs_5_.refs_7_.refs_6_.refs_9_, bf16[3,256,128]{2,1,0:T(8,128)(2,1)} %constant.9.clone.refs_2_.refs_6_.refs_8_.refs_7_.refs_10_, f32[2,16,8,256]{3,2,1,0:T(8,128)} %refs_6_.3, ...), custom_call_target="tpu_custom_call" | custom-call | flops 50331648 | bytes 1048576 | tf_op jit(solution)/shard_map/pallas_call | solution.py:353
  2.8 20.3 %all_to_all.40 = f32[32,1,1152]{2,1,0:T(1,128)S(1)} all-to-all(f32[32,1,1152]{2,1,0:T(1,128)} %bitcast.38), channel_id=1, replica_groups=mesh['macro'=16,'krow'=32] {'krow'}, dimensions={0} | all-to-all | bytes 294912 | tf_op jit(solution)/shard_map/all_to_all | solution.py:368
  23.2 1.1 shard_map.105
  24.3 4.5 %all-to-all-start.1 = ((f32[32,1,1024]{2,1,0:T(1,128)}), f32[32,1,1024]{2,1,0:T(1,128)S(1)}, u32[]{:S(2)}, u32[]{:S(2)}) async-start(f32[32,1,1024]{2,1,0:T(1,128)} %bitcast.4), calls=%async_computation.1 | async-start | bytes 262144 | tf_op jit(solution)/shard_map/all_to_all | solution.py:368
  28.8 9.0 %collective-permute-start = (f32[1,128]{1,0:T(1,128)S(1)}, f32[1,128]{1,0:T(1,128)S(1)}, u32[]{:S(2)}, u32[]{:S(2)}) collective-permute-start(f32[1,128]{1,0:T(1,128)S(1)} %get-tuple-element.21), channel_id=1, source_target_pairs={{0,256},{32,288},{64,320},{96,352},{128,384},{160,416},{192,448},{... | collective-permute-start | bytes 1544 | tf_op jit(solution)/shard_map/ppermute | solution.py:424
  37.8 1.3 collective-permute-done.refs_4_
  39.1 0.5 shard_map.106
  39.6 16.8 %all_to_all.41 = f32[32,1,1152]{2,1,0:T(1,128)S(1)} all-to-all(f32[32,1,1152]{2,1,0:T(1,128)S(1)} %bitcast.34), channel_id=1, replica_groups=mesh['macro'=16,'krow'=32] {'krow'}, dimensions={0} | all-to-all | bytes 294912 | tf_op jit(solution)/shard_map/all_to_all | solution.py:368
  56.5 1.1 shard_map.107
  57.5 4.3 %all-to-all-start.3 = ((f32[32,1,1024]{2,1,0:T(1,128)}), f32[32,1,1024]{2,1,0:T(1,128)S(1)}, u32[]{:S(2)}, u32[]{:S(2)}) async-start(f32[32,1,1024]{2,1,0:T(1,128)} %bitcast.8), calls=%async_computation.3 | async-start | bytes 262144 | tf_op jit(solution)/shard_map/all_to_all | solution.py:368
  61.8 3.4 %collective-permute-start.1 = (f32[1,128]{1,0:T(1,128)S(1)}, f32[1,128]{1,0:T(1,128)S(1)}, u32[]{:S(2)}, u32[]{:S(2)}) collective-permute-start(f32[1,128]{1,0:T(1,128)S(1)} %get-tuple-element.25.refs_5_.refs_7_), channel_id=1, source_target_pairs={{0,256},{32,288},{64,320},{96,352},{128,384},{160,416},{192,448},{... | collective-permute-start | bytes 1544 | tf_op jit(solution)/shard_map/ppermute | solution.py:424
  65.2 1.3 collective-permute-done.1.refs_6_
  66.5 5.1 %all-to-all-done.3 = f32[32,1,1024]{2,1,0:T(1,128)S(1)} async-done(((f32[32,1,1024]{2,1,0:T(1,128)}), f32[32,1,1024]{2,1,0:T(1,128)S(1)}, u32[]{:S(2)}, u32[]{:S(2)}) %all-to-all-start.3) | async-done | bytes 131104 | tf_op jit(solution)/shard_map/all_to_all | solution.py:368
  71.6 0.5 shard_map.108
  72.1 14.0 %all_to_all.42 = f32[32,1,1152]{2,1,0:T(1,128)S(1)} all-to-all(f32[32,1,1152]{2,1,0:T(1,128)S(1)} %bitcast.35), channel_id=1, replica_groups=mesh['macro'=16,'krow'=32] {'krow'}, dimensions={0} | all-to-all | bytes 294912 | tf_op jit(solution)/shard_map/all_to_all | solution.py:368
  86.1 0.4 shard_map.109
  86.6 13.8 %all_to_all.43 = f32[32,1,1024]{2,1,0:T(1,128)S(1)} all-to-all(f32[32,1,1024]{2,1,0:T(1,128)S(1)} %bitcast.37), channel_id=1, replica_groups=mesh['macro'=16,'krow'=32] {'krow'}, dimensions={0} | all-to-all | bytes 262144 | tf_op jit(solution)/shard_map/all_to_all | solution.py:368
  100.4 0.6 shard_map.110
  100.9 14.0 %all_to_all.44 = f32[32,1,1152]{2,1,0:T(1,128)S(1)} all-to-all(f32[32,1,1152]{2,1,0:T(1,128)S(1)} %bitcast.36), channel_id=1, replica_groups=mesh['macro'=16,'krow'=32] {'krow'}, dimensions={0} | all-to-all | bytes 294912 | tf_op jit(solution)/shard_map/all_to_all | solution.py:368
  115.0 1.3 collective-permute-start.2
  116.3 0.4 shard_map.111.blocks_ref
  116.7 0.9 collective-permute-done.2.row_ref
  117.6 19.7 %all_to_all.45 = f32[32,1,1152]{2,1,0:T(1,128)S(1)} all-to-all(f32[32,1,1152]{2,1,0:T(1,128)S(1)} %bitcast.24), channel_id=1, replica_groups=mesh['macro'=16,'krow'=32] {'krow'}, dimensions={0} | all-to-all | bytes 294912 | tf_op jit(solution)/shard_map/all_to_all | solution.py:368
  137.2 1.0 shard_map.114
  (17 shorter events, 0.1 us)
Async XLA Ops:
  0.6 22.5 %copy-start.2 = (bf16[3,2,128,256]{3,2,1,0:T(8,128)(2,1)S(1)}, bf16[3,2,128,256]{3,2,1,0:T(8,128)(2,1)}, u32[]{:S(2)}) copy-start(bf16[3,2,128,256]{3,2,1,0:T(8,128)(2,1)} %constant.10.clone.left_ref) | copy-start | bytes 1179652
  2.8 20.4 %copy-start.4 = (f32[2,256,128]{2,1,0:T(8,128)S(1)}, f32[2,256,128]{2,1,0:T(8,128)}, u32[]{:S(2)}) copy-start(f32[2,256,128]{2,1,0:T(8,128)} %constant.11.clone.spectrum_ref) | copy-start | bytes 786436
  23.2 15.9 %copy-start = (bf16[3,256,256]{2,1,0:T(8,128)(2,1)S(1)}, bf16[3,256,256]{2,1,0:T(8,128)(2,1)}, u32[]{:S(2)}) copy-start(bf16[3,256,256]{2,1,0:T(8,128)(2,1)} %constant.8.clone.refs_1_.refs_5_.refs_7_.refs_6_.refs_9_) | copy-start | bytes 1179652
  23.2 15.9 %copy-start.3 = (bf16[3,256,128]{2,1,0:T(8,128)(2,1)S(1)}, bf16[3,256,128]{2,1,0:T(8,128)(2,1)}, u32[]{:S(2)}) copy-start(bf16[3,256,128]{2,1,0:T(8,128)(2,1)} %constant.9.clone.refs_2_.refs_6_.refs_8_.refs_7_.refs_10_) | copy-start | bytes 589828
  23.2 15.9 %copy-start.5 = (f32[1,16,8,256]{3,2,1,0:T(8,128)S(1)}, f32[1,16,8,256]{3,2,1,0:T(8,128)}, u32[]{:S(2)}) copy-start(f32[1,16,8,256]{3,2,1,0:T(8,128)} %param.9) | copy-start | bytes 393220
  23.2 15.9 %copy-start.6 = (f32[5,8,256]{2,1,0:T(8,128)S(1)}, f32[5,8,256]{2,1,0:T(8,128)}, u32[]{:S(2)}) copy-start(f32[5,8,256]{2,1,0:T(8,128)} %get-tuple-element.20.refs_2_.refs_3_.refs_5_) | copy-start | bytes 122884
  24.3 14.8 %copy-start.1 = (f32[2,16,8,256]{3,2,1,0:T(8,128)S(1)}, f32[2,16,8,256]{3,2,1,0:T(8,128)}, u32[]{:S(2)}) copy-start(f32[2,16,8,256]{3,2,1,0:T(8,128)} %refs_6_.3) | copy-start | bytes 786436
  24.3 14.8 %all-to-all-start.1 = ((f32[32,1,1024]{2,1,0:T(1,128)}), f32[32,1,1024]{2,1,0:T(1,128)S(1)}, u32[]{:S(2)}, u32[]{:S(2)}) async-start(f32[32,1,1024]{2,1,0:T(1,128)} %bitcast.4), calls=%async_computation.1 | async-start | bytes 262144 | tf_op jit(solution)/shard_map/all_to_all | solution.py:368
  28.8 10.3 %collective-permute-start = (f32[1,128]{1,0:T(1,128)S(1)}, f32[1,128]{1,0:T(1,128)S(1)}, u32[]{:S(2)}, u32[]{:S(2)}) collective-permute-start(f32[1,128]{1,0:T(1,128)S(1)} %get-tuple-element.21), channel_id=1, source_target_pairs={{0,256},{32,288},{64,320},{96,352},{128,384},{160,416},{192,448},{... | collective-permute-start | bytes 1544 | tf_op jit(solution)/shard_map/ppermute | solution.py:424
  57.5 14.1 %all-to-all-start.3 = ((f32[32,1,1024]{2,1,0:T(1,128)}), f32[32,1,1024]{2,1,0:T(1,128)S(1)}, u32[]{:S(2)}, u32[]{:S(2)}) async-start(f32[32,1,1024]{2,1,0:T(1,128)} %bitcast.8), calls=%async_computation.3 | async-start | bytes 262144 | tf_op jit(solution)/shard_map/all_to_all | solution.py:368
  61.8 4.7 %collective-permute-start.1 = (f32[1,128]{1,0:T(1,128)S(1)}, f32[1,128]{1,0:T(1,128)S(1)}, u32[]{:S(2)}, u32[]{:S(2)}) collective-permute-start(f32[1,128]{1,0:T(1,128)S(1)} %get-tuple-element.25.refs_5_.refs_7_), channel_id=1, source_target_pairs={{0,256},{32,288},{64,320},{96,352},{128,384},{160,416},{192,448},{... | collective-permute-start | bytes 1544 | tf_op jit(solution)/shard_map/ppermute | solution.py:424
  115.0 2.6 %collective-permute-start.2 = (f32[1,128]{1,0:T(1,128)S(1)}, f32[1,128]{1,0:T(1,128)S(1)}, u32[]{:S(2)}, u32[]{:S(2)}) collective-permute-start(f32[1,128]{1,0:T(1,128)S(1)} %shard_map.112), channel_id=1, source_target_pairs={{0,256},{32,288},{64,320},{96,352},{128,384},{160,416},{192,448},{... | collective-permute-start | bytes 1544 | tf_op jit(solution)/shard_map/ppermute | solution.py:418

commit v19 on v16

--- a/solution.py
+++ b/solution.py
@@ -219,40 +219,39 @@
     return real, imag
 
 
-def signed_product(total, x, y, sign):
-    term = x * y
-    if total is None:
-        return term if sign > 0 else -term
-    return total + term if sign > 0 else total - term
-
-
 def commute(hamilton, channels):
     hr, hi = unpack(hamilton)
     rr, ri = unpack(channels)
 
-    def product(a, b):
-        real = imag = None
-        for m in range(BANDS):
-            real = signed_product(real, hr[a][m], rr[m][b], 1)
-            if hi[a][m] is not None and ri[m][b] is not None:
-                real = signed_product(
-                    real, hi[a][m][0], ri[m][b][0], -hi[a][m][1] * ri[m][b][1]
-                )
-            if ri[m][b] is not None:
-                imag = signed_product(imag, hr[a][m], ri[m][b][0], ri[m][b][1])
-            if hi[a][m] is not None:
-                imag = signed_product(imag, hi[a][m][0], rr[m][b], hi[a][m][1])
+    def add_product(real, imag, left, right, a, m, b, sign):
+        (lr, li), (qr, qi) = left, right
+        x, p = li[a][m]
+        y, q = qi[m][b]
+        for term, s in ((lr[a][m] * qr[m][b], sign), (x * y, -sign * p * q)):
+            real = real + term if s > 0 else real - term
+        for term, s in ((lr[a][m] * y, sign * q), (x * qr[m][b], sign * p)):
+            imag = imag + term if s > 0 else imag - term
         return real, imag
 
-    diagonal = [2.0 * product(a, a)[1] for a in range(BANDS)]
+    diagonal = [None] * BANDS
     upper_real = []
     upper_imag = []
     for a, b in PAIRS:
-        real_ab, imag_ab = product(a, b)
-        real_ba, imag_ba = product(b, a)
-        upper_real.append(imag_ab + imag_ba)
-        upper_imag.append(real_ba - real_ab)
-    return diagonal + upper_real + upper_imag
+        own, other = hi[a][b][0], ri[a][b][0]
+        flow = own * rr[a][b] - hr[a][b] * other
+        diagonal[a] = flow if diagonal[a] is None else diagonal[a] + flow
+        diagonal[b] = -flow if diagonal[b] is None else diagonal[b] - flow
+        gap = hr[a][a] - hr[b][b]
+        filling = rr[b][b] - rr[a][a]
+        real = gap * rr[a][b] + filling * hr[a][b]
+        imag = gap * other + filling * own
+        for m in range(BANDS):
+            if m not in (a, b):
+                real, imag = add_product(real, imag, (hr, hi), (rr, ri), a, m, b, 1)
+                real, imag = add_product(real, imag, (rr, ri), (hr, hi), a, m, b, -1)
+        upper_real.append(imag)
+        upper_imag.append(-real)
+    return [2.0 * value for value in diagonal] + upper_real + upper_imag
 
 
 def last_kernel(first_ref, second_ref, third_ref, fourth_ref, fields_ref, momentum_ref, out_ref):

time: 139 us -> 139 us (level)
  no operation moved by 1% of the time
where the time goes in v19:
time: 139 us; the launch traced here: 138 us
  blocking collectives  98.7 us (71%)
  starting transfers between devices  22.4 us (16%)
  waiting for transfers between devices  8.43 us (6%)
  Pallas kernels  7.88 us (6%)
    all_to_all x6, blocking collectives, swap(): return lax.all_to_all(blocks, 'krow', 0, 0, tiled=True).reshape(x.shape)  98.7 us
    ppermute x2, starting transfers between devices, per_device(): extra = extra + [lax.ppermute(total, ('macro', 'krow'), exchange)]  12.4 us
    all_to_all x2, starting transfers between devices, swap(): return lax.all_to_all(blocks, 'krow', 0, 0, tiled=True).reshape(x.shape)  8.79 us
    pallas_call x11, Pallas kernels, call(): pl.pallas_call(body, out_shape=shapes, in_specs=[hbm if n in in_hbm else...  7.88 us
    all_to_all x2, waiting for transfers between devices, swap(): return lax.all_to_all(blocks, 'krow', 0, 0, tiled=True).reshape(x.shape)  5.1 us
  transfers between devices with their start and end apart: 5, of which 4 were waited for; matrix products, arithmetic and copies ran while one was open for 0% of the time, Pallas kernels for 0%

profile of v19, /device:TPU:8, one launch (start us, length us, event | category | flops | bytes accessed | tf_op | source)
XLA Modules:
  0.0 138.2 jit_solution(2644351300081990275)
XLA Ops:
  0.6 2.2 %shard_map.104 = (f32[288,128]{1,0:T(8,128)}, f32[5,8,256]{2,1,0:T(8,128)}) custom-call(f32[16,8,256]{2,1,0:T(8,128)} %bitcast.19, bf16[3,256,256]{2,1,0:T(8,128)(2,1)} %constant.8.clone.refs_1_.refs_5_.refs_7_.refs_6_, bf16[3,256,128]{2,1,0:T(8,128)(2,1)} %constant.9.clone.refs_2_.refs_6_.refs_8_.refs_7_, f32[2,16,8,256]{3,2,1,0:T(8,128)} %refs_4_.7, ...), custom_call_target="tpu_custom_call" | custom-call | flops 50331648 | bytes 1048576 | tf_op jit(solution)/shard_map/pallas_call | solution.py:375
  2.8 20.3 %all_to_all.40 = f32[32,1,1152]{2,1,0:T(1,128)S(1)} all-to-all(f32[32,1,1152]{2,1,0:T(1,128)} %bitcast.38), channel_id=1, replica_groups=mesh['macro'=16,'krow'=32] {'krow'}, dimensions={0} | all-to-all | bytes 294912 | tf_op jit(solution)/shard_map/all_to_all | solution.py:390
  23.2 1.1 shard_map.105
  24.3 4.5 %all-to-all-start.1 = ((f32[32,1,1024]{2,1,0:T(1,128)}), f32[32,1,1024]{2,1,0:T(1,128)S(1)}, u32[]{:S(2)}, u32[]{:S(2)}) async-start(f32[32,1,1024]{2,1,0:T(1,128)} %bitcast.4), calls=%async_computation.1 | async-start | bytes 262144 | tf_op jit(solution)/shard_map/all_to_all | solution.py:390
  28.8 9.0 %collective-permute-start = (f32[1,128]{1,0:T(1,128)S(1)}, f32[1,128]{1,0:T(1,128)S(1)}, u32[]{:S(2)}, u32[]{:S(2)}) collective-permute-start(f32[1,128]{1,0:T(1,128)S(1)} %get-tuple-element.23), channel_id=1, source_target_pairs={{0,256},{32,288},{64,320},{96,352},{128,384},{160,416},{192,448},{... | collective-permute-start | bytes 1544 | tf_op jit(solution)/shard_map/ppermute | solution.py:455
  37.8 1.3 collective-permute-done.refs_4_
  39.1 0.5 shard_map.106
  39.6 16.8 %all_to_all.41 = f32[32,1,1152]{2,1,0:T(1,128)S(1)} all-to-all(f32[32,1,1152]{2,1,0:T(1,128)S(1)} %bitcast.34), channel_id=1, replica_groups=mesh['macro'=16,'krow'=32] {'krow'}, dimensions={0} | all-to-all | bytes 294912 | tf_op jit(solution)/shard_map/all_to_all | solution.py:390
  56.5 1.1 shard_map.107
  57.6 4.3 %all-to-all-start.3 = ((f32[32,1,1024]{2,1,0:T(1,128)}), f32[32,1,1024]{2,1,0:T(1,128)S(1)}, u32[]{:S(2)}, u32[]{:S(2)}) async-start(f32[32,1,1024]{2,1,0:T(1,128)} %bitcast.8), calls=%async_computation.3 | async-start | bytes 262144 | tf_op jit(solution)/shard_map/all_to_all | solution.py:390
  61.8 3.4 %collective-permute-start.1 = (f32[1,128]{1,0:T(1,128)S(1)}, f32[1,128]{1,0:T(1,128)S(1)}, u32[]{:S(2)}, u32[]{:S(2)}) collective-permute-start(f32[1,128]{1,0:T(1,128)S(1)} %get-tuple-element.27.refs_5_), channel_id=1, source_target_pairs={{0,256},{32,288},{64,320},{96,352},{128,384},{160,416},{192,448},{... | collective-permute-start | bytes 1544 | tf_op jit(solution)/shard_map/ppermute | solution.py:455
  65.2 1.3 collective-permute-done.1.refs_6_
  66.5 5.1 %all-to-all-done.3 = f32[32,1,1024]{2,1,0:T(1,128)S(1)} async-done(((f32[32,1,1024]{2,1,0:T(1,128)}), f32[32,1,1024]{2,1,0:T(1,128)S(1)}, u32[]{:S(2)}, u32[]{:S(2)}) %all-to-all-start.3) | async-done | bytes 131104 | tf_op jit(solution)/shard_map/all_to_all | solution.py:390
  71.6 0.5 shard_map.108
  72.2 14.0 %all_to_all.42 = f32[32,1,1152]{2,1,0:T(1,128)S(1)} all-to-all(f32[32,1,1152]{2,1,0:T(1,128)S(1)} %bitcast.35), channel_id=1, replica_groups=mesh['macro'=16,'krow'=32] {'krow'}, dimensions={0} | all-to-all | bytes 294912 | tf_op jit(solution)/shard_map/all_to_all | solution.py:390
  86.1 0.4 shard_map.109
  86.6 13.8 %all_to_all.43 = f32[32,1,1024]{2,1,0:T(1,128)S(1)} all-to-all(f32[32,1,1024]{2,1,0:T(1,128)S(1)} %bitcast.37), channel_id=1, replica_groups=mesh['macro'=16,'krow'=32] {'krow'}, dimensions={0} | all-to-all | bytes 262144 | tf_op jit(solution)/shard_map/all_to_all | solution.py:390
  100.4 0.5 shard_map.110
  100.9 14.0 %all_to_all.44 = f32[32,1,1152]{2,1,0:T(1,128)S(1)} all-to-all(f32[32,1,1152]{2,1,0:T(1,128)S(1)} %bitcast.36), channel_id=1, replica_groups=mesh['macro'=16,'krow'=32] {'krow'}, dimensions={0} | all-to-all | bytes 294912 | tf_op jit(solution)/shard_map/all_to_all | solution.py:390
  115.0 1.3 collective-permute-start.2
  116.3 0.5 shard_map.111
  116.8 0.8 collective-permute-done.2.row_ref
  117.6 19.6 %all_to_all.45 = f32[32,1,1152]{2,1,0:T(1,128)S(1)} all-to-all(f32[32,1,1152]{2,1,0:T(1,128)S(1)} %bitcast.27), channel_id=1, replica_groups=mesh['macro'=16,'krow'=32] {'krow'}, dimensions={0} | all-to-all | bytes 294912 | tf_op jit(solution)/shard_map/all_to_all | solution.py:390
  137.2 1.0 shard_map.114
  (17 shorter events, 0.1 us)
Async XLA Ops:
  0.6 22.6 %copy-start.2 = (bf16[3,2,128,256]{3,2,1,0:T(8,128)(2,1)S(1)}, bf16[3,2,128,256]{3,2,1,0:T(8,128)(2,1)}, u32[]{:S(2)}) copy-start(bf16[3,2,128,256]{3,2,1,0:T(8,128)(2,1)} %constant.10.clone.left_ref) | copy-start | bytes 1179652
  2.8 20.4 %copy-start.4 = (f32[2,256,128]{2,1,0:T(8,128)S(1)}, f32[2,256,128]{2,1,0:T(8,128)}, u32[]{:S(2)}) copy-start(f32[2,256,128]{2,1,0:T(8,128)} %constant.11.clone.spectrum_ref) | copy-start | bytes 786436
  23.2 15.9 %copy-start = (bf16[3,256,256]{2,1,0:T(8,128)(2,1)S(1)}, bf16[3,256,256]{2,1,0:T(8,128)(2,1)}, u32[]{:S(2)}) copy-start(bf16[3,256,256]{2,1,0:T(8,128)(2,1)} %constant.8.clone.refs_1_.refs_5_.refs_7_.refs_6_) | copy-start | bytes 1179652
  23.2 15.9 %copy-start.3 = (bf16[3,256,128]{2,1,0:T(8,128)(2,1)S(1)}, bf16[3,256,128]{2,1,0:T(8,128)(2,1)}, u32[]{:S(2)}) copy-start(bf16[3,256,128]{2,1,0:T(8,128)(2,1)} %constant.9.clone.refs_2_.refs_6_.refs_8_.refs_7_) | copy-start | bytes 589828
  23.2 15.9 %copy-start.5 = (f32[1,16,8,256]{3,2,1,0:T(8,128)S(1)}, f32[1,16,8,256]{3,2,1,0:T(8,128)}, u32[]{:S(2)}) copy-start(f32[1,16,8,256]{3,2,1,0:T(8,128)} %param.9) | copy-start | bytes 393220
  23.2 15.9 %copy-start.6 = (f32[5,8,256]{2,1,0:T(8,128)S(1)}, f32[5,8,256]{2,1,0:T(8,128)}, u32[]{:S(2)}) copy-start(f32[5,8,256]{2,1,0:T(8,128)} %get-tuple-element.22.refs_2_.refs_3_.refs_4_) | copy-start | bytes 122884
  24.3 14.8 %copy-start.1 = (f32[2,16,8,256]{3,2,1,0:T(8,128)S(1)}, f32[2,16,8,256]{3,2,1,0:T(8,128)}, u32[]{:S(2)}) copy-start(f32[2,16,8,256]{3,2,1,0:T(8,128)} %refs_4_.7) | copy-start | bytes 786436
  24.3 14.8 %all-to-all-start.1 = ((f32[32,1,1024]{2,1,0:T(1,128)}), f32[32,1,1024]{2,1,0:T(1,128)S(1)}, u32[]{:S(2)}, u32[]{:S(2)}) async-start(f32[32,1,1024]{2,1,0:T(1,128)} %bitcast.4), calls=%async_computation.1 | async-start | bytes 262144 | tf_op jit(solution)/shard_map/all_to_all | solution.py:390
  28.8 10.2 %collective-permute-start = (f32[1,128]{1,0:T(1,128)S(1)}, f32[1,128]{1,0:T(1,128)S(1)}, u32[]{:S(2)}, u32[]{:S(2)}) collective-permute-start(f32[1,128]{1,0:T(1,128)S(1)} %get-tuple-element.23), channel_id=1, source_target_pairs={{0,256},{32,288},{64,320},{96,352},{128,384},{160,416},{192,448},{... | collective-permute-start | bytes 1544 | tf_op jit(solution)/shard_map/ppermute | solution.py:455
  57.6 14.1 %all-to-all-start.3 = ((f32[32,1,1024]{2,1,0:T(1,128)}), f32[32,1,1024]{2,1,0:T(1,128)S(1)}, u32[]{:S(2)}, u32[]{:S(2)}) async-start(f32[32,1,1024]{2,1,0:T(1,128)} %bitcast.8), calls=%async_computation.3 | async-start | bytes 262144 | tf_op jit(solution)/shard_map/all_to_all | solution.py:390
  61.8 4.7 %collective-permute-start.1 = (f32[1,128]{1,0:T(1,128)S(1)}, f32[1,128]{1,0:T(1,128)S(1)}, u32[]{:S(2)}, u32[]{:S(2)}) collective-permute-start(f32[1,128]{1,0:T(1,128)S(1)} %get-tuple-element.27.refs_5_), channel_id=1, source_target_pairs={{0,256},{32,288},{64,320},{96,352},{128,384},{160,416},{192,448},{... | collective-permute-start | bytes 1544 | tf_op jit(solution)/shard_map/ppermute | solution.py:455
  115.0 2.6 %collective-permute-start.2 = (f32[1,128]{1,0:T(1,128)S(1)}, f32[1,128]{1,0:T(1,128)S(1)}, u32[]{:S(2)}, u32[]{:S(2)}) collective-permute-start(f32[1,128]{1,0:T(1,128)S(1)} %shard_map.112), channel_id=1, source_target_pairs={{0,256},{32,288},{64,320},{96,352},{128,384},{160,416},{192,448},{... | collective-permute-start | bytes 1544 | tf_op jit(solution)/shard_map/ppermute | solution.py:440
